TPU v7x, 32 devices: a whole 2x2x4 slice. The times are simulated.
32 devices in a mesh: group: 2 (over y), gz: 4 (over z), gx: 2 (over x), af: 2 (over core).
Axes of the slice: x: 2, y: 2, z: 4, core: 2. Of those that a mesh axis runs over, the one named last changes fastest.
Arguments:
- voltage_lateral_component: float32 [2, 256, 64, 128], P('af', ('group', 'gz'), 'gx'), parts along dimension 1, may hold values from -6 to 6
- voltage_vertical_component: float32 [2, 256, 64, 128], P('af', ('group', 'gz'), 'gx'), parts along dimension 1, may hold values from -6 to 6
- voltage_forward_component: float32 [2, 256, 64, 128], P('af', ('group', 'gz'), 'gx'), parts along dimension 1, may hold values from -6 to 6
- induction_lateral_component: float32 [2, 256, 64, 128], P('af', ('group', 'gz'), 'gx'), parts along dimension 1, may hold values from -6 to 6
- induction_vertical_component: float32 [2, 256, 64, 128], P('af', ('group', 'gz'), 'gx'), parts along dimension 1, may hold values from -6 to 6
- induction_forward_component: float32 [2, 256, 64, 128], P('af', ('group', 'gz'), 'gx'), parts along dimension 1, may hold values from -6 to 6
- medium_code: int32 [256, 64, 128], P(('group', 'gz'), 'gx'), parts along dimension 0, may hold values from 0 to 2
- nonlinear_coefficient_matrix: float32 [2, 3], replicated, may hold values from 0.3 to 3
- mobile_charge_density: float32 [64, 16], P(('group', 'gz', 'gx')), parts along dimension 0, may hold values from 0.5 to 2
Outputs:
- electric_x_out: float32 [2, 256, 64, 128], P('af', ('group', 'gz'), 'gx'), parts along dimension 1
- electric_y_out: float32 [2, 256, 64, 128], P('af', ('group', 'gz'), 'gx'), parts along dimension 1
- electric_z_out: float32 [2, 256, 64, 128], P('af', ('group', 'gz'), 'gx'), parts along dimension 1
- magnetic_x_out: float32 [2, 256, 64, 128], P('af', ('group', 'gz'), 'gx'), parts along dimension 1
- magnetic_y_out: float32 [2, 256, 64, 128], P('af', ('group', 'gz'), 'gx'), parts along dimension 1
- magnetic_z_out: float32 [2, 256, 64, 128], P('af', ('group', 'gz'), 'gx'), parts along dimension 1
- density_out: float32 [64, 16], P(('group', 'gz', 'gx')), parts along dimension 0
There are 2 independent parts, one for each index of `group`. A program takes and returns all parts, laid end to end along the dimension named above; an argument that names none is the same for every part. Nothing has to cross between parts.
All inputs are finite; a program needn't handle non-finite values.
Results may differ from a plain program's by a relative error of at most 0.0001.
Values sent between devices are 32-bit elements; how exact they have to be, the bound alone decides.
No kernel may reach another device: no remote copies, remote signals or barrier semaphores. Data moves between devices by JAX's collectives and lax.ppermute only.
A program may use at most 64 MiB of HBM per device.

v0:
```python
import jax
import jax.numpy as jnp
from jax import lax
from jax.sharding import PartitionSpec as P

BLOCK_FACTOR = 4
SUBSTEPS = 4
ROUNDS = 2
CSTEPS = 8


COURANT = 0.5
SILICON_PERM = 12.1
OXIDE_PERM = 2.1
SPREAD_COEFF = 0.2
MOBILITY_TERM = 0.1
LIFETIME_DECAY = 0.05
SOURCE_FACTOR = 0.02


def from_behind(shard, axis, by):
    count = lax.axis_size(axis)
    pairs = [(i, i + by) for i in range(count) if 0 <= i + by < count]
    return lax.ppermute(shard, axis, pairs)


def extended(block, sides, width):
    for axis, dim in sides:
        count = lax.axis_size(axis)
        forward = [(i, i + 1) for i in range(count - 1)]
        backward = [(target, source) for source, target in forward]
        low = lax.ppermute(
            lax.slice_in_dim(block, block.shape[dim] - width, None, axis=dim), axis, forward
        )
        high = lax.ppermute(lax.slice_in_dim(block, 0, width, axis=dim), axis, backward)
        block = jnp.concatenate([low, block, high], axis=dim)
    return block


def partner(shard, axis, distance):
    return lax.ppermute(shard, axis, [(i, i ^ 1 << distance) for i in range(lax.axis_size(axis))])


def upper_tiles(stacked):
    border = from_behind(stacked[:, :, 0], "gz", -1)
    return jnp.concatenate([stacked[:, :, 1:], border[:, :, None]], 2)


def lower_tiles(stacked):
    border = from_behind(stacked[:, :, -1], "gz", 1)
    return jnp.concatenate([border[:, :, None], stacked[:, :, :-1]], 2)


def right_cols(stacked):
    border = from_behind(stacked[:, :, :, 0], "gx", -1)
    return jnp.concatenate([stacked[:, :, :, 1:], border[:, :, :, None]], 3)


def left_cols(stacked):
    border = from_behind(stacked[:, :, :, -1], "gx", 1)
    return jnp.concatenate([border[:, :, :, None], stacked[:, :, :, :-1]], 3)


def above_height(field):
    return jnp.concatenate([field[..., 1:], jnp.zeros_like(field[..., :1])], -1)


def below_height(field):
    return jnp.concatenate([jnp.zeros_like(field[..., :1]), field[..., :-1]], -1)


def advance(
    voltage_gradient,
    induction_vector,
    inten_sum,
    base_perm,
    silicon,
    coeffs,
    optical_grid_charge,
    fetch_upper,
    fetch_lower,
):
    kerr_gain = coeffs[:, 0][:, None, None, None]
    absorb_two = coeffs[:, 1][:, None, None, None]
    absorb_free = coeffs[:, 2][:, None, None, None]
    forward_voltage_x, lateral_voltage_y, vertical_voltage_z = voltage_gradient
    induction_forward_x, induction_lateral_y, induction_vertical_z = induction_vector
    ahead = fetch_upper(jnp.stack([forward_voltage_x, lateral_voltage_y]))
    aside = right_cols(jnp.stack([lateral_voltage_y, vertical_voltage_z]))
    induction_forward_x = induction_forward_x - COURANT * (
        above_height(vertical_voltage_z) - vertical_voltage_z - (ahead[1] - lateral_voltage_y)
    )
    induction_lateral_y = induction_lateral_y - COURANT * (
        ahead[0] - forward_voltage_x - (aside[1] - vertical_voltage_z)
    )
    induction_vertical_z = induction_vertical_z - COURANT * (
        aside[0] - lateral_voltage_y - (above_height(forward_voltage_x) - forward_voltage_x)
    )
    behind = fetch_lower(jnp.stack([induction_forward_x, induction_lateral_y]))
    beside = left_cols(jnp.stack([induction_lateral_y, induction_vertical_z]))
    curl_x = (
        induction_vertical_z
        - below_height(induction_vertical_z)
        - (induction_lateral_y - behind[1])
    )
    curl_y = induction_forward_x - behind[0] - (induction_vertical_z - beside[1])
    curl_z = (
        induction_lateral_y - beside[0] - (induction_forward_x - below_height(induction_forward_x))
    )
    permit = base_perm + silicon * kerr_gain * inten_sum
    losses = silicon * (absorb_two * inten_sum + absorb_free * optical_grid_charge)
    keeping = permit - 0.5 * losses
    divisor = permit + 0.5 * losses
    forward_voltage_x = (keeping * forward_voltage_x + COURANT * curl_x) / divisor
    lateral_voltage_y = (keeping * lateral_voltage_y + COURANT * curl_y) / divisor
    vertical_voltage_z = (keeping * vertical_voltage_z + COURANT * curl_z) / divisor
    return (
        (forward_voltage_x, lateral_voltage_y, vertical_voltage_z),
        (induction_forward_x, induction_lateral_y, induction_vertical_z),
    )


def restrict_mean(generation):
    rows = generation.shape[0] // BLOCK_FACTOR
    cols = generation.shape[1] // BLOCK_FACTOR
    return generation.reshape(rows, BLOCK_FACTOR, cols, BLOCK_FACTOR, generation.shape[2]).mean(
        axis=(1, 3, 4)
    )


def charge_update_pass(charge_density_step, blocky_pair_creation):
    for upsample_copy in range(CSTEPS):
        including_lines = extended(charge_density_step, ((("gz", "gx"), 0),), 1)
        bordered_array = jnp.pad(including_lines, ((0, 0), (1, 1)))
        upward_neighbor = bordered_array[2:, 1:-1]
        downward_neighbor = bordered_array[:-2, 1:-1]
        second_derivative_sum = (
            upward_neighbor
            + downward_neighbor
            + bordered_array[1:-1, 2:]
            + bordered_array[1:-1, :-2]
            - 4.0 * charge_density_step
        )
        charge_density_step = (
            charge_density_step
            + SPREAD_COEFF * second_derivative_sum
            - MOBILITY_TERM * (charge_density_step - downward_neighbor)
            - LIFETIME_DECAY * charge_density_step
            + SOURCE_FACTOR * blocky_pair_creation
        )
    return charge_density_step


def local(
    voltage_lateral_component,
    voltage_vertical_component,
    voltage_forward_component,
    induction_lateral_component,
    induction_vertical_component,
    induction_forward_component,
    medium_code,
    nonlinear_coefficient_matrix,
    mobile_charge_density,
):
    voltage_gradient = (
        voltage_lateral_component,
        voltage_vertical_component,
        voltage_forward_component,
    )
    induction_vector = (
        induction_lateral_component,
        induction_vertical_component,
        induction_forward_component,
    )
    coeffs = lax.dynamic_slice_in_dim(nonlinear_coefficient_matrix, lax.axis_index("af"), 1, 0)
    silicon = (medium_code == 0).astype(jnp.float32)
    base_perm = jnp.where(
        medium_code == 0, SILICON_PERM, jnp.where(medium_code == 1, OXIDE_PERM, 1.0)
    ).astype(jnp.float32)
    absorb_two = coeffs[:, 1][:, None, None, None]
    charge_density_step = mobile_charge_density
    for rounds in range(ROUNDS):
        tile_density = lax.all_to_all(
            charge_density_step, "gx", split_axis=1, concat_axis=0, tiled=True
        )
        optical_grid_charge = jnp.repeat(jnp.repeat(tile_density, BLOCK_FACTOR, 0), BLOCK_FACTOR, 1)
        optical_grid_charge = optical_grid_charge[:, :, None]
        generation = jnp.zeros(medium_code.shape, jnp.float32)
        for upsample_copy in range(SUBSTEPS):
            intensity = (
                voltage_gradient[0] * voltage_gradient[0]
                + voltage_gradient[1] * voltage_gradient[1]
                + voltage_gradient[2] * voltage_gradient[2]
            )
            inten_sum = intensity[0] + partner(intensity[0], "af", 0)
            generation = generation + silicon * absorb_two[0] * intensity[0] * inten_sum
            voltage_gradient, induction_vector = advance(
                voltage_gradient,
                induction_vector,
                inten_sum,
                base_perm,
                silicon,
                coeffs,
                optical_grid_charge,
                upper_tiles,
                lower_tiles,
            )
        blocky_pair_creation = restrict_mean(lax.psum(generation, "af"))
        layer_pair_creation = lax.all_to_all(
            blocky_pair_creation, "gx", split_axis=0, concat_axis=1, tiled=True
        )
        charge_density_step = charge_update_pass(charge_density_step, layer_pair_creation)
    return (
        voltage_gradient[0],
        voltage_gradient[1],
        voltage_gradient[2],
        induction_vector[0],
        induction_vector[1],
        induction_vector[2],
        charge_density_step,
    )


def solution(mesh):
    in_specs = (
        P("af", ("group", "gz"), "gx", None),
        P("af", ("group", "gz"), "gx", None),
        P("af", ("group", "gz"), "gx", None),
        P("af", ("group", "gz"), "gx", None),
        P("af", ("group", "gz"), "gx", None),
        P("af", ("group", "gz"), "gx", None),
        P(("group", "gz"), "gx", None),
        P(),
        P(("group", "gz", "gx"), None),
    )
    out_specs = (
        P("af", ("group", "gz"), "gx", None),
        P("af", ("group", "gz"), "gx", None),
        P("af", ("group", "gz"), "gx", None),
        P("af", ("group", "gz"), "gx", None),
        P("af", ("group", "gz"), "gx", None),
        P("af", ("group", "gz"), "gx", None),
        P(("group", "gz", "gx"), None),
    )
    return jax.shard_map(local, mesh=mesh, in_specs=in_specs, out_specs=out_specs, check_vma=False)
```

profile of v0, /device:TPU:0, one launch (start us, length us, event | category | flops | bytes accessed | tf_op | source)
XLA Modules:
  0.0 397.1 jit_solution(14717045695465977539)
XLA Ops:
  8.5 4.2 %all-to-all-start = ((f32[4,2,8]{2,0,1:T(4,128)}), f32[4,2,8]{2,0,1:T(4,128)S(1)}, u32[]{:S(2)}, u32[]{:S(2)}) async-start(f32[4,2,8]{2,0,1:T(4,128)} %copy.201), calls=%async_computation | async-start | bytes 8192 | tf_op jit(solution)/shard_map/all_to_all | solution.py:183
  26.8 4.6 %collective-permute-start.3 = (f32[2,1,32,128]{3,2,0,1:T(8,128)S(1)}, f32[2,1,32,128]{3,2,0,1:T(8,128)S(1)}, u32[]{:S(2)}, u32[]{:S(2)}) collective-permute-start(f32[2,1,32,128]{3,2,0,1:T(8,128)S(1)} %maximum_bitcast_fusion.7), channel_id=1, source_target_pairs={{0,4},{4,8},{8,12},{1,5},{5,9},{9,13},{2,6},{6,10},{10,14},{3,7},{... | collective-permute-start | bytes 98312 | tf_op jit(solution)/shard_map/ppermute | solution.py:24
  48.6 4.5 %collective-permute-start.9 = (f32[2,1,32,128]{3,2,0,1:T(8,128)S(1)}, f32[2,1,32,128]{3,2,0,1:T(8,128)S(1)}, u32[]{:S(2)}, u32[]{:S(2)}) collective-permute-start(f32[2,1,32,128]{3,2,0,1:T(8,128)S(1)} %bitcast.1213), channel_id=1, source_target_pairs={{0,2},{1,3},{4,6},{5,7},{8,10},{9,11},{12,14},{13,15},{16,18},{17,... | collective-permute-start | bytes 98312 | tf_op jit(solution)/shard_map/ppermute | solution.py:24
  65.8 4.7 %collective-permute-done.11 = f32[2,1,32,128]{3,0,2,1:T(2,128)S(1)} collective-permute-done((f32[2,1,32,128]{3,0,2,1:T(2,128)S(1)}, f32[2,1,32,128]{3,0,2,1:T(2,128)S(1)}, u32[]{:S(2)}, u32[]{:S(2)}) %collective-permute-start.11) | collective-permute-done | bytes 32800 | tf_op jit(solution)/shard_map/ppermute | solution.py:24
  74.7 4.5 %collective-permute-start.14 = (f32[2,1,32,128]{3,2,0,1:T(8,128)S(1)}, f32[2,1,32,128]{3,2,0,1:T(8,128)S(1)}, u32[]{:S(2)}, u32[]{:S(2)}) collective-permute-start(f32[2,1,32,128]{3,2,0,1:T(8,128)S(1)} %bitcast.1214), channel_id=1, source_target_pairs={{0,2},{1,3},{4,6},{5,7},{8,10},{9,11},{12,14},{13,15},{16,18},{17,... | collective-permute-start | bytes 98312 | tf_op jit(solution)/shard_map/ppermute | solution.py:24
  96.0 4.5 %collective-permute-start.19 = (f32[2,1,32,128]{3,2,0,1:T(8,128)S(1)}, f32[2,1,32,128]{3,2,0,1:T(8,128)S(1)}, u32[]{:S(2)}, u32[]{:S(2)}) collective-permute-start(f32[2,1,32,128]{3,2,0,1:T(8,128)S(1)} %bitcast.1220), channel_id=1, source_target_pairs={{0,2},{1,3},{4,6},{5,7},{8,10},{9,11},{12,14},{13,15},{16,18},{17,... | collective-permute-start | bytes 98312 | tf_op jit(solution)/shard_map/ppermute | solution.py:24
  122.7 18.3 %all-reduce.51.cloned.1.call-done = f32[32,32,128]{2,1,0:T(8,128)} async-done(((f32[32,32,128]{2,1,0:T(8,128)}), f32[32,32,128]{2,1,0:T(8,128)}) %all-reduce.51.cloned.1.call-update) | async-done | bytes 524304 | tf_op jit(solution)/shard_map/psum | solution.py:208
  156.6 5.7 %collective-permute-done.23 = f32[1,16]{1,0:T(1,128)S(1)} collective-permute-done((f32[1,16]{1,0:T(1,128)S(1)}, f32[1,16]{1,0:T(1,128)S(1)}, u32[]{:S(2)}, u32[]{:S(2)}) %collective-permute-start.23) | collective-permute-done | bytes 96 | tf_op jit(solution)/shard_map/ppermute | solution.py:35
  162.5 4.8 %collective-permute-start.26 = (f32[1,16]{1,0:T(1,128)S(1)}, f32[1,16]{1,0:T(1,128)S(1)}, u32[]{:S(2)}, u32[]{:S(2)}) collective-permute-start(f32[1,16]{1,0:T(1,128)S(1)} %get-tuple-element.151), channel_id=1, source_target_pairs={{0,2},{2,4},{4,6},{6,8},{8,10},{10,12},{12,14},{1,3},{3,5},{5,7},{... | collective-permute-start | bytes 200 | tf_op jit(solution)/shard_map/ppermute | solution.py:32
  168.6 4.1 %collective-permute-done.25 = f32[1,16]{1,0:T(1,128)S(1)} collective-permute-done((f32[1,16]{1,0:T(1,128)S(1)}, f32[1,16]{1,0:T(1,128)S(1)}, u32[]{:S(2)}, u32[]{:S(2)}) %collective-permute-start.25) | collective-permute-done | bytes 96 | tf_op jit(solution)/shard_map/ppermute | solution.py:35
  177.1 4.1 %collective-permute-done.27 = f32[1,16]{1,0:T(1,128)S(1)} collective-permute-done((f32[1,16]{1,0:T(1,128)S(1)}, f32[1,16]{1,0:T(1,128)S(1)}, u32[]{:S(2)}, u32[]{:S(2)}) %collective-permute-start.27) | collective-permute-done | bytes 96 | tf_op jit(solution)/shard_map/ppermute | solution.py:35
  181.4 4.8 %collective-permute-start.30 = (f32[1,16]{1,0:T(1,128)S(1)}, f32[1,16]{1,0:T(1,128)S(1)}, u32[]{:S(2)}, u32[]{:S(2)}) collective-permute-start(f32[1,16]{1,0:T(1,128)S(1)} %get-tuple-element.143), channel_id=1, source_target_pairs={{0,2},{2,4},{4,6},{6,8},{8,10},{10,12},{12,14},{1,3},{3,5},{5,7},{... | collective-permute-start | bytes 200 | tf_op jit(solution)/shard_map/ppermute | solution.py:32
  187.5 4.1 %collective-permute-done.29 = f32[1,16]{1,0:T(1,128)S(1)} collective-permute-done((f32[1,16]{1,0:T(1,128)S(1)}, f32[1,16]{1,0:T(1,128)S(1)}, u32[]{:S(2)}, u32[]{:S(2)}) %collective-permute-start.29) | collective-permute-done | bytes 96 | tf_op jit(solution)/shard_map/ppermute | solution.py:35
  195.9 4.1 %collective-permute-done.31 = f32[1,16]{1,0:T(1,128)S(1)} collective-permute-done((f32[1,16]{1,0:T(1,128)S(1)}, f32[1,16]{1,0:T(1,128)S(1)}, u32[]{:S(2)}, u32[]{:S(2)}) %collective-permute-start.31) | collective-permute-done | bytes 96 | tf_op jit(solution)/shard_map/ppermute | solution.py:35
  204.4 4.1 %collective-permute-done.33 = f32[1,16]{1,0:T(1,128)S(1)} collective-permute-done((f32[1,16]{1,0:T(1,128)S(1)}, f32[1,16]{1,0:T(1,128)S(1)}, u32[]{:S(2)}, u32[]{:S(2)}) %collective-permute-start.33) | collective-permute-done | bytes 96 | tf_op jit(solution)/shard_map/ppermute | solution.py:35
  212.8 4.1 %collective-permute-done.35 = f32[1,16]{1,0:T(1,128)S(1)} collective-permute-done((f32[1,16]{1,0:T(1,128)S(1)}, f32[1,16]{1,0:T(1,128)S(1)}, u32[]{:S(2)}, u32[]{:S(2)}) %collective-permute-start.35) | collective-permute-done | bytes 96 | tf_op jit(solution)/shard_map/ppermute | solution.py:35
  240.8 4.5 %collective-permute-start.44 = (f32[2,1,32,128]{3,2,0,1:T(8,128)S(1)}, f32[2,1,32,128]{3,2,0,1:T(8,128)S(1)}, u32[]{:S(2)}, u32[]{:S(2)}) collective-permute-start(f32[2,1,32,128]{3,2,0,1:T(8,128)S(1)} %maximum_bitcast_fusion.2), channel_id=1, source_target_pairs={{0,4},{4,8},{8,12},{1,5},{5,9},{9,13},{2,6},{6,10},{10,14},{3,7},{... | collective-permute-start | bytes 98312 | tf_op jit(solution)/shard_map/ppermute | solution.py:24
  253.1 4.5 %collective-permute-start.57 = (f32[1,16]{1,0:T(1,128)S(1)}, f32[1,16]{1,0:T(1,128)S(1)}, u32[]{:S(2)}, u32[]{:S(2)}) collective-permute-start(f32[1,16]{1,0:T(1,128)S(1)} %get-tuple-element.127), channel_id=1, source_target_pairs={{0,2},{2,4},{4,6},{6,8},{8,10},{10,12},{12,14},{1,3},{3,5},{5,7},{... | collective-permute-start | bytes 200 | tf_op jit(solution)/shard_map/ppermute | solution.py:32
  261.0 4.5 %collective-permute-start.50 = (f32[2,1,32,128]{3,2,0,1:T(8,128)S(1)}, f32[2,1,32,128]{3,2,0,1:T(8,128)S(1)}, u32[]{:S(2)}, u32[]{:S(2)}) collective-permute-start(f32[2,1,32,128]{3,2,0,1:T(8,128)S(1)} %bitcast.1215), channel_id=1, source_target_pairs={{0,2},{1,3},{4,6},{5,7},{8,10},{9,11},{12,14},{13,15},{16,18},{17,... | collective-permute-start | bytes 98312 | tf_op jit(solution)/shard_map/ppermute | solution.py:24
  265.6 4.9 %collective-permute-start.49 = (f32[2,1,32,128]{3,2,0,1:T(8,128)S(1)}, f32[2,1,32,128]{3,2,0,1:T(8,128)S(1)}, u32[]{:S(2)}, u32[]{:S(2)}) collective-permute-start(f32[2,1,32,128]{3,2,0,1:T(8,128)S(1)} %maximum_bitcast_fusion.1), channel_id=1, source_target_pairs={{0,4},{4,8},{8,12},{1,5},{5,9},{9,13},{2,6},{6,10},{10,14},{3,7},{... | collective-permute-start | bytes 98312 | tf_op jit(solution)/shard_map/ppermute | solution.py:24
  283.3 4.5 %collective-permute-start.55 = (f32[2,1,32,128]{3,2,0,1:T(8,128)S(1)}, f32[2,1,32,128]{3,2,0,1:T(8,128)S(1)}, u32[]{:S(2)}, u32[]{:S(2)}) collective-permute-start(f32[2,1,32,128]{3,2,0,1:T(8,128)S(1)} %bitcast.1210), channel_id=1, source_target_pairs={{0,2},{1,3},{4,6},{5,7},{8,10},{9,11},{12,14},{13,15},{16,18},{17,... | collective-permute-start | bytes 98312 | tf_op jit(solution)/shard_map/ppermute | solution.py:24
  301.6 12.3 %all-reduce.53.cloned.1.call-done = f32[32,32,128]{2,1,0:T(8,128)} async-done(((f32[32,32,128]{2,1,0:T(8,128)}), f32[32,32,128]{2,1,0:T(8,128)}) %all-reduce.53.cloned.1.call-update) | async-done | bytes 524304 | tf_op jit(solution)/shard_map/psum | solution.py:208
  327.8 4.1 %collective-permute-done.58 = f32[1,16]{1,0:T(1,128)S(1)} collective-permute-done((f32[1,16]{1,0:T(1,128)S(1)}, f32[1,16]{1,0:T(1,128)S(1)}, u32[]{:S(2)}, u32[]{:S(2)}) %collective-permute-start.58) | collective-permute-done | bytes 96 | tf_op jit(solution)/shard_map/ppermute | solution.py:35
  332.1 4.6 %collective-permute-start.61 = (f32[1,16]{1,0:T(1,128)S(1)}, f32[1,16]{1,0:T(1,128)S(1)}, u32[]{:S(2)}, u32[]{:S(2)}) collective-permute-start(f32[1,16]{1,0:T(1,128)S(1)} %get-tuple-element.119), channel_id=1, source_target_pairs={{0,2},{2,4},{4,6},{6,8},{8,10},{10,12},{12,14},{1,3},{3,5},{5,7},{... | collective-permute-start | bytes 200 | tf_op jit(solution)/shard_map/ppermute | solution.py:32
  338.0 4.1 %collective-permute-done.60 = f32[1,16]{1,0:T(1,128)S(1)} collective-permute-done((f32[1,16]{1,0:T(1,128)S(1)}, f32[1,16]{1,0:T(1,128)S(1)}, u32[]{:S(2)}, u32[]{:S(2)}) %collective-permute-start.60) | collective-permute-done | bytes 96 | tf_op jit(solution)/shard_map/ppermute | solution.py:35
  347.0 4.1 %collective-permute-done.62 = f32[1,16]{1,0:T(1,128)S(1)} collective-permute-done((f32[1,16]{1,0:T(1,128)S(1)}, f32[1,16]{1,0:T(1,128)S(1)}, u32[]{:S(2)}, u32[]{:S(2)}) %collective-permute-start.62) | collective-permute-done | bytes 96 | tf_op jit(solution)/shard_map/ppermute | solution.py:35
  351.3 4.3 %collective-permute-start.65 = (f32[1,16]{1,0:T(1,128)S(1)}, f32[1,16]{1,0:T(1,128)S(1)}, u32[]{:S(2)}, u32[]{:S(2)}) collective-permute-start(f32[1,16]{1,0:T(1,128)S(1)} %get-tuple-element.111), channel_id=1, source_target_pairs={{0,2},{2,4},{4,6},{6,8},{8,10},{10,12},{12,14},{1,3},{3,5},{5,7},{... | collective-permute-start | bytes 200 | tf_op jit(solution)/shard_map/ppermute | solution.py:32
  356.9 4.1 %collective-permute-done.64 = f32[1,16]{1,0:T(1,128)S(1)} collective-permute-done((f32[1,16]{1,0:T(1,128)S(1)}, f32[1,16]{1,0:T(1,128)S(1)}, u32[]{:S(2)}, u32[]{:S(2)}) %collective-permute-start.64) | collective-permute-done | bytes 96 | tf_op jit(solution)/shard_map/ppermute | solution.py:35
  365.9 4.1 %collective-permute-done.66 = f32[1,16]{1,0:T(1,128)S(1)} collective-permute-done((f32[1,16]{1,0:T(1,128)S(1)}, f32[1,16]{1,0:T(1,128)S(1)}, u32[]{:S(2)}, u32[]{:S(2)}) %collective-permute-start.66) | collective-permute-done | bytes 96 | tf_op jit(solution)/shard_map/ppermute | solution.py:35
  370.2 4.3 %collective-permute-start.69 = (f32[1,16]{1,0:T(1,128)S(1)}, f32[1,16]{1,0:T(1,128)S(1)}, u32[]{:S(2)}, u32[]{:S(2)}) collective-permute-start(f32[1,16]{1,0:T(1,128)S(1)} %get-tuple-element.103), channel_id=1, source_target_pairs={{0,2},{2,4},{4,6},{6,8},{8,10},{10,12},{12,14},{1,3},{3,5},{5,7},{... | collective-permute-start | bytes 200 | tf_op jit(solution)/shard_map/ppermute | solution.py:32
  375.8 4.1 %collective-permute-done.68 = f32[1,16]{1,0:T(1,128)S(1)} collective-permute-done((f32[1,16]{1,0:T(1,128)S(1)}, f32[1,16]{1,0:T(1,128)S(1)}, u32[]{:S(2)}, u32[]{:S(2)}) %collective-permute-start.68) | collective-permute-done | bytes 96 | tf_op jit(solution)/shard_map/ppermute | solution.py:35
  384.8 4.1 %collective-permute-done.70 = f32[1,16]{1,0:T(1,128)S(1)} collective-permute-done((f32[1,16]{1,0:T(1,128)S(1)}, f32[1,16]{1,0:T(1,128)S(1)}, u32[]{:S(2)}, u32[]{:S(2)}) %collective-permute-start.70) | collective-permute-done | bytes 96 | tf_op jit(solution)/shard_map/ppermute | solution.py:35
  (381 shorter events, 218.3 us)
Async XLA Ops:
  8.5 22.9 %all-to-all-start = ((f32[4,2,8]{2,0,1:T(4,128)}), f32[4,2,8]{2,0,1:T(4,128)S(1)}, u32[]{:S(2)}, u32[]{:S(2)}) async-start(f32[4,2,8]{2,0,1:T(4,128)} %copy.201), calls=%async_computation | async-start | bytes 8192 | tf_op jit(solution)/shard_map/all_to_all | solution.py:183
  12.8 128.2 %all-reduce.51.cloned.1.call-start = ((), (), s32[]{:S(2)}) async-start(), calls=%async_computation.4 | async-start | bytes 1048576 | tf_op jit(solution)/shard_map/psum | solution.py:208
  13.6 7.2 %collective-permute-start.2 = (f32[2,1,32,128]{3,2,0,1:T(8,128)S(1)}, f32[2,1,32,128]{3,2,0,1:T(8,128)S(1)}, u32[]{:S(2)}, u32[]{:S(2)}) collective-permute-start(f32[2,1,32,128]{3,2,0,1:T(8,128)S(1)} %fusion.349), channel_id=1, source_target_pairs={{4,0},{8,4},{12,8},{5,1},{9,5},{13,9},{6,2},{10,6},{14,10},{7,3},{... | collective-permute-start | bytes 98312 | tf_op jit(solution)/shard_map/ppermute | solution.py:24
  23.4 9.9 %collective-permute-start = (f32[32,32,128]{2,1,0:T(8,128)}, f32[32,32,128]{2,1,0:T(8,128)S(1)}, u32[]{:S(2)}, u32[]{:S(2)}) collective-permute-start(f32[32,32,128]{2,1,0:T(8,128)} %get-tuple-element.67), channel_id=1, source_target_pairs={{0,1},{1,0},{2,3},{3,2},{4,5},{5,4},{6,7},{7,6},{8,9},{9,8},{10,11... | collective-permute-start | bytes 1572872 | tf_op jit(solution)/shard_map/ppermute | solution.py:41
  23.5 8.8 %collective-permute-start.4 = (f32[2,1,32,128]{3,2,0,1:T(8,128)S(1)}, f32[2,1,32,128]{3,2,0,1:T(8,128)S(1)}, u32[]{:S(2)}, u32[]{:S(2)}) collective-permute-start(f32[2,1,32,128]{3,2,0,1:T(8,128)S(1)} %bitcast.1212), channel_id=1, source_target_pairs={{0,2},{1,3},{4,6},{5,7},{8,10},{9,11},{12,14},{13,15},{16,18},{17,... | collective-permute-start | bytes 98312 | tf_op jit(solution)/shard_map/ppermute | solution.py:24
  43.5 16.5 %collective-permute-start.5 = (f32[32,32,128]{2,1,0:T(8,128)S(1)}, f32[32,32,128]{2,1,0:T(8,128)S(1)}, u32[]{:S(2)}, u32[]{:S(2)}) collective-permute-start(f32[32,32,128]{2,1,0:T(8,128)S(1)} %get-tuple-element.34), channel_id=1, source_target_pairs={{0,1},{1,0},{2,3},{3,2},{4,5},{5,4},{6,7},{7,6},{8,9},{9,8},{10,11... | collective-permute-start | bytes 1572872 | tf_op jit(solution)/shard_map/ppermute | solution.py:41
  48.6 11.1 %collective-permute-start.9 = (f32[2,1,32,128]{3,2,0,1:T(8,128)S(1)}, f32[2,1,32,128]{3,2,0,1:T(8,128)S(1)}, u32[]{:S(2)}, u32[]{:S(2)}) collective-permute-start(f32[2,1,32,128]{3,2,0,1:T(8,128)S(1)} %bitcast.1213), channel_id=1, source_target_pairs={{0,2},{1,3},{4,6},{5,7},{8,10},{9,11},{12,14},{13,15},{16,18},{17,... | collective-permute-start | bytes 98312 | tf_op jit(solution)/shard_map/ppermute | solution.py:24
  57.1 26.1 %collective-permute-start.22 = (f32[1,16]{1,0:T(1,128)S(1)}, f32[1,16]{1,0:T(1,128)S(1)}, u32[]{:S(2)}, u32[]{:S(2)}) collective-permute-start(f32[1,16]{1,0:T(1,128)S(1)} %get-tuple-element.159), channel_id=1, source_target_pairs={{0,2},{2,4},{4,6},{6,8},{8,10},{10,12},{12,14},{1,3},{3,5},{5,7},{... | collective-permute-start | bytes 200 | tf_op jit(solution)/shard_map/ppermute | solution.py:32
  58.4 24.8 %collective-permute-start.21 = (f32[1,16]{1,0:T(1,128)S(1)}, f32[1,16]{1,0:T(1,128)S(1)}, u32[]{:S(2)}, u32[]{:S(2)}) collective-permute-start(f32[1,16]{1,0:T(1,128)S(1)} %get-tuple-element.160), channel_id=1, source_target_pairs={{2,0},{4,2},{6,4},{8,6},{10,8},{12,10},{14,12},{3,1},{5,3},{7,5},{... | collective-permute-start | bytes 200 | tf_op jit(solution)/shard_map/ppermute | solution.py:35
  62.6 7.9 %collective-permute-start.11 = (f32[2,1,32,128]{3,0,2,1:T(2,128)S(1)}, f32[2,1,32,128]{3,0,2,1:T(2,128)S(1)}, u32[]{:S(2)}, u32[]{:S(2)}) collective-permute-start(f32[2,1,32,128]{3,0,2,1:T(2,128)S(1)} %bitcast.1218), channel_id=1, source_target_pairs={{2,0},{3,1},{6,4},{7,5},{10,8},{11,9},{14,12},{15,13},{18,16},{19,... | collective-permute-start | bytes 98312 | tf_op jit(solution)/shard_map/ppermute | solution.py:24
  63.9 10.0 %collective-permute-start.12 = (f32[2,1,32,128]{3,2,0,1:T(8,128)S(1)}, f32[2,1,32,128]{3,2,0,1:T(8,128)S(1)}, u32[]{:S(2)}, u32[]{:S(2)}) collective-permute-start(f32[2,1,32,128]{3,2,0,1:T(8,128)S(1)} %fusion.347), channel_id=1, source_target_pairs={{4,0},{8,4},{12,8},{5,1},{9,5},{13,9},{6,2},{10,6},{14,10},{7,3},{... | collective-permute-start | bytes 98312 | tf_op jit(solution)/shard_map/ppermute | solution.py:24
  65.7 19.2 %collective-permute-start.10 = (f32[32,32,128]{2,1,0:T(8,128)S(1)}, f32[32,32,128]{2,1,0:T(8,128)S(1)}, u32[]{:S(2)}, u32[]{:S(2)}) collective-permute-start(f32[32,32,128]{2,1,0:T(8,128)S(1)} %get-tuple-element.30), channel_id=1, source_target_pairs={{0,1},{1,0},{2,3},{3,2},{4,5},{5,4},{6,7},{7,6},{8,9},{9,8},{10,11... | collective-permute-start | bytes 1572872 | tf_op jit(solution)/shard_map/ppermute | solution.py:41
  74.7 8.5 %collective-permute-start.14 = (f32[2,1,32,128]{3,2,0,1:T(8,128)S(1)}, f32[2,1,32,128]{3,2,0,1:T(8,128)S(1)}, u32[]{:S(2)}, u32[]{:S(2)}) collective-permute-start(f32[2,1,32,128]{3,2,0,1:T(8,128)S(1)} %bitcast.1214), channel_id=1, source_target_pairs={{0,2},{1,3},{4,6},{5,7},{8,10},{9,11},{12,14},{13,15},{16,18},{17,... | collective-permute-start | bytes 98312 | tf_op jit(solution)/shard_map/ppermute | solution.py:24
  91.0 15.4 %collective-permute-start.15 = (f32[32,32,128]{2,1,0:T(8,128)S(1)}, f32[32,32,128]{2,1,0:T(8,128)S(1)}, u32[]{:S(2)}, u32[]{:S(2)}) collective-permute-start(f32[32,32,128]{2,1,0:T(8,128)S(1)} %get-tuple-element.26), channel_id=1, source_target_pairs={{0,1},{1,0},{2,3},{3,2},{4,5},{5,4},{6,7},{7,6},{8,9},{9,8},{10,11... | collective-permute-start | bytes 1572872 | tf_op jit(solution)/shard_map/ppermute | solution.py:41
  96.0 8.6 %collective-permute-start.19 = (f32[2,1,32,128]{3,2,0,1:T(8,128)S(1)}, f32[2,1,32,128]{3,2,0,1:T(8,128)S(1)}, u32[]{:S(2)}, u32[]{:S(2)}) collective-permute-start(f32[2,1,32,128]{3,2,0,1:T(8,128)S(1)} %bitcast.1220), channel_id=1, source_target_pairs={{0,2},{1,3},{4,6},{5,7},{8,10},{9,11},{12,14},{13,15},{16,18},{17,... | collective-permute-start | bytes 98312 | tf_op jit(solution)/shard_map/ppermute | solution.py:24
  118.9 106.6 %collective-permute-start.20 = (f32[32,32,128]{2,1,0:T(8,128)}, f32[32,32,128]{2,1,0:T(8,128)}, u32[]{:S(2)}, u32[]{:S(2)}) collective-permute-start(f32[32,32,128]{2,1,0:T(8,128)} %get-tuple-element.22), channel_id=1, source_target_pairs={{0,1},{1,0},{2,3},{3,2},{4,5},{5,4},{6,7},{7,6},{8,9},{9,8},{10,11... | collective-permute-start | bytes 1572872 | tf_op jit(solution)/shard_map/ppermute | solution.py:41
  143.0 10.8 %all-to-all-start.1 = ((f32[2,4,8]{2,1,0:T(4,128)}), f32[2,4,8]{2,1,0:T(4,128)S(1)}, u32[]{:S(2)}, u32[]{:S(2)}) async-start(f32[2,4,8]{2,1,0:T(4,128)} %bitcast.116), calls=%async_computation.1 | async-start | bytes 8192 | tf_op jit(solution)/shard_map/all_to_all | solution.py:209
  146.3 74.8 %collective-permute-start.40 = (f32[2,1,32,128]{3,2,0,1:T(8,128)S(1)}, f32[2,1,32,128]{3,2,0,1:T(8,128)S(1)}, u32[]{:S(2)}, u32[]{:S(2)}) collective-permute-start(f32[2,1,32,128]{3,2,0,1:T(8,128)S(1)} %bitcast.1209), channel_id=1, source_target_pairs={{0,2},{1,3},{4,6},{5,7},{8,10},{9,11},{12,14},{13,15},{16,18},{17,... | collective-permute-start | bytes 98312 | tf_op jit(solution)/shard_map/ppermute | solution.py:24
  150.2 70.9 %collective-permute-start.39 = (f32[2,1,32,128]{3,2,0,1:T(8,128)S(1)}, f32[2,1,32,128]{3,2,0,1:T(8,128)S(1)}, u32[]{:S(2)}, u32[]{:S(2)}) collective-permute-start(f32[2,1,32,128]{3,2,0,1:T(8,128)S(1)} %maximum_bitcast_fusion.3), channel_id=1, source_target_pairs={{0,4},{4,8},{8,12},{1,5},{5,9},{9,13},{2,6},{6,10},{10,14},{3,7},{... | collective-permute-start | bytes 98312 | tf_op jit(solution)/shard_map/ppermute | solution.py:24
  155.3 7.0 %collective-permute-start.23 = (f32[1,16]{1,0:T(1,128)S(1)}, f32[1,16]{1,0:T(1,128)S(1)}, u32[]{:S(2)}, u32[]{:S(2)}) collective-permute-start(f32[1,16]{1,0:T(1,128)S(1)} %get-tuple-element.156), channel_id=1, source_target_pairs={{2,0},{4,2},{6,4},{8,6},{10,8},{12,10},{14,12},{3,1},{5,3},{7,5},{... | collective-permute-start | bytes 200 | tf_op jit(solution)/shard_map/ppermute | solution.py:35
  217.8 7.0 %all-to-all-start.2 = ((f32[4,2,8]{2,0,1:T(4,128)}), f32[4,2,8]{2,0,1:T(4,128)S(1)}, u32[]{:S(2)}, u32[]{:S(2)}) async-start(f32[4,2,8]{2,0,1:T(4,128)} %copy.222), calls=%async_computation.2 | async-start | bytes 8192 | tf_op jit(solution)/shard_map/all_to_all | solution.py:183
  221.0 93.0 %all-reduce.53.cloned.1.call-start = ((), (), s32[]{:S(2)}) async-start(), calls=%async_computation.5 | async-start | bytes 1048576 | tf_op jit(solution)/shard_map/psum | solution.py:208
  234.6 12.7 %collective-permute-start.41 = (f32[32,32,128]{2,1,0:T(8,128)S(1)}, f32[32,32,128]{2,1,0:T(8,128)S(1)}, u32[]{:S(2)}, u32[]{:S(2)}) collective-permute-start(f32[32,32,128]{2,1,0:T(8,128)S(1)} %get-tuple-element.18), channel_id=1, source_target_pairs={{0,1},{1,0},{2,3},{3,2},{4,5},{5,4},{6,7},{7,6},{8,9},{9,8},{10,11... | collective-permute-start | bytes 1572872 | tf_op jit(solution)/shard_map/ppermute | solution.py:41
  249.9 10.3 %collective-permute-start.48 = (f32[2,1,32,128]{3,2,0,1:T(8,128)S(1)}, f32[2,1,32,128]{3,2,0,1:T(8,128)S(1)}, u32[]{:S(2)}, u32[]{:S(2)}) collective-permute-start(f32[2,1,32,128]{3,2,0,1:T(8,128)S(1)} %fusion.343), channel_id=1, source_target_pairs={{4,0},{8,4},{12,8},{5,1},{9,5},{13,9},{6,2},{10,6},{14,10},{7,3},{... | collective-permute-start | bytes 98312 | tf_op jit(solution)/shard_map/ppermute | solution.py:24
  251.8 8.4 %collective-permute-start.47 = (f32[2,1,32,128]{3,2,0,1:T(8,128)S(1)}, f32[2,1,32,128]{3,2,0,1:T(8,128)S(1)}, u32[]{:S(2)}, u32[]{:S(2)}) collective-permute-start(f32[2,1,32,128]{3,2,0,1:T(8,128)S(1)} %slice_bitcast_fusion.32), channel_id=1, source_target_pairs={{2,0},{3,1},{6,4},{7,5},{10,8},{11,9},{14,12},{15,13},{18,16},{19,... | collective-permute-start | bytes 98312 | tf_op jit(solution)/shard_map/ppermute | solution.py:24
  253.1 17.3 %collective-permute-start.57 = (f32[1,16]{1,0:T(1,128)S(1)}, f32[1,16]{1,0:T(1,128)S(1)}, u32[]{:S(2)}, u32[]{:S(2)}) collective-permute-start(f32[1,16]{1,0:T(1,128)S(1)} %get-tuple-element.127), channel_id=1, source_target_pairs={{0,2},{2,4},{4,6},{6,8},{8,10},{10,12},{12,14},{1,3},{3,5},{5,7},{... | collective-permute-start | bytes 200 | tf_op jit(solution)/shard_map/ppermute | solution.py:32
  257.7 12.8 %collective-permute-start.56 = (f32[1,16]{1,0:T(1,128)S(1)}, f32[1,16]{1,0:T(1,128)S(1)}, u32[]{:S(2)}, u32[]{:S(2)}) collective-permute-start(f32[1,16]{1,0:T(1,128)S(1)} %get-tuple-element.128), channel_id=1, source_target_pairs={{2,0},{4,2},{6,4},{8,6},{10,8},{12,10},{14,12},{3,1},{5,3},{7,5},{... | collective-permute-start | bytes 200 | tf_op jit(solution)/shard_map/ppermute | solution.py:35
  259.5 12.9 %collective-permute-start.46 = (f32[32,32,128]{2,1,0:T(8,128)S(1)}, f32[32,32,128]{2,1,0:T(8,128)S(1)}, u32[]{:S(2)}, u32[]{:S(2)}) collective-permute-start(f32[32,32,128]{2,1,0:T(8,128)S(1)} %get-tuple-element.14), channel_id=1, source_target_pairs={{0,1},{1,0},{2,3},{3,2},{4,5},{5,4},{6,7},{7,6},{8,9},{9,8},{10,11... | collective-permute-start | bytes 1572872 | tf_op jit(solution)/shard_map/ppermute | solution.py:41
  261.0 9.5 %collective-permute-start.50 = (f32[2,1,32,128]{3,2,0,1:T(8,128)S(1)}, f32[2,1,32,128]{3,2,0,1:T(8,128)S(1)}, u32[]{:S(2)}, u32[]{:S(2)}) collective-permute-start(f32[2,1,32,128]{3,2,0,1:T(8,128)S(1)} %bitcast.1215), channel_id=1, source_target_pairs={{0,2},{1,3},{4,6},{5,7},{8,10},{9,11},{12,14},{13,15},{16,18},{17,... | collective-permute-start | bytes 98312 | tf_op jit(solution)/shard_map/ppermute | solution.py:24
  278.2 14.2 %collective-permute-start.51 = (f32[32,32,128]{2,1,0:T(8,128)S(1)}, f32[32,32,128]{2,1,0:T(8,128)S(1)}, u32[]{:S(2)}, u32[]{:S(2)}) collective-permute-start(f32[32,32,128]{2,1,0:T(8,128)S(1)} %get-tuple-element.10), channel_id=1, source_target_pairs={{0,1},{1,0},{2,3},{3,2},{4,5},{5,4},{6,7},{7,6},{8,9},{9,8},{10,11... | collective-permute-start | bytes 1572872 | tf_op jit(solution)/shard_map/ppermute | solution.py:41
  283.3 13.2 %collective-permute-start.55 = (f32[2,1,32,128]{3,2,0,1:T(8,128)S(1)}, f32[2,1,32,128]{3,2,0,1:T(8,128)S(1)}, u32[]{:S(2)}, u32[]{:S(2)}) collective-permute-start(f32[2,1,32,128]{3,2,0,1:T(8,128)S(1)} %bitcast.1210), channel_id=1, source_target_pairs={{0,2},{1,3},{4,6},{5,7},{8,10},{9,11},{12,14},{13,15},{16,18},{17,... | collective-permute-start | bytes 98312 | tf_op jit(solution)/shard_map/ppermute | solution.py:24
  288.5 8.0 %collective-permute-start.54 = (f32[2,1,32,128]{3,2,0,1:T(8,128)}, f32[2,1,32,128]{3,2,0,1:T(8,128)S(1)}, u32[]{:S(2)}, u32[]{:S(2)}) collective-permute-start(f32[2,1,32,128]{3,2,0,1:T(8,128)} %maximum_bitcast_fusion), channel_id=1, source_target_pairs={{0,4},{4,8},{8,12},{1,5},{5,9},{9,13},{2,6},{6,10},{10,14},{3,7},{... | collective-permute-start | bytes 98312 | tf_op jit(solution)/shard_map/ppermute | solution.py:24
  (76 other events, 486.7 us)
Sparse Core Ops, SparseCore 0:
  119.0 21.9 all-reduce.50
  296.5 17.4 all-reduce.52
where the time goes:
time: 400 us; the launch traced here: 397 us
  starting transfers between devices  176 us (44%)
  waiting for transfers between devices  126 us (32%)
  other arithmetic  63.4 us (16%)
  local copies, waits for them, and re-layouts  16.3 us (4%)
  between operations  15.9 us (4%)
    ppermute x32, starting transfers between devices, from_behind(): return lax.ppermute(shard, axis, pairs)  86 us
    ppermute x16, waiting for transfers between devices, extended(): lax.ppermute(lax.slice_in_dim(block, 0, width, axis=dim), axis, backward)  59.3 us
    ppermute x16, starting transfers between devices, extended(): lax.ppermute(lax.slice_in_dim(block, block.shape[dim] - width, None, axis...  54.5 us
    ppermute x32, waiting for transfers between devices, from_behind(): return lax.ppermute(shard, axis, pairs)  33.4 us
    psum x2, waiting for transfers between devices, local(): blocky_pair_creation = restrict_mean(lax.psum(generation, 'af'))  30.7 us
    ppermute x16, starting transfers between devices, extended(): lax.ppermute(lax.slice_in_dim(block, 0, width, axis=dim), axis, backward)  20.7 us
    sub x7, other arithmetic, advance(): keeping = permit - 0.5 * losses  15.7 us
    squeeze x7, other arithmetic, local(): inten_sum = intensity[0] + partner(intensity[0], 'af', 0)  11 us
  transfers between devices with their start and end apart: 78, of which 35 were waited for; matrix products, arithmetic and copies ran while one was open for 11% of the time, Pallas kernels for 0%

commit v1 on v0

v1 whole, which is shorter than its diff:
```python
import functools

import jax
import jax.numpy as jnp
from jax import lax
from jax.experimental import pallas as pl
from jax.experimental.pallas import tpu as pltpu
from jax.sharding import PartitionSpec as P

BLOCK_FACTOR = 4
SUBSTEPS = 4
ROUNDS = 2
CSTEPS = 8

COURANT = 0.5
SILICON_PERM = 12.1
OXIDE_PERM = 2.1
SPREAD_COEFF = 0.2
MOBILITY_TERM = 0.1
LIFETIME_DECAY = 0.05
SOURCE_FACTOR = 0.02

DEEP = SUBSTEPS
LINE = ("gz", "gx", "af")
HBM = pl.BlockSpec(memory_space=pltpu.HBM)
SMEM = pl.BlockSpec(memory_space=pltpu.SMEM)
VMEM_LIMIT = 32 * 1024 * 1024
F32 = jnp.float32


class Plan:
    def __init__(self, planes, cols, lanes, slab):
        self.gz = lax.axis_size("gz")
        self.gx = lax.axis_size("gx")
        self.planes, self.cols, self.lanes, self.slab = planes, cols, lanes, slab
        self.own = planes // 2
        self.part = self.own + DEEP
        self.ext = self.own + 2 * DEEP
        self.paired = self.gx == 2
        self.sides = ("face",) if self.paired else ("low", "high")
        self.width = cols + (8 if self.paired else 16)
        self.rows = self.width + 8
        self.tiles = self.width // 8
        self.grid_rows = planes * self.gz // BLOCK_FACTOR
        self.grid_cols = cols * self.gx // BLOCK_FACTOR
        self.devices = self.gz * self.gx * 2

    def first_row(self):
        return 8 * lax.axis_index("gx") if self.paired else 8

    def own_rows(self):
        return pl.ds(pl.multiple_of(self.first_row(), 8), self.cols)


def each_side(plan, act):
    if plan.paired:
        across = lax.axis_index("gx")

        @pl.when(across == 0)
        def _():
            act(0, "high")

        @pl.when(across == 1)
        def _():
            act(0, "low")
    else:
        act(0, "low")
        act(1, "high")


def line_pairs(plan, target):
    pairs = []
    for z in range(plan.gz):
        for x in range(plan.gx):
            for k in range(2):
                tz, tx, tk = target(z, x, k)
                if 0 <= tz < plan.gz and 0 <= tx < plan.gx:
                    pairs.append(((z * plan.gx + x) * 2 + k, (tz * plan.gx + tx) * 2 + tk))
    return pairs


def across_step(side, x):
    if side == "face":
        return 1 - x
    return x + 1 if side == "low" else x - 1


class Copies:
    def __init__(self, sems):
        self.sems, self.made = sems, 0

    def start(self, source, target):
        copy = pltpu.make_async_copy(source, target, self.sems.at[self.made])
        self.made += 1
        copy.start()
        return copy


def wait(copies):
    for copy in copies:
        copy.wait()


def call(plan, body, name, shapes, in_specs, scratch, copies, flops=0, moved=0, aliases=None):
    return pl.pallas_call(
        functools.partial(body, plan),
        out_shape=[jax.ShapeDtypeStruct(s, F32) for s in shapes],
        in_specs=in_specs,
        out_specs=[HBM] * len(shapes),
        scratch_shapes=scratch + [pltpu.SemaphoreType.DMA((copies,))],
        input_output_aliases=aliases or {},
        compiler_params=pltpu.CompilerParams(vmem_limit_bytes=VMEM_LIMIT),
        cost_estimate=pl.CostEstimate(flops=flops, bytes_accessed=moved, transcendentals=0),
        name=name,
    )


def pack_kernel(plan, *refs):
    raw, medium = refs[:6], refs[6]
    z_same, z_cross = refs[7:9]
    nside = len(plan.sides)
    outs = refs[9 : 9 + 4 * nside]
    edge, edge_code, face_code, face_float, strips, sems = refs[9 + 4 * nside :]
    copies = Copies(sems)
    k = lax.axis_index("af")
    last = plan.planes - DEEP
    to_same = jnp.where(k == 0, last, 0)
    to_cross = jnp.where(k == 0, 0, last)
    if plan.paired:
        tile_rows = [pl.multiple_of((plan.cols - 8) * (1 - lax.axis_index("gx")), 8)]
    else:
        tile_rows = [plan.cols - 8, 0]
    fast, slow = [], []
    for n, row in enumerate(tile_rows):
        for c in range(6):
            fast.append(copies.start(raw[c].at[0, :, pl.ds(row, 8), :], edge.at[n, c]))
        fast.append(copies.start(medium.at[:, pl.ds(row, 8), :], edge_code.at[n]))
    fast.append(copies.start(medium.at[pl.ds(to_same, DEEP)], face_code))
    for c in range(6):
        slow.append(copies.start(raw[c].at[0, pl.ds(to_same, DEEP)], z_same.at[c]))
        slow.append(copies.start(raw[c].at[0, pl.ds(to_cross, DEEP)], z_cross.at[c]))
    wait(fast)
    face_float[...] = face_code[...].astype(F32)
    slow.append(copies.start(face_float, z_same.at[6]))

    def fill(slot, low):
        def rows(q, _):
            for h in range(2):
                half = slice(4 * h, 4 * h + 4)
                for c in range(6):
                    strips[slot, c, q, half, :] = edge[slot, c, 2 * q + h, low : low + 4, :]
                code = edge_code[slot, 2 * q + h, low : low + 4, :]
                strips[slot, 6, q, half, :] = code.astype(F32)
            return 0

        lax.fori_loop(0, plan.planes // 2, rows, 0)

    each_side(plan, lambda slot, side: fill(slot, 4 if plan.paired == (side == "high") else 0))
    quarter = (plan.own - DEEP) // 2
    for n in range(nside):
        x_same, x_cross, d_same, d_cross = outs[4 * n : 4 * n + 4]
        pairs, six = plan.part // 2, pl.ds(0, 6)
        for source, target in (
            (strips.at[n, :, pl.ds(quarter * k, pairs)], x_same),
            (strips.at[n, six, pl.ds(quarter * (1 - k), pairs)], x_cross),
            (strips.at[n, :, pl.ds(to_same // 2, DEEP // 2)], d_same),
            (strips.at[n, six, pl.ds(to_cross // 2, DEEP // 2)], d_cross),
        ):
            slow.append(copies.start(source, target))
    wait(slow)


def pack(plan, raw, medium):
    wide = (plan.cols, plan.lanes)
    nside = len(plan.sides)
    shapes = [(7, DEEP) + wide, (6, DEEP) + wide]
    for _ in plan.sides:
        for comps, rows in ((7, plan.part), (6, plan.part), (7, DEEP), (6, DEEP)):
            shapes.append((comps, rows // 2, 8, plan.lanes))
    scratch = [
        pltpu.VMEM((nside, 6, plan.planes, 8, plan.lanes), F32),
        pltpu.VMEM((nside, plan.planes, 8, plan.lanes), jnp.int32),
        pltpu.VMEM((DEEP,) + wide, jnp.int32),
        pltpu.VMEM((DEEP,) + wide, F32),
        pltpu.VMEM((nside, 7, plan.planes // 2, 8, plan.lanes), F32),
    ]
    return call(
        plan, pack_kernel, "pack", shapes, [HBM] * 7, scratch, 11 * nside + 14, moved=4_000_000
    )(*raw, medium)


def clear(plan, old, new, code):
    zero = jnp.zeros((8, plan.lanes), F32)

    def halo(slot, side):
        tile = plan.tiles - 1 if side == "high" else 0

        def one(p, _):
            for ref in list(old) + code:
                ref[p, 8 * tile : 8 * tile + 8, :] = zero
            return 0

        lax.fori_loop(0, plan.ext, one, 0)

    each_side(plan, halo)

    def above(p, _):
        for c in (1, 2, 7, 8):
            for ref in (old[c], new[c]):
                ref[p, plan.width : plan.width + 8, :] = zero
        return 0

    lax.fori_loop(0, plan.ext, above, 0)
    for c, ref in enumerate(new):
        plane = DEEP + plan.own if c % 6 < 3 else DEEP - 1
        for t in range(plan.tiles):
            ref[plane, 8 * t : 8 * t + 8, :] = zero


def strip_row(plan, side):
    if side == "low":
        return 4
    return plan.cols if plan.paired else 8 + plan.cols


def spread_strip(refs, strip, at, plane, pairs):
    def one(q, _):
        for c, ref in refs:
            for h in range(2):
                ref[plane + 2 * q + h, at : at + 4, :] = strip[c, q, 4 * h : 4 * h + 4, :]
        return 0

    lax.fori_loop(0, pairs, one, 0)


def substeps(plan, first, second, base, silicon, charge, gen, coef):
    lanes = plan.lanes
    tile = (8, lanes)
    lane = lax.broadcasted_iota(jnp.int32, tile, 1)
    row = lax.broadcasted_iota(jnp.int32, tile, 0)
    keep_up, keep_down, at_top = lane < lanes - 1, lane > 0, row == 0
    z, x, k = (lax.axis_index(a) for a in LINE)
    at_low = jnp.logical_and(z == 0, k == 0)
    at_high = jnp.logical_and(z == plan.gz - 1, k == 1)

    def up(v):
        return jnp.where(keep_up, pltpu.roll(v, lanes - 1, 1), 0.0)

    def down(v):
        return jnp.where(keep_down, pltpu.roll(v, 1, 1), 0.0)

    def edge_mask(t):
        if plan.paired or t not in (0, plan.tiles - 1):
            return None
        off = (x == 0) if t == 0 else (x == plan.gx - 1)
        return jnp.where(off, 0.0, 1.0)

    kerr, half_two, half_free, two = [], [], [], []
    for s in range(2):
        which = k if s == 0 else 1 - k
        kerr.append(coef[which, 0])
        two.append(coef[which, 1])
        half_two.append(0.5 * coef[which, 1])
        half_free.append(0.5 * coef[which, 2])

    def new_magnetic(old, new, s, p, t):
        ex, ey, ez, hx, hy, hz = old[6 * s : 6 * s + 6]
        here, beside = slice(8 * t, 8 * t + 8), slice(8 * t + 1, 8 * t + 9)
        vx, vy, vz = ex[p, here, :], ey[p, here, :], ez[p, here, :]
        nx = hx[p, here, :] - COURANT * ((up(vz) - vz) - (ey[p + 1, here, :] - vy))
        ny = hy[p, here, :] - COURANT * ((ex[p + 1, here, :] - vx) - (ez[p, beside, :] - vz))
        nz = hz[p, here, :] - COURANT * ((ey[p, beside, :] - vy) - (up(vx) - vx))
        mask = edge_mask(t)
        if mask is not None:
            nx, ny, nz = nx * mask, ny * mask, nz * mask
        new[6 * s + 3][p, here, :] = nx
        new[6 * s + 4][p, here, :] = ny
        new[6 * s + 5][p, here, :] = nz
        return vx, vy, vz, nx, ny, nz

    def full_plane(old, new, p):
        coarse = p // BLOCK_FACTOR
        zero = jnp.zeros(tile, F32)
        rolled = [[zero, zero], [zero, zero]]
        for t in range(plan.tiles):
            here = slice(8 * t, 8 * t + 8)
            back = [[new[6 * s + c][p - 1, here, :] for c in (3, 4)] for s in range(2)]
            vals = [new_magnetic(old, new, s, p, t) for s in range(2)]
            strength = [v[0] * v[0] + v[1] * v[1] + v[2] * v[2] for v in vals]
            is_silicon = silicon[p, here, :]
            total = (strength[0] + strength[1]) * is_silicon
            carriers = charge[coarse, here, :] * is_silicon
            ground = base[p, here, :]
            gen[p, here, :] += (two[0] * strength[0] + two[1] * strength[1]) * total
            mask = edge_mask(t)
            for s in range(2):
                vx, vy, vz, nx, ny, nz = vals[s]
                loss = half_two[s] * total + half_free[s] * carriers
                perm = ground + kerr[s] * total
                divisor = perm + loss
                inv = pl.reciprocal(divisor, approx=True)
                inv = inv * (2.0 - divisor * inv)
                keep = (perm - loss) * inv
                push = COURANT * inv
                if mask is not None:
                    push = push * mask
                turn_y, turn_z = pltpu.roll(ny, 1, 0), pltpu.roll(nz, 1, 0)
                left_y = jnp.where(at_top, rolled[s][0], turn_y)
                left_z = jnp.where(at_top, rolled[s][1], turn_z)
                rolled[s] = [turn_y, turn_z]
                curl_x = (nz - down(nz)) - (ny - back[s][1])
                curl_y = (nx - back[s][0]) - (nz - left_z)
                curl_z = (ny - left_y) - (nx - down(nx))
                new[6 * s][p, here, :] = keep * vx + push * curl_x
                new[6 * s + 1][p, here, :] = keep * vy + push * curl_y
                new[6 * s + 2][p, here, :] = keep * vz + push * curl_z

    def substep(old, new, n):
        @pl.when(jnp.logical_not(at_low))
        def _():
            for t in range(plan.tiles):
                for s in range(2):
                    new_magnetic(old, new, s, n, t)

        begin = jnp.where(at_low, DEEP, n + 1)
        end = jnp.where(at_high, DEEP + plan.own, plan.ext - 1 - n)

        def step(p, _):
            full_plane(old, new, p)
            return 0

        lax.fori_loop(begin, end, step, 0)

    def pair(m, _):
        substep(first, second, 2 * m)
        substep(second, first, 2 * m + 1)
        return 0

    lax.fori_loop(0, SUBSTEPS // 2, pair, 0)


def set_media(plan, code, base, silicon):
    def one(p, _):
        for t in range(plan.tiles):
            here = slice(8 * t, 8 * t + 8)
            v = code[p, here, :]
            base[p, here, :] = jnp.where(v == 0.0, SILICON_PERM, jnp.where(v == 1.0, OXIDE_PERM, 1.0))
            silicon[p, here, :] = jnp.where(v == 0.0, 1.0, 0.0)
        return 0

    lax.fori_loop(0, plan.ext, one, 0)


def clear_generation(plan, gen):
    def one(p, _):
        gen[p] = jnp.zeros((plan.rows, plan.lanes), F32)
        return 0

    lax.fori_loop(DEEP, DEEP + plan.own, one, 0)


def sum_generation(plan, gen, message):
    blocks = plan.cols // BLOCK_FACTOR
    lane = lax.broadcasted_iota(jnp.int32, (blocks, plan.lanes), 1)
    across = plan.own_rows()
    out = jnp.zeros((blocks, plan.lanes), F32)
    for a in range(plan.own // BLOCK_FACTOR):
        p = DEEP + BLOCK_FACTOR * a
        rows = (gen[p, across, :] + gen[p + 1, across, :]) + (
            gen[p + 2, across, :] + gen[p + 3, across, :]
        )
        cells = rows.reshape(blocks, BLOCK_FACTOR, plan.lanes).sum(1)
        mean = cells.sum(1, keepdims=True) * (1.0 / (BLOCK_FACTOR * BLOCK_FACTOR * plan.lanes))
        out = jnp.where(lane == a, mean, out)
    message[...] = out


def round_scratch(plan):
    wide = (plan.ext, plan.rows, plan.lanes)
    return [pltpu.VMEM(wide, F32)] * 27 + [
        pltpu.VMEM((plan.ext // BLOCK_FACTOR, plan.width, plan.lanes), F32),
        pltpu.VMEM((plan.cols // BLOCK_FACTOR, plan.lanes), F32),
    ]


def round_flops(plan):
    return SUBSTEPS * plan.ext * plan.width * plan.lanes * 150


def generation_shape(plan):
    return (plan.devices, plan.cols // BLOCK_FACTOR, plan.lanes)


def first_kernel(plan, *refs):
    nside = len(plan.sides)
    coef, density = refs[:2]
    raw, medium, swap, z_same, z_cross = refs[2:8], refs[8], refs[9:15], refs[15], refs[16]
    strips_in = refs[17 : 17 + 4 * nside]
    outs = refs[17 + 4 * nside : 22 + 7 * nside]
    own_out, z_out, core_out, gen_out, code_out = outs[:5]
    strip_out = outs[5:]
    rest = refs[22 + 7 * nside :]
    old, new, (base, silicon, gen, charge, message) = rest[:12], rest[12:24], rest[24:29]
    code, codes = rest[29:31]
    strips, strip_mine, sems = rest[31 : 31 + 4 * nside], rest[31 + 4 * nside : -1], rest[-1]
    copies = Copies(sems)
    z, x, k = (lax.axis_index(a) for a in LINE)
    near = DEEP * (1 - k)
    far = plan.part * k
    begin = (plan.own - DEEP) * k
    across = plan.own_rows()
    here, there = pl.ds(near, plan.part), pl.ds(far, DEEP)
    mine = pl.ds(begin, plan.part)
    early = [copies.start(medium.at[mine], codes)]
    early.append(copies.start(z_same.at[6], code.at[there, across]))
    for source, target in zip(strips_in, strips):
        early.append(copies.start(source, target))
    late = []
    for c in range(6):
        late.append(copies.start(raw[c].at[0, mine], old[c].at[here, across]))
        late.append(copies.start(swap[c].at[0, mine], old[6 + c].at[here, across]))
        late.append(copies.start(z_same.at[c], old[c].at[there, across]))
        late.append(copies.start(z_cross.at[c], old[6 + c].at[there, across]))
    clear(plan, old, new, [code])
    clear_generation(plan, gen)
    for a in range(plan.ext // BLOCK_FACTOR):
        top = (plan.planes * z + plan.own * k - DEEP) // BLOCK_FACTOR + a
        top = jnp.clip(top, 0, plan.grid_rows - 1)
        for c in range(plan.width // BLOCK_FACTOR):
            left = (plan.cols * x - plan.first_row()) // BLOCK_FACTOR + c
            left = jnp.clip(left, 0, plan.grid_cols - 1)
            value = density[top // plan.slab, top % plan.slab, left]
            charge[a, 4 * c : 4 * c + 4, :] = jnp.full((4, plan.lanes), value)
    wait(early)

    def settle(p, _):
        code[near + p, across, :] = codes[p].astype(F32)
        return 0

    lax.fori_loop(0, plan.part, settle, 0)

    def place(slot, side):
        x_same, x_cross, d_same, d_cross = strips[4 * slot : 4 * slot + 4]
        at = strip_row(plan, side)
        same = list(enumerate(list(old[:6]) + [code]))
        cross = list(enumerate(old[6:]))
        spread_strip(same, x_same, at, near, plan.part // 2)
        spread_strip(cross, x_cross, at, near, plan.part // 2)
        spread_strip(same, d_same, at, far, DEEP // 2)
        spread_strip(cross, d_cross, at, far, DEEP // 2)

    each_side(plan, place)
    set_media(plan, code, base, silicon)
    wait(late)
    substeps(plan, old, new, base, silicon, charge, gen, coef)
    toward = DEEP + (plan.own - DEEP) * k
    inward = DEEP + (plan.own - DEEP) * (1 - k)
    copies = Copies(sems)
    late = []
    for c in range(12):
        late.append(copies.start(old[c].at[pl.ds(toward, DEEP), across], z_out.at[c]))
        late.append(copies.start(old[c].at[pl.ds(inward, DEEP), across], core_out.at[c]))
        late.append(copies.start(old[c].at[pl.ds(DEEP, plan.own), across], own_out.at[c]))
    late.append(copies.start(code, code_out))

    def gather(slot, side):
        high_end = (side == "high") if plan.paired else (side == "low")
        low = 0 if plan.paired and side == "high" else 8
        at = low + plan.cols - 4 if high_end else low

        def one(q, _):
            for c in range(12):
                for h in range(2):
                    strip_mine[slot][c, q, 4 * h : 4 * h + 4, :] = old[c][
                        DEEP + 2 * q + h, at : at + 4, :
                    ]
            return 0

        lax.fori_loop(0, plan.own // 2, one, 0)

    each_side(plan, gather)
    half, top = DEEP // 2, (plan.own - DEEP) // 2
    for n in range(nside):
        whole, inner, corner = strip_out[3 * n : 3 * n + 3]
        late.append(copies.start(strip_mine[n], whole))
        late.append(copies.start(strip_mine[n].at[:, pl.ds(top * (1 - k), half)], inner))
        late.append(copies.start(strip_mine[n].at[:, pl.ds(top * k, half)], corner))
    sum_generation(plan, gen, message)
    for d in range(plan.devices):
        late.append(copies.start(message, gen_out.at[d]))
    wait(late)


def first_round(plan, coef, density, raw, medium, swap, z_same, z_cross, strips):
    wide = (plan.cols, plan.lanes)
    nside = len(plan.sides)
    shapes = [
        (12, plan.own) + wide,
        (12, DEEP) + wide,
        (12, DEEP) + wide,
        generation_shape(plan),
        (plan.ext, plan.rows, plan.lanes),
    ]
    for _ in plan.sides:
        for rows in (plan.own, DEEP, DEEP):
            shapes.append((12, rows // 2, 8, plan.lanes))
    scratch = round_scratch(plan) + [
        pltpu.VMEM((plan.ext, plan.rows, plan.lanes), F32),
        pltpu.VMEM((plan.part,) + wide, jnp.int32),
    ]
    scratch += [pltpu.VMEM(s.shape, F32) for s in strips]
    scratch += [pltpu.VMEM((12, plan.own // 2, 8, plan.lanes), F32)] * nside
    return call(
        plan,
        first_kernel,
        "first_round",
        shapes,
        [SMEM, SMEM] + [HBM] * (15 + 4 * nside),
        scratch,
        37 + 3 * nside + plan.devices,
        round_flops(plan),
        10_000_000,
    )(coef, density, *raw, medium, *swap, z_same, z_cross, *strips)


def second_kernel(plan, *refs):
    nside = len(plan.sides)
    coef, charge_in, code_in, own_in, z_in, core_in = refs[:6]
    strips_in = refs[6 : 6 + 3 * nside]
    outs = refs[6 + 3 * nside : 14 + 3 * nside]
    kept, sent, gen_out = outs[:6], outs[6], outs[7]
    rest = refs[14 + 3 * nside :]
    old, new, (base, silicon, gen, charge, message) = rest[:12], rest[12:24], rest[24:29]
    code, strips, sems = rest[29], rest[30:-1], rest[-1]
    copies = Copies(sems)
    k = lax.axis_index("af")
    across = plan.own_rows()
    outward = plan.part * k
    inner = plan.part * (1 - k)
    early = [copies.start(code_in, code), copies.start(charge_in, charge)]
    for source, target in zip(strips_in, strips):
        early.append(copies.start(source, target))
    late = []
    for c in range(12):
        flip = (c + 6) % 12
        late.append(copies.start(own_in.at[c], old[c].at[pl.ds(DEEP, plan.own), across]))
        late.append(copies.start(z_in.at[flip], old[c].at[pl.ds(outward, DEEP), across]))
        late.append(copies.start(core_in.at[flip], old[c].at[pl.ds(inner, DEEP), across]))
    clear(plan, old, new, [])
    clear_generation(plan, gen)
    wait(early)

    def place(slot, side):
        x_same, x_cross, diag = strips[3 * slot : 3 * slot + 3]
        at = strip_row(plan, side)
        same = list(enumerate(old))
        flipped = list(enumerate(list(old[6:]) + list(old[:6])))
        spread_strip(same, x_same, at, DEEP, plan.own // 2)
        spread_strip(flipped, x_cross, at, inner, DEEP // 2)
        spread_strip(flipped, diag, at, outward, DEEP // 2)

    each_side(plan, place)
    set_media(plan, code, base, silicon)
    wait(late)
    substeps(plan, old, new, base, silicon, charge, gen, coef)
    copies = Copies(sems)
    late = []
    for c in range(6):
        late.append(copies.start(old[6 + c].at[pl.ds(DEEP, plan.own), across], sent.at[c]))
    sum_generation(plan, gen, message)
    for d in range(plan.devices):
        late.append(copies.start(message, gen_out.at[d]))
    for c in range(6):
        target = kept[c].at[0, pl.ds(plan.own * k, plan.own)]
        late.append(copies.start(old[c].at[pl.ds(DEEP, plan.own), across], target))
    wait(late)


def second_round(plan, coef, charge, code, own_in, z_in, core_in, strips):
    wide = (plan.cols, plan.lanes)
    nside = len(plan.sides)
    shapes = [(1, plan.planes) + wide] * 6 + [(6, plan.own) + wide, generation_shape(plan)]
    scratch = round_scratch(plan) + [pltpu.VMEM((plan.ext, plan.rows, plan.lanes), F32)]
    scratch += [pltpu.VMEM(s.shape, F32) for s in strips]
    return call(
        plan,
        second_kernel,
        "second_round",
        shapes,
        [SMEM] + [HBM] * (5 + 3 * nside),
        scratch,
        max(38 + 3 * nside, 12 + plan.devices),
        round_flops(plan),
        10_000_000,
    )(coef, charge, code, own_in, z_in, core_in, *strips)


def join_kernel(plan, *refs):
    got, outs, sems = refs[6], refs[7:13], refs[13]
    copies = Copies(sems)
    k = lax.axis_index("af")
    rows = pl.ds(plan.own * (1 - k), plan.own)
    wait([copies.start(got.at[c], outs[c].at[0, rows]) for c in range(6)])


def join(plan, halves, got):
    shapes = [h.shape for h in halves]
    aliases = {c: c for c in range(6)}
    return call(
        plan, join_kernel, "join", shapes, [HBM] * 7, [], 6, moved=3_000_000, aliases=aliases
    )(*halves, got)


def carrier_kernel(plan, last, *refs):
    density_in, gens_in = refs[:2]
    outs = refs[2:3] if last else refs[2:4]
    gens, one, two, source, charge, sems = refs[2 + len(outs) :]
    copies = Copies(sems)
    rows, cols, lanes = plan.grid_rows, plan.grid_cols, plan.lanes
    z, x, k = (lax.axis_index(a) for a in LINE)
    blocks, own = plan.cols // BLOCK_FACTOR, plan.own // BLOCK_FACTOR
    early = [copies.start(gens_in, gens)]
    if last:
        early.append(copies.start(density_in, one.at[pl.ds(1, rows), pl.ds(8, cols)]))
    zero = jnp.zeros((8, lanes), F32)

    def clean(i, _):
        for ref in (one, two):
            ref[i, 0:8, :] = zero
            ref[i, 8 + cols : 16 + cols, :] = zero
        return 0

    lax.fori_loop(0, rows + 2, clean, 0)
    for ref in (one, two):
        for i in (0, rows + 1):
            for c in range(8, 8 + cols, 8):
                ref[i, c : c + 8, :] = zero
    if not last:

        def read(i, _):
            for c in range(cols):
                value = density_in[i // plan.slab, i % plan.slab, c]
                one[i + 1, 8 + c : 9 + c, :] = jnp.full((1, lanes), value)
            return 0

        lax.fori_loop(0, rows, read, 0)
    wait(early)

    def unpack(line, _):
        for dx in range(plan.gx):
            for dk in range(2):
                tile = gens[(line * plan.gx + dx) * 2 + dk]
                for a in range(own):
                    source[(line * 2 + dk) * own + a, blocks * dx : blocks * dx + blocks, :] = (
                        jnp.broadcast_to(tile[:, a : a + 1], (blocks, lanes))
                    )
        return 0

    lax.fori_loop(0, plan.gz, unpack, 0)

    def step(old, new):
        def row(i, _):
            for c in range(8, 8 + cols, 8):
                now, before = old[i + 1, c : c + 8, :], old[i, c : c + 8, :]
                around = (
                    old[i + 2, c : c + 8, :]
                    + before
                    + old[i + 1, c + 1 : c + 9, :]
                    + old[i + 1, c - 1 : c + 7, :]
                    - 4.0 * now
                )
                new[i + 1, c : c + 8, :] = (
                    now
                    + SPREAD_COEFF * around
                    - MOBILITY_TERM * (now - before)
                    - LIFETIME_DECAY * now
                    + SOURCE_FACTOR * source[i, c - 8 : c, :]
                )
            return 0

        lax.fori_loop(0, rows, row, 0, unroll=4)

    def pair(_, carry):
        step(one, two)
        step(two, one)
        return carry

    lax.fori_loop(0, CSTEPS // 2, pair, 0)
    if last:
        rows_out = pl.ds(1 + (z * plan.gx + x) * plan.slab, plan.slab)
        wait([copies.start(one.at[rows_out, pl.ds(8, cols)], outs[0])])
        return
    late = [copies.start(one.at[pl.ds(1, rows), pl.ds(8, cols)], outs[0])]
    for a in range(plan.ext // BLOCK_FACTOR):
        top = (plan.planes * z + plan.own * k - DEEP) // BLOCK_FACTOR + a
        top = 1 + jnp.clip(top, 0, rows - 1)
        for c in range(plan.width // BLOCK_FACTOR):
            left = (plan.cols * x - plan.first_row()) // BLOCK_FACTOR + c
            left = 8 + jnp.clip(left, 0, cols - 1)
            value = one[top, pl.ds(left, 1), :]
            charge[a, 4 * c : 4 * c + 4, :] = jnp.broadcast_to(value, (4, lanes))
    late.append(copies.start(charge, outs[1]))
    wait(late)


def carriers(plan, last, density, gens):
    rows, cols, lanes = plan.grid_rows, plan.grid_cols, plan.lanes
    charge = (plan.ext // BLOCK_FACTOR, plan.width, lanes)
    shapes = [(plan.slab, cols, lanes)] if last else [(rows, cols, lanes), charge]
    scratch = [
        pltpu.VMEM(gens.shape, F32),
        pltpu.VMEM((rows + 2, cols + 16, lanes), F32),
        pltpu.VMEM((rows + 2, cols + 16, lanes), F32),
        pltpu.VMEM((rows, cols, lanes), F32),
        pltpu.VMEM(charge, F32),
    ]
    return call(
        plan,
        lambda plan, *refs: carrier_kernel(plan, last, *refs),
        "carriers",
        shapes,
        [HBM if last else SMEM, HBM],
        scratch,
        4,
        2_000_000,
        1_000_000,
    )(density, gens)


def local(ex, ey, ez, hx, hy, hz, medium, coef, density):
    raw = (ex, ey, ez, hx, hy, hz)
    plan = Plan(*medium.shape, density.shape[0])

    def send(message, target):
        return lax.ppermute(message, LINE, line_pairs(plan, target))

    def spread(message, axes):
        return lax.all_to_all(message, axes, split_axis=0, concat_axis=0, tiled=True)

    toward = lambda z, goal: z + 1 if goal == 0 else z - 1
    core = lambda z, x, k: (z, x, 1 - k)

    packed = pack(plan, raw, medium)
    z_same, z_cross = packed[:2]
    strips = []
    for n, side in enumerate(plan.sides):
        to = functools.partial(across_step, side)
        x_same, x_cross, d_same, d_cross = packed[2 + 4 * n : 6 + 4 * n]
        strips.append(send(x_same, lambda z, x, k: (z, to(x), k)))
        strips.append(send(x_cross, lambda z, x, k: (z, to(x), 1 - k)))
        strips.append(send(d_same, lambda z, x, k: (toward(z, k), to(x), k)))
        strips.append(send(d_cross, lambda z, x, k: (toward(z, 1 - k), to(x), 1 - k)))
    z_same = send(z_same, lambda z, x, k: (toward(z, k), x, k))
    z_cross = send(z_cross, lambda z, x, k: (toward(z, 1 - k), x, 1 - k))
    swap = [send(r, core) for r in raw]
    tiles = plan.gz * plan.gx
    density = spread(jnp.broadcast_to(density, (tiles,) + density.shape), ("gz", "gx"))
    outs = first_round(plan, coef, density, raw, medium, swap, z_same, z_cross, strips)
    own, z_msg, core_msg, gens, code = outs[:5]
    gens = spread(gens, LINE)
    strips = []
    for n, side in enumerate(plan.sides):
        to = functools.partial(across_step, side)
        whole, inner, corner = outs[5 + 3 * n : 8 + 3 * n]
        strips.append(send(whole, lambda z, x, k: (z, to(x), k)))
        strips.append(send(inner, lambda z, x, k: (z, to(x), 1 - k)))
        strips.append(send(corner, lambda z, x, k: (toward(z, 1 - k), to(x), 1 - k)))
    z_msg = send(z_msg, lambda z, x, k: (toward(z, 1 - k), x, 1 - k))
    core_msg = send(core_msg, core)
    density, charge = carriers(plan, False, density, gens)
    outs = second_round(plan, coef, charge, code, own, z_msg, core_msg, strips)
    halves, sent, gens = outs[:6], outs[6], outs[7]
    gens = spread(gens, LINE)
    got = send(sent, core)
    (slab,) = carriers(plan, True, density, gens)
    return tuple(join(plan, halves, got)) + (slab[:, :, 0],)


def solution(mesh):
    field = P("af", ("group", "gz"), "gx", None)
    slabs = P(("group", "gz", "gx"), None)
    in_specs = (field,) * 6 + (P(("group", "gz"), "gx", None), P(), slabs)
    out_specs = (field,) * 6 + (slabs,)
    return jax.shard_map(local, mesh=mesh, in_specs=in_specs, out_specs=out_specs, check_vma=False)
```

time: 400 us -> 128 us (0.32)
  starting transfers between devices: 176 us -> 32.4 us
  waiting for transfers between devices: 126 us -> 17.2 us
  other arithmetic: 63.4 us -> 0 us
  Pallas kernels: 0 us -> 42.3 us
  blocking collectives: 0 us -> 22.3 us
  between operations: 15.9 us -> 0.83 us
    ppermute x72 -> x18, starting transfers between devices: 162 us -> 28.3 us  [send(): return lax.ppermute(message, LINE, line_pairs(plan, target))]
    ppermute x72 -> x18, waiting for transfers between devices: 92.7 us -> 11.9 us  [send(): return lax.ppermute(message, LINE, line_pairs(plan, target))]
    pallas_call x0 -> x6, Pallas kernels: none -> 42.3 us  [the longest x1 17 us: first_round(): call(plan, first_kernel, 'first_round', shapes, [SMEM, SMEM] + [HBM] * (1...]
    psum x2 -> x0, waiting for transfers between devices: 30.7 us -> none  [local(): blocky_pair_creation = restrict_mean(lax.psum(generation, 'af'))]
    sub x15 -> x0, other arithmetic: 25.3 us -> none  [the longest x7 15.7 us: advance(): keeping = permit - 0.5 * losses]
    all_to_all x0 -> x2, blocking collectives: none -> 22.3 us  [spread(): lax.all_to_all(message, axes, split_axis=0, concat_axis=0, tiled=True)]
    squeeze x23 -> x0, other arithmetic: 12.5 us -> none  [the longest x7 11 us: local(): inten_sum = intensity[0] + partner(intensity[0], 'af', 0)]
    all_to_all x4 -> x1, starting transfers between devices: 13.8 us -> 4.15 us  [spread(): lax.all_to_all(message, axes, split_axis=0, concat_axis=0, tiled=True)]
  transfers between devices with their start and end apart: 78 -> 19, of which waited for: 35 -> 3; matrix products, arithmetic and copies ran while one was open for 11% -> 1% of each run, Pallas kernels for 0% -> 6%
where the time goes in v1:
time: 128 us; the launch traced here: 127 us
  Pallas kernels  42.3 us (33%)
  starting transfers between devices  32.4 us (25%)
  blocking collectives  22.3 us (17%)
  waiting for transfers between devices  17.2 us (13%)
  local copies, waits for them, and re-layouts  12.4 us (10%)
    ppermute x18, starting transfers between devices, send(): return lax.ppermute(message, LINE, line_pairs(plan, target))  28.3 us
    all_to_all x2, blocking collectives, spread(): lax.all_to_all(message, axes, split_axis=0, concat_axis=0, tiled=True)  22.3 us
    pallas_call x1, Pallas kernels, first_round(): call(plan, first_kernel, 'first_round', shapes, [SMEM, SMEM] + [HBM] * (1...  17 us
    pallas_call x1, Pallas kernels, second_round(): call(plan, second_kernel, 'second_round', shapes, [SMEM] + [HBM] * (5 + 3...  16.3 us
    ppermute x18, waiting for transfers between devices, send(): return lax.ppermute(message, LINE, line_pairs(plan, target))  11.9 us
    unnamed x30, local copies, waits for them, and re-layouts  11.7 us
    pallas_call x2, Pallas kernels, carriers(): call(plan, lambda plan, *refs: carrier_kernel(plan, last, *refs), 'carrie...  5.9 us
    all_to_all x1, waiting for transfers between devices, spread(): lax.all_to_all(message, axes, split_axis=0, concat_axis=0, tiled=True)  5.27 us
  transfers between devices with their start and end apart: 19, of which 3 were waited for; matrix products, arithmetic and copies ran while one was open for 1% of the time, Pallas kernels for 6%

profile of v1, /device:TPU:0, one launch (start us, length us, event | category | flops | bytes accessed | tf_op | source)
XLA Modules:
  0.0 127.5 jit_solution(10134172896001657868)
XLA Ops:
  1.2 1.0 copy-done
  2.2 1.0 copy-done.1
  3.2 1.0 copy-done.2
  4.3 1.0 copy-done.3
  5.3 1.0 copy-done.4
  6.4 1.0 copy-done.5
  7.4 1.0 copy-done.6
  8.5 1.9 %pack.1 = (f32[7,4,32,128]{3,2,1,0:T(8,128)S(1)}, f32[6,4,32,128]{3,2,1,0:T(8,128)S(1)}, f32[7,10,8,128]{3,2,1,0:T(8,128)S(1)}, f32[6,10,8,128]{3,2,1,0:T(8,128)...) custom-call(f32[1,32,32,128]{3,2,1,0:T(8,128)S(1)} %copy-done, f32[1,32,32,128]{3,2,1,0:T(8,128)S(1)} %copy-done.1, ...), custom_call_target="tpu_custom_call" | custom-call | bytes 4000000 | tf_op jit(solution)/shard_map/pack/pallas_call | solution.py:187
  10.3 4.5 %collective-permute-start.6 = (f32[7,4,32,128]{3,2,1,0:T(8,128)S(1)}, f32[7,4,32,128]{3,2,1,0:T(8,128)S(1)}, u32[]{:S(2)}, u32[]{:S(2)}) collective-permute-start(f32[7,4,32,128]{3,2,1,0:T(8,128)S(1)} %get-tuple-element.37), channel_id=1, source_target_pairs={{0,4},{2,6},{4,8},{5,1},{6,10},{7,3},{8,12},{9,5},{10,14},{11,7},{... | collective-permute-start | bytes 1376264 | tf_op jit(solution)/shard_map/ppermute | solution.py:735
  14.8 0.7 collective-permute-start.7
  16.2 8.6 %collective-permute-start.10 = (f32[7,2,8,128]{3,2,1,0:T(8,128)S(1)}, f32[7,2,8,128]{3,2,1,0:T(8,128)S(1)}, u32[]{:S(2)}, u32[]{:S(2)}) collective-permute-start(f32[7,2,8,128]{3,2,1,0:T(8,128)S(1)} %get-tuple-element.41), channel_id=1, source_target_pairs={{0,6},{2,4},{4,10},{5,3},{6,8},{7,1},{8,14},{9,7},{10,12},{11,5},{... | collective-permute-start | bytes 172040 | tf_op jit(solution)/shard_map/ppermute | solution.py:735
  24.8 1.6 %collective-permute-start.8 = (f32[7,10,8,128]{3,2,1,0:T(8,128)S(1)}, f32[7,10,8,128]{3,2,1,0:T(8,128)S(1)}, u32[]{:S(2)}, u32[]{:S(2)}) collective-permute-start(f32[7,10,8,128]{3,2,1,0:T(8,128)S(1)} %get-tuple-element.39), channel_id=1, source_target_pairs={{0,2},{1,3},{2,0},{3,1},{4,6},{5,7},{6,4},{7,5},{8,10},{9,11},{10,... | collective-permute-start | bytes 860168 | tf_op jit(solution)/shard_map/ppermute | solution.py:735
  26.6 1.6 %collective-permute-start.9 = (f32[6,10,8,128]{3,2,1,0:T(8,128)S(1)}, f32[6,10,8,128]{3,2,1,0:T(8,128)S(1)}, u32[]{:S(2)}, u32[]{:S(2)}) collective-permute-start(f32[6,10,8,128]{3,2,1,0:T(8,128)S(1)} %get-tuple-element.40), channel_id=1, source_target_pairs={{0,3},{1,2},{2,1},{3,0},{4,7},{5,6},{6,5},{7,4},{8,11},{9,10},{10,... | collective-permute-start | bytes 737288 | tf_op jit(solution)/shard_map/ppermute | solution.py:735
  28.2 11.6 %collective-permute-done.9.refs_18_ = f32[6,10,8,128]{3,2,1,0:T(8,128)S(1)} collective-permute-done((f32[6,10,8,128]{3,2,1,0:T(8,128)S(1)}, f32[6,10,8,128]{3,2,1,0:T(8,128)S(1)}, u32[]{:S(2)}, u32[]{:S(2)}) %collective-permute-start.9) | collective-permute-done | bytes 245792 | tf_op jit(solution)/shard_map/ppermute | solution.py:735
  40.9 12.0 %all_to_all.15.refs_1_.refs_0_ = f32[8,4,16]{2,1,0:T(4,128)S(1)} all-to-all(f32[8,4,16]{2,1,0:T(4,128)S(1)} %broadcast_in_dim.3), channel_id=1, replica_groups=mesh['group'=2,'gz'=4,'gx'=2,'af'=2] {'gz','gx'}, dimensions={0} | all-to-all | bytes 4096 | tf_op jit(solution)/shard_map/all_to_all | solution.py:738
  53.0 17.0 %first_round.1 = (f32[12,16,32,128]{3,2,1,0:T(8,128)S(1)}, f32[12,4,32,128]{3,2,1,0:T(8,128)}, f32[12,4,32,128]{3,2,1,0:T(8,128)}, f32[16,8,128]{2,1,0:T(8,128)S...) custom-call(f32[2,3]{1,0:T(2,128)S(1)} %copy-done.10, ...), custom_call_target="tpu_custom_call" | custom-call | flops 73728000 | bytes 10000000 | tf_op jit(solution)/shard_map/first_round/pallas_call | solution.py:513
  70.0 0.8 copy-done.7
  72.7 1.5 %collective-permute-start.12 = (f32[12,4,32,128]{3,2,1,0:T(8,128)}, f32[12,4,32,128]{3,2,1,0:T(8,128)}, u32[]{:S(2)}, u32[]{:S(2)}) collective-permute-start(f32[12,4,32,128]{3,2,1,0:T(8,128)} %get-tuple-element.47), channel_id=1, source_target_pairs={{1,4},{3,6},{4,1},{5,8},{6,3},{7,10},{8,5},{9,12},{10,7},{11,14},{... | collective-permute-start | bytes 2359304 | tf_op jit(solution)/shard_map/ppermute | solution.py:735
  74.3 2.4 %collective-permute-start.13 = (f32[12,4,32,128]{3,2,1,0:T(8,128)}, f32[12,4,32,128]{3,2,1,0:T(8,128)}, u32[]{:S(2)}, u32[]{:S(2)}) collective-permute-start(f32[12,4,32,128]{3,2,1,0:T(8,128)} %get-tuple-element.48), channel_id=1, source_target_pairs={{0,1},{1,0},{2,3},{3,2},{4,5},{5,4},{6,7},{7,6},{8,9},{9,8},{10,11... | collective-permute-start | bytes 2359304 | tf_op jit(solution)/shard_map/ppermute | solution.py:735
  76.7 0.7 collective-permute-start.14
  77.4 4.2 %all-to-all-start.1 = ((f32[16,8,128]{2,1,0:T(8,128)}), f32[16,8,128]{2,1,0:T(8,128)}, u32[]{:S(2)}, u32[]{:S(2)}) async-start(f32[16,8,128]{2,1,0:T(8,128)} %copy-done.9), calls=%async_computation.1 | async-start | bytes 131072 | tf_op jit(solution)/shard_map/all_to_all | solution.py:738
  81.5 1.5 %collective-permute-start.15 = (f32[12,2,8,128]{3,2,1,0:T(8,128)}, f32[12,2,8,128]{3,2,1,0:T(8,128)}, u32[]{:S(2)}, u32[]{:S(2)}) collective-permute-start(f32[12,2,8,128]{3,2,1,0:T(8,128)} %copy-done.13), channel_id=1, source_target_pairs={{0,3},{1,2},{2,1},{3,0},{4,7},{5,6},{6,5},{7,4},{8,11},{9,10},{10,... | collective-permute-start | bytes 294920 | tf_op jit(solution)/shard_map/ppermute | solution.py:735
  83.0 1.3 %collective-permute-start.16 = (f32[12,2,8,128]{3,2,1,0:T(8,128)}, f32[12,2,8,128]{3,2,1,0:T(8,128)}, u32[]{:S(2)}, u32[]{:S(2)}) collective-permute-start(f32[12,2,8,128]{3,2,1,0:T(8,128)} %copy-done.12), channel_id=1, source_target_pairs={{1,6},{3,4},{4,3},{5,10},{6,1},{7,8},{8,7},{9,14},{10,5},{11,12},{... | collective-permute-start | bytes 294920 | tf_op jit(solution)/shard_map/ppermute | solution.py:735
  84.3 5.3 %all-to-all-done.1.refs_1_ = f32[16,8,128]{2,1,0:T(8,128)} async-done(((f32[16,8,128]{2,1,0:T(8,128)}), f32[16,8,128]{2,1,0:T(8,128)}, u32[]{:S(2)}, u32[]{:S(2)}) %all-to-all-start.1) | async-done | bytes 65568 | tf_op jit(solution)/shard_map/all_to_all | solution.py:738
  89.6 3.8 %carriers.2 = (f32[32,16,128]{2,1,0:T(8,128)S(1)}, f32[6,40,128]{2,1,0:T(8,128)S(1)}) custom-call(f32[8,4,16]{2,1,0:T(4,128)S(1)} %all_to_all.15.refs_1_.refs_0_, f32[16,8,128]{2,1,0:T(8,128)} %all-to-all-done.1.refs_1_), custom_call_target="tpu_custom_call" | custom-call | flops 2000000 | bytes 1000000 | tf_op jit(solution)/shard_map/carriers/pallas_call | solution.py:717
  93.4 1.1 copy-done.8
  94.5 0.7 copy-done.11
  95.2 16.3 %second_round.1 = (f32[1,32,32,128]{3,2,1,0:T(8,128)}, f32[1,32,32,128]{3,2,1,0:T(8,128)}, f32[1,32,32,128]{3,2,1,0:T(8,128)}, f32[1,32,32,128]{3,2,1,0:T(8,128)...) custom-call(f32[2,3]{1,0:T(2,128)S(1)} %copy-done.11, ...), custom_call_target="tpu_custom_call" | custom-call | flops 73728000 | bytes 10000000 | tf_op jit(solution)/shard_map/second_round/pallas_call | solution.py:585
  111.4 1.7 %collective-permute-start.17 = (f32[6,16,32,128]{3,2,1,0:T(8,128)S(1)}, f32[6,16,32,128]{3,2,1,0:T(8,128)S(1)}, u32[]{:S(2)}, u32[]{:S(2)}) collective-permute-start(f32[6,16,32,128]{3,2,1,0:T(8,128)S(1)} %get-tuple-element.58), channel_id=1, source_target_pairs={{0,1},{1,0},{2,3},{3,2},{4,5},{5,4},{6,7},{7,6},{8,9},{9,8},{10,11... | collective-permute-start | bytes 4718600 | tf_op jit(solution)/shard_map/ppermute | solution.py:735
  113.1 10.3 %all_to_all.16.refs_1_ = f32[16,8,128]{2,1,0:T(8,128)S(1)} all-to-all(f32[16,8,128]{2,1,0:T(8,128)S(1)} %get-tuple-element.66), channel_id=1, replica_groups=mesh['group'=2,'gz'=4,'gx'=2,'af'=2] {'gz','gx','af'}, dimensions={0} | all-to-all | bytes 131072 | tf_op jit(solution)/shard_map/all_to_all | solution.py:738
  123.5 2.1 %carriers.3 = f32[4,16,128]{2,1,0:T(8,128)S(1)} custom-call(f32[32,16,128]{2,1,0:T(8,128)S(1)} %get-tuple-element.65.refs_0_, f32[16,8,128]{2,1,0:T(8,128)S(1)} %all_to_all.16.refs_1_), custom_call_target="tpu_custom_call" | custom-call | flops 2000000 | bytes 1000000 | tf_op jit(solution)/shard_map/carriers/pallas_call | solution.py:717
  126.3 1.2 join.1
  (46 shorter events, 5.2 us)
Async XLA Ops:
  0.6 40.2 %collective-permute-start = (f32[1,32,32,128]{3,2,1,0:T(8,128)}, f32[1,32,32,128]{3,2,1,0:T(8,128)S(1)}, u32[]{:S(2)}, u32[]{:S(2)}) collective-permute-start(f32[1,32,32,128]{3,2,1,0:T(8,128)} %refs_2_.3), channel_id=1, source_target_pairs={{0,1},{1,0},{2,3},{3,2},{4,5},{5,4},{6,7},{7,6},{8,9},{9,8},{10,11... | collective-permute-start | bytes 1572872 | tf_op jit(solution)/shard_map/ppermute | solution.py:735
  1.2 1.0 copy-start
  2.2 1.0 copy-start.1
  3.2 1.0 copy-start.2
  4.3 1.0 copy-start.3
  5.3 1.0 copy-start.4
  6.4 1.0 copy-start.5
  7.4 1.0 copy-start.6
  8.4 32.5 %copy-start.14 = (f32[4,16]{1,0:T(4,128)S(1)}, f32[4,16]{1,0:T(4,128)}, u32[]{:S(2)}) copy-start(f32[4,16]{1,0:T(4,128)} %param.17) | copy-start | bytes 772
  8.4 44.5 %copy-start.10 = (f32[2,3]{1,0:T(2,128)S(1)}, f32[2,3]{1,0:T(2,128)}, u32[]{:S(2)}) copy-start(f32[2,3]{1,0:T(2,128)} %refs_0_.5) | copy-start | bytes 76
  10.3 30.1 %collective-permute-start.6 = (f32[7,4,32,128]{3,2,1,0:T(8,128)S(1)}, f32[7,4,32,128]{3,2,1,0:T(8,128)S(1)}, u32[]{:S(2)}, u32[]{:S(2)}) collective-permute-start(f32[7,4,32,128]{3,2,1,0:T(8,128)S(1)} %get-tuple-element.37), channel_id=1, source_target_pairs={{0,4},{2,6},{4,8},{5,1},{6,10},{7,3},{8,12},{9,5},{10,14},{11,7},{... | collective-permute-start | bytes 1376264 | tf_op jit(solution)/shard_map/ppermute | solution.py:735
  14.8 25.5 %collective-permute-start.7 = (f32[6,4,32,128]{3,2,1,0:T(8,128)S(1)}, f32[6,4,32,128]{3,2,1,0:T(8,128)S(1)}, u32[]{:S(2)}, u32[]{:S(2)}) collective-permute-start(f32[6,4,32,128]{3,2,1,0:T(8,128)S(1)} %get-tuple-element.38), channel_id=1, source_target_pairs={{1,4},{3,6},{4,1},{5,8},{6,3},{7,10},{8,5},{9,12},{10,7},{11,14},{... | collective-permute-start | bytes 1179656 | tf_op jit(solution)/shard_map/ppermute | solution.py:735
  15.5 9.3 %collective-permute-start.11 = (f32[6,2,8,128]{3,2,1,0:T(8,128)S(1)}, f32[6,2,8,128]{3,2,1,0:T(8,128)S(1)}, u32[]{:S(2)}, u32[]{:S(2)}) collective-permute-start(f32[6,2,8,128]{3,2,1,0:T(8,128)S(1)} %get-tuple-element.42), channel_id=1, source_target_pairs={{1,6},{3,4},{4,3},{5,10},{6,1},{7,8},{8,7},{9,14},{10,5},{11,12},{... | collective-permute-start | bytes 147464 | tf_op jit(solution)/shard_map/ppermute | solution.py:735
  16.2 10.4 %collective-permute-start.10 = (f32[7,2,8,128]{3,2,1,0:T(8,128)S(1)}, f32[7,2,8,128]{3,2,1,0:T(8,128)S(1)}, u32[]{:S(2)}, u32[]{:S(2)}) collective-permute-start(f32[7,2,8,128]{3,2,1,0:T(8,128)S(1)} %get-tuple-element.41), channel_id=1, source_target_pairs={{0,6},{2,4},{4,10},{5,3},{6,8},{7,1},{8,14},{9,7},{10,12},{11,5},{... | collective-permute-start | bytes 172040 | tf_op jit(solution)/shard_map/ppermute | solution.py:735
  24.8 15.0 %collective-permute-start.8 = (f32[7,10,8,128]{3,2,1,0:T(8,128)S(1)}, f32[7,10,8,128]{3,2,1,0:T(8,128)S(1)}, u32[]{:S(2)}, u32[]{:S(2)}) collective-permute-start(f32[7,10,8,128]{3,2,1,0:T(8,128)S(1)} %get-tuple-element.39), channel_id=1, source_target_pairs={{0,2},{1,3},{2,0},{3,1},{4,6},{5,7},{6,4},{7,5},{8,10},{9,11},{10,... | collective-permute-start | bytes 860168 | tf_op jit(solution)/shard_map/ppermute | solution.py:735
  26.6 13.2 %collective-permute-start.9 = (f32[6,10,8,128]{3,2,1,0:T(8,128)S(1)}, f32[6,10,8,128]{3,2,1,0:T(8,128)S(1)}, u32[]{:S(2)}, u32[]{:S(2)}) collective-permute-start(f32[6,10,8,128]{3,2,1,0:T(8,128)S(1)} %get-tuple-element.40), channel_id=1, source_target_pairs={{0,3},{1,2},{2,1},{3,0},{4,7},{5,6},{6,5},{7,4},{8,11},{9,10},{10,... | collective-permute-start | bytes 737288 | tf_op jit(solution)/shard_map/ppermute | solution.py:735
  39.8 13.1 %collective-permute-start.1 = (f32[1,32,32,128]{3,2,1,0:T(8,128)S(1)}, f32[1,32,32,128]{3,2,1,0:T(8,128)S(1)}, u32[]{:S(2)}, u32[]{:S(2)}) collective-permute-start(f32[1,32,32,128]{3,2,1,0:T(8,128)S(1)} %copy-done.1), channel_id=1, source_target_pairs={{0,1},{1,0},{2,3},{3,2},{4,5},{5,4},{6,7},{7,6},{8,9},{9,8},{10,11... | collective-permute-start | bytes 1572872 | tf_op jit(solution)/shard_map/ppermute | solution.py:735
  39.8 13.1 %collective-permute-start.2 = (f32[1,32,32,128]{3,2,1,0:T(8,128)S(1)}, f32[1,32,32,128]{3,2,1,0:T(8,128)S(1)}, u32[]{:S(2)}, u32[]{:S(2)}) collective-permute-start(f32[1,32,32,128]{3,2,1,0:T(8,128)S(1)} %copy-done.2), channel_id=1, source_target_pairs={{0,1},{1,0},{2,3},{3,2},{4,5},{5,4},{6,7},{7,6},{8,9},{9,8},{10,11... | collective-permute-start | bytes 1572872 | tf_op jit(solution)/shard_map/ppermute | solution.py:735
  40.4 12.6 %collective-permute-start.3 = (f32[1,32,32,128]{3,2,1,0:T(8,128)S(1)}, f32[1,32,32,128]{3,2,1,0:T(8,128)S(1)}, u32[]{:S(2)}, u32[]{:S(2)}) collective-permute-start(f32[1,32,32,128]{3,2,1,0:T(8,128)S(1)} %copy-done.3), channel_id=1, source_target_pairs={{0,1},{1,0},{2,3},{3,2},{4,5},{5,4},{6,7},{7,6},{8,9},{9,8},{10,11... | collective-permute-start | bytes 1572872 | tf_op jit(solution)/shard_map/ppermute | solution.py:735
  40.4 12.5 %collective-permute-start.4 = (f32[1,32,32,128]{3,2,1,0:T(8,128)S(1)}, f32[1,32,32,128]{3,2,1,0:T(8,128)S(1)}, u32[]{:S(2)}, u32[]{:S(2)}) collective-permute-start(f32[1,32,32,128]{3,2,1,0:T(8,128)S(1)} %copy-done.4), channel_id=1, source_target_pairs={{0,1},{1,0},{2,3},{3,2},{4,5},{5,4},{6,7},{7,6},{8,9},{9,8},{10,11... | collective-permute-start | bytes 1572872 | tf_op jit(solution)/shard_map/ppermute | solution.py:735
  40.9 12.1 %collective-permute-start.5 = (f32[1,32,32,128]{3,2,1,0:T(8,128)S(1)}, f32[1,32,32,128]{3,2,1,0:T(8,128)S(1)}, u32[]{:S(2)}, u32[]{:S(2)}) collective-permute-start(f32[1,32,32,128]{3,2,1,0:T(8,128)S(1)} %copy-done.5), channel_id=1, source_target_pairs={{0,1},{1,0},{2,3},{3,2},{4,5},{5,4},{6,7},{7,6},{8,9},{9,8},{10,11... | collective-permute-start | bytes 1572872 | tf_op jit(solution)/shard_map/ppermute | solution.py:735
  70.0 0.8 copy-start.7
  71.5 0.6 copy-start.12
  72.7 20.6 %collective-permute-start.12 = (f32[12,4,32,128]{3,2,1,0:T(8,128)}, f32[12,4,32,128]{3,2,1,0:T(8,128)}, u32[]{:S(2)}, u32[]{:S(2)}) collective-permute-start(f32[12,4,32,128]{3,2,1,0:T(8,128)} %get-tuple-element.47), channel_id=1, source_target_pairs={{1,4},{3,6},{4,1},{5,8},{6,3},{7,10},{8,5},{9,12},{10,7},{11,14},{... | collective-permute-start | bytes 2359304 | tf_op jit(solution)/shard_map/ppermute | solution.py:735
  74.3 19.1 %collective-permute-start.13 = (f32[12,4,32,128]{3,2,1,0:T(8,128)}, f32[12,4,32,128]{3,2,1,0:T(8,128)}, u32[]{:S(2)}, u32[]{:S(2)}) collective-permute-start(f32[12,4,32,128]{3,2,1,0:T(8,128)} %get-tuple-element.48), channel_id=1, source_target_pairs={{0,1},{1,0},{2,3},{3,2},{4,5},{5,4},{6,7},{7,6},{8,9},{9,8},{10,11... | collective-permute-start | bytes 2359304 | tf_op jit(solution)/shard_map/ppermute | solution.py:735
  76.7 16.7 %collective-permute-start.14 = (f32[12,8,8,128]{3,2,1,0:T(8,128)}, f32[12,8,8,128]{3,2,1,0:T(8,128)S(1)}, u32[]{:S(2)}, u32[]{:S(2)}) collective-permute-start(f32[12,8,8,128]{3,2,1,0:T(8,128)} %get-tuple-element.49), channel_id=1, source_target_pairs={{0,2},{1,3},{2,0},{3,1},{4,6},{5,7},{6,4},{7,5},{8,10},{9,11},{10,... | collective-permute-start | bytes 1179656 | tf_op jit(solution)/shard_map/ppermute | solution.py:735
  77.4 12.2 %all-to-all-start.1 = ((f32[16,8,128]{2,1,0:T(8,128)}), f32[16,8,128]{2,1,0:T(8,128)}, u32[]{:S(2)}, u32[]{:S(2)}) async-start(f32[16,8,128]{2,1,0:T(8,128)} %copy-done.9), calls=%async_computation.1 | async-start | bytes 131072 | tf_op jit(solution)/shard_map/all_to_all | solution.py:738
  81.5 11.8 %collective-permute-start.15 = (f32[12,2,8,128]{3,2,1,0:T(8,128)}, f32[12,2,8,128]{3,2,1,0:T(8,128)}, u32[]{:S(2)}, u32[]{:S(2)}) collective-permute-start(f32[12,2,8,128]{3,2,1,0:T(8,128)} %copy-done.13), channel_id=1, source_target_pairs={{0,3},{1,2},{2,1},{3,0},{4,7},{5,6},{6,5},{7,4},{8,11},{9,10},{10,... | collective-permute-start | bytes 294920 | tf_op jit(solution)/shard_map/ppermute | solution.py:735
  83.0 10.3 %collective-permute-start.16 = (f32[12,2,8,128]{3,2,1,0:T(8,128)}, f32[12,2,8,128]{3,2,1,0:T(8,128)}, u32[]{:S(2)}, u32[]{:S(2)}) collective-permute-start(f32[12,2,8,128]{3,2,1,0:T(8,128)} %copy-done.12), channel_id=1, source_target_pairs={{1,6},{3,4},{4,3},{5,10},{6,1},{7,8},{8,7},{9,14},{10,5},{11,12},{... | collective-permute-start | bytes 294920 | tf_op jit(solution)/shard_map/ppermute | solution.py:735
  93.4 1.1 copy-start.8
  94.5 0.7 copy-start.11
  111.4 14.8 %collective-permute-start.17 = (f32[6,16,32,128]{3,2,1,0:T(8,128)S(1)}, f32[6,16,32,128]{3,2,1,0:T(8,128)S(1)}, u32[]{:S(2)}, u32[]{:S(2)}) collective-permute-start(f32[6,16,32,128]{3,2,1,0:T(8,128)S(1)} %get-tuple-element.58), channel_id=1, source_target_pairs={{0,1},{1,0},{2,3},{3,2},{4,5},{5,4},{6,7},{7,6},{8,9},{9,8},{10,11... | collective-permute-start | bytes 4718600 | tf_op jit(solution)/shard_map/ppermute | solution.py:735
  (2 other events, 1.3 us)

commit v2 on v1

--- a/solution.py
+++ b/solution.py
@@ -25,6 +25,7 @@
 HBM = pl.BlockSpec(memory_space=pltpu.HBM)
 SMEM = pl.BlockSpec(memory_space=pltpu.SMEM)
 VMEM_LIMIT = 32 * 1024 * 1024
+PACK_LIMIT = 60 * 1024 * 1024
 F32 = jnp.float32
 
 
@@ -101,7 +102,7 @@
         copy.wait()
 
 
-def call(plan, body, name, shapes, in_specs, scratch, copies, flops=0, moved=0, aliases=None):
+def call(plan, body, name, shapes, in_specs, scratch, copies, flops=0, moved=0, aliases=None, limit=VMEM_LIMIT):
     return pl.pallas_call(
         functools.partial(body, plan),
         out_shape=[jax.ShapeDtypeStruct(s, F32) for s in shapes],
@@ -109,39 +110,29 @@
         out_specs=[HBM] * len(shapes),
         scratch_shapes=scratch + [pltpu.SemaphoreType.DMA((copies,))],
         input_output_aliases=aliases or {},
-        compiler_params=pltpu.CompilerParams(vmem_limit_bytes=VMEM_LIMIT),
+        compiler_params=pltpu.CompilerParams(vmem_limit_bytes=limit),
         cost_estimate=pl.CostEstimate(flops=flops, bytes_accessed=moved, transcendentals=0),
         name=name,
     )
 
 
-def pack_kernel(plan, *refs):
+def pack_strips_kernel(plan, *refs):
     raw, medium = refs[:6], refs[6]
-    z_same, z_cross = refs[7:9]
     nside = len(plan.sides)
-    outs = refs[9 : 9 + 4 * nside]
-    edge, edge_code, face_code, face_float, strips, sems = refs[9 + 4 * nside :]
+    outs = refs[7 : 7 + 4 * nside]
+    edge, edge_code, strips, sems = refs[7 + 4 * nside :]
     copies = Copies(sems)
     k = lax.axis_index("af")
-    last = plan.planes - DEEP
-    to_same = jnp.where(k == 0, last, 0)
-    to_cross = jnp.where(k == 0, 0, last)
     if plan.paired:
         tile_rows = [pl.multiple_of((plan.cols - 8) * (1 - lax.axis_index("gx")), 8)]
     else:
         tile_rows = [plan.cols - 8, 0]
-    fast, slow = [], []
+    fast = []
     for n, row in enumerate(tile_rows):
         for c in range(6):
             fast.append(copies.start(raw[c].at[0, :, pl.ds(row, 8), :], edge.at[n, c]))
         fast.append(copies.start(medium.at[:, pl.ds(row, 8), :], edge_code.at[n]))
-    fast.append(copies.start(medium.at[pl.ds(to_same, DEEP)], face_code))
-    for c in range(6):
-        slow.append(copies.start(raw[c].at[0, pl.ds(to_same, DEEP)], z_same.at[c]))
-        slow.append(copies.start(raw[c].at[0, pl.ds(to_cross, DEEP)], z_cross.at[c]))
     wait(fast)
-    face_float[...] = face_code[...].astype(F32)
-    slow.append(copies.start(face_float, z_same.at[6]))
 
     def fill(slot, low):
         def rows(q, _):
@@ -157,6 +148,9 @@
 
     each_side(plan, lambda slot, side: fill(slot, 4 if plan.paired == (side == "high") else 0))
     quarter = (plan.own - DEEP) // 2
+    last = plan.planes - DEEP
+    to_same, to_cross = last * (1 - k), last * k
+    late = []
     for n in range(nside):
         x_same, x_cross, d_same, d_cross = outs[4 * n : 4 * n + 4]
         pairs, six = plan.part // 2, pl.ds(0, 6)
@@ -166,27 +160,70 @@
             (strips.at[n, :, pl.ds(to_same // 2, DEEP // 2)], d_same),
             (strips.at[n, six, pl.ds(to_cross // 2, DEEP // 2)], d_cross),
         ):
-            slow.append(copies.start(source, target))
-    wait(slow)
-
-
-def pack(plan, raw, medium):
-    wide = (plan.cols, plan.lanes)
+            late.append(copies.start(source, target))
+    wait(late)
+
+
+def pack_strips(plan, raw, medium):
     nside = len(plan.sides)
-    shapes = [(7, DEEP) + wide, (6, DEEP) + wide]
+    shapes = []
     for _ in plan.sides:
         for comps, rows in ((7, plan.part), (6, plan.part), (7, DEEP), (6, DEEP)):
             shapes.append((comps, rows // 2, 8, plan.lanes))
     scratch = [
         pltpu.VMEM((nside, 6, plan.planes, 8, plan.lanes), F32),
         pltpu.VMEM((nside, plan.planes, 8, plan.lanes), jnp.int32),
-        pltpu.VMEM((DEEP,) + wide, jnp.int32),
-        pltpu.VMEM((DEEP,) + wide, F32),
         pltpu.VMEM((nside, 7, plan.planes // 2, 8, plan.lanes), F32),
     ]
     return call(
-        plan, pack_kernel, "pack", shapes, [HBM] * 7, scratch, 11 * nside + 14, moved=4_000_000
+        plan,
+        pack_strips_kernel,
+        "pack_strips",
+        shapes,
+        [HBM] * 7,
+        scratch,
+        11 * nside,
+        moved=1_000_000,
+        limit=PACK_LIMIT,
     )(*raw, medium)
+
+
+def pack_faces_kernel(plan, *refs):
+    raw, medium = refs[:6], refs[6]
+    z_same, z_cross, swap = refs[8:11]
+    face_code, face_float, sems = refs[11:]
+    copies = Copies(sems)
+    k = lax.axis_index("af")
+    last = plan.planes - DEEP
+    to_same, to_cross = last * (1 - k), last * k
+    early = copies.start(medium.at[pl.ds(to_same, DEEP)], face_code)
+    late = []
+    for c in range(6):
+        late.append(copies.start(raw[c].at[0, pl.ds(to_same, DEEP)], z_same.at[c]))
+        late.append(copies.start(raw[c].at[0, pl.ds(to_cross, DEEP)], z_cross.at[c]))
+        part = pl.ds((plan.own - DEEP) * (1 - k), plan.part)
+        late.append(copies.start(raw[c].at[0, part], swap.at[c]))
+    early.wait()
+    face_float[...] = face_code[...].astype(F32)
+    late.append(copies.start(face_float, z_same.at[6]))
+    wait(late)
+
+
+def pack_faces(plan, raw, medium, after):
+    wide = (plan.cols, plan.lanes)
+    shapes = [(7, DEEP) + wide, (6, DEEP) + wide, (6, plan.part) + wide]
+    scratch = [pltpu.VMEM((DEEP,) + wide, jnp.int32), pltpu.VMEM((DEEP,) + wide, F32)]
+    return call(
+        plan,
+        pack_faces_kernel,
+        "pack_faces",
+        shapes,
+        [HBM] * 8,
+        scratch,
+        20,
+        moved=4_000_000,
+        limit=PACK_LIMIT,
+    )(*raw, medium, after)
 
 
 def clear(plan, old, new, code):
@@ -372,14 +409,16 @@
         cells = rows.reshape(blocks, BLOCK_FACTOR, plan.lanes).sum(1)
         mean = cells.sum(1, keepdims=True) * (1.0 / (BLOCK_FACTOR * BLOCK_FACTOR * plan.lanes))
         out = jnp.where(lane == a, mean, out)
-    message[...] = out
+    z, x, k = (lax.axis_index(axis) for axis in LINE)
+    message[...] = jnp.zeros(message.shape, F32)
+    message[(z * plan.gx + x) * 2 + k] = out
 
 
 def round_scratch(plan):
     wide = (plan.ext, plan.rows, plan.lanes)
     return [pltpu.VMEM(wide, F32)] * 27 + [
         pltpu.VMEM((plan.ext // BLOCK_FACTOR, plan.width, plan.lanes), F32),
-        pltpu.VMEM((plan.cols // BLOCK_FACTOR, plan.lanes), F32),
+        pltpu.VMEM(generation_shape(plan), F32),
     ]
 
 
@@ -394,12 +433,16 @@
 def first_kernel(plan, *refs):
     nside = len(plan.sides)
     coef, density = refs[:2]
-    raw, medium, swap, z_same, z_cross = refs[2:8], refs[8], refs[9:15], refs[15], refs[16]
-    strips_in = refs[17 : 17 + 4 * nside]
-    outs = refs[17 + 4 * nside : 22 + 7 * nside]
+    x_in, d_in = refs[2 : 2 + 2 * nside], refs[5 + 2 * nside : 5 + 4 * nside]
+    z_same, z_cross, swap = refs[2 + 2 * nside : 5 + 2 * nside]
+    raw, medium = refs[5 + 4 * nside : 11 + 4 * nside], refs[11 + 4 * nside]
+    strips_in = []
+    for n in range(nside):
+        strips_in += [*x_in[2 * n : 2 * n + 2], *d_in[2 * n : 2 * n + 2]]
+    outs = refs[12 + 4 * nside : 17 + 7 * nside]
     own_out, z_out, core_out, gen_out, code_out = outs[:5]
     strip_out = outs[5:]
-    rest = refs[22 + 7 * nside :]
+    rest = refs[17 + 7 * nside :]
     old, new, (base, silicon, gen, charge, message) = rest[:12], rest[12:24], rest[24:29]
     code, codes = rest[29:31]
     strips, strip_mine, sems = rest[31 : 31 + 4 * nside], rest[31 + 4 * nside : -1], rest[-1]
@@ -418,7 +461,7 @@
     late = []
     for c in range(6):
         late.append(copies.start(raw[c].at[0, mine], old[c].at[here, across]))
-        late.append(copies.start(swap[c].at[0, mine], old[6 + c].at[here, across]))
+        late.append(copies.start(swap.at[c], old[6 + c].at[here, across]))
         late.append(copies.start(z_same.at[c], old[c].at[there, across]))
         late.append(copies.start(z_cross.at[c], old[6 + c].at[there, across]))
     clear(plan, old, new, [code])
@@ -429,7 +472,7 @@
         for c in range(plan.width // BLOCK_FACTOR):
             left = (plan.cols * x - plan.first_row()) // BLOCK_FACTOR + c
             left = jnp.clip(left, 0, plan.grid_cols - 1)
-            value = density[top // plan.slab, top % plan.slab, left]
+            value = density[2 * (top // plan.slab), top % plan.slab, left]
             charge[a, 4 * c : 4 * c + 4, :] = jnp.full((4, plan.lanes), value)
     wait(early)
 
@@ -486,8 +529,7 @@
         late.append(copies.start(strip_mine[n].at[:, pl.ds(top * (1 - k), half)], inner))
         late.append(copies.start(strip_mine[n].at[:, pl.ds(top * k, half)], corner))
     sum_generation(plan, gen, message)
-    for d in range(plan.devices):
-        late.append(copies.start(message, gen_out.at[d]))
+    late.append(copies.start(message, gen_out))
     wait(late)
 
 
@@ -510,23 +552,27 @@
     ]
     scratch += [pltpu.VMEM(s.shape, F32) for s in strips]
     scratch += [pltpu.VMEM((12, plan.own // 2, 8, plan.lanes), F32)] * nside
+    x_in, d_in = [], []
+    for n in range(nside):
+        x_in += strips[4 * n : 4 * n + 2]
+        d_in += strips[4 * n + 2 : 4 * n + 4]
     return call(
         plan,
         first_kernel,
         "first_round",
         shapes,
-        [SMEM, SMEM] + [HBM] * (15 + 4 * nside),
+        [SMEM, SMEM] + [HBM] * (10 + 4 * nside),
         scratch,
-        37 + 3 * nside + plan.devices,
+        38 + 3 * nside,
         round_flops(plan),
         10_000_000,
-    )(coef, density, *raw, medium, *swap, z_same, z_cross, *strips)
+    )(coef, density, *x_in, z_same, z_cross, swap, *d_in, *raw, medium)
 
 
 def second_kernel(plan, *refs):
     nside = len(plan.sides)
-    coef, charge_in, code_in, own_in, z_in, core_in = refs[:6]
-    strips_in = refs[6 : 6 + 3 * nside]
+    strips_in = refs[: 3 * nside]
+    z_in, core_in, own_in, code_in, charge_in, coef = refs[3 * nside : 6 + 3 * nside]
     outs = refs[6 + 3 * nside : 14 + 3 * nside]
     kept, sent, gen_out = outs[:6], outs[6], outs[7]
     rest = refs[14 + 3 * nside :]
@@ -568,8 +614,7 @@
     for c in range(6):
         late.append(copies.start(old[6 + c].at[pl.ds(DEEP, plan.own), across], sent.at[c]))
     sum_generation(plan, gen, message)
-    for d in range(plan.devices):
-        late.append(copies.start(message, gen_out.at[d]))
+    late.append(copies.start(message, gen_out))
     for c in range(6):
         target = kept[c].at[0, pl.ds(plan.own * k, plan.own)]
         late.append(copies.start(old[c].at[pl.ds(DEEP, plan.own), across], target))
@@ -587,12 +632,12 @@
         second_kernel,
         "second_round",
         shapes,
-        [SMEM] + [HBM] * (5 + 3 * nside),
+        [HBM] * (5 + 3 * nside) + [SMEM],
         scratch,
-        max(38 + 3 * nside, 12 + plan.devices),
+        38 + 3 * nside,
         round_flops(plan),
         10_000_000,
-    )(coef, charge, code, own_in, z_in, core_in, *strips)
+    )(*strips, z_in, core_in, own_in, code, charge, coef)
 
 
 def join_kernel(plan, *refs):
@@ -639,7 +684,7 @@
 
         def read(i, _):
             for c in range(cols):
-                value = density_in[i // plan.slab, i % plan.slab, c]
+                value = density_in[2 * (i // plan.slab), i % plan.slab, c]
                 one[i + 1, 8 + c : 9 + c, :] = jnp.full((1, lanes), value)
             return 0
 
@@ -734,30 +779,30 @@
     def send(message, target):
         return lax.ppermute(message, LINE, line_pairs(plan, target))
 
-    def spread(message, axes):
-        return lax.all_to_all(message, axes, split_axis=0, concat_axis=0, tiled=True)
-
     toward = lambda z, goal: z + 1 if goal == 0 else z - 1
     core = lambda z, x, k: (z, x, 1 - k)
 
-    packed = pack(plan, raw, medium)
-    z_same, z_cross = packed[:2]
+    z, x, k = (lax.axis_index(axis) for axis in LINE)
+    slabs = jnp.zeros(generation_shape(plan), F32)
+    slabs = lax.dynamic_update_slice(slabs, density[None], ((z * plan.gx + x) * 2 + k, 0, 0))
+    density = lax.psum(slabs, LINE)[:, : plan.slab, : plan.grid_cols]
+
+    packed = pack_strips(plan, raw, medium)
     strips = []
     for n, side in enumerate(plan.sides):
         to = functools.partial(across_step, side)
-        x_same, x_cross, d_same, d_cross = packed[2 + 4 * n : 6 + 4 * n]
+        x_same, x_cross, d_same, d_cross = packed[4 * n : 4 * n + 4]
         strips.append(send(x_same, lambda z, x, k: (z, to(x), k)))
         strips.append(send(x_cross, lambda z, x, k: (z, to(x), 1 - k)))
         strips.append(send(d_same, lambda z, x, k: (toward(z, k), to(x), k)))
         strips.append(send(d_cross, lambda z, x, k: (toward(z, 1 - k), to(x), 1 - k)))
+    z_same, z_cross, swap = pack_faces(plan, raw, medium, packed[3])
     z_same = send(z_same, lambda z, x, k: (toward(z, k), x, k))
     z_cross = send(z_cross, lambda z, x, k: (toward(z, 1 - k), x, 1 - k))
-    swap = [send(r, core) for r in raw]
-    tiles = plan.gz * plan.gx
-    density = spread(jnp.broadcast_to(density, (tiles,) + density.shape), ("gz", "gx"))
+    swap = send(swap, core)
     outs = first_round(plan, coef, density, raw, medium, swap, z_same, z_cross, strips)
     own, z_msg, core_msg, gens, code = outs[:5]
-    gens = spread(gens, LINE)
+    gens = lax.psum(gens, LINE)
     strips = []
     for n, side in enumerate(plan.sides):
         to = functools.partial(across_step, side)
@@ -770,7 +815,7 @@
     density, charge = carriers(plan, False, density, gens)
     outs = second_round(plan, coef, charge, code, own, z_msg, core_msg, strips)
     halves, sent, gens = outs[:6], outs[6], outs[7]
-    gens = spread(gens, LINE)
+    gens = lax.psum(gens, LINE)
     got = send(sent, core)
     (slab,) = carriers(plan, True, density, gens)
     return tuple(join(plan, halves, got)) + (slab[:, :, 0],)

time: 128 us -> 449 us (3.51)
  waiting for transfers between devices: 17.2 us -> 259 us
  Pallas kernels: 42.3 us -> 128 us
  blocking collectives: 22.3 us -> 0 us
  between operations: 0.83 us -> 14.1 us
    psum x0 -> x3, waiting for transfers between devices: none -> 259 us  [the longest x2 173 us: local(): gens = lax.psum(gens, LINE)]
    pallas_call x2 -> x3, Pallas kernels: 18.1 us -> 104 us  [the longest x1 84.7 us: pack_faces(): call(plan, pack_faces_kernel, 'pack_faces', shapes, [HBM] * 8, scratch, 2...]
    all_to_all x2 -> x0, blocking collectives: 22.3 us -> none  [spread(): lax.all_to_all(message, axes, split_axis=0, concat_axis=0, tiled=True)]
    ppermute x18 -> x13, waiting for transfers between devices: 11.9 us -> 0.03 us  [send(): return lax.ppermute(message, LINE, line_pairs(plan, target))]
    all_to_all x1 -> x0, waiting for transfers between devices: 5.27 us -> none  [spread(): lax.all_to_all(message, axes, split_axis=0, concat_axis=0, tiled=True)]
    ppermute x18 -> x13, starting transfers between devices: 28.3 us -> 30.1 us  [send(): return lax.ppermute(message, LINE, line_pairs(plan, target))]
    unnamed x30 -> x48, local copies, waits for them, and re-layouts: 11.7 us -> 12.4 us
  transfers between devices with their start and end apart: 19 -> 16, of which waited for: 3 -> 3; matrix products, arithmetic and copies ran while one was open for 1% -> 1% of each run, Pallas kernels for 6% -> 1%
where the time goes in v2:
time: 449 us; the launch traced here: 448 us
  waiting for transfers between devices  259 us (58%)
  Pallas kernels  128 us (29%)
  starting transfers between devices  30.2 us (7%)
  local copies, waits for them, and re-layouts  16 us (4%)
  between operations  14.1 us (3%)
    psum x2, waiting for transfers between devices, local(): gens = lax.psum(gens, LINE)  173 us
    psum x1, waiting for transfers between devices, local(): density = lax.psum(slabs, LINE)[:, :plan.slab, :plan.grid_cols]  86.3 us
    pallas_call x1, Pallas kernels, pack_faces(): call(plan, pack_faces_kernel, 'pack_faces', shapes, [HBM] * 8, scratch, 2...  84.7 us
    ppermute x13, starting transfers between devices, send(): return lax.ppermute(message, LINE, line_pairs(plan, target))  30.1 us
    pallas_call x1, Pallas kernels, second_round(): call(plan, second_kernel, 'second_round', shapes, [HBM] * (5 + 3 * nside)...  17 us
    pallas_call x1, Pallas kernels, first_round(): call(plan, first_kernel, 'first_round', shapes, [SMEM, SMEM] + [HBM] * (1...  16.9 us
    unnamed x48, local copies, waits for them, and re-layouts  12.4 us
  transfers between devices with their start and end apart: 16, of which 3 were waited for; matrix products, arithmetic and copies ran while one was open for 1% of the time, Pallas kernels for 1%

profile of v2, /device:TPU:0, one launch (start us, length us, event | category | flops | bytes accessed | tf_op | source)
XLA Modules:
  0.0 447.7 jit_solution(2433534145308683926)
XLA Ops:
  7.2 2.3 pack_strips.1
  9.7 84.7 %pack_faces.1 = (f32[7,4,32,128]{3,2,1,0:T(8,128)}, f32[6,4,32,128]{3,2,1,0:T(8,128)}, f32[6,20,32,128]{3,2,1,0:T(8,128)}) custom-call(f32[1,32,32,128]{3,2,1,0:T(8,128)} %refs_9_.1, f32[1,32,32,128]{3,2,1,0:T(8,128)} %refs_10_.1, f32[1,32,32,128]{3,2,1,0:T(8,128)} %refs_11_.1, f32[1,32,32,128]{3,2,1,0:T(8,128)} %refs_12_.1, f32[1,32,32,128]{3,2,1,0:T(8,128)} %refs_13_.1, ...), custom_call_target="tpu_custom_call" | custom-call | bytes 4000000 | tf_op jit(solution)/shard_map/pack_faces/pallas_call | solution.py:216
  94.9 5.3 %collective-permute-start.2 = (f32[7,4,32,128]{3,2,1,0:T(8,128)}, f32[7,4,32,128]{3,2,1,0:T(8,128)}, u32[]{:S(2)}, u32[]{:S(2)}) collective-permute-start(f32[7,4,32,128]{3,2,1,0:T(8,128)} %get-tuple-element.41), channel_id=1, source_target_pairs={{0,4},{2,6},{4,8},{5,1},{6,10},{7,3},{8,12},{9,5},{10,14},{11,7},{... | collective-permute-start | bytes 1376264 | tf_op jit(solution)/shard_map/ppermute | solution.py:780
  100.1 0.7 collective-permute-start.3
  101.5 7.8 %collective-permute-start.5 = (f32[7,2,8,128]{3,2,1,0:T(8,128)S(1)}, f32[7,2,8,128]{3,2,1,0:T(8,128)S(1)}, u32[]{:S(2)}, u32[]{:S(2)}) collective-permute-start(f32[7,2,8,128]{3,2,1,0:T(8,128)S(1)} %copy-done.23), channel_id=1, source_target_pairs={{0,6},{2,4},{4,10},{5,3},{6,8},{7,1},{8,14},{9,7},{10,12},{11,5},{... | collective-permute-start | bytes 172040 | tf_op jit(solution)/shard_map/ppermute | solution.py:780
  110.0 1.5 collective-permute-start
  112.1 2.3 collective-permute-start.1
  115.0 1.4 dynamic_update_slice.3
  116.5 86.3 %all-reduce.4.cloned.1.call-done = f32[16,8,128]{2,1,0:T(8,128)} async-done(((f32[16,8,128]{2,1,0:T(8,128)}), f32[16,8,128]{2,1,0:T(8,128)}) %all-reduce.4.cloned.1.call-update) | async-done | bytes 65552 | tf_op jit(solution)/shard_map/psum | solution.py:788
  202.7 0.8 slice.8.refs_1_.refs_0_
  203.7 1.0 copy-done.6
  204.7 0.8 copy-done.17
  205.6 0.8 copy-done.19
  206.4 16.9 %first_round.1 = (f32[12,16,32,128]{3,2,1,0:T(8,128)S(1)}, f32[12,4,32,128]{3,2,1,0:T(8,128)}, f32[12,4,32,128]{3,2,1,0:T(8,128)}, f32[16,8,128]{2,1,0:T(8,128)S...) custom-call(f32[2,3]{1,0:T(2,128)S(1)} %copy-done.20, ...), custom_call_target="tpu_custom_call" | custom-call | flops 73728000 | bytes 10000000 | tf_op jit(solution)/shard_map/first_round/pallas_call | solution.py:559
  223.2 1.6 copy-done.7
  224.9 0.9 copy-done.9
  226.3 0.7 collective-permute-start.10
  227.1 6.8 %collective-permute-start.11 = (f32[12,4,32,128]{3,2,1,0:T(8,128)}, f32[12,4,32,128]{3,2,1,0:T(8,128)S(1)}, u32[]{:S(2)}, u32[]{:S(2)}) collective-permute-start(f32[12,4,32,128]{3,2,1,0:T(8,128)} %get-tuple-element.49), channel_id=1, source_target_pairs={{0,1},{1,0},{2,3},{3,2},{4,5},{5,4},{6,7},{7,6},{8,9},{9,8},{10,11... | collective-permute-start | bytes 2359304 | tf_op jit(solution)/shard_map/ppermute | solution.py:780
  234.4 0.9 collective-permute-start.8
  236.0 86.7 %all-reduce.6.cloned.1.call-done.refs_1_ = f32[16,8,128]{2,1,0:T(8,128)} async-done(((f32[16,8,128]{2,1,0:T(8,128)}), f32[16,8,128]{2,1,0:T(8,128)}) %all-reduce.6.cloned.1.call-update) | async-done | bytes 65552 | tf_op jit(solution)/shard_map/psum | solution.py:805
  322.7 0.8 copy-done.12
  323.4 0.8 copy-done.13
  324.3 4.1 carriers.2
  328.5 1.9 copy-done.8
  330.4 1.1 copy-done.10
  331.4 17.0 %second_round.1 = (f32[1,32,32,128]{3,2,1,0:T(8,128)}, f32[1,32,32,128]{3,2,1,0:T(8,128)}, f32[1,32,32,128]{3,2,1,0:T(8,128)}, f32[1,32,32,128]{3,2,1,0:T(8,128)...) custom-call(f32[12,8,8,128]{3,2,1,0:T(8,128)S(1)} %collective-permut, ...), custom_call_target="tpu_custom_call" | custom-call | flops 73728000 | bytes 10000000 | tf_op jit(solution)/shard_map/second_round/pallas_call | solution.py:630
  348.4 1.8 collective-permute-start.12
  350.2 86.0 %all-reduce.8.cloned.1.call-done.refs_1_ = f32[16,8,128]{2,1,0:T(8,128)} async-done(((f32[16,8,128]{2,1,0:T(8,128)}), f32[16,8,128]{2,1,0:T(8,128)}) %all-reduce.8.cloned.1.call-update) | async-done | bytes 65552 | tf_op jit(solution)/shard_map/psum | solution.py:818
  436.3 0.8 copy-done.15
  437.1 2.1 carriers.3
  439.3 0.7 slice_reduce_fusion
  439.9 1.2 join.1
  (62 shorter events, 5.2 us)
Async XLA Ops:
  7.2 195.6 %all-reduce.4.cloned.1.call-start = ((), (), s32[]{:S(2)}) async-start(), calls=%async_computation | async-start | bytes 131072 | tf_op jit(solution)/shard_map/psum | solution.py:788
  9.5 91.3 %copy-start.21 = (f32[6,2,8,128]{3,2,1,0:T(8,128)S(1)}, f32[6,2,8,128]{3,2,1,0:T(8,128)}, u32[]{:S(2)}) copy-start(f32[6,2,8,128]{3,2,1,0:T(8,128)} %get-tuple-element.40.refs_7_) | copy-start | bytes 147460
  9.5 92.0 %copy-start.23 = (f32[7,2,8,128]{3,2,1,0:T(8,128)S(1)}, f32[7,2,8,128]{3,2,1,0:T(8,128)}, u32[]{:S(2)}) copy-start(f32[7,2,8,128]{3,2,1,0:T(8,128)} %get-tuple-element.44) | copy-start | bytes 172036
  9.6 105.5 %copy-start.22 = (f32[4,16]{1,0:T(4,128)S(1)}, f32[4,16]{1,0:T(4,128)}, u32[]{:S(2)}) copy-start(f32[4,16]{1,0:T(4,128)} %param.17) | copy-start | bytes 772
  9.6 194.1 %copy-start = (f32[1,32,32,128]{3,2,1,0:T(8,128)S(1)}, f32[1,32,32,128]{3,2,1,0:T(8,128)}, u32[]{:S(2)}) copy-start(f32[1,32,32,128]{3,2,1,0:T(8,128)} %refs_9_.1) | copy-start | bytes 1572868
  9.6 194.1 %copy-start.1 = (f32[1,32,32,128]{3,2,1,0:T(8,128)S(1)}, f32[1,32,32,128]{3,2,1,0:T(8,128)}, u32[]{:S(2)}) copy-start(f32[1,32,32,128]{3,2,1,0:T(8,128)} %refs_10_.1) | copy-start | bytes 1572868
  9.6 194.1 %copy-start.2 = (f32[1,32,32,128]{3,2,1,0:T(8,128)S(1)}, f32[1,32,32,128]{3,2,1,0:T(8,128)}, u32[]{:S(2)}) copy-start(f32[1,32,32,128]{3,2,1,0:T(8,128)} %refs_11_.1) | copy-start | bytes 1572868
  9.6 194.1 %copy-start.3 = (f32[1,32,32,128]{3,2,1,0:T(8,128)S(1)}, f32[1,32,32,128]{3,2,1,0:T(8,128)}, u32[]{:S(2)}) copy-start(f32[1,32,32,128]{3,2,1,0:T(8,128)} %refs_12_.1) | copy-start | bytes 1572868
  9.6 194.0 %copy-start.4 = (f32[1,32,32,128]{3,2,1,0:T(8,128)S(1)}, f32[1,32,32,128]{3,2,1,0:T(8,128)}, u32[]{:S(2)}) copy-start(f32[1,32,32,128]{3,2,1,0:T(8,128)} %refs_13_.1) | copy-start | bytes 1572868
  9.6 194.0 %copy-start.5 = (f32[1,32,32,128]{3,2,1,0:T(8,128)S(1)}, f32[1,32,32,128]{3,2,1,0:T(8,128)}, u32[]{:S(2)}) copy-start(f32[1,32,32,128]{3,2,1,0:T(8,128)} %refs_14_.1) | copy-start | bytes 1572868
  9.6 194.0 %copy-start.20 = (f32[2,3]{1,0:T(2,128)S(1)}, f32[2,3]{1,0:T(2,128)}, u32[]{:S(2)}) copy-start(f32[2,3]{1,0:T(2,128)} %refs_8_.1) | copy-start | bytes 76
  94.3 109.3 %collective-permute-start.4 = (f32[6,20,32,128]{3,2,1,0:T(8,128)}, f32[6,20,32,128]{3,2,1,0:T(8,128)}, u32[]{:S(2)}, u32[]{:S(2)}) collective-permute-start(f32[6,20,32,128]{3,2,1,0:T(8,128)} %get-tuple-element.43), channel_id=1, source_target_pairs={{0,1},{1,0},{2,3},{3,2},{4,5},{5,4},{6,7},{7,6},{8,9},{9,8},{10,11... | collective-permute-start | bytes 5898248 | tf_op jit(solution)/shard_map/ppermute | solution.py:780
  94.9 108.8 %collective-permute-start.2 = (f32[7,4,32,128]{3,2,1,0:T(8,128)}, f32[7,4,32,128]{3,2,1,0:T(8,128)}, u32[]{:S(2)}, u32[]{:S(2)}) collective-permute-start(f32[7,4,32,128]{3,2,1,0:T(8,128)} %get-tuple-element.41), channel_id=1, source_target_pairs={{0,4},{2,6},{4,8},{5,1},{6,10},{7,3},{8,12},{9,5},{10,14},{11,7},{... | collective-permute-start | bytes 1376264 | tf_op jit(solution)/shard_map/ppermute | solution.py:780
  100.1 103.4 %collective-permute-start.3 = (f32[6,4,32,128]{3,2,1,0:T(8,128)}, f32[6,4,32,128]{3,2,1,0:T(8,128)S(1)}, u32[]{:S(2)}, u32[]{:S(2)}) collective-permute-start(f32[6,4,32,128]{3,2,1,0:T(8,128)} %get-tuple-element.42), channel_id=1, source_target_pairs={{1,4},{3,6},{4,1},{5,8},{6,3},{7,10},{8,5},{9,12},{10,7},{11,14},{... | collective-permute-start | bytes 1179656 | tf_op jit(solution)/shard_map/ppermute | solution.py:780
  100.8 8.5 %collective-permute-start.6 = (f32[6,2,8,128]{3,2,1,0:T(8,128)S(1)}, f32[6,2,8,128]{3,2,1,0:T(8,128)S(1)}, u32[]{:S(2)}, u32[]{:S(2)}) collective-permute-start(f32[6,2,8,128]{3,2,1,0:T(8,128)S(1)} %copy-done.21), channel_id=1, source_target_pairs={{1,6},{3,4},{4,3},{5,10},{6,1},{7,8},{8,7},{9,14},{10,5},{11,12},{... | collective-permute-start | bytes 147464 | tf_op jit(solution)/shard_map/ppermute | solution.py:780
  101.5 9.9 %collective-permute-start.5 = (f32[7,2,8,128]{3,2,1,0:T(8,128)S(1)}, f32[7,2,8,128]{3,2,1,0:T(8,128)S(1)}, u32[]{:S(2)}, u32[]{:S(2)}) collective-permute-start(f32[7,2,8,128]{3,2,1,0:T(8,128)S(1)} %copy-done.23), channel_id=1, source_target_pairs={{0,6},{2,4},{4,10},{5,3},{6,8},{7,1},{8,14},{9,7},{10,12},{11,5},{... | collective-permute-start | bytes 172040 | tf_op jit(solution)/shard_map/ppermute | solution.py:780
  110.0 93.6 %collective-permute-start = (f32[7,10,8,128]{3,2,1,0:T(8,128)}, f32[7,10,8,128]{3,2,1,0:T(8,128)}, u32[]{:S(2)}, u32[]{:S(2)}) collective-permute-start(f32[7,10,8,128]{3,2,1,0:T(8,128)} %get-tuple-element.38), channel_id=1, source_target_pairs={{0,2},{1,3},{2,0},{3,1},{4,6},{5,7},{6,4},{7,5},{8,10},{9,11},{10,... | collective-permute-start | bytes 860168 | tf_op jit(solution)/shard_map/ppermute | solution.py:780
  112.1 91.5 %collective-permute-start.1 = (f32[6,10,8,128]{3,2,1,0:T(8,128)}, f32[6,10,8,128]{3,2,1,0:T(8,128)}, u32[]{:S(2)}, u32[]{:S(2)}) collective-permute-start(f32[6,10,8,128]{3,2,1,0:T(8,128)} %get-tuple-element.39), channel_id=1, source_target_pairs={{0,3},{1,2},{2,1},{3,0},{4,7},{5,6},{6,5},{7,4},{8,11},{9,10},{10,... | collective-permute-start | bytes 737288 | tf_op jit(solution)/shard_map/ppermute | solution.py:780
  116.4 206.3 %all-reduce.6.cloned.1.call-start = ((), (), s32[]{:S(2)}) async-start(), calls=%async_computation.1 | async-start | bytes 131072 | tf_op jit(solution)/shard_map/psum | solution.py:805
  203.6 19.6 %copy-start.11 = (f32[16,4,16]{2,1,0:T(4,128)}, f32[16,4,16]{2,1,0:T(4,128)S(1)}, u32[]{:S(2)}) copy-start(f32[16,4,16]{2,1,0:T(4,128)S(1)} %slice.8.refs_1_.refs_0_) | copy-start | bytes 12292
  203.7 1.0 copy-start.6
  223.2 1.6 copy-start.7
  224.9 0.9 copy-start.9
  226.3 102.1 %collective-permute-start.10 = (f32[12,4,32,128]{3,2,1,0:T(8,128)}, f32[12,4,32,128]{3,2,1,0:T(8,128)S(1)}, u32[]{:S(2)}, u32[]{:S(2)}) collective-permute-start(f32[12,4,32,128]{3,2,1,0:T(8,128)} %get-tuple-element.48), channel_id=1, source_target_pairs={{1,4},{3,6},{4,1},{5,8},{6,3},{7,10},{8,5},{9,12},{10,7},{11,14},{... | collective-permute-start | bytes 2359304 | tf_op jit(solution)/shard_map/ppermute | solution.py:780
  227.1 101.4 %collective-permute-start.11 = (f32[12,4,32,128]{3,2,1,0:T(8,128)}, f32[12,4,32,128]{3,2,1,0:T(8,128)S(1)}, u32[]{:S(2)}, u32[]{:S(2)}) collective-permute-start(f32[12,4,32,128]{3,2,1,0:T(8,128)} %get-tuple-element.49), channel_id=1, source_target_pairs={{0,1},{1,0},{2,3},{3,2},{4,5},{5,4},{6,7},{7,6},{8,9},{9,8},{10,11... | collective-permute-start | bytes 2359304 | tf_op jit(solution)/shard_map/ppermute | solution.py:780
  233.9 94.6 %collective-permute-start.7 = (f32[12,8,8,128]{3,2,1,0:T(8,128)}, f32[12,8,8,128]{3,2,1,0:T(8,128)S(1)}, u32[]{:S(2)}, u32[]{:S(2)}) collective-permute-start(f32[12,8,8,128]{3,2,1,0:T(8,128)} %get-tuple-element.45), channel_id=1, source_target_pairs={{0,2},{1,3},{2,0},{3,1},{4,6},{5,7},{6,4},{7,5},{8,10},{9,11},{10,... | collective-permute-start | bytes 1179656 | tf_op jit(solution)/shard_map/ppermute | solution.py:780
  234.4 94.0 %collective-permute-start.8 = (f32[12,2,8,128]{3,2,1,0:T(8,128)}, f32[12,2,8,128]{3,2,1,0:T(8,128)S(1)}, u32[]{:S(2)}, u32[]{:S(2)}) collective-permute-start(f32[12,2,8,128]{3,2,1,0:T(8,128)} %get-tuple-element.46), channel_id=1, source_target_pairs={{0,3},{1,2},{2,1},{3,0},{4,7},{5,6},{6,5},{7,4},{8,11},{9,10},{10,... | collective-permute-start | bytes 294920 | tf_op jit(solution)/shard_map/ppermute | solution.py:780
  235.3 93.1 %collective-permute-start.9 = (f32[12,2,8,128]{3,2,1,0:T(8,128)}, f32[12,2,8,128]{3,2,1,0:T(8,128)S(1)}, u32[]{:S(2)}, u32[]{:S(2)}) collective-permute-start(f32[12,2,8,128]{3,2,1,0:T(8,128)} %get-tuple-element.47), channel_id=1, source_target_pairs={{1,6},{3,4},{4,3},{5,10},{6,1},{7,8},{8,7},{9,14},{10,5},{11,12},{... | collective-permute-start | bytes 294920 | tf_op jit(solution)/shard_map/ppermute | solution.py:780
  236.0 200.3 %all-reduce.8.cloned.1.call-start = ((), (), s32[]{:S(2)}) async-start(), calls=%async_computation.2 | async-start | bytes 131072 | tf_op jit(solution)/shard_map/psum | solution.py:818
  328.5 1.9 copy-start.8
  330.4 1.1 copy-start.10
  348.4 91.5 %collective-permute-start.12 = (f32[6,16,32,128]{3,2,1,0:T(8,128)}, f32[6,16,32,128]{3,2,1,0:T(8,128)S(1)}, u32[]{:S(2)}, u32[]{:S(2)}) collective-permute-start(f32[6,16,32,128]{3,2,1,0:T(8,128)} %get-tuple-element.60), channel_id=1, source_target_pairs={{0,1},{1,0},{2,3},{3,2},{4,5},{5,4},{6,7},{7,6},{8,9},{9,8},{10,11... | collective-permute-start | bytes 4718600 | tf_op jit(solution)/shard_map/ppermute | solution.py:780
  (8 other events, 5.9 us)
Sparse Core Ops, SparseCore 0:
  116.5 86.1 all-reduce.3
  236.1 86.5 all-reduce.5
  350.3 85.8 all-reduce.7

commit v3 on v1

v3 whole, which is shorter than its diff:
```python
import functools

import jax
import jax.numpy as jnp
from jax import lax
from jax.experimental import pallas as pl
from jax.experimental.pallas import tpu as pltpu
from jax.sharding import PartitionSpec as P

BLOCK_FACTOR = 4
SUBSTEPS = 4
ROUNDS = 2
CSTEPS = 8

COURANT = 0.5
SILICON_PERM = 12.1
OXIDE_PERM = 2.1
SPREAD_COEFF = 0.2
MOBILITY_TERM = 0.1
LIFETIME_DECAY = 0.05
SOURCE_FACTOR = 0.02

DEEP = SUBSTEPS
LINE = ("gz", "gx", "af")
HBM = pl.BlockSpec(memory_space=pltpu.HBM)
SMEM = pl.BlockSpec(memory_space=pltpu.SMEM)
VMEM_LIMIT = 24 * 1024 * 1024
PACK_LIMIT = 60 * 1024 * 1024
F32 = jnp.float32


class Plan:
    def __init__(self, planes, cols, lanes, slab):
        self.gz = lax.axis_size("gz")
        self.gx = lax.axis_size("gx")
        self.planes, self.cols, self.lanes, self.slab = planes, cols, lanes, slab
        self.own = planes // 2
        self.part = self.own + DEEP
        self.ext = self.own + 2 * DEEP
        self.paired = self.gx == 2
        self.sides = ("face",) if self.paired else ("low", "high")
        self.width = cols + (8 if self.paired else 16)
        self.rows = self.width + 8
        self.tiles = self.width // 8
        self.grid_rows = planes * self.gz // BLOCK_FACTOR
        self.grid_cols = cols * self.gx // BLOCK_FACTOR
        self.devices = self.gz * self.gx * 2

    def first_row(self):
        return 8 * lax.axis_index("gx") if self.paired else 8

    def own_rows(self):
        return pl.ds(pl.multiple_of(self.first_row(), 8), self.cols)


def each_side(plan, act):
    if plan.paired:
        across = lax.axis_index("gx")

        @pl.when(across == 0)
        def _():
            act(0, "high")

        @pl.when(across == 1)
        def _():
            act(0, "low")
    else:
        act(0, "low")
        act(1, "high")


def line_pairs(plan, target):
    pairs = []
    for z in range(plan.gz):
        for x in range(plan.gx):
            for k in range(2):
                tz, tx, tk = target(z, x, k)
                if 0 <= tz < plan.gz and 0 <= tx < plan.gx:
                    pairs.append(((z * plan.gx + x) * 2 + k, (tz * plan.gx + tx) * 2 + tk))
    return pairs


def across_step(side, x):
    if side == "face":
        return 1 - x
    return x + 1 if side == "low" else x - 1


class Copies:
    def __init__(self, sems):
        self.sems, self.made = sems, 0

    def start(self, source, target):
        copy = pltpu.make_async_copy(source, target, self.sems.at[self.made])
        self.made += 1
        copy.start()
        return copy


def wait(copies):
    for copy in copies:
        copy.wait()


def call(plan, body, name, shapes, in_specs, scratch, copies, flops=0, moved=0, aliases=None, limit=VMEM_LIMIT):
    return pl.pallas_call(
        functools.partial(body, plan),
        out_shape=[jax.ShapeDtypeStruct(s, F32) for s in shapes],
        in_specs=in_specs,
        out_specs=[HBM] * len(shapes),
        scratch_shapes=scratch + [pltpu.SemaphoreType.DMA((copies,))],
        input_output_aliases=aliases or {},
        compiler_params=pltpu.CompilerParams(vmem_limit_bytes=limit),
        cost_estimate=pl.CostEstimate(flops=flops, bytes_accessed=moved, transcendentals=0),
        name=name,
    )


def pack_kernel(plan, *refs):
    raw, other, medium, nside = refs[:6], refs[6:12], refs[12], len(plan.sides)
    outs = refs[14 : 15 + 3 * nside]
    edge, edge_code, face, face_code, strips, sems = refs[15 + 3 * nside :]
    copies = Copies(sems)
    k = lax.axis_index("af")
    mine = pl.ds(plan.own * k, plan.own)
    outer = pl.ds((plan.planes - DEEP) * k, DEEP)
    if plan.paired:
        tile_rows = [pl.multiple_of((plan.cols - 8) * (1 - lax.axis_index("gx")), 8)]
    else:
        tile_rows = [plan.cols - 8, 0]
    early, late, last = [], [], []
    for n, row in enumerate(tile_rows):
        for c in range(6):
            side = pl.ds(row, 8)
            early.append(copies.start(raw[c].at[0, mine, side, :], edge.at[n, c]))
            early.append(copies.start(other[c].at[0, mine, side, :], edge.at[n, 6 + c]))
        early.append(copies.start(medium.at[mine, pl.ds(row, 8), :], edge_code.at[n]))
    for c in range(6):
        late.append(copies.start(raw[c].at[0, outer], face.at[c]))
        late.append(copies.start(other[c].at[0, outer], face.at[6 + c]))
    late.append(copies.start(medium.at[outer], face_code))
    wait(early)

    def fill(slot, low):
        def rows(q, _):
            for h in range(2):
                half = slice(4 * h, 4 * h + 4)
                for c in range(12):
                    strips[slot, c, q, half, :] = edge[slot, c, 2 * q + h, low : low + 4, :]
                code = edge_code[slot, 2 * q + h, low : low + 4, :]
                strips[slot, 12, q, half, :] = code.astype(F32)
            return 0

        lax.fori_loop(0, plan.own // 2, rows, 0)

    each_side(plan, lambda slot, side: fill(slot, 4 if plan.paired == (side == "high") else 0))
    send_strips(plan, copies, last, strips, outs[1:])
    wait(late)
    face[12] = face_code[...].astype(F32)
    last.append(copies.start(face, outs[0]))
    wait(last)


def send_strips(plan, copies, started, strips, outs):
    k = lax.axis_index("af")
    half, top = DEEP // 2, (plan.own - DEEP) // 2
    for n in range(len(plan.sides)):
        whole, inner, corner = outs[3 * n : 3 * n + 3]
        started.append(copies.start(strips.at[n], whole))
        started.append(copies.start(strips.at[n, :, pl.ds(top * (1 - k), half)], inner))
        started.append(copies.start(strips.at[n, :, pl.ds(top * k, half)], corner))


def strip_shapes(plan, comps):
    shapes = []
    for _ in plan.sides:
        for rows in (plan.own, DEEP, DEEP):
            shapes.append((comps, rows // 2, 8, plan.lanes))
    return shapes


def pack(plan, raw, other, medium, after):
    wide = (plan.cols, plan.lanes)
    nside = len(plan.sides)
    scratch = [
        pltpu.VMEM((nside, 12, plan.own, 8, plan.lanes), F32),
        pltpu.VMEM((nside, plan.own, 8, plan.lanes), jnp.int32),
        pltpu.VMEM((13, DEEP) + wide, F32),
        pltpu.VMEM((DEEP,) + wide, jnp.int32),
        pltpu.VMEM((nside, 13, plan.own // 2, 8, plan.lanes), F32),
    ]
    return call(
        plan,
        pack_kernel,
        "pack",
        [(13, DEEP) + wide] + strip_shapes(plan, 13),
        [HBM] * 14,
        scratch,
        16 * nside + 14,
        moved=4_000_000,
        limit=PACK_LIMIT,
    )(*raw, *other, medium, after)


def clear(plan, old, new, code):
    zero = jnp.zeros((8, plan.lanes), F32)

    def halo(slot, side):
        tile = plan.tiles - 1 if side == "high" else 0

        def one(p, _):
            for ref in list(old) + code:
                ref[p, 8 * tile : 8 * tile + 8, :] = zero
            return 0

        lax.fori_loop(0, plan.ext, one, 0)

    each_side(plan, halo)

    def above(p, _):
        for c in (1, 2, 7, 8):
            for ref in (old[c], new[c]):
                ref[p, plan.width : plan.width + 8, :] = zero
        return 0

    lax.fori_loop(0, plan.ext, above, 0)
    for c, ref in enumerate(new):
        plane = DEEP + plan.own if c % 6 < 3 else DEEP - 1
        for t in range(plan.tiles):
            ref[plane, 8 * t : 8 * t + 8, :] = zero


def strip_row(plan, side):
    if side == "low":
        return 4
    return plan.cols if plan.paired else 8 + plan.cols


def spread_strip(refs, strip, at, plane, pairs):
    def one(q, _):
        for c, ref in refs:
            for h in range(2):
                ref[plane + 2 * q + h, at : at + 4, :] = strip[c, q, 4 * h : 4 * h + 4, :]
        return 0

    lax.fori_loop(0, pairs, one, 0)


def substeps(plan, first, second, base, silicon, charge, gen, coef):
    lanes = plan.lanes
    tile = (8, lanes)
    lane = lax.broadcasted_iota(jnp.int32, tile, 1)
    row = lax.broadcasted_iota(jnp.int32, tile, 0)
    keep_up, keep_down, at_top = lane < lanes - 1, lane > 0, row == 0
    z, x, k = (lax.axis_index(a) for a in LINE)
    at_low = jnp.logical_and(z == 0, k == 0)
    at_high = jnp.logical_and(z == plan.gz - 1, k == 1)

    def up(v):
        return jnp.where(keep_up, pltpu.roll(v, lanes - 1, 1), 0.0)

    def down(v):
        return jnp.where(keep_down, pltpu.roll(v, 1, 1), 0.0)

    def edge_mask(t):
        if plan.paired or t not in (0, plan.tiles - 1):
            return None
        off = (x == 0) if t == 0 else (x == plan.gx - 1)
        return jnp.where(off, 0.0, 1.0)

    def new_magnetic(old, new, s, p, t):
        ex, ey, ez, hx, hy, hz = old[6 * s : 6 * s + 6]
        here, beside = slice(8 * t, 8 * t + 8), slice(8 * t + 1, 8 * t + 9)
        vx, vy, vz = ex[p, here, :], ey[p, here, :], ez[p, here, :]
        nx = hx[p, here, :] - COURANT * ((up(vz) - vz) - (ey[p + 1, here, :] - vy))
        ny = hy[p, here, :] - COURANT * ((ex[p + 1, here, :] - vx) - (ez[p, beside, :] - vz))
        nz = hz[p, here, :] - COURANT * ((ey[p, beside, :] - vy) - (up(vx) - vx))
        mask = edge_mask(t)
        if mask is not None:
            nx, ny, nz = nx * mask, ny * mask, nz * mask
        new[6 * s + 3][p, here, :] = nx
        new[6 * s + 4][p, here, :] = ny
        new[6 * s + 5][p, here, :] = nz
        return vx, vy, vz, nx, ny, nz

    def full_plane(old, new, p):
        coarse = p // BLOCK_FACTOR
        kerr, two = (coef[0], coef[4]), (coef[1], coef[5])
        half_two, half_free = (coef[2], coef[6]), (coef[3], coef[7])
        zero = jnp.zeros(tile, F32)
        rolled = [[zero, zero], [zero, zero]]
        for t in range(plan.tiles):
            here = slice(8 * t, 8 * t + 8)
            back = [[new[6 * s + c][p - 1, here, :] for c in (3, 4)] for s in range(2)]
            vals = [new_magnetic(old, new, s, p, t) for s in range(2)]
            strength = [v[0] * v[0] + v[1] * v[1] + v[2] * v[2] for v in vals]
            is_silicon = silicon[p, here, :]
            total = (strength[0] + strength[1]) * is_silicon
            carriers = charge[coarse, here, :] * is_silicon
            ground = base[p, here, :]
            gen[p, here, :] += (two[0] * strength[0] + two[1] * strength[1]) * total
            mask = edge_mask(t)
            for s in range(2):
                vx, vy, vz, nx, ny, nz = vals[s]
                loss = half_two[s] * total + half_free[s] * carriers
                perm = ground + kerr[s] * total
                divisor = perm + loss
                inv = pl.reciprocal(divisor, approx=True)
                inv = inv * (2.0 - divisor * inv)
                keep = (perm - loss) * inv
                push = COURANT * inv
                if mask is not None:
                    push = push * mask
                turn_y, turn_z = pltpu.roll(ny, 1, 0), pltpu.roll(nz, 1, 0)
                left_y = jnp.where(at_top, rolled[s][0], turn_y)
                left_z = jnp.where(at_top, rolled[s][1], turn_z)
                rolled[s] = [turn_y, turn_z]
                curl_x = (nz - down(nz)) - (ny - back[s][1])
                curl_y = (nx - back[s][0]) - (nz - left_z)
                curl_z = (ny - left_y) - (nx - down(nx))
                new[6 * s][p, here, :] = keep * vx + push * curl_x
                new[6 * s + 1][p, here, :] = keep * vy + push * curl_y
                new[6 * s + 2][p, here, :] = keep * vz + push * curl_z

    def substep(old, new, n):
        @pl.when(jnp.logical_not(at_low))
        def _():
            for t in range(plan.tiles):
                for s in range(2):
                    new_magnetic(old, new, s, n, t)

        begin = jnp.where(at_low, DEEP, n + 1)
        end = jnp.where(at_high, DEEP + plan.own, plan.ext - 1 - n)

        def step(p, _):
            full_plane(old, new, p)
            return 0

        lax.fori_loop(begin, end, step, 0)

    def pair(m, _):
        substep(first, second, 2 * m)
        substep(second, first, 2 * m + 1)
        return 0

    lax.fori_loop(0, SUBSTEPS // 2, pair, 0)


def set_media(plan, code, base, silicon):
    def one(p, _):
        for t in range(plan.tiles):
            here = slice(8 * t, 8 * t + 8)
            v = code[p, here, :]
            base[p, here, :] = jnp.where(v == 0.0, SILICON_PERM, jnp.where(v == 1.0, OXIDE_PERM, 1.0))
            silicon[p, here, :] = jnp.where(v == 0.0, 1.0, 0.0)
        return 0

    lax.fori_loop(0, plan.ext, one, 0)


def clear_generation(plan, gen):
    def one(p, _):
        gen[p] = jnp.zeros((plan.rows, plan.lanes), F32)
        return 0

    lax.fori_loop(DEEP, DEEP + plan.own, one, 0)


def sum_generation(plan, gen, message):
    blocks = plan.cols // BLOCK_FACTOR
    lane = lax.broadcasted_iota(jnp.int32, (blocks, plan.lanes), 1)
    across = plan.own_rows()
    out = jnp.zeros((blocks, plan.lanes), F32)
    for a in range(plan.own // BLOCK_FACTOR):
        p = DEEP + BLOCK_FACTOR * a
        rows = (gen[p, across, :] + gen[p + 1, across, :]) + (
            gen[p + 2, across, :] + gen[p + 3, across, :]
        )
        cells = rows.reshape(blocks, BLOCK_FACTOR, plan.lanes).sum(1)
        mean = cells.sum(1, keepdims=True) * (1.0 / (BLOCK_FACTOR * BLOCK_FACTOR * plan.lanes))
        out = jnp.where(lane == a, mean, out)
    message[...] = out


def round_scratch(plan):
    wide = (plan.ext, plan.rows, plan.lanes)
    return [pltpu.VMEM(wide, F32)] * 27 + [
        pltpu.VMEM((plan.ext // BLOCK_FACTOR, plan.width, plan.lanes), F32),
        pltpu.VMEM(generation_shape(plan)[1:], F32),
        pltpu.VMEM((8, 8, plan.lanes), F32),
        pltpu.VMEM(wide, F32),
    ]


def round_flops(plan):
    return SUBSTEPS * plan.ext * plan.width * plan.lanes * 150


def generation_shape(plan):
    return (plan.devices, plan.cols // BLOCK_FACTOR, plan.lanes)


def place_strips(plan, old, code, strips):
    k = lax.axis_index("af")
    outward, inner = plan.part * k, plan.part * (1 - k)

    def place(slot, side):
        whole, beside, corner = strips[3 * slot : 3 * slot + 3]
        at = strip_row(plan, side)
        same = list(enumerate(list(old) + code))
        flipped = list(enumerate(list(old[6:]) + list(old[:6]) + code))
        spread_strip(same, whole, at, DEEP, plan.own // 2)
        spread_strip(flipped, beside, at, inner, DEEP // 2)
        spread_strip(flipped, corner, at, outward, DEEP // 2)

    each_side(plan, place)


def send_generation(plan, copies, started, gen, message, gen_out):
    sum_generation(plan, gen, message)
    for d in range(plan.devices):
        started.append(copies.start(message, gen_out.at[d]))


def first_kernel(plan, *refs):
    nside = len(plan.sides)
    strips_in = refs[: 3 * nside]
    z_in, raw, other = refs[3 * nside], refs[1 + 3 * nside : 7 + 3 * nside], refs[7 + 3 * nside : 13 + 3 * nside]
    medium, charge_in, coef_in = refs[13 + 3 * nside : 16 + 3 * nside]
    outs = refs[16 + 3 * nside : 21 + 6 * nside]
    own_out, z_out, core_out, gen_out, code_out = outs[:5]
    rest = refs[21 + 6 * nside :]
    old, new, (base, silicon, gen, charge, message, coef, code) = rest[:12], rest[12:24], rest[24:31]
    codes, strips, strip_mine, sems = rest[31], rest[32 : 32 + 3 * nside], rest[-2], rest[-1]
    copies = Copies(sems)
    k = lax.axis_index("af")
    near = DEEP * (1 - k)
    far = plan.part * k
    across = plan.own_rows()
    here, there = pl.ds(near, plan.part), pl.ds(far, DEEP)
    mine = pl.ds((plan.own - DEEP) * k, plan.part)
    early = [copies.start(medium.at[mine], codes)]
    early.append(copies.start(z_in.at[12], code.at[there, across]))
    early.append(copies.start(charge_in, charge))
    early.append(copies.start(coef_in, coef))
    for source, target in zip(strips_in, strips):
        early.append(copies.start(source, target))
    late = []
    for c in range(6):
        late.append(copies.start(raw[c].at[0, mine], old[c].at[here, across]))
        late.append(copies.start(other[c].at[0, mine], old[6 + c].at[here, across]))
    for c in range(12):
        late.append(copies.start(z_in.at[(c + 6) % 12], old[c].at[there, across]))
    clear(plan, old, new, [code])
    clear_generation(plan, gen)
    wait(early)

    def settle(p, _):
        code[near + p, across, :] = codes[p].astype(F32)
        return 0

    lax.fori_loop(0, plan.part, settle, 0)
    place_strips(plan, old, [code], strips)
    set_media(plan, code, base, silicon)
    wait(late)
    substeps(plan, old, new, base, silicon, charge, gen, coef)
    copies = Copies(sems)
    late = []

    def gather(slot, side):
        high_end = (side == "high") if plan.paired else (side == "low")
        low = 0 if plan.paired and side == "high" else 8
        at = low + plan.cols - 4 if high_end else low

        def one(q, _):
            for c in range(12):
                for h in range(2):
                    strip_mine[slot, c, q, 4 * h : 4 * h + 4, :] = old[c][
                        DEEP + 2 * q + h, at : at + 4, :
                    ]
            return 0

        lax.fori_loop(0, plan.own // 2, one, 0)

    toward = DEEP + (plan.own - DEEP) * k
    inward = DEEP + (plan.own - DEEP) * (1 - k)
    for c in range(12):
        late.append(copies.start(old[c].at[pl.ds(toward, DEEP), across], z_out.at[c]))
        late.append(copies.start(old[c].at[pl.ds(inward, DEEP), across], core_out.at[c]))
        late.append(copies.start(old[c].at[pl.ds(DEEP, plan.own), across], own_out.at[c]))
    late.append(copies.start(code, code_out))
    each_side(plan, gather)
    send_strips(plan, copies, late, strip_mine, outs[5:])
    send_generation(plan, copies, late, gen, message, gen_out)
    wait(late)


def first_round(plan, strips, z_in, raw, other, medium, charge, coef):
    wide = (plan.cols, plan.lanes)
    nside = len(plan.sides)
    shapes = [
        (12, plan.own) + wide,
        (12, DEEP) + wide,
        (12, DEEP) + wide,
        generation_shape(plan),
        (plan.ext, plan.rows, plan.lanes),
    ] + strip_shapes(plan, 12)
    scratch = round_scratch(plan) + [pltpu.VMEM((plan.part,) + wide, jnp.int32)]
    scratch += [pltpu.VMEM(s.shape, F32) for s in strips]
    scratch += [pltpu.VMEM((nside, 12, plan.own // 2, 8, plan.lanes), F32)]
    return call(
        plan,
        first_kernel,
        "first_round",
        shapes,
        [HBM] * (16 + 3 * nside),
        scratch,
        37 + 3 * nside + plan.devices,
        round_flops(plan),
        10_000_000,
    )(*strips, z_in, *raw, *other, medium, charge, coef)


def second_kernel(plan, *refs):
    nside = len(plan.sides)
    strips_in = refs[: 3 * nside]
    z_in, core_in, own_in, code_in, charge_in, coef_in = refs[3 * nside : 6 + 3 * nside]
    outs = refs[6 + 3 * nside : 14 + 3 * nside]
    kept, sent, gen_out = outs[:6], outs[6], outs[7]
    rest = refs[14 + 3 * nside :]
    old, new, (base, silicon, gen, charge, message, coef, code) = rest[:12], rest[12:24], rest[24:31]
    strips, sems = rest[31:-1], rest[-1]
    copies = Copies(sems)
    k = lax.axis_index("af")
    across = plan.own_rows()
    outward = plan.part * k
    inner = plan.part * (1 - k)
    early = [copies.start(code_in, code), copies.start(charge_in, charge)]
    early.append(copies.start(coef_in, coef))
    for source, target in zip(strips_in, strips):
        early.append(copies.start(source, target))
    late = []
    for c in range(12):
        flip = (c + 6) % 12
        late.append(copies.start(own_in.at[c], old[c].at[pl.ds(DEEP, plan.own), across]))
        late.append(copies.start(z_in.at[flip], old[c].at[pl.ds(outward, DEEP), across]))
        late.append(copies.start(core_in.at[flip], old[c].at[pl.ds(inner, DEEP), across]))
    clear(plan, old, new, [])
    clear_generation(plan, gen)
    wait(early)
    place_strips(plan, old, [], strips)
    set_media(plan, code, base, silicon)
    wait(late)
    substeps(plan, old, new, base, silicon, charge, gen, coef)
    copies = Copies(sems)
    late = []
    for c in range(6):
        late.append(copies.start(old[6 + c].at[pl.ds(DEEP, plan.own), across], sent.at[c]))
    for c in range(6):
        target = kept[c].at[0, pl.ds(plan.own * k, plan.own)]
        late.append(copies.start(old[c].at[pl.ds(DEEP, plan.own), across], target))
    send_generation(plan, copies, late, gen, message, gen_out)
    wait(late)


def second_round(plan, strips, z_in, core_in, own_in, code, charge, coef):
    wide = (plan.cols, plan.lanes)
    nside = len(plan.sides)
    shapes = [(1, plan.planes) + wide] * 6 + [(6, plan.own) + wide, generation_shape(plan)]
    scratch = round_scratch(plan) + [pltpu.VMEM(s.shape, F32) for s in strips]
    return call(
        plan,
        second_kernel,
        "second_round",
        shapes,
        [HBM] * (6 + 3 * nside),
        scratch,
        39 + 3 * nside + plan.devices,
        round_flops(plan),
        10_000_000,
    )(*strips, z_in, core_in, own_in, code, charge, coef)


def join_kernel(plan, *refs):
    got, outs, sems = refs[6], refs[7:13], refs[13]
    copies = Copies(sems)
    k = lax.axis_index("af")
    rows = pl.ds(plan.own * (1 - k), plan.own)
    wait([copies.start(got.at[c], outs[c].at[0, rows]) for c in range(6)])


def join(plan, halves, got):
    shapes = [h.shape for h in halves]
    aliases = {c: c for c in range(6)}
    return call(
        plan, join_kernel, "join", shapes, [HBM] * 7, [], 6, moved=3_000_000, aliases=aliases
    )(*halves, got)


def under_cells(plan, grid, charge):
    z, x, k = (lax.axis_index(a) for a in LINE)
    for a in range(plan.ext // BLOCK_FACTOR):
        top = (plan.planes * z + plan.own * k - DEEP) // BLOCK_FACTOR + a
        top = 1 + jnp.clip(top, 0, plan.grid_rows - 1)
        for c in range(plan.width // BLOCK_FACTOR):
            left = (plan.cols * x - plan.first_row()) // BLOCK_FACTOR + c
            left = 8 + jnp.clip(left, 0, plan.grid_cols - 1)
            value = grid[top, pl.ds(left, 1), :]
            charge[a, 4 * c : 4 * c + 4, :] = jnp.broadcast_to(value, (4, plan.lanes))


def grid_shape(plan):
    return (plan.grid_rows + 2, plan.grid_cols + 16, plan.lanes)


def charge_shape(plan):
    return (plan.ext // BLOCK_FACTOR, plan.width, plan.lanes)


def spread_kernel(plan, density, table, grid_out, charge_out, coef_out, grid, charge, coef, sems):
    copies = Copies(sems)
    k = lax.axis_index("af")
    rows, cols, lanes = plan.grid_rows, plan.grid_cols, plan.lanes

    def clean(i, _):
        for c in range(0, cols + 16, 8):
            grid[i, c : c + 8, :] = jnp.zeros((8, lanes), F32)
        return 0

    lax.fori_loop(0, rows + 2, clean, 0)

    def read(i, _):
        for c in range(cols):
            value = density[i // plan.slab, i % plan.slab, c]
            grid[i + 1, 8 + c : 9 + c, :] = jnp.full((1, lanes), value)
        return 0

    lax.fori_loop(0, rows, read, 0)
    under_cells(plan, grid, charge)
    for s in range(2):
        which = k if s == 0 else 1 - k
        kerr, two, free = table[which, 0], table[which, 1], table[which, 2]
        for n, value in enumerate((kerr, two, 0.5 * two, 0.5 * free)):
            coef[4 * s + n] = jnp.full((8, lanes), value)
    pairs = ((grid, grid_out), (charge, charge_out), (coef, coef_out))
    wait([copies.start(source, target) for source, target in pairs])


def spread(plan, density, table):
    shapes = [grid_shape(plan), charge_shape(plan), (8, 8, plan.lanes)]
    scratch = [pltpu.VMEM(shape, F32) for shape in shapes]
    return call(
        plan, spread_kernel, "spread", shapes, [SMEM, SMEM], scratch, 3, 10_000, 1_000_000
    )(density, table)


def carrier_kernel(plan, last, density_in, gens_in, *refs):
    outs = refs[:1] if last else refs[:2]
    gens, one, two, source, charge, sems = refs[len(outs) :]
    copies = Copies(sems)
    rows, cols, lanes = plan.grid_rows, plan.grid_cols, plan.lanes
    z, x = lax.axis_index("gz"), lax.axis_index("gx")
    blocks, own = plan.cols // BLOCK_FACTOR, plan.own // BLOCK_FACTOR
    early = [copies.start(gens_in, gens), copies.start(density_in, one)]
    zero = jnp.zeros((8, lanes), F32)

    def clean(i, _):
        two[i, 0:8, :] = zero
        two[i, 8 + cols : 16 + cols, :] = zero
        return 0

    lax.fori_loop(0, rows + 2, clean, 0)
    for i in (0, rows + 1):
        for c in range(8, 8 + cols, 8):
            two[i, c : c + 8, :] = zero
    wait(early)

    def unpack(line, _):
        for dx in range(plan.gx):
            for dk in range(2):
                tile = gens[(line * plan.gx + dx) * 2 + dk]
                for a in range(own):
                    source[(line * 2 + dk) * own + a, blocks * dx : blocks * dx + blocks, :] = (
                        jnp.broadcast_to(SOURCE_FACTOR * tile[:, a : a + 1], (blocks, lanes))
                    )
        return 0

    lax.fori_loop(0, plan.gz, unpack, 0)

    def step(old, new):
        def row(m, _):
            for h in range(4):
                i = 4 * m + h
                for c in range(8, 8 + cols, 8):
                    now, before = old[i + 1, c : c + 8, :], old[i, c : c + 8, :]
                    around = (
                        old[i + 2, c : c + 8, :]
                        + before
                        + old[i + 1, c + 1 : c + 9, :]
                        + old[i + 1, c - 1 : c + 7, :]
                        - 4.0 * now
                    )
                    new[i + 1, c : c + 8, :] = (
                        now
                        + SPREAD_COEFF * around
                        - MOBILITY_TERM * (now - before)
                        - LIFETIME_DECAY * now
                        + source[i, c - 8 : c, :]
                    )
            return 0

        lax.fori_loop(0, rows // 4, row, 0)

    def pair(_, carry):
        step(one, two)
        step(two, one)
        return carry

    lax.fori_loop(0, CSTEPS // 2, pair, 0)
    if last:
        rows_out = pl.ds(1 + (z * plan.gx + x) * plan.slab, plan.slab)
        wait([copies.start(one.at[rows_out, pl.ds(8, cols)], outs[0])])
        return
    under_cells(plan, one, charge)
    wait([copies.start(one, outs[0]), copies.start(charge, outs[1])])


def carriers(plan, last, density, gens):
    grid, lanes = grid_shape(plan), plan.lanes
    shapes = [(plan.slab, plan.grid_cols, lanes)] if last else [grid, charge_shape(plan)]
    scratch = [
        pltpu.VMEM(gens.shape, F32),
        pltpu.VMEM(grid, F32),
        pltpu.VMEM(grid, F32),
        pltpu.VMEM((plan.grid_rows, plan.grid_cols, lanes), F32),
        pltpu.VMEM(charge_shape(plan), F32),
    ]
    return call(
        plan,
        lambda plan, *refs: carrier_kernel(plan, last, *refs),
        "carriers",
        shapes,
        [HBM, HBM],
        scratch,
        4,
        2_000_000,
        1_000_000,
    )(density, gens)


def local(ex, ey, ez, hx, hy, hz, medium, table, density):
    raw = (ex, ey, ez, hx, hy, hz)
    plan = Plan(*medium.shape, density.shape[0])

    def send(message, target):
        return lax.ppermute(message, LINE, line_pairs(plan, target))

    def everywhere(message, axes):
        return lax.all_to_all(message, axes, split_axis=0, concat_axis=0, tiled=True)

    core = lambda z, x, k: (z, x, 1 - k)
    beyond = lambda z, k: z - 1 if k == 0 else z + 1

    def exchange(z_msg, strips):
        got = []
        for n, side in enumerate(plan.sides):
            to = functools.partial(across_step, side)
            whole, inner, corner = strips[3 * n : 3 * n + 3]
            got.append(send(whole, lambda z, x, k: (z, to(x), k)))
            got.append(send(inner, lambda z, x, k: (z, to(x), 1 - k)))
            got.append(send(corner, lambda z, x, k: (beyond(z, k), to(x), 1 - k)))
        return send(z_msg, lambda z, x, k: (beyond(z, k), x, 1 - k)), got

    other = [send(r, core) for r in raw]
    tiles = plan.gz * plan.gx
    slabs = everywhere(jnp.broadcast_to(density, (tiles,) + density.shape), ("gz", "gx"))
    packed = pack(plan, raw, other, medium, slabs)
    grid, charge, coef = spread(plan, slabs, table)
    z_in, strips = exchange(packed[0], packed[1:])
    outs = first_round(plan, strips, z_in, raw, other, medium, charge, coef)
    own, z_msg, core_msg, gens, code = outs[:5]
    gens = everywhere(gens, LINE)
    z_in, strips = exchange(z_msg, outs[5:])
    core_in = send(core_msg, core)
    grid, charge = carriers(plan, False, grid, gens)
    outs = second_round(plan, strips, z_in, core_in, own, code, charge, coef)
    halves, sent, gens = outs[:6], outs[6], outs[7]
    gens = everywhere(gens, LINE)
    got = send(sent, core)
    (slab,) = carriers(plan, True, grid, gens)
    return tuple(join(plan, halves, got)) + (slab[:, :, 0],)


def solution(mesh):
    field = P("af", ("group", "gz"), "gx", None)
    slabs = P(("group", "gz", "gx"), None)
    in_specs = (field,) * 6 + (P(("group", "gz"), "gx", None), P(), slabs)
    out_specs = (field,) * 6 + (slabs,)
    return jax.shard_map(local, mesh=mesh, in_specs=in_specs, out_specs=out_specs, check_vma=False)
```

time: 128 us -> 129 us (level)
  starting transfers between devices: 32.4 us -> 21.3 us
  local copies, waits for them, and re-layouts: 12.4 us -> 22.3 us
    ppermute x18 -> x16, starting transfers between devices: 28.3 us -> 17.2 us  [send(): return lax.ppermute(message, LINE, line_pairs(plan, target))]
    unnamed x30 -> x60, local copies, waits for them, and re-layouts: 11.7 us -> 20.9 us
    pallas_call x3 -> x4, Pallas kernels: 35.2 us -> 36.8 us  [the longest x1 16.3 us: first_round(): call(plan, first_kernel, 'first_round', shapes, [HBM] * (16 + 3 * nside),...]
    ppermute x18 -> x16, waiting for transfers between devices: 11.9 us -> 10.4 us  [send(): return lax.ppermute(message, LINE, line_pairs(plan, target))]
  transfers between devices with their start and end apart: 19 -> 17, of which waited for: 3 -> 3; matrix products, arithmetic and copies ran while one was open for 1% -> 1% of each run, Pallas kernels for 6% -> 6%
where the time goes in v3:
time: 129 us; the launch traced here: 128 us
  Pallas kernels  43.3 us (34%)
  blocking collectives  22.9 us (18%)
  local copies, waits for them, and re-layouts  22.3 us (17%)
  starting transfers between devices  21.3 us (17%)
  waiting for transfers between devices  16.9 us (13%)
    all_to_all x2, blocking collectives, everywhere(): lax.all_to_all(message, axes, split_axis=0, concat_axis=0, tiled=True)  22.9 us
    unnamed x60, local copies, waits for them, and re-layouts  20.9 us
    ppermute x16, starting transfers between devices, send(): return lax.ppermute(message, LINE, line_pairs(plan, target))  17.2 us
    pallas_call x1, Pallas kernels, first_round(): call(plan, first_kernel, 'first_round', shapes, [HBM] * (16 + 3 * nside),...  16.3 us
    pallas_call x1, Pallas kernels, second_round(): call(plan, second_kernel, 'second_round', shapes, [HBM] * (6 + 3 * nside)...  15.8 us
    ppermute x16, waiting for transfers between devices, send(): return lax.ppermute(message, LINE, line_pairs(plan, target))  10.4 us
    all_to_all x1, waiting for transfers between devices, everywhere(): lax.all_to_all(message, axes, split_axis=0, concat_axis=0, tiled=True)  6.46 us
    pallas_call x2, Pallas kernels, carriers(): call(plan, lambda plan, *refs: carrier_kernel(plan, last, *refs), 'carrie...  5.29 us
  transfers between devices with their start and end apart: 17, of which 3 were waited for; matrix products, arithmetic and copies ran while one was open for 1% of the time, Pallas kernels for 6%

profile of v3, /device:TPU:0, one launch (start us, length us, event | category | flops | bytes accessed | tf_op | source)
XLA Modules:
  0.0 127.5 jit_solution(10957524574417790986)
XLA Ops:
  4.0 13.4 %all_to_all.15.refs_13_.density = f32[8,4,16]{2,1,0:T(4,128)} all-to-all(f32[8,4,16]{2,1,0:T(4,128)S(1)} %broadcast_in_dim.3), channel_id=1, replica_groups=mesh['group'=2,'gz'=4,'gx'=2,'af'=2] {'gz','gx'}, dimensions={0} | all-to-all | bytes 4096 | tf_op jit(solution)/shard_map/all_to_all | solution.py:759
  19.5 2.7 %pack.1 = (f32[13,4,32,128]{3,2,1,0:T(8,128)}, f32[13,8,8,128]{3,2,1,0:T(8,128)}, f32[13,2,8,128]{3,2,1,0:T(8,128)}, f32[13,2,8,128]{3,2,1,0:T(8,128)}) custom-call(f32[1,32,32,128]{3,2,1,0:T(8,128)} %refs_4_.3, f32[1,32,32,128]{3,2,1,0:T(8,128)} %refs_5_.3, f32[1,32,32,128]{3,2,1,0:T(8,128)} %refs_6_.1, f32[1,32,32,128]{3,2,1,0:T(8,128)} %refs_7_.1, ...), custom_call_target="tpu_custom_call" | custom-call | bytes 4000000 | tf_op jit(solution)/shard_map/pack/pallas_call | solution.py:192
  23.5 2.6 %collective-permute-start.7 = (f32[13,2,8,128]{3,2,1,0:T(8,128)}, f32[13,2,8,128]{3,2,1,0:T(8,128)S(1)}, u32[]{:S(2)}, u32[]{:S(2)}) collective-permute-start(f32[13,2,8,128]{3,2,1,0:T(8,128)} %get-tuple-element.39), channel_id=1, source_target_pairs={{0,3},{1,2},{2,1},{3,0},{4,7},{5,6},{6,5},{7,4},{8,11},{9,10},{10,... | collective-permute-start | bytes 319496 | tf_op jit(solution)/shard_map/ppermute | solution.py:756
  26.8 2.0 %spread.1 = (f32[34,32,128]{2,1,0:T(8,128)S(1)}, f32[6,40,128]{2,1,0:T(8,128)S(1)}, f32[8,8,128]{2,1,0:T(8,128)S(1)}) custom-call(f32[8,4,16]{2,1,0:T(4,128)S(1)} %copy-done.23, f32[2,3]{1,0:T(2,128)S(1)} %copy-done.27), custom_call_target="tpu_custom_call" | custom-call | flops 10000 | bytes 1000000 | tf_op jit(solution)/shard_map/spread/pallas_call | solution.py:652
  29.7 9.6 %collective-permute-done.7.refs_1_ = f32[13,2,8,128]{3,2,1,0:T(8,128)S(1)} collective-permute-done((f32[13,2,8,128]{3,2,1,0:T(8,128)}, f32[13,2,8,128]{3,2,1,0:T(8,128)S(1)}, u32[]{:S(2)}, u32[]{:S(2)}) %collective-permute-start.7) | collective-permute-done | bytes 106528 | tf_op jit(solution)/shard_map/ppermute | solution.py:756
  39.4 1.0 copy-done.1
  40.4 1.0 copy-done.2
  41.5 1.0 copy-done.3
  42.5 1.0 copy-done.4
  43.5 1.0 copy-done.5
  44.6 1.0 copy-done.6
  45.6 1.0 copy-done.8
  46.7 1.0 copy-done.10
  47.7 1.0 copy-done.12
  48.7 1.0 copy-done.14
  49.8 1.0 copy-done.16
  50.8 1.0 copy-done.18
  51.9 16.3 %first_round.1 = (f32[12,16,32,128]{3,2,1,0:T(8,128)S(1)}, f32[12,4,32,128]{3,2,1,0:T(8,128)}, f32[12,4,32,128]{3,2,1,0:T(8,128)}, f32[16,8,128]{2,1,0:T(8,128)S...) custom-call(f32[13,8,8,128]{3,2,1,0:T(8,128)S(1)} %collective-permut, ...), custom_call_target="tpu_custom_call" | custom-call | flops 73728000 | bytes 10000000 | tf_op jit(solution)/shard_map/first_round/pallas_call | solution.py:511
  70.9 1.5 %collective-permute-start.13 = (f32[12,4,32,128]{3,2,1,0:T(8,128)}, f32[12,4,32,128]{3,2,1,0:T(8,128)}, u32[]{:S(2)}, u32[]{:S(2)}) collective-permute-start(f32[12,4,32,128]{3,2,1,0:T(8,128)} %get-tuple-element.47), channel_id=1, source_target_pairs={{1,4},{3,6},{4,1},{5,8},{6,3},{7,10},{8,5},{9,12},{10,7},{11,14},{... | collective-permute-start | bytes 2359304 | tf_op jit(solution)/shard_map/ppermute | solution.py:756
  72.4 4.2 %collective-permute-start.14 = (f32[12,4,32,128]{3,2,1,0:T(8,128)}, f32[12,4,32,128]{3,2,1,0:T(8,128)}, u32[]{:S(2)}, u32[]{:S(2)}) collective-permute-start(f32[12,4,32,128]{3,2,1,0:T(8,128)} %get-tuple-element.48), channel_id=1, source_target_pairs={{0,1},{1,0},{2,3},{3,2},{4,5},{5,4},{6,7},{7,6},{8,9},{9,8},{10,11... | collective-permute-start | bytes 2359304 | tf_op jit(solution)/shard_map/ppermute | solution.py:756
  77.1 4.2 %all-to-all-start.1 = ((f32[16,8,128]{2,1,0:T(8,128)}), f32[16,8,128]{2,1,0:T(8,128)}, u32[]{:S(2)}, u32[]{:S(2)}) async-start(f32[16,8,128]{2,1,0:T(8,128)} %copy-done.26), calls=%async_computation.1 | async-start | bytes 131072 | tf_op jit(solution)/shard_map/all_to_all | solution.py:759
  81.3 1.5 %collective-permute-start.11 = (f32[12,2,8,128]{3,2,1,0:T(8,128)}, f32[12,2,8,128]{3,2,1,0:T(8,128)}, u32[]{:S(2)}, u32[]{:S(2)}) collective-permute-start(f32[12,2,8,128]{3,2,1,0:T(8,128)} %copy-done.29), channel_id=1, source_target_pairs={{0,3},{1,2},{2,1},{3,0},{4,7},{5,6},{6,5},{7,4},{8,11},{9,10},{10,... | collective-permute-start | bytes 294920 | tf_op jit(solution)/shard_map/ppermute | solution.py:756
  82.8 1.3 %collective-permute-start.12 = (f32[12,2,8,128]{3,2,1,0:T(8,128)}, f32[12,2,8,128]{3,2,1,0:T(8,128)}, u32[]{:S(2)}, u32[]{:S(2)}) collective-permute-start(f32[12,2,8,128]{3,2,1,0:T(8,128)} %copy-done.28), channel_id=1, source_target_pairs={{1,6},{3,4},{4,3},{5,10},{6,1},{7,8},{8,7},{9,14},{10,5},{11,12},{... | collective-permute-start | bytes 294920 | tf_op jit(solution)/shard_map/ppermute | solution.py:756
  84.1 6.5 %all-to-all-done.1.refs_1_ = f32[16,8,128]{2,1,0:T(8,128)} async-done(((f32[16,8,128]{2,1,0:T(8,128)}), f32[16,8,128]{2,1,0:T(8,128)}, u32[]{:S(2)}, u32[]{:S(2)}) %all-to-all-start.1) | async-done | bytes 65568 | tf_op jit(solution)/shard_map/all_to_all | solution.py:759
  90.6 1.1 copy-done.22
  91.6 3.1 %carriers.2 = (f32[34,32,128]{2,1,0:T(8,128)S(1)}, f32[6,40,128]{2,1,0:T(8,128)S(1)}) custom-call(f32[34,32,128]{2,1,0:T(8,128)S(1)} %copy-done.22, f32[16,8,128]{2,1,0:T(8,128)} %all-to-all-done.1.refs_1_), custom_call_target="tpu_custom_call" | custom-call | flops 2000000 | bytes 1000000 | tf_op jit(solution)/shard_map/carriers/pallas_call | solution.py:738
  94.7 1.1 copy-done.20
  96.6 15.8 %second_round.1 = (f32[1,32,32,128]{3,2,1,0:T(8,128)}, f32[1,32,32,128]{3,2,1,0:T(8,128)}, f32[1,32,32,128]{3,2,1,0:T(8,128)}, f32[1,32,32,128]{3,2,1,0:T(8,128)...) custom-call(f32[12,8,8,128]{3,2,1,0:T(8,128)S(1)} %collective-permut, ...), custom_call_target="tpu_custom_call" | custom-call | flops 73728000 | bytes 10000000 | tf_op jit(solution)/shard_map/second_round/pallas_call | solution.py:571
  112.3 1.6 %collective-permute-start.15 = (f32[6,16,32,128]{3,2,1,0:T(8,128)S(1)}, f32[6,16,32,128]{3,2,1,0:T(8,128)S(1)}, u32[]{:S(2)}, u32[]{:S(2)}) collective-permute-start(f32[6,16,32,128]{3,2,1,0:T(8,128)S(1)} %get-tuple-element.60), channel_id=1, source_target_pairs={{0,1},{1,0},{2,3},{3,2},{4,5},{5,4},{6,7},{7,6},{8,9},{9,8},{10,11... | collective-permute-start | bytes 4718600 | tf_op jit(solution)/shard_map/ppermute | solution.py:756
  114.0 9.5 %all_to_all.16.refs_1_ = f32[16,8,128]{2,1,0:T(8,128)S(1)} all-to-all(f32[16,8,128]{2,1,0:T(8,128)S(1)} %get-tuple-element.68), channel_id=1, replica_groups=mesh['group'=2,'gz'=4,'gx'=2,'af'=2] {'gz','gx','af'}, dimensions={0} | all-to-all | bytes 131072 | tf_op jit(solution)/shard_map/all_to_all | solution.py:759
  123.4 2.2 %carriers.3 = f32[4,16,128]{2,1,0:T(8,128)S(1)} custom-call(f32[34,32,128]{2,1,0:T(8,128)S(1)} %get-tuple-element.67.refs_0_, f32[16,8,128]{2,1,0:T(8,128)S(1)} %all_to_all.16.refs_1_), custom_call_target="tpu_custom_call" | custom-call | flops 2000000 | bytes 1000000 | tf_op jit(solution)/shard_map/carriers/pallas_call | solution.py:738
  126.4 1.2 join.1
  (73 shorter events, 12.8 us)
Async XLA Ops:
  0.6 2.3 %collective-permute-start = (f32[1,32,32,128]{3,2,1,0:T(8,128)}, f32[1,32,32,128]{3,2,1,0:T(8,128)S(1)}, u32[]{:S(2)}, u32[]{:S(2)}) collective-permute-start(f32[1,32,32,128]{3,2,1,0:T(8,128)} %refs_4_.3), channel_id=1, source_target_pairs={{0,1},{1,0},{2,3},{3,2},{4,5},{5,4},{6,7},{7,6},{8,9},{9,8},{10,11... | collective-permute-start | bytes 1572872 | tf_op jit(solution)/shard_map/ppermute | solution.py:756
  1.1 16.3 %collective-permute-start.1 = (f32[1,32,32,128]{3,2,1,0:T(8,128)}, f32[1,32,32,128]{3,2,1,0:T(8,128)S(1)}, u32[]{:S(2)}, u32[]{:S(2)}) collective-permute-start(f32[1,32,32,128]{3,2,1,0:T(8,128)} %refs_5_.3), channel_id=1, source_target_pairs={{0,1},{1,0},{2,3},{3,2},{4,5},{5,4},{6,7},{7,6},{8,9},{9,8},{10,11... | collective-permute-start | bytes 1572872 | tf_op jit(solution)/shard_map/ppermute | solution.py:756
  1.2 16.2 %collective-permute-start.2 = (f32[1,32,32,128]{3,2,1,0:T(8,128)}, f32[1,32,32,128]{3,2,1,0:T(8,128)S(1)}, u32[]{:S(2)}, u32[]{:S(2)}) collective-permute-start(f32[1,32,32,128]{3,2,1,0:T(8,128)} %refs_6_.1), channel_id=1, source_target_pairs={{0,1},{1,0},{2,3},{3,2},{4,5},{5,4},{6,7},{7,6},{8,9},{9,8},{10,11... | collective-permute-start | bytes 1572872 | tf_op jit(solution)/shard_map/ppermute | solution.py:756
  1.7 15.8 %collective-permute-start.3 = (f32[1,32,32,128]{3,2,1,0:T(8,128)}, f32[1,32,32,128]{3,2,1,0:T(8,128)S(1)}, u32[]{:S(2)}, u32[]{:S(2)}) collective-permute-start(f32[1,32,32,128]{3,2,1,0:T(8,128)} %refs_7_.1), channel_id=1, source_target_pairs={{0,1},{1,0},{2,3},{3,2},{4,5},{5,4},{6,7},{7,6},{8,9},{9,8},{10,11... | collective-permute-start | bytes 1572872 | tf_op jit(solution)/shard_map/ppermute | solution.py:756
  1.7 15.7 %collective-permute-start.4 = (f32[1,32,32,128]{3,2,1,0:T(8,128)}, f32[1,32,32,128]{3,2,1,0:T(8,128)S(1)}, u32[]{:S(2)}, u32[]{:S(2)}) collective-permute-start(f32[1,32,32,128]{3,2,1,0:T(8,128)} %refs_8_.1), channel_id=1, source_target_pairs={{0,1},{1,0},{2,3},{3,2},{4,5},{5,4},{6,7},{7,6},{8,9},{9,8},{10,11... | collective-permute-start | bytes 1572872 | tf_op jit(solution)/shard_map/ppermute | solution.py:756
  2.9 14.6 %copy-start.7 = (f32[1,32,32,128]{3,2,1,0:T(8,128)}, f32[1,32,32,128]{3,2,1,0:T(8,128)S(1)}, u32[]{:S(2)}) copy-start(f32[1,32,32,128]{3,2,1,0:T(8,128)S(1)} %collective-permute-done.refs_6_.refs_10_) | copy-start | bytes 1572868
  2.9 14.6 %collective-permute-start.5 = (f32[1,32,32,128]{3,2,1,0:T(8,128)}, f32[1,32,32,128]{3,2,1,0:T(8,128)S(1)}, u32[]{:S(2)}, u32[]{:S(2)}) collective-permute-start(f32[1,32,32,128]{3,2,1,0:T(8,128)} %refs_9_.1), channel_id=1, source_target_pairs={{0,1},{1,0},{2,3},{3,2},{4,5},{5,4},{6,7},{7,6},{8,9},{9,8},{10,11... | collective-permute-start | bytes 1572872 | tf_op jit(solution)/shard_map/ppermute | solution.py:756
  17.4 9.4 %copy-start.23 = (f32[8,4,16]{2,1,0:T(4,128)S(1)}, f32[8,4,16]{2,1,0:T(4,128)}, u32[]{:S(2)}) copy-start(f32[8,4,16]{2,1,0:T(4,128)} %all_to_all.15.refs_13_.density) | copy-start | bytes 6148
  17.4 9.4 %copy-start.27 = (f32[2,3]{1,0:T(2,128)S(1)}, f32[2,3]{1,0:T(2,128)}, u32[]{:S(2)}) copy-start(f32[2,3]{1,0:T(2,128)} %table.1) | copy-start | bytes 76
  17.4 22.0 %copy-start = (f32[1,32,32,128]{3,2,1,0:T(8,128)S(1)}, f32[1,32,32,128]{3,2,1,0:T(8,128)}, u32[]{:S(2)}) copy-start(f32[1,32,32,128]{3,2,1,0:T(8,128)} %refs_4_.3) | copy-start | bytes 1572868
  17.5 1.1 copy-start.13
  17.5 1.2 copy-start.15
  22.2 17.1 %collective-permute-start.9 = (f32[13,4,32,128]{3,2,1,0:T(8,128)}, f32[13,4,32,128]{3,2,1,0:T(8,128)S(1)}, u32[]{:S(2)}, u32[]{:S(2)}) collective-permute-start(f32[13,4,32,128]{3,2,1,0:T(8,128)} %get-tuple-element.41), channel_id=1, source_target_pairs={{1,4},{3,6},{4,1},{5,8},{6,3},{7,10},{8,5},{9,12},{10,7},{11,14},{... | collective-permute-start | bytes 2555912 | tf_op jit(solution)/shard_map/ppermute | solution.py:756
  22.9 16.4 %collective-permute-start.6 = (f32[13,8,8,128]{3,2,1,0:T(8,128)}, f32[13,8,8,128]{3,2,1,0:T(8,128)S(1)}, u32[]{:S(2)}, u32[]{:S(2)}) collective-permute-start(f32[13,8,8,128]{3,2,1,0:T(8,128)} %get-tuple-element.38), channel_id=1, source_target_pairs={{0,2},{1,3},{2,0},{3,1},{4,6},{5,7},{6,4},{7,5},{8,10},{9,11},{10,... | collective-permute-start | bytes 1277960 | tf_op jit(solution)/shard_map/ppermute | solution.py:756
  23.5 15.8 %collective-permute-start.7 = (f32[13,2,8,128]{3,2,1,0:T(8,128)}, f32[13,2,8,128]{3,2,1,0:T(8,128)S(1)}, u32[]{:S(2)}, u32[]{:S(2)}) collective-permute-start(f32[13,2,8,128]{3,2,1,0:T(8,128)} %get-tuple-element.39), channel_id=1, source_target_pairs={{0,3},{1,2},{2,1},{3,0},{4,7},{5,6},{6,5},{7,4},{8,11},{9,10},{10,... | collective-permute-start | bytes 319496 | tf_op jit(solution)/shard_map/ppermute | solution.py:756
  26.1 13.2 %collective-permute-start.8 = (f32[13,2,8,128]{3,2,1,0:T(8,128)}, f32[13,2,8,128]{3,2,1,0:T(8,128)S(1)}, u32[]{:S(2)}, u32[]{:S(2)}) collective-permute-start(f32[13,2,8,128]{3,2,1,0:T(8,128)} %get-tuple-element.40), channel_id=1, source_target_pairs={{1,6},{3,4},{4,3},{5,10},{6,1},{7,8},{8,7},{9,14},{10,5},{11,12},{... | collective-permute-start | bytes 319496 | tf_op jit(solution)/shard_map/ppermute | solution.py:756
  29.7 38.5 %copy-start.24 = (f32[8,8,128]{2,1,0:T(8,128)}, f32[8,8,128]{2,1,0:T(8,128)S(1)}, u32[]{:S(2)}) copy-start(f32[8,8,128]{2,1,0:T(8,128)S(1)} %get-tuple-element.43.refs_18_.refs_8_) | copy-start | bytes 98308
  39.4 1.0 copy-start.1
  40.4 1.0 copy-start.2
  41.4 1.0 copy-start.3
  42.5 1.0 copy-start.4
  43.5 1.0 copy-start.5
  44.6 1.0 copy-start.6
  70.9 23.8 %collective-permute-start.13 = (f32[12,4,32,128]{3,2,1,0:T(8,128)}, f32[12,4,32,128]{3,2,1,0:T(8,128)}, u32[]{:S(2)}, u32[]{:S(2)}) collective-permute-start(f32[12,4,32,128]{3,2,1,0:T(8,128)} %get-tuple-element.47), channel_id=1, source_target_pairs={{1,4},{3,6},{4,1},{5,8},{6,3},{7,10},{8,5},{9,12},{10,7},{11,14},{... | collective-permute-start | bytes 2359304 | tf_op jit(solution)/shard_map/ppermute | solution.py:756
  72.4 22.3 %collective-permute-start.14 = (f32[12,4,32,128]{3,2,1,0:T(8,128)}, f32[12,4,32,128]{3,2,1,0:T(8,128)}, u32[]{:S(2)}, u32[]{:S(2)}) collective-permute-start(f32[12,4,32,128]{3,2,1,0:T(8,128)} %get-tuple-element.48), channel_id=1, source_target_pairs={{0,1},{1,0},{2,3},{3,2},{4,5},{5,4},{6,7},{7,6},{8,9},{9,8},{10,11... | collective-permute-start | bytes 2359304 | tf_op jit(solution)/shard_map/ppermute | solution.py:756
  76.6 18.1 %collective-permute-start.10 = (f32[12,8,8,128]{3,2,1,0:T(8,128)}, f32[12,8,8,128]{3,2,1,0:T(8,128)S(1)}, u32[]{:S(2)}, u32[]{:S(2)}) collective-permute-start(f32[12,8,8,128]{3,2,1,0:T(8,128)} %get-tuple-element.44), channel_id=1, source_target_pairs={{0,2},{1,3},{2,0},{3,1},{4,6},{5,7},{6,4},{7,5},{8,10},{9,11},{10,... | collective-permute-start | bytes 1179656 | tf_op jit(solution)/shard_map/ppermute | solution.py:756
  77.1 13.4 %all-to-all-start.1 = ((f32[16,8,128]{2,1,0:T(8,128)}), f32[16,8,128]{2,1,0:T(8,128)}, u32[]{:S(2)}, u32[]{:S(2)}) async-start(f32[16,8,128]{2,1,0:T(8,128)} %copy-done.26), calls=%async_computation.1 | async-start | bytes 131072 | tf_op jit(solution)/shard_map/all_to_all | solution.py:759
  81.3 13.4 %collective-permute-start.11 = (f32[12,2,8,128]{3,2,1,0:T(8,128)}, f32[12,2,8,128]{3,2,1,0:T(8,128)}, u32[]{:S(2)}, u32[]{:S(2)}) collective-permute-start(f32[12,2,8,128]{3,2,1,0:T(8,128)} %copy-done.29), channel_id=1, source_target_pairs={{0,3},{1,2},{2,1},{3,0},{4,7},{5,6},{6,5},{7,4},{8,11},{9,10},{10,... | collective-permute-start | bytes 294920 | tf_op jit(solution)/shard_map/ppermute | solution.py:756
  82.8 11.9 %collective-permute-start.12 = (f32[12,2,8,128]{3,2,1,0:T(8,128)}, f32[12,2,8,128]{3,2,1,0:T(8,128)}, u32[]{:S(2)}, u32[]{:S(2)}) collective-permute-start(f32[12,2,8,128]{3,2,1,0:T(8,128)} %copy-done.28), channel_id=1, source_target_pairs={{1,6},{3,4},{4,3},{5,10},{6,1},{7,8},{8,7},{9,14},{10,5},{11,12},{... | collective-permute-start | bytes 294920 | tf_op jit(solution)/shard_map/ppermute | solution.py:756
  90.6 1.1 copy-start.22
  94.7 1.1 copy-start.20
  112.3 14.0 %collective-permute-start.15 = (f32[6,16,32,128]{3,2,1,0:T(8,128)S(1)}, f32[6,16,32,128]{3,2,1,0:T(8,128)S(1)}, u32[]{:S(2)}, u32[]{:S(2)}) collective-permute-start(f32[6,16,32,128]{3,2,1,0:T(8,128)S(1)} %get-tuple-element.60), channel_id=1, source_target_pairs={{0,1},{1,0},{2,3},{3,2},{4,5},{5,4},{6,7},{7,6},{8,9},{9,8},{10,11... | collective-permute-start | bytes 4718600 | tf_op jit(solution)/shard_map/ppermute | solution.py:756
  (15 other events, 13.1 us)

commit v4 on v3

--- a/solution.py
+++ b/solution.py
@@ -23,9 +23,9 @@
 DEEP = SUBSTEPS
 LINE = ("gz", "gx", "af")
 HBM = pl.BlockSpec(memory_space=pltpu.HBM)
+ANY = pl.BlockSpec(memory_space=pl.ANY)
 SMEM = pl.BlockSpec(memory_space=pltpu.SMEM)
 VMEM_LIMIT = 24 * 1024 * 1024
-PACK_LIMIT = 60 * 1024 * 1024
 F32 = jnp.float32
 
 
@@ -102,24 +102,34 @@
         copy.wait()
 
 
-def call(plan, body, name, shapes, in_specs, scratch, copies, flops=0, moved=0, aliases=None, limit=VMEM_LIMIT):
-    return pl.pallas_call(
+def call(plan, body, name, shapes, in_specs, scratch, copies, flops=0, moved=0, aliases=None):
+    kernel = pl.pallas_call(
         functools.partial(body, plan),
-        out_shape=[jax.ShapeDtypeStruct(s, F32) for s in shapes],
+        out_shape=[pltpu.HBM(s, F32) for s in shapes],
         in_specs=in_specs,
         out_specs=[HBM] * len(shapes),
         scratch_shapes=scratch + [pltpu.SemaphoreType.DMA((copies,))],
         input_output_aliases=aliases or {},
-        compiler_params=pltpu.CompilerParams(vmem_limit_bytes=limit),
+        compiler_params=pltpu.CompilerParams(vmem_limit_bytes=VMEM_LIMIT),
         cost_estimate=pl.CostEstimate(flops=flops, bytes_accessed=moved, transcendentals=0),
         name=name,
     )
 
+    def run(*args):
+        placed = []
+        for arg, spec in zip(args, in_specs):
+            in_hbm = spec.memory_space is pltpu.HBM
+            placed.append(pltpu.with_memory_space_constraint(arg, pltpu.HBM) if in_hbm else arg)
+        return kernel(*placed)
+
+    return run
+
 
 def pack_kernel(plan, *refs):
     raw, other, medium, nside = refs[:6], refs[6:12], refs[12], len(plan.sides)
-    outs = refs[14 : 15 + 3 * nside]
-    edge, edge_code, face, face_code, strips, sems = refs[15 + 3 * nside :]
+    slab_in, table = refs[13:15]
+    outs = refs[15 : 17 + 3 * nside]
+    edge, edge_code, face, face_code, strips, slab, coef, sems = refs[17 + 3 * nside :]
     copies = Copies(sems)
     k = lax.axis_index("af")
     mine = pl.ds(plan.own * k, plan.own)
@@ -139,7 +149,20 @@
         late.append(copies.start(raw[c].at[0, outer], face.at[c]))
         late.append(copies.start(other[c].at[0, outer], face.at[6 + c]))
     late.append(copies.start(medium.at[outer], face_code))
+    early.append(copies.start(slab_in, slab))
+    for s in range(2):
+        which = k if s == 0 else 1 - k
+        kerr, two, free = table[which, 0], table[which, 1], table[which, 2]
+        for n, value in enumerate((kerr, two, 0.5 * two, 0.5 * free)):
+            coef[4 * s + n] = jnp.full((8, plan.lanes), value)
+    last.append(copies.start(coef, outs[-1]))
     wait(early)
+    page = slab[...]
+    face[13] = jnp.broadcast_to(page[None, 0:1], (DEEP, plan.cols, plan.lanes))
+    face[13, 0, 0:8, :] = page
+    for n in range(nside):
+        for q in range(plan.own // 2):
+            strips[n, 13, q] = page
 
     def fill(slot, low):
         def rows(q, _):
@@ -154,7 +177,7 @@
         lax.fori_loop(0, plan.own // 2, rows, 0)
 
     each_side(plan, lambda slot, side: fill(slot, 4 if plan.paired == (side == "high") else 0))
-    send_strips(plan, copies, last, strips, outs[1:])
+    send_strips(plan, copies, last, strips, outs[1:-1])
     wait(late)
     face[12] = face_code[...].astype(F32)
     last.append(copies.start(face, outs[0]))
@@ -179,27 +202,28 @@
     return shapes
 
 
-def pack(plan, raw, other, medium, after):
+def pack(plan, raw, other, medium, slab, table):
     wide = (plan.cols, plan.lanes)
     nside = len(plan.sides)
     scratch = [
         pltpu.VMEM((nside, 12, plan.own, 8, plan.lanes), F32),
         pltpu.VMEM((nside, plan.own, 8, plan.lanes), jnp.int32),
-        pltpu.VMEM((13, DEEP) + wide, F32),
+        pltpu.VMEM((14, DEEP) + wide, F32),
         pltpu.VMEM((DEEP,) + wide, jnp.int32),
-        pltpu.VMEM((nside, 13, plan.own // 2, 8, plan.lanes), F32),
+        pltpu.VMEM((nside, 14, plan.own // 2, 8, plan.lanes), F32),
+        pltpu.VMEM((8, plan.lanes), F32),
+        pltpu.VMEM((8, 8, plan.lanes), F32),
     ]
     return call(
         plan,
         pack_kernel,
         "pack",
-        [(13, DEEP) + wide] + strip_shapes(plan, 13),
-        [HBM] * 14,
+        [(14, DEEP) + wide] + strip_shapes(plan, 14) + [(8, 8, plan.lanes)],
+        [HBM] * 6 + [ANY] * 6 + [HBM, ANY, SMEM],
         scratch,
-        16 * nside + 14,
+        16 * nside + 16,
         moved=4_000_000,
-        limit=PACK_LIMIT,
-    )(*raw, *other, medium, after)
+    )(*raw, *other, medium, slab, table)
 
 
 def clear(plan, old, new, code):
@@ -396,8 +420,8 @@
     return SUBSTEPS * plan.ext * plan.width * plan.lanes * 150
 
 
-def generation_shape(plan):
-    return (plan.devices, plan.cols // BLOCK_FACTOR, plan.lanes)
+def generation_shape(plan, rows=0):
+    return (plan.devices, plan.cols // BLOCK_FACTOR + rows, plan.lanes)
 
 
 def place_strips(plan, old, code, strips):
@@ -419,19 +443,39 @@
 def send_generation(plan, copies, started, gen, message, gen_out):
     sum_generation(plan, gen, message)
     for d in range(plan.devices):
-        started.append(copies.start(message, gen_out.at[d]))
+        started.append(copies.start(message, gen_out.at[d, pl.ds(0, plan.cols // BLOCK_FACTOR)]))
+
+
+def charge_from_slabs(plan, charge, mine, across, chip, corner):
+    across, chip = chip, across
+    x, k = lax.axis_index("gx"), lax.axis_index("af")
+    slab = plan.slab
+    left = jnp.where(x == 0, mine, across)
+    right = jnp.where(x == 0, across, mine)
+    beyond = jnp.where(x != k, chip, corner)
+    body = jnp.where(k == 0, left, right)
+    before = jnp.where(k == 0, beyond, left)[slab - 1 : slab]
+    after = jnp.where(k == 0, right, beyond)[0:1]
+    skip = (plan.cols - 8) // BLOCK_FACTOR
+    for a in range(slab + 2):
+        row = before if a == 0 else after if a == slab + 1 else body[a - 1 : a]
+        row = jnp.broadcast_to(row, (8, plan.lanes))
+        row = jnp.where(x == 0, row, pltpu.roll(row, plan.lanes - skip, 1))
+        for c in range(plan.width // BLOCK_FACTOR):
+            value = jnp.broadcast_to(row[0:4, c : c + 1], (4, plan.lanes))
+            charge[a, 4 * c : 4 * c + 4, :] = value
 
 
 def first_kernel(plan, *refs):
     nside = len(plan.sides)
     strips_in = refs[: 3 * nside]
     z_in, raw, other = refs[3 * nside], refs[1 + 3 * nside : 7 + 3 * nside], refs[7 + 3 * nside : 13 + 3 * nside]
-    medium, charge_in, coef_in = refs[13 + 3 * nside : 16 + 3 * nside]
-    outs = refs[16 + 3 * nside : 21 + 6 * nside]
+    medium, slab_in, under_in, coef_in = refs[13 + 3 * nside : 17 + 3 * nside]
+    outs = refs[17 + 3 * nside : 22 + 6 * nside]
     own_out, z_out, core_out, gen_out, code_out = outs[:5]
-    rest = refs[21 + 6 * nside :]
+    rest = refs[22 + 6 * nside :]
     old, new, (base, silicon, gen, charge, message, coef, code) = rest[:12], rest[12:24], rest[24:31]
-    codes, strips, strip_mine, sems = rest[31], rest[32 : 32 + 3 * nside], rest[-2], rest[-1]
+    codes, strips, (strip_mine, slabs, sems) = rest[31], rest[32 : 32 + 3 * nside], rest[-3:]
     copies = Copies(sems)
     k = lax.axis_index("af")
     near = DEEP * (1 - k)
@@ -441,7 +485,11 @@
     mine = pl.ds((plan.own - DEEP) * k, plan.part)
     early = [copies.start(medium.at[mine], codes)]
     early.append(copies.start(z_in.at[12], code.at[there, across]))
-    early.append(copies.start(charge_in, charge))
+    early.append(copies.start(slab_in, slabs.at[0]))
+    if plan.paired:
+        early.append(copies.start(z_in.at[13, 0, pl.ds(0, 8)], slabs.at[1]))
+    else:
+        early.append(copies.start(under_in, charge))
     early.append(copies.start(coef_in, coef))
     for source, target in zip(strips_in, strips):
         early.append(copies.start(source, target))
@@ -462,6 +510,8 @@
     lax.fori_loop(0, plan.part, settle, 0)
     place_strips(plan, old, [code], strips)
     set_media(plan, code, base, silicon)
+    if plan.paired:
+        charge_from_slabs(plan, charge, slabs[0], slabs[1], strips[0][13, 0], strips[2][13, 0])
     wait(late)
     substeps(plan, old, new, base, silicon, charge, gen, coef)
     copies = Copies(sems)
@@ -489,36 +539,42 @@
         late.append(copies.start(old[c].at[pl.ds(inward, DEEP), across], core_out.at[c]))
         late.append(copies.start(old[c].at[pl.ds(DEEP, plan.own), across], own_out.at[c]))
     late.append(copies.start(code, code_out))
+    slab_rows = pl.ds(plan.cols // BLOCK_FACTOR, 8)
+    for d in range(plan.devices):
+        late.append(copies.start(slabs.at[0], gen_out.at[d, slab_rows]))
     each_side(plan, gather)
     send_strips(plan, copies, late, strip_mine, outs[5:])
     send_generation(plan, copies, late, gen, message, gen_out)
     wait(late)
 
 
-def first_round(plan, strips, z_in, raw, other, medium, charge, coef):
+def first_round(plan, strips, z_in, raw, other, medium, slab, under, coef):
     wide = (plan.cols, plan.lanes)
     nside = len(plan.sides)
     shapes = [
         (12, plan.own) + wide,
         (12, DEEP) + wide,
         (12, DEEP) + wide,
-        generation_shape(plan),
+        generation_shape(plan, 8),
         (plan.ext, plan.rows, plan.lanes),
     ] + strip_shapes(plan, 12)
     scratch = round_scratch(plan) + [pltpu.VMEM((plan.part,) + wide, jnp.int32)]
     scratch += [pltpu.VMEM(s.shape, F32) for s in strips]
-    scratch += [pltpu.VMEM((nside, 12, plan.own // 2, 8, plan.lanes), F32)]
+    scratch += [
+        pltpu.VMEM((nside, 12, plan.own // 2, 8, plan.lanes), F32),
+        pltpu.VMEM((2, 8, plan.lanes), F32),
+    ]
     return call(
         plan,
         first_kernel,
         "first_round",
         shapes,
-        [HBM] * (16 + 3 * nside),
+        [ANY] * (1 + 3 * nside) + [HBM] * 6 + [ANY] * 6 + [HBM, ANY, ANY, HBM],
         scratch,
-        37 + 3 * nside + plan.devices,
+        40 + 3 * nside + 2 * plan.devices,
         round_flops(plan),
         10_000_000,
-    )(*strips, z_in, *raw, *other, medium, charge, coef)
+    )(*strips, z_in, *raw, *other, medium, slab, under, coef)
 
 
 def second_kernel(plan, *refs):
@@ -573,7 +629,7 @@
         second_kernel,
         "second_round",
         shapes,
-        [HBM] * (6 + 3 * nside),
+        [ANY] * (2 + 3 * nside) + [HBM] * 4,
         scratch,
         39 + 3 * nside + plan.devices,
         round_flops(plan),
@@ -582,18 +638,23 @@
 
 
 def join_kernel(plan, *refs):
-    got, outs, sems = refs[6], refs[7:13], refs[13]
+    got, outs, (half, sems) = refs[6], refs[7:13], refs[13:]
     copies = Copies(sems)
-    k = lax.axis_index("af")
-    rows = pl.ds(plan.own * (1 - k), plan.own)
-    wait([copies.start(got.at[c], outs[c].at[0, rows]) for c in range(6)])
+    rows = pl.ds(plan.own * (1 - lax.axis_index("af")), plan.own)
+    early = [copies.start(got.at[c], half.at[c]) for c in range(6)]
+    late = []
+    for c in range(6):
+        early[c].wait()
+        late.append(copies.start(half.at[c], outs[c].at[0, rows]))
+    wait(late)
 
 
 def join(plan, halves, got):
     shapes = [h.shape for h in halves]
     aliases = {c: c for c in range(6)}
+    scratch = [pltpu.VMEM(got.shape, F32)]
     return call(
-        plan, join_kernel, "join", shapes, [HBM] * 7, [], 6, moved=3_000_000, aliases=aliases
+        plan, join_kernel, "join", shapes, [HBM] * 6 + [ANY], scratch, 12, moved=3_000_000, aliases=aliases
     )(*halves, got)
 
 
@@ -617,9 +678,8 @@
     return (plan.ext // BLOCK_FACTOR, plan.width, plan.lanes)
 
 
-def spread_kernel(plan, density, table, grid_out, charge_out, coef_out, grid, charge, coef, sems):
+def spread_kernel(plan, density, charge_out, grid, charge, sems):
     copies = Copies(sems)
-    k = lax.axis_index("af")
     rows, cols, lanes = plan.grid_rows, plan.grid_cols, plan.lanes
 
     def clean(i, _):
@@ -637,48 +697,61 @@
 
     lax.fori_loop(0, rows, read, 0)
     under_cells(plan, grid, charge)
-    for s in range(2):
-        which = k if s == 0 else 1 - k
-        kerr, two, free = table[which, 0], table[which, 1], table[which, 2]
-        for n, value in enumerate((kerr, two, 0.5 * two, 0.5 * free)):
-            coef[4 * s + n] = jnp.full((8, lanes), value)
-    pairs = ((grid, grid_out), (charge, charge_out), (coef, coef_out))
-    wait([copies.start(source, target) for source, target in pairs])
-
-
-def spread(plan, density, table):
-    shapes = [grid_shape(plan), charge_shape(plan), (8, 8, plan.lanes)]
-    scratch = [pltpu.VMEM(shape, F32) for shape in shapes]
-    return call(
-        plan, spread_kernel, "spread", shapes, [SMEM, SMEM], scratch, 3, 10_000, 1_000_000
-    )(density, table)
-
-
-def carrier_kernel(plan, last, density_in, gens_in, *refs):
+    copies.start(charge, charge_out).wait()
+
+
+def spread(plan, density):
+    scratch = [pltpu.VMEM(grid_shape(plan), F32), pltpu.VMEM(charge_shape(plan), F32)]
+    shapes = [charge_shape(plan)]
+    return call(plan, spread_kernel, "spread", shapes, [SMEM], scratch, 1, 10_000, 1_000_000)(density)
+
+
+def carrier_kernel(plan, last, *refs):
+    gens_in, refs = refs[0], refs[1:]
+    if last:
+        density_in, refs = refs[0], refs[1:]
     outs = refs[:1] if last else refs[:2]
-    gens, one, two, source, charge, sems = refs[len(outs) :]
+    gens, one, two, source, charge, slab_out, sems = refs[len(outs) :]
     copies = Copies(sems)
     rows, cols, lanes = plan.grid_rows, plan.grid_cols, plan.lanes
     z, x = lax.axis_index("gz"), lax.axis_index("gx")
     blocks, own = plan.cols // BLOCK_FACTOR, plan.own // BLOCK_FACTOR
-    early = [copies.start(gens_in, gens), copies.start(density_in, one)]
+    early = [copies.start(gens_in, gens)]
+    if last:
+        early.append(copies.start(density_in, one))
     zero = jnp.zeros((8, lanes), F32)
+    both = (two,) if last else (one, two)
 
     def clean(i, _):
-        two[i, 0:8, :] = zero
-        two[i, 8 + cols : 16 + cols, :] = zero
+        for ref in both:
+            ref[i, 0:8, :] = zero
+            ref[i, 8 + cols : 16 + cols, :] = zero
         return 0
 
     lax.fori_loop(0, rows + 2, clean, 0)
-    for i in (0, rows + 1):
-        for c in range(8, 8 + cols, 8):
-            two[i, c : c + 8, :] = zero
+    for ref in both:
+        for i in (0, rows + 1):
+            for c in range(8, 8 + cols, 8):
+                ref[i, c : c + 8, :] = zero
     wait(early)
+    diagonal = lax.broadcasted_iota(jnp.int32, (cols, lanes), 0) == lax.broadcasted_iota(
+        jnp.int32, (cols, lanes), 1
+    )
+    if not last:
+
+        def turn(d, _):
+            for r in range(plan.slab):
+                row = jnp.broadcast_to(gens[2 * d, blocks + r : blocks + r + 1, :], (cols, lanes))
+                upright = jnp.where(diagonal, row, 0.0).sum(1, keepdims=True)
+                one[1 + d * plan.slab + r, 8 : 8 + cols, :] = jnp.broadcast_to(upright, (cols, lanes))
+            return 0
+
+        lax.fori_loop(0, plan.gz * plan.gx, turn, 0)
 
     def unpack(line, _):
         for dx in range(plan.gx):
             for dk in range(2):
-                tile = gens[(line * plan.gx + dx) * 2 + dk]
+                tile = gens[(line * plan.gx + dx) * 2 + dk, 0:blocks, :]
                 for a in range(own):
                     source[(line * 2 + dk) * own + a, blocks * dx : blocks * dx + blocks, :] = (
                         jnp.broadcast_to(SOURCE_FACTOR * tile[:, a : a + 1], (blocks, lanes))
@@ -718,34 +791,38 @@
 
     lax.fori_loop(0, CSTEPS // 2, pair, 0)
     if last:
-        rows_out = pl.ds(1 + (z * plan.gx + x) * plan.slab, plan.slab)
-        wait([copies.start(one.at[rows_out, pl.ds(8, cols)], outs[0])])
+        for r in range(plan.slab):
+            upright = one[1 + (z * plan.gx + x) * plan.slab + r, 8 : 8 + cols, :]
+            flat = jnp.where(diagonal, upright, 0.0).sum(0, keepdims=True)
+            slab_out[r : r + 1, :] = flat
+        copies.start(slab_out, outs[0]).wait()
         return
     under_cells(plan, one, charge)
     wait([copies.start(one, outs[0]), copies.start(charge, outs[1])])
 
 
-def carriers(plan, last, density, gens):
+def carriers(plan, last, *arrays):
     grid, lanes = grid_shape(plan), plan.lanes
-    shapes = [(plan.slab, plan.grid_cols, lanes)] if last else [grid, charge_shape(plan)]
+    shapes = [(8, lanes)] if last else [grid, charge_shape(plan)]
     scratch = [
-        pltpu.VMEM(gens.shape, F32),
+        pltpu.VMEM(arrays[0].shape, F32),
         pltpu.VMEM(grid, F32),
         pltpu.VMEM(grid, F32),
         pltpu.VMEM((plan.grid_rows, plan.grid_cols, lanes), F32),
         pltpu.VMEM(charge_shape(plan), F32),
+        pltpu.VMEM((8, lanes), F32),
     ]
     return call(
         plan,
         lambda plan, *refs: carrier_kernel(plan, last, *refs),
         "carriers",
         shapes,
-        [HBM, HBM],
+        [ANY] + [HBM] * (len(arrays) - 1),
         scratch,
         4,
         2_000_000,
         1_000_000,
-    )(density, gens)
+    )(*arrays)
 
 
 def local(ex, ey, ez, hx, hy, hz, medium, table, density):
@@ -772,23 +849,28 @@
         return send(z_msg, lambda z, x, k: (beyond(z, k), x, 1 - k)), got
 
     other = [send(r, core) for r in raw]
-    tiles = plan.gz * plan.gx
-    slabs = everywhere(jnp.broadcast_to(density, (tiles,) + density.shape), ("gz", "gx"))
-    packed = pack(plan, raw, other, medium, slabs)
-    grid, charge, coef = spread(plan, slabs, table)
-    z_in, strips = exchange(packed[0], packed[1:])
-    outs = first_round(plan, strips, z_in, raw, other, medium, charge, coef)
+    slab = jnp.pad(density, ((0, 8 - plan.slab), (0, plan.lanes - plan.grid_cols)))
+    packed = pack(plan, raw, other, medium, slab, table)
+    z_in, strips = exchange(packed[0], packed[1:-1])
+    coef = packed[-1]
+    under = slab
+    if not plan.paired:
+        tiles = plan.gz * plan.gx
+        slabs = everywhere(jnp.broadcast_to(density, (tiles,) + density.shape), ("gz", "gx"))
+        (under,) = spread(plan, slabs)
+    outs = first_round(plan, strips, z_in, raw, other, medium, slab, under, coef)
     own, z_msg, core_msg, gens, code = outs[:5]
     gens = everywhere(gens, LINE)
     z_in, strips = exchange(z_msg, outs[5:])
     core_in = send(core_msg, core)
-    grid, charge = carriers(plan, False, grid, gens)
+    grid, charge = carriers(plan, False, gens)
     outs = second_round(plan, strips, z_in, core_in, own, code, charge, coef)
     halves, sent, gens = outs[:6], outs[6], outs[7]
     gens = everywhere(gens, LINE)
     got = send(sent, core)
-    (slab,) = carriers(plan, True, grid, gens)
-    return tuple(join(plan, halves, got)) + (slab[:, :, 0],)
+    (new_slab,) = carriers(plan, True, gens, grid)
+    new_slab = new_slab[: plan.slab, : plan.grid_cols]
+    return tuple(join(plan, halves, got)) + (new_slab,)
 
 
 def solution(mesh):

time: 129 us -> 111 us (0.86)
  local copies, waits for them, and re-layouts: 22.3 us -> 2.62 us
  blocking collectives: 22.9 us -> 12.5 us
  waiting for transfers between devices: 16.9 us -> 22.8 us
  starting transfers between devices: 21.3 us -> 25.1 us
  Pallas kernels: 43.3 us -> 46.3 us
    unnamed x60 -> x2, local copies, waits for them, and re-layouts: 20.9 us -> 0.68 us
    all_to_all x2 -> x1, blocking collectives: 22.9 us -> 12.5 us  [everywhere(): lax.all_to_all(message, axes, split_axis=0, concat_axis=0, tiled=True)]
    ppermute x16, waiting for transfers between devices: 10.4 us -> 15.3 us  [send(): return lax.ppermute(message, LINE, line_pairs(plan, target))]
    ppermute x16, starting transfers between devices: 17.2 us -> 21.5 us  [send(): return lax.ppermute(message, LINE, line_pairs(plan, target))]
    pallas_call x7 -> x6, Pallas kernels: 43.3 us -> 46.3 us  [run(): return kernel(*placed)]
  transfers between devices with their start and end apart: 17 -> 17, of which waited for: 3 -> 7; matrix products, arithmetic and copies ran while one was open for 1% -> 2% of each run, Pallas kernels for 6% -> 7%
where the time goes in v4:
time: 111 us; the launch traced here: 110 us
  Pallas kernels  46.3 us (42%)
  starting transfers between devices  25.1 us (23%)
  waiting for transfers between devices  22.8 us (21%)
  blocking collectives  12.5 us (11%)
  local copies, waits for them, and re-layouts  2.62 us (2%)
    pallas_call x6, Pallas kernels, run(): return kernel(*placed)  46.3 us
    ppermute x16, starting transfers between devices, send(): return lax.ppermute(message, LINE, line_pairs(plan, target))  21.5 us
    ppermute x16, waiting for transfers between devices, send(): return lax.ppermute(message, LINE, line_pairs(plan, target))  15.3 us
    all_to_all x1, blocking collectives, everywhere(): lax.all_to_all(message, axes, split_axis=0, concat_axis=0, tiled=True)  12.5 us
    all_to_all x1, waiting for transfers between devices, everywhere(): lax.all_to_all(message, axes, split_axis=0, concat_axis=0, tiled=True)  7.55 us
    all_to_all x1, starting transfers between devices, everywhere(): lax.all_to_all(message, axes, split_axis=0, concat_axis=0, tiled=True)  3.51 us
  transfers between devices with their start and end apart: 17, of which 7 were waited for; matrix products, arithmetic and copies ran while one was open for 2% of the time, Pallas kernels for 7%

profile of v4, /device:TPU:0, one launch (start us, length us, event | category | flops | bytes accessed | tf_op | source)
XLA Modules:
  0.0 110.2 jit_solution(4707074808289226563)
XLA Ops:
  0.6 0.5 collective-permute-start
  1.2 0.4 collective-permute-start.2
  1.7 0.4 collective-permute-start.4
  2.2 0.7 collective-permute-done.refs_6_.refs_10_
  2.9 0.4 collective-permute-start.5
  3.3 0.7 pad.4.refs_13_.refs_17_.refs_18_
  4.0 0.4 collective-permute-done.2.refs_8_.refs_12_
  4.4 0.7 collective-permute-done.3.refs_9_.refs_13_
  5.1 0.7 collective-permute-done.4.refs_10_.refs_14_
  5.9 0.7 collective-permute-done.5.refs_11_.refs_15_
  6.6 0.7 copy-done
  7.3 3.3 %pack.1 = (f32[14,4,32,128]{3,2,1,0:T(8,128)}, f32[14,8,8,128]{3,2,1,0:T(8,128)}, f32[14,2,8,128]{3,2,1,0:T(8,128)}, f32[14,2,8,128]{3,2,1,0:T(8,128)}, f32[8,8,128]{2,1,0:T(8,128)}) custom-call(f32[1,32,32,128]{3,2,1,0:T(8,128)} %refs_4_.3, f32[1,32,32,128]{3,2,1,0:T(8,128)} %refs_5_.3, f32[1,32,32,128]{3,2,1,0:T(8,128)} %refs_6_.1, ...), custom_call_target="tpu_custom_call" | custom-call | bytes 4000000 | tf_op jit(solution)/shard_map/pack/pallas_call | solution.py:123
  10.6 0.7 collective-permute-start.9
  11.4 2.9 %collective-permute-start.6 = (f32[14,8,8,128]{3,2,1,0:T(8,128)}, f32[14,8,8,128]{3,2,1,0:T(8,128)S(1)}, u32[]{:S(2)}, u32[]{:S(2)}) collective-permute-start(f32[14,8,8,128]{3,2,1,0:T(8,128)} %get-tuple-element.36), channel_id=1, source_target_pairs={{0,2},{1,3},{2,0},{3,1},{4,6},{5,7},{6,4},{7,5},{8,10},{9,11},{10,... | collective-permute-start | bytes 1376264 | tf_op jit(solution)/shard_map/ppermute | solution.py:833
  14.3 2.7 %collective-permute-start.7 = (f32[14,2,8,128]{3,2,1,0:T(8,128)}, f32[14,2,8,128]{3,2,1,0:T(8,128)S(1)}, u32[]{:S(2)}, u32[]{:S(2)}) collective-permute-start(f32[14,2,8,128]{3,2,1,0:T(8,128)} %get-tuple-element.37), channel_id=1, source_target_pairs={{0,3},{1,2},{2,1},{3,0},{4,7},{5,6},{6,5},{7,4},{8,11},{9,10},{10,... | collective-permute-start | bytes 344072 | tf_op jit(solution)/shard_map/ppermute | solution.py:833
  17.0 0.7 collective-permute-start.8
  17.7 11.9 %collective-permute-done.7.refs_1_ = f32[14,2,8,128]{3,2,1,0:T(8,128)S(1)} collective-permute-done((f32[14,2,8,128]{3,2,1,0:T(8,128)}, f32[14,2,8,128]{3,2,1,0:T(8,128)S(1)}, u32[]{:S(2)}, u32[]{:S(2)}) %collective-permute-start.7) | collective-permute-done | bytes 114720 | tf_op jit(solution)/shard_map/ppermute | solution.py:833
  29.6 17.7 %first_round.1 = (f32[12,16,32,128]{3,2,1,0:T(8,128)}, f32[12,4,32,128]{3,2,1,0:T(8,128)}, f32[12,4,32,128]{3,2,1,0:T(8,128)}, f32[16,16,128]{2,1,0:T(8,128)}, f...) custom-call(f32[14,8,8,128]{3,2,1,0:T(8,128)S(1)} %collective-permute-, ...), custom_call_target="tpu_custom_call" | custom-call | flops 73728000 | bytes 10000000 | tf_op jit(solution)/shard_map/first_round/pallas_call | solution.py:123
  47.3 0.7 collective-permute-start.13
  48.0 7.3 %collective-permute-start.14 = (f32[12,4,32,128]{3,2,1,0:T(8,128)}, f32[12,4,32,128]{3,2,1,0:T(8,128)S(1)}, u32[]{:S(2)}, u32[]{:S(2)}) collective-permute-start(f32[12,4,32,128]{3,2,1,0:T(8,128)} %get-tuple-element.45), channel_id=1, source_target_pairs={{0,1},{1,0},{2,3},{3,2},{4,5},{5,4},{6,7},{7,6},{8,9},{9,8},{10,11... | collective-permute-start | bytes 2359304 | tf_op jit(solution)/shard_map/ppermute | solution.py:833
  55.3 1.7 %collective-permute-start.10 = (f32[12,8,8,128]{3,2,1,0:T(8,128)}, f32[12,8,8,128]{3,2,1,0:T(8,128)S(1)}, u32[]{:S(2)}, u32[]{:S(2)}) collective-permute-start(f32[12,8,8,128]{3,2,1,0:T(8,128)} %get-tuple-element.41), channel_id=1, source_target_pairs={{0,2},{1,3},{2,0},{3,1},{4,6},{5,7},{6,4},{7,5},{8,10},{9,11},{10,... | collective-permute-start | bytes 1179656 | tf_op jit(solution)/shard_map/ppermute | solution.py:833
  57.0 3.5 %all-to-all-start = ((f32[16,16,128]{2,1,0:T(8,128)}), f32[16,16,128]{2,1,0:T(8,128)S(1)}, u32[]{:S(2)}, u32[]{:S(2)}) async-start(f32[16,16,128]{2,1,0:T(8,128)} %get-tuple-element.48), calls=%async_computation | async-start | bytes 262144 | tf_op jit(solution)/shard_map/all_to_all | solution.py:836
  60.5 1.6 %collective-permute-start.11 = (f32[12,2,8,128]{3,2,1,0:T(8,128)}, f32[12,2,8,128]{3,2,1,0:T(8,128)S(1)}, u32[]{:S(2)}, u32[]{:S(2)}) collective-permute-start(f32[12,2,8,128]{3,2,1,0:T(8,128)} %get-tuple-element.42), channel_id=1, source_target_pairs={{0,3},{1,2},{2,1},{3,0},{4,7},{5,6},{6,5},{7,4},{8,11},{9,10},{10,... | collective-permute-start | bytes 294920 | tf_op jit(solution)/shard_map/ppermute | solution.py:833
  62.0 0.7 collective-permute-start.12
  62.7 7.5 %all-to-all-done.refs_0_ = f32[16,16,128]{2,1,0:T(8,128)S(1)} async-done(((f32[16,16,128]{2,1,0:T(8,128)}), f32[16,16,128]{2,1,0:T(8,128)S(1)}, u32[]{:S(2)}, u32[]{:S(2)}) %all-to-all-start) | async-done | bytes 131104 | tf_op jit(solution)/shard_map/all_to_all | solution.py:836
  70.3 3.8 %carriers.2 = (f32[34,32,128]{2,1,0:T(8,128)}, f32[6,40,128]{2,1,0:T(8,128)}) custom-call(f32[16,16,128]{2,1,0:T(8,128)S(1)} %all-to-all-done.refs_0_), custom_call_target="tpu_custom_call" | custom-call | flops 2000000 | bytes 1000000 | tf_op jit(solution)/shard_map/carriers/pallas_call | solution.py:123
  74.1 16.6 %second_round.1 = (f32[1,32,32,128]{3,2,1,0:T(8,128)}, f32[1,32,32,128]{3,2,1,0:T(8,128)}, f32[1,32,32,128]{3,2,1,0:T(8,128)}, f32[1,32,32,128]{3,2,1,0:T(8,128)...) custom-call(f32[12,8,8,128]{3,2,1,0:T(8,128)S(1)} %collective-permut, ...), custom_call_target="tpu_custom_call" | custom-call | flops 73728000 | bytes 10000000 | tf_op jit(solution)/shard_map/second_round/pallas_call | solution.py:123
  90.7 0.7 collective-permute-start.15
  91.4 12.5 %all_to_all.10.refs_0_ = f32[16,8,128]{2,1,0:T(8,128)S(1)} all-to-all(f32[16,8,128]{2,1,0:T(8,128)} %get-tuple-element.63), channel_id=1, replica_groups=mesh['group'=2,'gz'=4,'gx'=2,'af'=2] {'gz','gx','af'}, dimensions={0} | all-to-all | bytes 131072 | tf_op jit(solution)/shard_map/all_to_all | solution.py:836
  104.0 3.6 %carriers.3 = f32[8,128]{1,0:T(8,128)} custom-call(f32[16,8,128]{2,1,0:T(8,128)S(1)} %all_to_all.10.refs_0_, f32[34,32,128]{2,1,0:T(8,128)} %get-tuple-element.64.refs_1_), custom_call_target="tpu_custom_call" | custom-call | flops 2000000 | bytes 1000000 | tf_op jit(solution)/shard_map/carriers/pallas_call | solution.py:123
  107.6 1.3 %slice.3 = f32[4,16]{1,0:T(4,128)} slice(f32[8,128]{1,0:T(8,128)} %carriers.3), slice={[0:4], [0:16]} | slice | bytes 512 | tf_op jit(solution)/shard_map/slice | solution.py:872
  108.8 1.3 %join.1 = (f32[1,32,32,128]{3,2,1,0:T(8,128)}, f32[1,32,32,128]{3,2,1,0:T(8,128)}, f32[1,32,32,128]{3,2,1,0:T(8,128)}, f32[1,32,32,128]{3,2,1,0:T(8,128)}, f32[1...) custom-call(f32[1,32,32,128]{3,2,1,0:T(8,128)} %get-tuple-element.50, ...), custom_call_target="tpu_custom_call", output_to_operand_aliasing={{0}: (0, {}), {1}: (1, {}), {2}: (2, {}), {3}: (3, {}), {4}... | custom-call | bytes 3000000 | tf_op jit(solution)/shard_map/join/pallas_call | solution.py:123
  (13 shorter events, 0.2 us)
Async XLA Ops:
  0.6 2.3 %collective-permute-start = (f32[1,32,32,128]{3,2,1,0:T(8,128)}, f32[1,32,32,128]{3,2,1,0:T(8,128)S(1)}, u32[]{:S(2)}, u32[]{:S(2)}) collective-permute-start(f32[1,32,32,128]{3,2,1,0:T(8,128)} %refs_4_.3), channel_id=1, source_target_pairs={{0,1},{1,0},{2,3},{3,2},{4,5},{5,4},{6,7},{7,6},{8,9},{9,8},{10,11... | collective-permute-start | bytes 1572872 | tf_op jit(solution)/shard_map/ppermute | solution.py:833
  1.1 2.8 %collective-permute-start.1 = (f32[1,32,32,128]{3,2,1,0:T(8,128)}, f32[1,32,32,128]{3,2,1,0:T(8,128)S(1)}, u32[]{:S(2)}, u32[]{:S(2)}) collective-permute-start(f32[1,32,32,128]{3,2,1,0:T(8,128)} %refs_5_.3), channel_id=1, source_target_pairs={{0,1},{1,0},{2,3},{3,2},{4,5},{5,4},{6,7},{7,6},{8,9},{9,8},{10,11... | collective-permute-start | bytes 1572872 | tf_op jit(solution)/shard_map/ppermute | solution.py:833
  1.2 3.2 %collective-permute-start.2 = (f32[1,32,32,128]{3,2,1,0:T(8,128)}, f32[1,32,32,128]{3,2,1,0:T(8,128)S(1)}, u32[]{:S(2)}, u32[]{:S(2)}) collective-permute-start(f32[1,32,32,128]{3,2,1,0:T(8,128)} %refs_6_.1), channel_id=1, source_target_pairs={{0,1},{1,0},{2,3},{3,2},{4,5},{5,4},{6,7},{7,6},{8,9},{9,8},{10,11... | collective-permute-start | bytes 1572872 | tf_op jit(solution)/shard_map/ppermute | solution.py:833
  1.7 3.5 %collective-permute-start.3 = (f32[1,32,32,128]{3,2,1,0:T(8,128)}, f32[1,32,32,128]{3,2,1,0:T(8,128)S(1)}, u32[]{:S(2)}, u32[]{:S(2)}) collective-permute-start(f32[1,32,32,128]{3,2,1,0:T(8,128)} %refs_7_.1), channel_id=1, source_target_pairs={{0,1},{1,0},{2,3},{3,2},{4,5},{5,4},{6,7},{7,6},{8,9},{9,8},{10,11... | collective-permute-start | bytes 1572872 | tf_op jit(solution)/shard_map/ppermute | solution.py:833
  1.7 4.2 %collective-permute-start.4 = (f32[1,32,32,128]{3,2,1,0:T(8,128)}, f32[1,32,32,128]{3,2,1,0:T(8,128)S(1)}, u32[]{:S(2)}, u32[]{:S(2)}) collective-permute-start(f32[1,32,32,128]{3,2,1,0:T(8,128)} %refs_8_.1), channel_id=1, source_target_pairs={{0,1},{1,0},{2,3},{3,2},{4,5},{5,4},{6,7},{7,6},{8,9},{9,8},{10,11... | collective-permute-start | bytes 1572872 | tf_op jit(solution)/shard_map/ppermute | solution.py:833
  2.9 3.7 %collective-permute-start.5 = (f32[1,32,32,128]{3,2,1,0:T(8,128)}, f32[1,32,32,128]{3,2,1,0:T(8,128)S(1)}, u32[]{:S(2)}, u32[]{:S(2)}) collective-permute-start(f32[1,32,32,128]{3,2,1,0:T(8,128)} %refs_9_.1), channel_id=1, source_target_pairs={{0,1},{1,0},{2,3},{3,2},{4,5},{5,4},{6,7},{7,6},{8,9},{9,8},{10,11... | collective-permute-start | bytes 1572872 | tf_op jit(solution)/shard_map/ppermute | solution.py:833
  6.6 0.7 copy-start
  10.6 18.9 %collective-permute-start.9 = (f32[14,4,32,128]{3,2,1,0:T(8,128)}, f32[14,4,32,128]{3,2,1,0:T(8,128)S(1)}, u32[]{:S(2)}, u32[]{:S(2)}) collective-permute-start(f32[14,4,32,128]{3,2,1,0:T(8,128)} %get-tuple-element.39), channel_id=1, source_target_pairs={{1,4},{3,6},{4,1},{5,8},{6,3},{7,10},{8,5},{9,12},{10,7},{11,14},{... | collective-permute-start | bytes 2752520 | tf_op jit(solution)/shard_map/ppermute | solution.py:833
  11.4 18.2 %collective-permute-start.6 = (f32[14,8,8,128]{3,2,1,0:T(8,128)}, f32[14,8,8,128]{3,2,1,0:T(8,128)S(1)}, u32[]{:S(2)}, u32[]{:S(2)}) collective-permute-start(f32[14,8,8,128]{3,2,1,0:T(8,128)} %get-tuple-element.36), channel_id=1, source_target_pairs={{0,2},{1,3},{2,0},{3,1},{4,6},{5,7},{6,4},{7,5},{8,10},{9,11},{10,... | collective-permute-start | bytes 1376264 | tf_op jit(solution)/shard_map/ppermute | solution.py:833
  14.3 15.3 %collective-permute-start.7 = (f32[14,2,8,128]{3,2,1,0:T(8,128)}, f32[14,2,8,128]{3,2,1,0:T(8,128)S(1)}, u32[]{:S(2)}, u32[]{:S(2)}) collective-permute-start(f32[14,2,8,128]{3,2,1,0:T(8,128)} %get-tuple-element.37), channel_id=1, source_target_pairs={{0,3},{1,2},{2,1},{3,0},{4,7},{5,6},{6,5},{7,4},{8,11},{9,10},{10,... | collective-permute-start | bytes 344072 | tf_op jit(solution)/shard_map/ppermute | solution.py:833
  17.0 12.5 %collective-permute-start.8 = (f32[14,2,8,128]{3,2,1,0:T(8,128)}, f32[14,2,8,128]{3,2,1,0:T(8,128)S(1)}, u32[]{:S(2)}, u32[]{:S(2)}) collective-permute-start(f32[14,2,8,128]{3,2,1,0:T(8,128)} %get-tuple-element.38), channel_id=1, source_target_pairs={{1,6},{3,4},{4,3},{5,10},{6,1},{7,8},{8,7},{9,14},{10,5},{11,12},{... | collective-permute-start | bytes 344072 | tf_op jit(solution)/shard_map/ppermute | solution.py:833
  47.3 26.9 %collective-permute-start.13 = (f32[12,4,32,128]{3,2,1,0:T(8,128)}, f32[12,4,32,128]{3,2,1,0:T(8,128)S(1)}, u32[]{:S(2)}, u32[]{:S(2)}) collective-permute-start(f32[12,4,32,128]{3,2,1,0:T(8,128)} %get-tuple-element.44), channel_id=1, source_target_pairs={{1,4},{3,6},{4,1},{5,8},{6,3},{7,10},{8,5},{9,12},{10,7},{11,14},{... | collective-permute-start | bytes 2359304 | tf_op jit(solution)/shard_map/ppermute | solution.py:833
  48.0 26.1 %collective-permute-start.14 = (f32[12,4,32,128]{3,2,1,0:T(8,128)}, f32[12,4,32,128]{3,2,1,0:T(8,128)S(1)}, u32[]{:S(2)}, u32[]{:S(2)}) collective-permute-start(f32[12,4,32,128]{3,2,1,0:T(8,128)} %get-tuple-element.45), channel_id=1, source_target_pairs={{0,1},{1,0},{2,3},{3,2},{4,5},{5,4},{6,7},{7,6},{8,9},{9,8},{10,11... | collective-permute-start | bytes 2359304 | tf_op jit(solution)/shard_map/ppermute | solution.py:833
  55.3 18.8 %collective-permute-start.10 = (f32[12,8,8,128]{3,2,1,0:T(8,128)}, f32[12,8,8,128]{3,2,1,0:T(8,128)S(1)}, u32[]{:S(2)}, u32[]{:S(2)}) collective-permute-start(f32[12,8,8,128]{3,2,1,0:T(8,128)} %get-tuple-element.41), channel_id=1, source_target_pairs={{0,2},{1,3},{2,0},{3,1},{4,6},{5,7},{6,4},{7,5},{8,10},{9,11},{10,... | collective-permute-start | bytes 1179656 | tf_op jit(solution)/shard_map/ppermute | solution.py:833
  57.0 13.3 %all-to-all-start = ((f32[16,16,128]{2,1,0:T(8,128)}), f32[16,16,128]{2,1,0:T(8,128)S(1)}, u32[]{:S(2)}, u32[]{:S(2)}) async-start(f32[16,16,128]{2,1,0:T(8,128)} %get-tuple-element.48), calls=%async_computation | async-start | bytes 262144 | tf_op jit(solution)/shard_map/all_to_all | solution.py:836
  60.5 13.6 %collective-permute-start.11 = (f32[12,2,8,128]{3,2,1,0:T(8,128)}, f32[12,2,8,128]{3,2,1,0:T(8,128)S(1)}, u32[]{:S(2)}, u32[]{:S(2)}) collective-permute-start(f32[12,2,8,128]{3,2,1,0:T(8,128)} %get-tuple-element.42), channel_id=1, source_target_pairs={{0,3},{1,2},{2,1},{3,0},{4,7},{5,6},{6,5},{7,4},{8,11},{9,10},{10,... | collective-permute-start | bytes 294920 | tf_op jit(solution)/shard_map/ppermute | solution.py:833
  62.0 12.1 %collective-permute-start.12 = (f32[12,2,8,128]{3,2,1,0:T(8,128)}, f32[12,2,8,128]{3,2,1,0:T(8,128)S(1)}, u32[]{:S(2)}, u32[]{:S(2)}) collective-permute-start(f32[12,2,8,128]{3,2,1,0:T(8,128)} %get-tuple-element.43), channel_id=1, source_target_pairs={{1,6},{3,4},{4,3},{5,10},{6,1},{7,8},{8,7},{9,14},{10,5},{11,12},{... | collective-permute-start | bytes 294920 | tf_op jit(solution)/shard_map/ppermute | solution.py:833
  90.7 18.1 %collective-permute-start.15 = (f32[6,16,32,128]{3,2,1,0:T(8,128)}, f32[6,16,32,128]{3,2,1,0:T(8,128)S(1)}, u32[]{:S(2)}, u32[]{:S(2)}) collective-permute-start(f32[6,16,32,128]{3,2,1,0:T(8,128)} %get-tuple-element.56), channel_id=1, source_target_pairs={{0,1},{1,0},{2,3},{3,2},{4,5},{5,4},{6,7},{7,6},{8,9},{9,8},{10,11... | collective-permute-start | bytes 4718600 | tf_op jit(solution)/shard_map/ppermute | solution.py:833

commit v5 on v4

--- a/solution.py
+++ b/solution.py
@@ -292,7 +292,7 @@
         off = (x == 0) if t == 0 else (x == plan.gx - 1)
         return jnp.where(off, 0.0, 1.0)
 
-    def new_magnetic(old, new, s, p, t):
+    def magnetic(old, new, s, p, t):
         ex, ey, ez, hx, hy, hz = old[6 * s : 6 * s + 6]
         here, beside = slice(8 * t, 8 * t + 8), slice(8 * t + 1, 8 * t + 9)
         vx, vy, vz = ex[p, here, :], ey[p, here, :], ez[p, here, :]
@@ -305,59 +305,62 @@
         new[6 * s + 3][p, here, :] = nx
         new[6 * s + 4][p, here, :] = ny
         new[6 * s + 5][p, here, :] = nz
-        return vx, vy, vz, nx, ny, nz
-
-    def full_plane(old, new, p):
+
+    def electric(old, new, p, t):
         coarse = p // BLOCK_FACTOR
-        kerr, two = (coef[0], coef[4]), (coef[1], coef[5])
-        half_two, half_free = (coef[2], coef[6]), (coef[3], coef[7])
-        zero = jnp.zeros(tile, F32)
-        rolled = [[zero, zero], [zero, zero]]
+        here = slice(8 * t, 8 * t + 8)
+        volts = [[old[6 * s + c][p, here, :] for c in range(3)] for s in range(2)]
+        strength = [v[0] * v[0] + v[1] * v[1] + v[2] * v[2] for v in volts]
+        is_silicon = silicon[p, here, :]
+        total = (strength[0] + strength[1]) * is_silicon
+        carriers = charge[coarse, here, :] * is_silicon
+        ground = base[p, here, :]
+        gen[p, here, :] += (coef[1] * strength[0] + coef[5] * strength[1]) * total
+        mask = edge_mask(t)
+        for s in range(2):
+            vx, vy, vz = volts[s]
+            hx, hy, hz = new[6 * s + 3 : 6 * s + 6]
+            nx, ny, nz = hx[p, here, :], hy[p, here, :], hz[p, here, :]
+            if t == 0:
+                left_y = jnp.where(at_top, 0.0, pltpu.roll(ny, 1, 0))
+                left_z = jnp.where(at_top, 0.0, pltpu.roll(nz, 1, 0))
+            else:
+                before = slice(8 * t - 1, 8 * t + 7)
+                left_y, left_z = hy[p, before, :], hz[p, before, :]
+            loss = coef[4 * s + 2] * total + coef[4 * s + 3] * carriers
+            perm = ground + coef[4 * s] * total
+            inv = pl.reciprocal(perm + loss, approx=True)
+            keep = (perm - loss) * inv
+            push = COURANT * inv
+            if mask is not None:
+                push = push * mask
+            curl_x = (nz - down(nz)) - (ny - hy[p - 1, here, :])
+            curl_y = (nx - hx[p - 1, here, :]) - (nz - left_z)
+            curl_z = (ny - left_y) - (nx - down(nx))
+            new[6 * s][p, here, :] = keep * vx + push * curl_x
+            new[6 * s + 1][p, here, :] = keep * vy + push * curl_y
+            new[6 * s + 2][p, here, :] = keep * vz + push * curl_z
+
+    def magnetic_plane(old, new, p):
         for t in range(plan.tiles):
-            here = slice(8 * t, 8 * t + 8)
-            back = [[new[6 * s + c][p - 1, here, :] for c in (3, 4)] for s in range(2)]
-            vals = [new_magnetic(old, new, s, p, t) for s in range(2)]
-            strength = [v[0] * v[0] + v[1] * v[1] + v[2] * v[2] for v in vals]
-            is_silicon = silicon[p, here, :]
-            total = (strength[0] + strength[1]) * is_silicon
-            carriers = charge[coarse, here, :] * is_silicon
-            ground = base[p, here, :]
-            gen[p, here, :] += (two[0] * strength[0] + two[1] * strength[1]) * total
-            mask = edge_mask(t)
             for s in range(2):
-                vx, vy, vz, nx, ny, nz = vals[s]
-                loss = half_two[s] * total + half_free[s] * carriers
-                perm = ground + kerr[s] * total
-                divisor = perm + loss
-                inv = pl.reciprocal(divisor, approx=True)
-                inv = inv * (2.0 - divisor * inv)
-                keep = (perm - loss) * inv
-                push = COURANT * inv
-                if mask is not None:
-                    push = push * mask
-                turn_y, turn_z = pltpu.roll(ny, 1, 0), pltpu.roll(nz, 1, 0)
-                left_y = jnp.where(at_top, rolled[s][0], turn_y)
-                left_z = jnp.where(at_top, rolled[s][1], turn_z)
-                rolled[s] = [turn_y, turn_z]
-                curl_x = (nz - down(nz)) - (ny - back[s][1])
-                curl_y = (nx - back[s][0]) - (nz - left_z)
-                curl_z = (ny - left_y) - (nx - down(nx))
-                new[6 * s][p, here, :] = keep * vx + push * curl_x
-                new[6 * s + 1][p, here, :] = keep * vy + push * curl_y
-                new[6 * s + 2][p, here, :] = keep * vz + push * curl_z
+                magnetic(old, new, s, p, t)
 
     def substep(old, new, n):
+        begin = jnp.where(at_low, DEEP, n + 1)
+        end = jnp.where(at_high, DEEP + plan.own, plan.ext - 1 - n)
+
         @pl.when(jnp.logical_not(at_low))
         def _():
+            magnetic_plane(old, new, n)
+
+        magnetic_plane(old, new, begin)
+
+        def step(p, _):
             for t in range(plan.tiles):
+                electric(old, new, p, t)
                 for s in range(2):
-                    new_magnetic(old, new, s, n, t)
-
-        begin = jnp.where(at_low, DEEP, n + 1)
-        end = jnp.where(at_high, DEEP + plan.own, plan.ext - 1 - n)
-
-        def step(p, _):
-            full_plane(old, new, p)
+                    magnetic(old, new, s, p + 1, t)
             return 0
 
         lax.fori_loop(begin, end, step, 0)
@@ -392,9 +395,10 @@
 
 def sum_generation(plan, gen, message):
     blocks = plan.cols // BLOCK_FACTOR
-    lane = lax.broadcasted_iota(jnp.int32, (blocks, plan.lanes), 1)
+    shape = (blocks, plan.lanes)
+    column = lax.broadcasted_iota(jnp.int32, shape, 0) + blocks * lax.axis_index("gx")
+    upright = lax.broadcasted_iota(jnp.int32, shape, 1) == column
     across = plan.own_rows()
-    out = jnp.zeros((blocks, plan.lanes), F32)
     for a in range(plan.own // BLOCK_FACTOR):
         p = DEEP + BLOCK_FACTOR * a
         rows = (gen[p, across, :] + gen[p + 1, across, :]) + (
@@ -402,15 +406,16 @@
         )
         cells = rows.reshape(blocks, BLOCK_FACTOR, plan.lanes).sum(1)
         mean = cells.sum(1, keepdims=True) * (1.0 / (BLOCK_FACTOR * BLOCK_FACTOR * plan.lanes))
-        out = jnp.where(lane == a, mean, out)
-    message[...] = out
+        message[a : a + 1, :] = jnp.where(upright, mean, 0.0).sum(0, keepdims=True)
 
 
 def round_scratch(plan):
     wide = (plan.ext, plan.rows, plan.lanes)
-    return [pltpu.VMEM(wide, F32)] * 27 + [
+    return [pltpu.VMEM((plan.ext + 1, plan.rows, plan.lanes), F32)] * 24 + [
+        pltpu.VMEM(wide, F32)
+    ] * 3 + [
         pltpu.VMEM((plan.ext // BLOCK_FACTOR, plan.width, plan.lanes), F32),
-        pltpu.VMEM(generation_shape(plan)[1:], F32),
+        pltpu.VMEM((8, plan.lanes), F32),
         pltpu.VMEM((8, 8, plan.lanes), F32),
         pltpu.VMEM(wide, F32),
     ]
@@ -420,8 +425,8 @@
     return SUBSTEPS * plan.ext * plan.width * plan.lanes * 150
 
 
-def generation_shape(plan, rows=0):
-    return (plan.devices, plan.cols // BLOCK_FACTOR + rows, plan.lanes)
+def generation_shape(plan):
+    return (plan.devices, 8, plan.lanes)
 
 
 def place_strips(plan, old, code, strips):
@@ -443,7 +448,7 @@
 def send_generation(plan, copies, started, gen, message, gen_out):
     sum_generation(plan, gen, message)
     for d in range(plan.devices):
-        started.append(copies.start(message, gen_out.at[d, pl.ds(0, plan.cols // BLOCK_FACTOR)]))
+        started.append(copies.start(message, gen_out.at[d]))
 
 
 def charge_from_slabs(plan, charge, mine, across, chip, corner):
@@ -456,14 +461,17 @@
     body = jnp.where(k == 0, left, right)
     before = jnp.where(k == 0, beyond, left)[slab - 1 : slab]
     after = jnp.where(k == 0, right, beyond)[0:1]
-    skip = (plan.cols - 8) // BLOCK_FACTOR
     for a in range(slab + 2):
         row = before if a == 0 else after if a == slab + 1 else body[a - 1 : a]
-        row = jnp.broadcast_to(row, (8, plan.lanes))
-        row = jnp.where(x == 0, row, pltpu.roll(row, plan.lanes - skip, 1))
-        for c in range(plan.width // BLOCK_FACTOR):
-            value = jnp.broadcast_to(row[0:4, c : c + 1], (4, plan.lanes))
-            charge[a, 4 * c : 4 * c + 4, :] = value
+        spread_row(plan, row, charge, a)
+
+
+def spread_row(plan, row, charge, a):
+    left = (plan.cols * lax.axis_index("gx") - plan.first_row()) // BLOCK_FACTOR
+    row = jnp.broadcast_to(row, (8, plan.lanes))
+    row = pltpu.roll(row, lax.rem(plan.lanes - left, plan.lanes), 1)
+    for c in range(plan.width // BLOCK_FACTOR):
+        charge[a, 4 * c : 4 * c + 4, :] = jnp.broadcast_to(row[0:4, c : c + 1], (4, plan.lanes))
 
 
 def first_kernel(plan, *refs):
@@ -539,9 +547,7 @@
         late.append(copies.start(old[c].at[pl.ds(inward, DEEP), across], core_out.at[c]))
         late.append(copies.start(old[c].at[pl.ds(DEEP, plan.own), across], own_out.at[c]))
     late.append(copies.start(code, code_out))
-    slab_rows = pl.ds(plan.cols // BLOCK_FACTOR, 8)
-    for d in range(plan.devices):
-        late.append(copies.start(slabs.at[0], gen_out.at[d, slab_rows]))
+    message[4:8, :] = slabs[0, 0:4, :]
     each_side(plan, gather)
     send_strips(plan, copies, late, strip_mine, outs[5:])
     send_generation(plan, copies, late, gen, message, gen_out)
@@ -555,7 +561,7 @@
         (12, plan.own) + wide,
         (12, DEEP) + wide,
         (12, DEEP) + wide,
-        generation_shape(plan, 8),
+        generation_shape(plan),
         (plan.ext, plan.rows, plan.lanes),
     ] + strip_shapes(plan, 12)
     scratch = round_scratch(plan) + [pltpu.VMEM((plan.part,) + wide, jnp.int32)]
@@ -571,7 +577,7 @@
         shapes,
         [ANY] * (1 + 3 * nside) + [HBM] * 6 + [ANY] * 6 + [HBM, ANY, ANY, HBM],
         scratch,
-        40 + 3 * nside + 2 * plan.devices,
+        40 + 3 * nside + plan.devices,
         round_flops(plan),
         10_000_000,
     )(*strips, z_in, *raw, *other, medium, slab, under, coef)
@@ -615,6 +621,7 @@
     for c in range(6):
         target = kept[c].at[0, pl.ds(plan.own * k, plan.own)]
         late.append(copies.start(old[c].at[pl.ds(DEEP, plan.own), across], target))
+    message[...] = jnp.zeros(message.shape, F32)
     send_generation(plan, copies, late, gen, message, gen_out)
     wait(late)
 
@@ -658,52 +665,18 @@
     )(*halves, got)
 
 
-def under_cells(plan, grid, charge):
-    z, x, k = (lax.axis_index(a) for a in LINE)
-    for a in range(plan.ext // BLOCK_FACTOR):
-        top = (plan.planes * z + plan.own * k - DEEP) // BLOCK_FACTOR + a
-        top = 1 + jnp.clip(top, 0, plan.grid_rows - 1)
-        for c in range(plan.width // BLOCK_FACTOR):
-            left = (plan.cols * x - plan.first_row()) // BLOCK_FACTOR + c
-            left = 8 + jnp.clip(left, 0, plan.grid_cols - 1)
-            value = grid[top, pl.ds(left, 1), :]
-            charge[a, 4 * c : 4 * c + 4, :] = jnp.broadcast_to(value, (4, plan.lanes))
-
-
-def grid_shape(plan):
-    return (plan.grid_rows + 2, plan.grid_cols + 16, plan.lanes)
-
-
 def charge_shape(plan):
     return (plan.ext // BLOCK_FACTOR, plan.width, plan.lanes)
 
 
-def spread_kernel(plan, density, charge_out, grid, charge, sems):
-    copies = Copies(sems)
-    rows, cols, lanes = plan.grid_rows, plan.grid_cols, plan.lanes
-
-    def clean(i, _):
-        for c in range(0, cols + 16, 8):
-            grid[i, c : c + 8, :] = jnp.zeros((8, lanes), F32)
-        return 0
-
-    lax.fori_loop(0, rows + 2, clean, 0)
-
-    def read(i, _):
-        for c in range(cols):
-            value = density[i // plan.slab, i % plan.slab, c]
-            grid[i + 1, 8 + c : 9 + c, :] = jnp.full((1, lanes), value)
-        return 0
-
-    lax.fori_loop(0, rows, read, 0)
-    under_cells(plan, grid, charge)
-    copies.start(charge, charge_out).wait()
-
-
-def spread(plan, density):
-    scratch = [pltpu.VMEM(grid_shape(plan), F32), pltpu.VMEM(charge_shape(plan), F32)]
-    shapes = [charge_shape(plan)]
-    return call(plan, spread_kernel, "spread", shapes, [SMEM], scratch, 1, 10_000, 1_000_000)(density)
+def spread_whole(plan, density):
+    z, x, k = (lax.axis_index(a) for a in LINE)
+    side = plan.width // BLOCK_FACTOR
+    padded = jnp.pad(density, ((1, 1), (side, side)))
+    top = (plan.planes * z + plan.own * k) // BLOCK_FACTOR
+    left = side + (plan.cols * x - plan.first_row()) // BLOCK_FACTOR
+    tile = lax.dynamic_slice(padded, (top, left), (plan.ext // BLOCK_FACTOR, side))
+    return jnp.broadcast_to(jnp.repeat(tile, BLOCK_FACTOR, 1)[:, :, None], charge_shape(plan))
 
 
 def carrier_kernel(plan, last, *refs):
@@ -714,109 +687,77 @@
     gens, one, two, source, charge, slab_out, sems = refs[len(outs) :]
     copies = Copies(sems)
     rows, cols, lanes = plan.grid_rows, plan.grid_cols, plan.lanes
-    z, x = lax.axis_index("gz"), lax.axis_index("gx")
-    blocks, own = plan.cols // BLOCK_FACTOR, plan.own // BLOCK_FACTOR
+    z, x, k = (lax.axis_index(a) for a in LINE)
+    own = plan.own // BLOCK_FACTOR
     early = [copies.start(gens_in, gens)]
     if last:
         early.append(copies.start(density_in, one))
     zero = jnp.zeros((8, lanes), F32)
-    both = (two,) if last else (one, two)
-
-    def clean(i, _):
-        for ref in both:
-            ref[i, 0:8, :] = zero
-            ref[i, 8 + cols : 16 + cols, :] = zero
+    for ref in (two,) if last else (one, two):
+        ref[0:8, :] = zero
+        ref[8 + rows : 16 + rows, :] = zero
+    wait(early)
+
+    def unpack(line, _):
+        top = pl.multiple_of(8 * line, 8)
+        for dk in range(2):
+            tiles = [gens[(line * plan.gx + dx) * 2 + dk, 0:own, :] for dx in range(plan.gx)]
+            source[pl.ds(top + own * dk, own), :] = SOURCE_FACTOR * functools.reduce(jnp.add, tiles)
+        if not last:
+            for dx in range(plan.gx):
+                slab = gens[(line * plan.gx + dx) * 2, 4 : 4 + plan.slab, :]
+                one[pl.ds(8 + top + plan.slab * dx, plan.slab), :] = slab
         return 0
 
-    lax.fori_loop(0, rows + 2, clean, 0)
-    for ref in both:
-        for i in (0, rows + 1):
-            for c in range(8, 8 + cols, 8):
-                ref[i, c : c + 8, :] = zero
-    wait(early)
-    diagonal = lax.broadcasted_iota(jnp.int32, (cols, lanes), 0) == lax.broadcasted_iota(
-        jnp.int32, (cols, lanes), 1
-    )
-    if not last:
-
-        def turn(d, _):
-            for r in range(plan.slab):
-                row = jnp.broadcast_to(gens[2 * d, blocks + r : blocks + r + 1, :], (cols, lanes))
-                upright = jnp.where(diagonal, row, 0.0).sum(1, keepdims=True)
-                one[1 + d * plan.slab + r, 8 : 8 + cols, :] = jnp.broadcast_to(upright, (cols, lanes))
-            return 0
-
-        lax.fori_loop(0, plan.gz * plan.gx, turn, 0)
-
-    def unpack(line, _):
-        for dx in range(plan.gx):
-            for dk in range(2):
-                tile = gens[(line * plan.gx + dx) * 2 + dk, 0:blocks, :]
-                for a in range(own):
-                    source[(line * 2 + dk) * own + a, blocks * dx : blocks * dx + blocks, :] = (
-                        jnp.broadcast_to(SOURCE_FACTOR * tile[:, a : a + 1], (blocks, lanes))
-                    )
-        return 0
-
-    lax.fori_loop(0, plan.gz, unpack, 0)
-
-    def step(old, new):
-        def row(m, _):
-            for h in range(4):
-                i = 4 * m + h
-                for c in range(8, 8 + cols, 8):
-                    now, before = old[i + 1, c : c + 8, :], old[i, c : c + 8, :]
-                    around = (
-                        old[i + 2, c : c + 8, :]
-                        + before
-                        + old[i + 1, c + 1 : c + 9, :]
-                        + old[i + 1, c - 1 : c + 7, :]
-                        - 4.0 * now
-                    )
-                    new[i + 1, c : c + 8, :] = (
-                        now
-                        + SPREAD_COEFF * around
-                        - MOBILITY_TERM * (now - before)
-                        - LIFETIME_DECAY * now
-                        + source[i, c - 8 : c, :]
-                    )
-            return 0
-
-        lax.fori_loop(0, rows // 4, row, 0)
-
-    def pair(_, carry):
-        step(one, two)
-        step(two, one)
-        return carry
-
-    lax.fori_loop(0, CSTEPS // 2, pair, 0)
+    lax.fori_loop(0, plan.gz, unpack, 0, unroll=plan.gz <= 4)
+    inside = lax.broadcasted_iota(jnp.int32, (8, lanes), 1) < cols
+    for step in range(CSTEPS):
+        old, new = (one, two) if step % 2 == 0 else (two, one)
+        for r in range(8, 8 + rows, 8):
+            now, before = old[r : r + 8, :], old[r - 1 : r + 7, :]
+            around = (
+                old[r + 1 : r + 9, :]
+                + before
+                + pltpu.roll(now, lanes - 1, 1)
+                + pltpu.roll(now, 1, 1)
+                - 4.0 * now
+            )
+            later = (
+                now
+                + SPREAD_COEFF * around
+                - MOBILITY_TERM * (now - before)
+                - LIFETIME_DECAY * now
+                + source[r - 8 : r, :]
+            )
+            new[r : r + 8, :] = jnp.where(inside, later, 0.0)
     if last:
-        for r in range(plan.slab):
-            upright = one[1 + (z * plan.gx + x) * plan.slab + r, 8 : 8 + cols, :]
-            flat = jnp.where(diagonal, upright, 0.0).sum(0, keepdims=True)
-            slab_out[r : r + 1, :] = flat
+        mine = one[pl.ds(8 + (z * plan.gx + x) * plan.slab, plan.slab), :]
+        slab_out[...] = mine[:, :cols]
         copies.start(slab_out, outs[0]).wait()
         return
-    under_cells(plan, one, charge)
-    wait([copies.start(one, outs[0]), copies.start(charge, outs[1])])
+    late = [copies.start(one, outs[0])]
+    for a in range(plan.ext // BLOCK_FACTOR):
+        top = (plan.planes * z + plan.own * k - DEEP) // BLOCK_FACTOR + a
+        spread_row(plan, one[pl.ds(8 + jnp.clip(top, 0, rows - 1), 1), :], charge, a)
+    late.append(copies.start(charge, outs[1]))
+    wait(late)
 
 
 def carriers(plan, last, *arrays):
-    grid, lanes = grid_shape(plan), plan.lanes
-    shapes = [(8, lanes)] if last else [grid, charge_shape(plan)]
+    grid, slab = (plan.grid_rows + 16, plan.lanes), (plan.slab, plan.grid_cols)
     scratch = [
         pltpu.VMEM(arrays[0].shape, F32),
         pltpu.VMEM(grid, F32),
         pltpu.VMEM(grid, F32),
-        pltpu.VMEM((plan.grid_rows, plan.grid_cols, lanes), F32),
+        pltpu.VMEM((plan.grid_rows, plan.lanes), F32),
         pltpu.VMEM(charge_shape(plan), F32),
-        pltpu.VMEM((8, lanes), F32),
+        pltpu.VMEM(slab, F32),
     ]
     return call(
         plan,
         lambda plan, *refs: carrier_kernel(plan, last, *refs),
         "carriers",
-        shapes,
+        [slab] if last else [grid, charge_shape(plan)],
         [ANY] + [HBM] * (len(arrays) - 1),
         scratch,
         4,
@@ -857,7 +798,7 @@
     if not plan.paired:
         tiles = plan.gz * plan.gx
         slabs = everywhere(jnp.broadcast_to(density, (tiles,) + density.shape), ("gz", "gx"))
-        (under,) = spread(plan, slabs)
+        under = spread_whole(plan, slabs.reshape(plan.grid_rows, plan.grid_cols))
     outs = first_round(plan, strips, z_in, raw, other, medium, slab, under, coef)
     own, z_msg, core_msg, gens, code = outs[:5]
     gens = everywhere(gens, LINE)
@@ -869,7 +810,6 @@
     gens = everywhere(gens, LINE)
     got = send(sent, core)
     (new_slab,) = carriers(plan, True, gens, grid)
-    new_slab = new_slab[: plan.slab, : plan.grid_cols]
     return tuple(join(plan, halves, got)) + (new_slab,)
 
 

time: 111 us -> 99.1 us (0.89)
  Pallas kernels: 46.3 us -> 37.2 us
  local copies, waits for them, and re-layouts: 2.62 us -> 1.36 us
    pallas_call x6, Pallas kernels: 46.3 us -> 37.2 us  [run(): return kernel(*placed)]
    slice x1 -> x0, local copies, waits for them, and re-layouts: 1.25 us -> none  [local(): new_slab = new_slab[:plan.slab, :plan.grid_cols]]
  transfers between devices with their start and end apart: 17 -> 17, of which waited for: 7 -> 7; matrix products, arithmetic and copies ran while one was open for 2% -> 1% of each run, Pallas kernels for 7% -> 4%
where the time goes in v5:
time: 99.1 us; the launch traced here: 98.6 us
  Pallas kernels  37.2 us (38%)
  starting transfers between devices  24.9 us (25%)
  waiting for transfers between devices  21.8 us (22%)
  blocking collectives  12.6 us (13%)
  local copies, waits for them, and re-layouts  1.36 us (1%)
    pallas_call x6, Pallas kernels, run(): return kernel(*placed)  37.2 us
    ppermute x16, starting transfers between devices, send(): return lax.ppermute(message, LINE, line_pairs(plan, target))  21.4 us
    ppermute x16, waiting for transfers between devices, send(): return lax.ppermute(message, LINE, line_pairs(plan, target))  15.3 us
    all_to_all x1, blocking collectives, everywhere(): lax.all_to_all(message, axes, split_axis=0, concat_axis=0, tiled=True)  12.6 us
    all_to_all x1, waiting for transfers between devices, everywhere(): lax.all_to_all(message, axes, split_axis=0, concat_axis=0, tiled=True)  6.48 us
    all_to_all x1, starting transfers between devices, everywhere(): lax.all_to_all(message, axes, split_axis=0, concat_axis=0, tiled=True)  3.5 us
  transfers between devices with their start and end apart: 17, of which 7 were waited for; matrix products, arithmetic and copies ran while one was open for 1% of the time, Pallas kernels for 4%

profile of v5, /device:TPU:0, one launch (start us, length us, event | category | flops | bytes accessed | tf_op | source)
XLA Modules:
  0.0 98.6 jit_solution(10672508947744841600)
XLA Ops:
  0.6 0.5 collective-permute-start
  1.2 0.4 collective-permute-start.2
  1.7 0.1 collective-permute-start.3
  1.7 0.4 collective-permute-start.4
  2.2 0.7 collective-permute-done.refs_6_.refs_10_
  2.9 0.4 collective-permute-start.5
  3.3 0.7 pad.4.refs_13_.refs_17_.refs_18_
  4.0 0.4 collective-permute-done.2.refs_8_.refs_12_
  4.4 0.7 collective-permute-done.3.refs_9_.refs_13_
  5.1 0.7 collective-permute-done.4.refs_10_.refs_14_
  5.9 0.7 collective-permute-done.5.refs_11_.refs_15_
  6.6 0.7 copy-done
  7.3 3.3 %pack.1 = (f32[14,4,32,128]{3,2,1,0:T(8,128)}, f32[14,8,8,128]{3,2,1,0:T(8,128)}, f32[14,2,8,128]{3,2,1,0:T(8,128)}, f32[14,2,8,128]{3,2,1,0:T(8,128)}, f32[8,8,128]{2,1,0:T(8,128)}) custom-call(f32[1,32,32,128]{3,2,1,0:T(8,128)} %refs_4_.3, f32[1,32,32,128]{3,2,1,0:T(8,128)} %refs_5_.3, f32[1,32,32,128]{3,2,1,0:T(8,128)} %refs_6_.1, ...), custom_call_target="tpu_custom_call" | custom-call | bytes 4000000 | tf_op jit(solution)/shard_map/pack/pallas_call | solution.py:123
  10.6 0.7 collective-permute-start.9
  11.4 2.9 %collective-permute-start.6 = (f32[14,8,8,128]{3,2,1,0:T(8,128)}, f32[14,8,8,128]{3,2,1,0:T(8,128)S(1)}, u32[]{:S(2)}, u32[]{:S(2)}) collective-permute-start(f32[14,8,8,128]{3,2,1,0:T(8,128)} %get-tuple-element.36), channel_id=1, source_target_pairs={{0,2},{1,3},{2,0},{3,1},{4,6},{5,7},{6,4},{7,5},{8,10},{9,11},{10,... | collective-permute-start | bytes 1376264 | tf_op jit(solution)/shard_map/ppermute | solution.py:774
  14.3 2.7 %collective-permute-start.7 = (f32[14,2,8,128]{3,2,1,0:T(8,128)}, f32[14,2,8,128]{3,2,1,0:T(8,128)S(1)}, u32[]{:S(2)}, u32[]{:S(2)}) collective-permute-start(f32[14,2,8,128]{3,2,1,0:T(8,128)} %get-tuple-element.37), channel_id=1, source_target_pairs={{0,3},{1,2},{2,1},{3,0},{4,7},{5,6},{6,5},{7,4},{8,11},{9,10},{10,... | collective-permute-start | bytes 344072 | tf_op jit(solution)/shard_map/ppermute | solution.py:774
  17.0 0.7 collective-permute-start.8
  17.7 11.9 %collective-permute-done.7.refs_1_ = f32[14,2,8,128]{3,2,1,0:T(8,128)S(1)} collective-permute-done((f32[14,2,8,128]{3,2,1,0:T(8,128)}, f32[14,2,8,128]{3,2,1,0:T(8,128)S(1)}, u32[]{:S(2)}, u32[]{:S(2)}) %collective-permute-start.7) | collective-permute-done | bytes 114720 | tf_op jit(solution)/shard_map/ppermute | solution.py:774
  29.6 14.8 %first_round.1 = (f32[12,16,32,128]{3,2,1,0:T(8,128)}, f32[12,4,32,128]{3,2,1,0:T(8,128)}, f32[12,4,32,128]{3,2,1,0:T(8,128)}, f32[16,8,128]{2,1,0:T(8,128)}, f3...) custom-call(f32[14,8,8,128]{3,2,1,0:T(8,128)S(1)} %collective-permute-d, ...), custom_call_target="tpu_custom_call" | custom-call | flops 73728000 | bytes 10000000 | tf_op jit(solution)/shard_map/first_round/pallas_call | solution.py:123
  44.3 0.7 collective-permute-start.13
  45.1 7.0 %collective-permute-start.14 = (f32[12,4,32,128]{3,2,1,0:T(8,128)}, f32[12,4,32,128]{3,2,1,0:T(8,128)S(1)}, u32[]{:S(2)}, u32[]{:S(2)}) collective-permute-start(f32[12,4,32,128]{3,2,1,0:T(8,128)} %get-tuple-element.45), channel_id=1, source_target_pairs={{0,1},{1,0},{2,3},{3,2},{4,5},{5,4},{6,7},{7,6},{8,9},{9,8},{10,11... | collective-permute-start | bytes 2359304 | tf_op jit(solution)/shard_map/ppermute | solution.py:774
  52.1 1.7 %collective-permute-start.10 = (f32[12,8,8,128]{3,2,1,0:T(8,128)}, f32[12,8,8,128]{3,2,1,0:T(8,128)S(1)}, u32[]{:S(2)}, u32[]{:S(2)}) collective-permute-start(f32[12,8,8,128]{3,2,1,0:T(8,128)} %get-tuple-element.41), channel_id=1, source_target_pairs={{0,2},{1,3},{2,0},{3,1},{4,6},{5,7},{6,4},{7,5},{8,10},{9,11},{10,... | collective-permute-start | bytes 1179656 | tf_op jit(solution)/shard_map/ppermute | solution.py:774
  53.8 3.5 %all-to-all-start = ((f32[16,8,128]{2,1,0:T(8,128)}), f32[16,8,128]{2,1,0:T(8,128)S(1)}, u32[]{:S(2)}, u32[]{:S(2)}) async-start(f32[16,8,128]{2,1,0:T(8,128)} %get-tuple-element.48), calls=%async_computation | async-start | bytes 131072 | tf_op jit(solution)/shard_map/all_to_all | solution.py:777
  57.3 1.6 %collective-permute-start.11 = (f32[12,2,8,128]{3,2,1,0:T(8,128)}, f32[12,2,8,128]{3,2,1,0:T(8,128)S(1)}, u32[]{:S(2)}, u32[]{:S(2)}) collective-permute-start(f32[12,2,8,128]{3,2,1,0:T(8,128)} %get-tuple-element.42), channel_id=1, source_target_pairs={{0,3},{1,2},{2,1},{3,0},{4,7},{5,6},{6,5},{7,4},{8,11},{9,10},{10,... | collective-permute-start | bytes 294920 | tf_op jit(solution)/shard_map/ppermute | solution.py:774
  58.8 0.7 collective-permute-start.12
  59.5 6.5 %all-to-all-done.refs_0_ = f32[16,8,128]{2,1,0:T(8,128)S(1)} async-done(((f32[16,8,128]{2,1,0:T(8,128)}), f32[16,8,128]{2,1,0:T(8,128)S(1)}, u32[]{:S(2)}, u32[]{:S(2)}) %all-to-all-start) | async-done | bytes 65568 | tf_op jit(solution)/shard_map/all_to_all | solution.py:777
  66.0 1.6 %carriers.2 = (f32[48,128]{1,0:T(8,128)}, f32[6,40,128]{2,1,0:T(8,128)}) custom-call(f32[16,8,128]{2,1,0:T(8,128)S(1)} %all-to-all-done.refs_0_), custom_call_target="tpu_custom_call" | custom-call | flops 2000000 | bytes 1000000 | tf_op jit(solution)/shard_map/carriers/pallas_call | solution.py:123
  67.7 14.1 %second_round.1 = (f32[1,32,32,128]{3,2,1,0:T(8,128)}, f32[1,32,32,128]{3,2,1,0:T(8,128)}, f32[1,32,32,128]{3,2,1,0:T(8,128)}, f32[1,32,32,128]{3,2,1,0:T(8,128)...) custom-call(f32[12,8,8,128]{3,2,1,0:T(8,128)S(1)} %collective-permut, ...), custom_call_target="tpu_custom_call" | custom-call | flops 73728000 | bytes 10000000 | tf_op jit(solution)/shard_map/second_round/pallas_call | solution.py:123
  81.8 0.8 collective-permute-start.15
  82.5 12.6 %all_to_all.10.refs_0_ = f32[16,8,128]{2,1,0:T(8,128)S(1)} all-to-all(f32[16,8,128]{2,1,0:T(8,128)} %get-tuple-element.63), channel_id=1, replica_groups=mesh['group'=2,'gz'=4,'gx'=2,'af'=2] {'gz','gx','af'}, dimensions={0} | all-to-all | bytes 131072 | tf_op jit(solution)/shard_map/all_to_all | solution.py:777
  95.2 2.1 %carriers.3 = f32[4,16]{1,0:T(4,128)} custom-call(f32[16,8,128]{2,1,0:T(8,128)S(1)} %all_to_all.10.refs_0_, f32[48,128]{1,0:T(8,128)} %get-tuple-element.64.refs_1_), custom_call_target="tpu_custom_call" | custom-call | flops 2000000 | bytes 1000000 | tf_op jit(solution)/shard_map/carriers/pallas_call | solution.py:123
  97.2 1.4 %join.1 = (f32[1,32,32,128]{3,2,1,0:T(8,128)}, f32[1,32,32,128]{3,2,1,0:T(8,128)}, f32[1,32,32,128]{3,2,1,0:T(8,128)}, f32[1,32,32,128]{3,2,1,0:T(8,128)}, f32[1...) custom-call(f32[1,32,32,128]{3,2,1,0:T(8,128)} %get-tuple-element.50, ...), custom_call_target="tpu_custom_call", output_to_operand_aliasing={{0}: (0, {}), {1}: (1, {}), {2}: (2, {}), {3}: (3, {}), {4}... | custom-call | bytes 3000000 | tf_op jit(solution)/shard_map/join/pallas_call | solution.py:123
  (12 shorter events, 0.1 us)
Async XLA Ops:
  0.6 2.3 %collective-permute-start = (f32[1,32,32,128]{3,2,1,0:T(8,128)}, f32[1,32,32,128]{3,2,1,0:T(8,128)S(1)}, u32[]{:S(2)}, u32[]{:S(2)}) collective-permute-start(f32[1,32,32,128]{3,2,1,0:T(8,128)} %refs_4_.3), channel_id=1, source_target_pairs={{0,1},{1,0},{2,3},{3,2},{4,5},{5,4},{6,7},{7,6},{8,9},{9,8},{10,11... | collective-permute-start | bytes 1572872 | tf_op jit(solution)/shard_map/ppermute | solution.py:774
  1.1 2.8 %collective-permute-start.1 = (f32[1,32,32,128]{3,2,1,0:T(8,128)}, f32[1,32,32,128]{3,2,1,0:T(8,128)S(1)}, u32[]{:S(2)}, u32[]{:S(2)}) collective-permute-start(f32[1,32,32,128]{3,2,1,0:T(8,128)} %refs_5_.3), channel_id=1, source_target_pairs={{0,1},{1,0},{2,3},{3,2},{4,5},{5,4},{6,7},{7,6},{8,9},{9,8},{10,11... | collective-permute-start | bytes 1572872 | tf_op jit(solution)/shard_map/ppermute | solution.py:774
  1.2 3.2 %collective-permute-start.2 = (f32[1,32,32,128]{3,2,1,0:T(8,128)}, f32[1,32,32,128]{3,2,1,0:T(8,128)S(1)}, u32[]{:S(2)}, u32[]{:S(2)}) collective-permute-start(f32[1,32,32,128]{3,2,1,0:T(8,128)} %refs_6_.1), channel_id=1, source_target_pairs={{0,1},{1,0},{2,3},{3,2},{4,5},{5,4},{6,7},{7,6},{8,9},{9,8},{10,11... | collective-permute-start | bytes 1572872 | tf_op jit(solution)/shard_map/ppermute | solution.py:774
  1.7 3.5 %collective-permute-start.3 = (f32[1,32,32,128]{3,2,1,0:T(8,128)}, f32[1,32,32,128]{3,2,1,0:T(8,128)S(1)}, u32[]{:S(2)}, u32[]{:S(2)}) collective-permute-start(f32[1,32,32,128]{3,2,1,0:T(8,128)} %refs_7_.1), channel_id=1, source_target_pairs={{0,1},{1,0},{2,3},{3,2},{4,5},{5,4},{6,7},{7,6},{8,9},{9,8},{10,11... | collective-permute-start | bytes 1572872 | tf_op jit(solution)/shard_map/ppermute | solution.py:774
  1.7 4.2 %collective-permute-start.4 = (f32[1,32,32,128]{3,2,1,0:T(8,128)}, f32[1,32,32,128]{3,2,1,0:T(8,128)S(1)}, u32[]{:S(2)}, u32[]{:S(2)}) collective-permute-start(f32[1,32,32,128]{3,2,1,0:T(8,128)} %refs_8_.1), channel_id=1, source_target_pairs={{0,1},{1,0},{2,3},{3,2},{4,5},{5,4},{6,7},{7,6},{8,9},{9,8},{10,11... | collective-permute-start | bytes 1572872 | tf_op jit(solution)/shard_map/ppermute | solution.py:774
  2.9 3.7 %collective-permute-start.5 = (f32[1,32,32,128]{3,2,1,0:T(8,128)}, f32[1,32,32,128]{3,2,1,0:T(8,128)S(1)}, u32[]{:S(2)}, u32[]{:S(2)}) collective-permute-start(f32[1,32,32,128]{3,2,1,0:T(8,128)} %refs_9_.1), channel_id=1, source_target_pairs={{0,1},{1,0},{2,3},{3,2},{4,5},{5,4},{6,7},{7,6},{8,9},{9,8},{10,11... | collective-permute-start | bytes 1572872 | tf_op jit(solution)/shard_map/ppermute | solution.py:774
  6.6 0.7 copy-start
  10.6 18.9 %collective-permute-start.9 = (f32[14,4,32,128]{3,2,1,0:T(8,128)}, f32[14,4,32,128]{3,2,1,0:T(8,128)S(1)}, u32[]{:S(2)}, u32[]{:S(2)}) collective-permute-start(f32[14,4,32,128]{3,2,1,0:T(8,128)} %get-tuple-element.39), channel_id=1, source_target_pairs={{1,4},{3,6},{4,1},{5,8},{6,3},{7,10},{8,5},{9,12},{10,7},{11,14},{... | collective-permute-start | bytes 2752520 | tf_op jit(solution)/shard_map/ppermute | solution.py:774
  11.4 18.2 %collective-permute-start.6 = (f32[14,8,8,128]{3,2,1,0:T(8,128)}, f32[14,8,8,128]{3,2,1,0:T(8,128)S(1)}, u32[]{:S(2)}, u32[]{:S(2)}) collective-permute-start(f32[14,8,8,128]{3,2,1,0:T(8,128)} %get-tuple-element.36), channel_id=1, source_target_pairs={{0,2},{1,3},{2,0},{3,1},{4,6},{5,7},{6,4},{7,5},{8,10},{9,11},{10,... | collective-permute-start | bytes 1376264 | tf_op jit(solution)/shard_map/ppermute | solution.py:774
  14.3 15.3 %collective-permute-start.7 = (f32[14,2,8,128]{3,2,1,0:T(8,128)}, f32[14,2,8,128]{3,2,1,0:T(8,128)S(1)}, u32[]{:S(2)}, u32[]{:S(2)}) collective-permute-start(f32[14,2,8,128]{3,2,1,0:T(8,128)} %get-tuple-element.37), channel_id=1, source_target_pairs={{0,3},{1,2},{2,1},{3,0},{4,7},{5,6},{6,5},{7,4},{8,11},{9,10},{10,... | collective-permute-start | bytes 344072 | tf_op jit(solution)/shard_map/ppermute | solution.py:774
  17.0 12.5 %collective-permute-start.8 = (f32[14,2,8,128]{3,2,1,0:T(8,128)}, f32[14,2,8,128]{3,2,1,0:T(8,128)S(1)}, u32[]{:S(2)}, u32[]{:S(2)}) collective-permute-start(f32[14,2,8,128]{3,2,1,0:T(8,128)} %get-tuple-element.38), channel_id=1, source_target_pairs={{1,6},{3,4},{4,3},{5,10},{6,1},{7,8},{8,7},{9,14},{10,5},{11,12},{... | collective-permute-start | bytes 344072 | tf_op jit(solution)/shard_map/ppermute | solution.py:774
  44.3 23.3 %collective-permute-start.13 = (f32[12,4,32,128]{3,2,1,0:T(8,128)}, f32[12,4,32,128]{3,2,1,0:T(8,128)S(1)}, u32[]{:S(2)}, u32[]{:S(2)}) collective-permute-start(f32[12,4,32,128]{3,2,1,0:T(8,128)} %get-tuple-element.44), channel_id=1, source_target_pairs={{1,4},{3,6},{4,1},{5,8},{6,3},{7,10},{8,5},{9,12},{10,7},{11,14},{... | collective-permute-start | bytes 2359304 | tf_op jit(solution)/shard_map/ppermute | solution.py:774
  45.1 22.6 %collective-permute-start.14 = (f32[12,4,32,128]{3,2,1,0:T(8,128)}, f32[12,4,32,128]{3,2,1,0:T(8,128)S(1)}, u32[]{:S(2)}, u32[]{:S(2)}) collective-permute-start(f32[12,4,32,128]{3,2,1,0:T(8,128)} %get-tuple-element.45), channel_id=1, source_target_pairs={{0,1},{1,0},{2,3},{3,2},{4,5},{5,4},{6,7},{7,6},{8,9},{9,8},{10,11... | collective-permute-start | bytes 2359304 | tf_op jit(solution)/shard_map/ppermute | solution.py:774
  52.1 15.6 %collective-permute-start.10 = (f32[12,8,8,128]{3,2,1,0:T(8,128)}, f32[12,8,8,128]{3,2,1,0:T(8,128)S(1)}, u32[]{:S(2)}, u32[]{:S(2)}) collective-permute-start(f32[12,8,8,128]{3,2,1,0:T(8,128)} %get-tuple-element.41), channel_id=1, source_target_pairs={{0,2},{1,3},{2,0},{3,1},{4,6},{5,7},{6,4},{7,5},{8,10},{9,11},{10,... | collective-permute-start | bytes 1179656 | tf_op jit(solution)/shard_map/ppermute | solution.py:774
  53.8 12.2 %all-to-all-start = ((f32[16,8,128]{2,1,0:T(8,128)}), f32[16,8,128]{2,1,0:T(8,128)S(1)}, u32[]{:S(2)}, u32[]{:S(2)}) async-start(f32[16,8,128]{2,1,0:T(8,128)} %get-tuple-element.48), calls=%async_computation | async-start | bytes 131072 | tf_op jit(solution)/shard_map/all_to_all | solution.py:777
  57.3 10.4 %collective-permute-start.11 = (f32[12,2,8,128]{3,2,1,0:T(8,128)}, f32[12,2,8,128]{3,2,1,0:T(8,128)S(1)}, u32[]{:S(2)}, u32[]{:S(2)}) collective-permute-start(f32[12,2,8,128]{3,2,1,0:T(8,128)} %get-tuple-element.42), channel_id=1, source_target_pairs={{0,3},{1,2},{2,1},{3,0},{4,7},{5,6},{6,5},{7,4},{8,11},{9,10},{10,... | collective-permute-start | bytes 294920 | tf_op jit(solution)/shard_map/ppermute | solution.py:774
  58.8 8.8 %collective-permute-start.12 = (f32[12,2,8,128]{3,2,1,0:T(8,128)}, f32[12,2,8,128]{3,2,1,0:T(8,128)S(1)}, u32[]{:S(2)}, u32[]{:S(2)}) collective-permute-start(f32[12,2,8,128]{3,2,1,0:T(8,128)} %get-tuple-element.43), channel_id=1, source_target_pairs={{1,6},{3,4},{4,3},{5,10},{6,1},{7,8},{8,7},{9,14},{10,5},{11,12},{... | collective-permute-start | bytes 294920 | tf_op jit(solution)/shard_map/ppermute | solution.py:774
  81.8 15.5 %collective-permute-start.15 = (f32[6,16,32,128]{3,2,1,0:T(8,128)}, f32[6,16,32,128]{3,2,1,0:T(8,128)S(1)}, u32[]{:S(2)}, u32[]{:S(2)}) collective-permute-start(f32[6,16,32,128]{3,2,1,0:T(8,128)} %get-tuple-element.56), channel_id=1, source_target_pairs={{0,1},{1,0},{2,3},{3,2},{4,5},{5,4},{6,7},{7,6},{8,9},{9,8},{10,11... | collective-permute-start | bytes 4718600 | tf_op jit(solution)/shard_map/ppermute | solution.py:774

commit v6 on v5

--- a/solution.py
+++ b/solution.py
@@ -127,9 +127,9 @@
 
 def pack_kernel(plan, *refs):
     raw, other, medium, nside = refs[:6], refs[6:12], refs[12], len(plan.sides)
-    slab_in, table = refs[13:15]
-    outs = refs[15 : 17 + 3 * nside]
-    edge, edge_code, face, face_code, strips, slab, coef, sems = refs[17 + 3 * nside :]
+    slab_in, table_in = refs[13:15]
+    outs = refs[15 : 18 + 3 * nside]
+    edge, edge_code, face, face_code, strips, corners, slab, table, coef, sems = refs[18 + 3 * nside :]
     copies = Copies(sems)
     k = lax.axis_index("af")
     mine = pl.ds(plan.own * k, plan.own)
@@ -139,6 +139,8 @@
     else:
         tile_rows = [plan.cols - 8, 0]
     early, late, last = [], [], []
+    early.append(copies.start(slab_in, slab))
+    early.append(copies.start(table_in, table))
     for n, row in enumerate(tile_rows):
         for c in range(6):
             side = pl.ds(row, 8)
@@ -146,82 +148,128 @@
             early.append(copies.start(other[c].at[0, mine, side, :], edge.at[n, 6 + c]))
         early.append(copies.start(medium.at[mine, pl.ds(row, 8), :], edge_code.at[n]))
     for c in range(6):
-        late.append(copies.start(raw[c].at[0, outer], face.at[c]))
-        late.append(copies.start(other[c].at[0, outer], face.at[6 + c]))
+        late.append(copies.start(raw[c].at[0, outer], face.at[pl.ds(DEEP * c, DEEP)]))
+        late.append(copies.start(other[c].at[0, outer], face.at[pl.ds(DEEP * (6 + c), DEEP)]))
     late.append(copies.start(medium.at[outer], face_code))
-    early.append(copies.start(slab_in, slab))
-    for s in range(2):
-        which = k if s == 0 else 1 - k
-        kerr, two, free = table[which, 0], table[which, 1], table[which, 2]
-        for n, value in enumerate((kerr, two, 0.5 * two, 0.5 * free)):
-            coef[4 * s + n] = jnp.full((8, plan.lanes), value)
-    last.append(copies.start(coef, outs[-1]))
     wait(early)
-    page = slab[...]
-    face[13] = jnp.broadcast_to(page[None, 0:1], (DEEP, plan.cols, plan.lanes))
-    face[13, 0, 0:8, :] = page
-    for n in range(nside):
-        for q in range(plan.own // 2):
-            strips[n, 13, q] = page
+    rows = plan.own // 2
 
     def fill(slot, low):
-        def rows(q, _):
+        def one(q, _):
             for h in range(2):
                 half = slice(4 * h, 4 * h + 4)
                 for c in range(12):
-                    strips[slot, c, q, half, :] = edge[slot, c, 2 * q + h, low : low + 4, :]
+                    strips[slot, c * rows + q, half, :] = edge[slot, c, 2 * q + h, low : low + 4, :]
                 code = edge_code[slot, 2 * q + h, low : low + 4, :]
-                strips[slot, 12, q, half, :] = code.astype(F32)
+                strips[slot, 12 * rows + q, half, :] = code.astype(F32)
             return 0
 
-        lax.fori_loop(0, plan.own // 2, rows, 0)
+        lax.fori_loop(0, rows, one, 0)
 
     each_side(plan, lambda slot, side: fill(slot, 4 if plan.paired == (side == "high") else 0))
-    send_strips(plan, copies, last, strips, outs[1:-1])
+    page = slab[...]
+    for n in range(nside):
+        for extra in range(13 * rows, strip_tiles(plan, 13)):
+            strips[n, extra] = page
+        corners[n, 0, 13 * DEEP // 2] = page
+        corners[n, 1, 13 * DEEP // 2] = page
+    send_strips(plan, copies, last, strips, corners, outs[2:-1], 13)
+    own, partner = jnp.where(k == 0, table[0:1], table[1:2]), jnp.where(k == 0, table[1:2], table[0:1])
+    for s, row in enumerate((own, partner)):
+        kerr, two, free = row[:, 0:1], row[:, 1:2], row[:, 2:3]
+        for n, value in enumerate((kerr, two, 0.5 * two, 0.5 * free)):
+            coef[4 * s + n] = jnp.broadcast_to(value, (8, plan.lanes))
+    last.append(copies.start(coef, outs[-1]))
     wait(late)
-    face[12] = face_code[...].astype(F32)
-    last.append(copies.start(face, outs[0]))
+    face[12 * DEEP : 13 * DEEP] = face_code[...].astype(F32)
+    face[13 * DEEP, 0:8, :] = page
+    for r in range(8, plan.cols, 8):
+        face[13 * DEEP, r : r + 8, :] = page
+    send_face(plan, copies, last, face, outs[:2])
     wait(last)
 
 
-def send_strips(plan, copies, started, strips, outs):
+def face_split(plan, pages):
+    if pages == 12 * DEEP:
+        return ((0, pages),)
+    first = (pages + 1) // 2
+    return ((0, first), (first, pages - first))
+
+
+def send_face(plan, copies, started, face, outs):
+    for out, (start, count) in zip(outs, face_split(plan, face.shape[0])):
+        started.append(copies.start(face.at[pl.ds(start, count)], out))
+
+
+def get_face(plan, copies, parts, pages, first, targets):
+    started = []
+    for part, (start, count) in zip(parts, face_split(plan, pages)):
+        low, high = max(first, start), min(first + DEEP, start + count)
+        if low < high:
+            source = part.at[pl.ds(low - start, high - low)]
+            started.append(copies.start(source, targets(low - first, high - low)))
+    return started
+
+
+def strip_tiles(plan, comps):
+    pages = DEEP * comps + (comps > 12)
+    if comps == 12:
+        return comps * plan.own // 2
+    return max(comps * plan.own // 2, (pages + 1) // 2 * (plan.cols // 8)) + 1
+
+
+def send_strips(plan, copies, started, strips, corners, outs, comps):
     k = lax.axis_index("af")
     half, top = DEEP // 2, (plan.own - DEEP) // 2
     for n in range(len(plan.sides)):
-        whole, inner, corner = outs[3 * n : 3 * n + 3]
-        started.append(copies.start(strips.at[n], whole))
-        started.append(copies.start(strips.at[n, :, pl.ds(top * (1 - k), half)], inner))
-        started.append(copies.start(strips.at[n, :, pl.ds(top * k, half)], corner))
+        started.append(copies.start(strips.at[n], outs[3 * n]))
+        for e, begin in enumerate((top * (1 - k), top * k)):
+            for c in range(comps):
+                for h in range(half):
+                    corners[n, e, half * c + h] = strips[n, plan.own // 2 * c + begin + h]
+            started.append(copies.start(corners.at[n, e], outs[3 * n + 1 + e]))
+
+
+def corner_tiles(plan, comps):
+    return comps * DEEP // 2 + (comps > 12)
 
 
 def strip_shapes(plan, comps):
     shapes = []
     for _ in plan.sides:
-        for rows in (plan.own, DEEP, DEEP):
-            shapes.append((comps, rows // 2, 8, plan.lanes))
+        tiles = corner_tiles(plan, comps)
+        for tiles in (strip_tiles(plan, comps), tiles, tiles):
+            shapes.append((tiles, 8, plan.lanes))
     return shapes
+
+
+def face_shapes(plan, pages):
+    return [(count, plan.cols, plan.lanes) for _, count in face_split(plan, pages)]
 
 
 def pack(plan, raw, other, medium, slab, table):
     wide = (plan.cols, plan.lanes)
     nside = len(plan.sides)
+    pages = 13 * DEEP + 1
     scratch = [
         pltpu.VMEM((nside, 12, plan.own, 8, plan.lanes), F32),
         pltpu.VMEM((nside, plan.own, 8, plan.lanes), jnp.int32),
-        pltpu.VMEM((14, DEEP) + wide, F32),
+        pltpu.VMEM((pages,) + wide, F32),
         pltpu.VMEM((DEEP,) + wide, jnp.int32),
-        pltpu.VMEM((nside, 14, plan.own // 2, 8, plan.lanes), F32),
+        pltpu.VMEM((nside, strip_tiles(plan, 13), 8, plan.lanes), F32),
+        pltpu.VMEM((nside, 2, corner_tiles(plan, 13), 8, plan.lanes), F32),
         pltpu.VMEM((8, plan.lanes), F32),
+        pltpu.VMEM(table.shape, F32),
         pltpu.VMEM((8, 8, plan.lanes), F32),
     ]
     return call(
         plan,
         pack_kernel,
         "pack",
-        [(14, DEEP) + wide] + strip_shapes(plan, 14) + [(8, 8, plan.lanes)],
-        [HBM] * 6 + [ANY] * 6 + [HBM, ANY, SMEM],
+        face_shapes(plan, pages) + strip_shapes(plan, 13) + [(8, 8, plan.lanes)],
+        [HBM] * 6 + [ANY] * 6 + [HBM, ANY, ANY],
         scratch,
-        16 * nside + 16,
+        16 * nside + 18,
         moved=4_000_000,
     )(*raw, *other, medium, slab, table)
 
@@ -260,11 +308,12 @@
     return plan.cols if plan.paired else 8 + plan.cols
 
 
-def spread_strip(refs, strip, at, plane, pairs):
+def spread_strip(refs, strip, each, begin, at, plane, pairs):
     def one(q, _):
         for c, ref in refs:
             for h in range(2):
-                ref[plane + 2 * q + h, at : at + 4, :] = strip[c, q, 4 * h : 4 * h + 4, :]
+                tile = c * each + begin + q
+                ref[plane + 2 * q + h, at : at + 4, :] = strip[tile, 4 * h : 4 * h + 4, :]
         return 0
 
     lax.fori_loop(0, pairs, one, 0)
@@ -349,21 +398,34 @@
     def substep(old, new, n):
         begin = jnp.where(at_low, DEEP, n + 1)
         end = jnp.where(at_high, DEEP + plan.own, plan.ext - 1 - n)
+        odd = lax.rem(end - begin, 2)
 
         @pl.when(jnp.logical_not(at_low))
         def _():
             magnetic_plane(old, new, n)
-
-        magnetic_plane(old, new, begin)
-
-        def step(p, _):
+            magnetic_plane(old, new, n + 1)
+
+        @pl.when(at_low)
+        def _():
+            magnetic_plane(old, new, DEEP)
+
+        def advance(p):
             for t in range(plan.tiles):
                 electric(old, new, p, t)
                 for s in range(2):
                     magnetic(old, new, s, p + 1, t)
+
+        @pl.when(odd == 1)
+        def _():
+            advance(begin)
+
+        def step(m, _):
+            p = begin + odd + 2 * m
+            advance(p)
+            advance(p + 1)
             return 0
 
-        lax.fori_loop(begin, end, step, 0)
+        lax.fori_loop(0, (end - begin) // 2, step, 0)
 
     def pair(m, _):
         substep(first, second, 2 * m)
@@ -438,9 +500,10 @@
         at = strip_row(plan, side)
         same = list(enumerate(list(old) + code))
         flipped = list(enumerate(list(old[6:]) + list(old[:6]) + code))
-        spread_strip(same, whole, at, DEEP, plan.own // 2)
-        spread_strip(flipped, beside, at, inner, DEEP // 2)
-        spread_strip(flipped, corner, at, outward, DEEP // 2)
+        half, rows = DEEP // 2, plan.own // 2
+        spread_strip(same, whole, rows, 0, at, DEEP, rows)
+        spread_strip(flipped, beside, half, 0, at, inner, half)
+        spread_strip(flipped, corner, half, 0, at, outward, half)
 
     each_side(plan, place)
 
@@ -476,26 +539,29 @@
 
 def first_kernel(plan, *refs):
     nside = len(plan.sides)
-    strips_in = refs[: 3 * nside]
-    z_in, raw, other = refs[3 * nside], refs[1 + 3 * nside : 7 + 3 * nside], refs[7 + 3 * nside : 13 + 3 * nside]
-    medium, slab_in, under_in, coef_in = refs[13 + 3 * nside : 17 + 3 * nside]
-    outs = refs[17 + 3 * nside : 22 + 6 * nside]
-    own_out, z_out, core_out, gen_out, code_out = outs[:5]
-    rest = refs[22 + 6 * nside :]
+    strips_in, refs = refs[: 3 * nside], refs[3 * nside :]
+    z_in, raw, other = refs[:2], refs[2:8], refs[8:14]
+    medium, slab_in, under_in, coef_in = refs[14:18]
+    own_out, core_out, gen_out, code_out = refs[18:22]
+    z_out, strip_out = refs[22], refs[23 : 23 + 3 * nside]
+    rest = refs[23 + 3 * nside :]
     old, new, (base, silicon, gen, charge, message, coef, code) = rest[:12], rest[12:24], rest[24:31]
-    codes, strips, (strip_mine, slabs, sems) = rest[31], rest[32 : 32 + 3 * nside], rest[-3:]
+    codes, strips, (strip_mine, corners, slabs, sems) = rest[31], rest[32 : 32 + 3 * nside], rest[-4:]
     copies = Copies(sems)
     k = lax.axis_index("af")
     near = DEEP * (1 - k)
     far = plan.part * k
     across = plan.own_rows()
-    here, there = pl.ds(near, plan.part), pl.ds(far, DEEP)
+    here = pl.ds(near, plan.part)
     mine = pl.ds((plan.own - DEEP) * k, plan.part)
     early = [copies.start(medium.at[mine], codes)]
-    early.append(copies.start(z_in.at[12], code.at[there, across]))
+    pages = 13 * DEEP + 1
+    early += get_face(
+        plan, copies, z_in, pages, 12 * DEEP, lambda p, n: code.at[pl.ds(far + p, n), across]
+    )
     early.append(copies.start(slab_in, slabs.at[0]))
     if plan.paired:
-        early.append(copies.start(z_in.at[13, 0, pl.ds(0, 8)], slabs.at[1]))
+        early.append(copies.start(z_in[1].at[z_in[1].shape[0] - 1, pl.ds(0, 8)], slabs.at[1]))
     else:
         early.append(copies.start(under_in, charge))
     early.append(copies.start(coef_in, coef))
@@ -506,7 +572,14 @@
         late.append(copies.start(raw[c].at[0, mine], old[c].at[here, across]))
         late.append(copies.start(other[c].at[0, mine], old[6 + c].at[here, across]))
     for c in range(12):
-        late.append(copies.start(z_in.at[(c + 6) % 12], old[c].at[there, across]))
+        late += get_face(
+            plan,
+            copies,
+            z_in,
+            pages,
+            DEEP * ((c + 6) % 12),
+            lambda p, n, ref=old[c]: ref.at[pl.ds(far + p, n), across],
+        )
     clear(plan, old, new, [code])
     clear_generation(plan, gen)
     wait(early)
@@ -519,7 +592,9 @@
     place_strips(plan, old, [code], strips)
     set_media(plan, code, base, silicon)
     if plan.paired:
-        charge_from_slabs(plan, charge, slabs[0], slabs[1], strips[0][13, 0], strips[2][13, 0])
+        charge_from_slabs(
+            plan, charge, slabs[0], slabs[1], strips[0][13 * plan.own // 2], strips[2][13 * DEEP // 2]
+        )
     wait(late)
     substeps(plan, old, new, base, silicon, charge, gen, coef)
     copies = Copies(sems)
@@ -533,7 +608,8 @@
         def one(q, _):
             for c in range(12):
                 for h in range(2):
-                    strip_mine[slot, c, q, 4 * h : 4 * h + 4, :] = old[c][
+                    tile = plan.own // 2 * c + q
+                    strip_mine[slot, tile, 4 * h : 4 * h + 4, :] = old[c][
                         DEEP + 2 * q + h, at : at + 4, :
                     ]
             return 0
@@ -543,13 +619,14 @@
     toward = DEEP + (plan.own - DEEP) * k
     inward = DEEP + (plan.own - DEEP) * (1 - k)
     for c in range(12):
-        late.append(copies.start(old[c].at[pl.ds(toward, DEEP), across], z_out.at[c]))
+        source = old[c].at[pl.ds(toward, DEEP), across]
+        late.append(copies.start(source, z_out.at[pl.ds(DEEP * c, DEEP)]))
         late.append(copies.start(old[c].at[pl.ds(inward, DEEP), across], core_out.at[c]))
         late.append(copies.start(old[c].at[pl.ds(DEEP, plan.own), across], own_out.at[c]))
     late.append(copies.start(code, code_out))
     message[4:8, :] = slabs[0, 0:4, :]
     each_side(plan, gather)
-    send_strips(plan, copies, late, strip_mine, outs[5:])
+    send_strips(plan, copies, late, strip_mine, corners, strip_out, 12)
     send_generation(plan, copies, late, gen, message, gen_out)
     wait(late)
 
@@ -560,14 +637,15 @@
     shapes = [
         (12, plan.own) + wide,
         (12, DEEP) + wide,
-        (12, DEEP) + wide,
         generation_shape(plan),
         (plan.ext, plan.rows, plan.lanes),
-    ] + strip_shapes(plan, 12)
+    ]
+    shapes += face_shapes(plan, 12 * DEEP) + strip_shapes(plan, 12)
     scratch = round_scratch(plan) + [pltpu.VMEM((plan.part,) + wide, jnp.int32)]
     scratch += [pltpu.VMEM(s.shape, F32) for s in strips]
     scratch += [
-        pltpu.VMEM((nside, 12, plan.own // 2, 8, plan.lanes), F32),
+        pltpu.VMEM((nside, strip_tiles(plan, 12), 8, plan.lanes), F32),
+        pltpu.VMEM((nside, 2, corner_tiles(plan, 12), 8, plan.lanes), F32),
         pltpu.VMEM((2, 8, plan.lanes), F32),
     ]
     return call(
@@ -575,21 +653,19 @@
         first_kernel,
         "first_round",
         shapes,
-        [ANY] * (1 + 3 * nside) + [HBM] * 6 + [ANY] * 6 + [HBM, ANY, ANY, HBM],
+        [ANY] * (2 + 3 * nside) + [HBM] * 6 + [ANY] * 6 + [HBM, ANY, ANY, HBM],
         scratch,
-        40 + 3 * nside + plan.devices,
+        42 + 3 * nside + plan.devices,
         round_flops(plan),
         10_000_000,
-    )(*strips, z_in, *raw, *other, medium, slab, under, coef)
+    )(*strips, *z_in, *raw, *other, medium, slab, under, coef)
 
 
 def second_kernel(plan, *refs):
     nside = len(plan.sides)
-    strips_in = refs[: 3 * nside]
-    z_in, core_in, own_in, code_in, charge_in, coef_in = refs[3 * nside : 6 + 3 * nside]
-    outs = refs[6 + 3 * nside : 14 + 3 * nside]
-    kept, sent, gen_out = outs[:6], outs[6], outs[7]
-    rest = refs[14 + 3 * nside :]
+    strips_in, refs = refs[: 3 * nside], refs[3 * nside :]
+    z_in, (core_in, own_in, code_in, charge_in, coef_in) = refs[:1], refs[1:6]
+    kept, sent, gen_out, rest = refs[6:12], refs[12], refs[13], refs[14:]
     old, new, (base, silicon, gen, charge, message, coef, code) = rest[:12], rest[12:24], rest[24:31]
     strips, sems = rest[31:-1], rest[-1]
     copies = Copies(sems)
@@ -605,7 +681,14 @@
     for c in range(12):
         flip = (c + 6) % 12
         late.append(copies.start(own_in.at[c], old[c].at[pl.ds(DEEP, plan.own), across]))
-        late.append(copies.start(z_in.at[flip], old[c].at[pl.ds(outward, DEEP), across]))
+        late += get_face(
+            plan,
+            copies,
+            z_in,
+            12 * DEEP,
+            DEEP * flip,
+            lambda p, n, ref=old[c]: ref.at[pl.ds(outward + p, n), across],
+        )
         late.append(copies.start(core_in.at[flip], old[c].at[pl.ds(inner, DEEP), across]))
     clear(plan, old, new, [])
     clear_generation(plan, gen)
@@ -641,7 +724,7 @@
         39 + 3 * nside + plan.devices,
         round_flops(plan),
         10_000_000,
-    )(*strips, z_in, core_in, own_in, code, charge, coef)
+    )(*strips, *z_in, core_in, own_in, code, charge, coef)
 
 
 def join_kernel(plan, *refs):
@@ -779,20 +862,19 @@
     core = lambda z, x, k: (z, x, 1 - k)
     beyond = lambda z, k: z - 1 if k == 0 else z + 1
 
-    def exchange(z_msg, strips):
+    def exchange(face, strips):
         got = []
         for n, side in enumerate(plan.sides):
             to = functools.partial(across_step, side)
-            whole, inner, corner = strips[3 * n : 3 * n + 3]
-            got.append(send(whole, lambda z, x, k: (z, to(x), k)))
-            got.append(send(inner, lambda z, x, k: (z, to(x), 1 - k)))
-            got.append(send(corner, lambda z, x, k: (beyond(z, k), to(x), 1 - k)))
-        return send(z_msg, lambda z, x, k: (beyond(z, k), x, 1 - k)), got
+            got.append(send(strips[3 * n], lambda z, x, k: (z, to(x), k)))
+            got.append(send(strips[3 * n + 1], lambda z, x, k: (z, to(x), 1 - k)))
+            got.append(send(strips[3 * n + 2], lambda z, x, k: (beyond(z, k), to(x), 1 - k)))
+        return [send(part, lambda z, x, k: (beyond(z, k), x, 1 - k)) for part in face], got
 
     other = [send(r, core) for r in raw]
     slab = jnp.pad(density, ((0, 8 - plan.slab), (0, plan.lanes - plan.grid_cols)))
     packed = pack(plan, raw, other, medium, slab, table)
-    z_in, strips = exchange(packed[0], packed[1:-1])
+    z_in, strips = exchange(packed[:2], packed[2:-1])
     coef = packed[-1]
     under = slab
     if not plan.paired:
@@ -800,9 +882,9 @@
         slabs = everywhere(jnp.broadcast_to(density, (tiles,) + density.shape), ("gz", "gx"))
         under = spread_whole(plan, slabs.reshape(plan.grid_rows, plan.grid_cols))
     outs = first_round(plan, strips, z_in, raw, other, medium, slab, under, coef)
-    own, z_msg, core_msg, gens, code = outs[:5]
+    own, core_msg, gens, code = outs[:4]
     gens = everywhere(gens, LINE)
-    z_in, strips = exchange(z_msg, outs[5:])
+    z_in, strips = exchange(outs[4:5], outs[5:])
     core_in = send(core_msg, core)
     grid, charge = carriers(plan, False, gens)
     outs = second_round(plan, strips, z_in, core_in, own, code, charge, coef)

time: 99.1 us -> 93.7 us (0.946)
  waiting for transfers between devices: 21.8 us -> 16.5 us
  starting transfers between devices: 24.9 us -> 27.2 us
  Pallas kernels: 37.2 us -> 35.1 us
    ppermute x16 -> x17, waiting for transfers between devices: 15.3 us -> 9.69 us  [send(): return lax.ppermute(message, LINE, line_pairs(plan, target))]
    ppermute x16 -> x17, starting transfers between devices: 21.4 us -> 23.7 us  [send(): return lax.ppermute(message, LINE, line_pairs(plan, target))]
    pallas_call x6, Pallas kernels: 37.2 us -> 35.1 us  [run(): return kernel(*placed)]
  transfers between devices with their start and end apart: 17 -> 18, of which waited for: 7 -> 7; matrix products, arithmetic and copies ran while one was open for 1% -> 1% of each run, Pallas kernels for 4% -> 4%
where the time goes in v6:
time: 93.7 us; the launch traced here: 93.2 us
  Pallas kernels  35.1 us (37%)
  starting transfers between devices  27.2 us (29%)
  waiting for transfers between devices  16.5 us (18%)
  blocking collectives  12.3 us (13%)
  local copies, waits for them, and re-layouts  1.36 us (1%)
    pallas_call x6, Pallas kernels, run(): return kernel(*placed)  35.1 us
    ppermute x17, starting transfers between devices, send(): return lax.ppermute(message, LINE, line_pairs(plan, target))  23.7 us
    all_to_all x1, blocking collectives, everywhere(): lax.all_to_all(message, axes, split_axis=0, concat_axis=0, tiled=True)  12.3 us
    ppermute x17, waiting for transfers between devices, send(): return lax.ppermute(message, LINE, line_pairs(plan, target))  9.69 us
    all_to_all x1, waiting for transfers between devices, everywhere(): lax.all_to_all(message, axes, split_axis=0, concat_axis=0, tiled=True)  6.79 us
    all_to_all x1, starting transfers between devices, everywhere(): lax.all_to_all(message, axes, split_axis=0, concat_axis=0, tiled=True)  3.5 us
  transfers between devices with their start and end apart: 18, of which 7 were waited for; matrix products, arithmetic and copies ran while one was open for 1% of the time, Pallas kernels for 4%

profile of v6, /device:TPU:0, one launch (start us, length us, event | category | flops | bytes accessed | tf_op | source)
XLA Modules:
  0.0 93.2 jit_solution(1569249228140966306)
XLA Ops:
  0.6 0.5 collective-permute-start
  1.2 0.4 collective-permute-start.2
  1.7 0.4 collective-permute-start.4
  2.2 0.7 collective-permute-done.refs_6_.refs_11_
  2.9 0.4 collective-permute-start.5
  3.3 0.7 pad.4.refs_13_.refs_18_.refs_19_
  4.0 0.4 collective-permute-done.2.refs_8_.refs_13_
  4.4 0.7 collective-permute-done.3.refs_9_.refs_14_
  5.1 0.7 collective-permute-done.4.refs_10_.refs_15_
  5.9 0.7 collective-permute-done.5.refs_11_.refs_16_
  6.6 0.7 copy-done
  7.3 2.7 %pack.1 = (f32[27,32,128]{2,1,0:T(8,128)}, f32[26,32,128]{2,1,0:T(8,128)}, f32[109,8,128]{2,1,0:T(8,128)}, f32[27,8,128]{2,1,0:T(8,128)}, f32[27,8,128]{2,1,0:T(8,128)}, /*index=5*/f32[8,8,128]{2,1,0:T(8,128)}) custom-call(f32[1,32,32,128]{3,2,1,0:T(8,128)} %refs_5_.3, f32[1,32,32,128]{3,2,1,0:T(8,128)} %refs_6_.1, f32[1,32,32,128]{3,2,1,0:T(8,128)} %refs_7_.1, ...), custom_call_target="tpu_custom_call" | custom-call | bytes 4000000 | tf_op jit(solution)/shard_map/pack/pallas_call | solution.py:123
  10.1 2.9 %collective-permute-start.6 = (f32[109,8,128]{2,1,0:T(8,128)}, f32[109,8,128]{2,1,0:T(8,128)S(1)}, u32[]{:S(2)}, u32[]{:S(2)}) collective-permute-start(f32[109,8,128]{2,1,0:T(8,128)} %get-tuple-element.37), channel_id=1, source_target_pairs={{0,2},{1,3},{2,0},{3,1},{4,6},{5,7},{6,4},{7,5},{8,10},{9,11},{10,... | collective-permute-start | bytes 1339400 | tf_op jit(solution)/shard_map/ppermute | solution.py:857
  13.0 0.7 collective-permute-start.9
  13.7 0.7 collective-permute-start.10
  14.4 4.3 %collective-permute-start.7 = (f32[27,8,128]{2,1,0:T(8,128)}, f32[27,8,128]{2,1,0:T(8,128)S(1)}, u32[]{:S(2)}, u32[]{:S(2)}) collective-permute-start(f32[27,8,128]{2,1,0:T(8,128)} %get-tuple-element.38), channel_id=1, source_target_pairs={{0,3},{1,2},{2,1},{3,0},{4,7},{5,6},{6,5},{7,4},{8,11},{9,10},{10,... | collective-permute-start | bytes 331784 | tf_op jit(solution)/shard_map/ppermute | solution.py:857
  18.7 0.7 collective-permute-start.8
  19.4 6.3 %collective-permute-done.7.refs_1_ = f32[27,8,128]{2,1,0:T(8,128)S(1)} collective-permute-done((f32[27,8,128]{2,1,0:T(8,128)}, f32[27,8,128]{2,1,0:T(8,128)S(1)}, u32[]{:S(2)}, u32[]{:S(2)}) %collective-permute-start.7) | collective-permute-done | bytes 110624 | tf_op jit(solution)/shard_map/ppermute | solution.py:857
  25.7 14.1 %first_round.1 = (f32[12,16,32,128]{3,2,1,0:T(8,128)}, f32[12,4,32,128]{3,2,1,0:T(8,128)}, f32[16,8,128]{2,1,0:T(8,128)}, f32[24,48,128]{2,1,0:T(8,128)}, f32[48...) custom-call(f32[109,8,128]{2,1,0:T(8,128)S(1)} %collective-permute-done.6.refs_0_, ...), custom_call_target="tpu_custom_call" | custom-call | flops 73728000 | bytes 10000000 | tf_op jit(solution)/shard_map/first_round/pallas_call | solution.py:123
  39.8 0.7 collective-permute-start.14
  40.5 7.7 %collective-permute-start.15 = (f32[12,4,32,128]{3,2,1,0:T(8,128)}, f32[12,4,32,128]{3,2,1,0:T(8,128)S(1)}, u32[]{:S(2)}, u32[]{:S(2)}) collective-permute-start(f32[12,4,32,128]{3,2,1,0:T(8,128)} %get-tuple-element.47), channel_id=1, source_target_pairs={{0,1},{1,0},{2,3},{3,2},{4,5},{5,4},{6,7},{7,6},{8,9},{9,8},{10,11... | collective-permute-start | bytes 2359304 | tf_op jit(solution)/shard_map/ppermute | solution.py:857
  48.1 1.5 %collective-permute-start.11 = (f32[96,8,128]{2,1,0:T(8,128)}, f32[96,8,128]{2,1,0:T(8,128)S(1)}, u32[]{:S(2)}, u32[]{:S(2)}) collective-permute-start(f32[96,8,128]{2,1,0:T(8,128)} %get-tuple-element.43), channel_id=1, source_target_pairs={{0,2},{1,3},{2,0},{3,1},{4,6},{5,7},{6,4},{7,5},{8,10},{9,11},{10,... | collective-permute-start | bytes 1179656 | tf_op jit(solution)/shard_map/ppermute | solution.py:857
  49.6 3.5 %all-to-all-start = ((f32[16,8,128]{2,1,0:T(8,128)}), f32[16,8,128]{2,1,0:T(8,128)S(1)}, u32[]{:S(2)}, u32[]{:S(2)}) async-start(f32[16,8,128]{2,1,0:T(8,128)} %get-tuple-element.50), calls=%async_computation | async-start | bytes 131072 | tf_op jit(solution)/shard_map/all_to_all | solution.py:860
  53.1 1.6 %collective-permute-start.12 = (f32[24,8,128]{2,1,0:T(8,128)}, f32[24,8,128]{2,1,0:T(8,128)S(1)}, u32[]{:S(2)}, u32[]{:S(2)}) collective-permute-start(f32[24,8,128]{2,1,0:T(8,128)} %get-tuple-element.44), channel_id=1, source_target_pairs={{0,3},{1,2},{2,1},{3,0},{4,7},{5,6},{6,5},{7,4},{8,11},{9,10},{10,... | collective-permute-start | bytes 294920 | tf_op jit(solution)/shard_map/ppermute | solution.py:857
  54.7 0.7 collective-permute-start.13
  55.4 6.8 %all-to-all-done.refs_0_ = f32[16,8,128]{2,1,0:T(8,128)S(1)} async-done(((f32[16,8,128]{2,1,0:T(8,128)}), f32[16,8,128]{2,1,0:T(8,128)S(1)}, u32[]{:S(2)}, u32[]{:S(2)}) %all-to-all-start) | async-done | bytes 65568 | tf_op jit(solution)/shard_map/all_to_all | solution.py:860
  62.2 1.6 %carriers.2 = (f32[48,128]{1,0:T(8,128)}, f32[6,40,128]{2,1,0:T(8,128)}) custom-call(f32[16,8,128]{2,1,0:T(8,128)S(1)} %all-to-all-done.refs_0_), custom_call_target="tpu_custom_call" | custom-call | flops 2000000 | bytes 1000000 | tf_op jit(solution)/shard_map/carriers/pallas_call | solution.py:123
  63.9 13.2 %second_round.1 = (f32[1,32,32,128]{3,2,1,0:T(8,128)}, f32[1,32,32,128]{3,2,1,0:T(8,128)}, f32[1,32,32,128]{3,2,1,0:T(8,128)}, f32[1,32,32,128]{3,2,1,0:T(8,128)...) custom-call(f32[96,8,128]{2,1,0:T(8,128)S(1)} %collective-permute-do, ...), custom_call_target="tpu_custom_call" | custom-call | flops 73728000 | bytes 10000000 | tf_op jit(solution)/shard_map/second_round/pallas_call | solution.py:123
  77.0 0.4 collective-permute-start.16
  77.4 12.3 %all_to_all.10.refs_0_ = f32[16,8,128]{2,1,0:T(8,128)S(1)} all-to-all(f32[16,8,128]{2,1,0:T(8,128)} %get-tuple-element.65), channel_id=1, replica_groups=mesh['group'=2,'gz'=4,'gx'=2,'af'=2] {'gz','gx','af'}, dimensions={0} | all-to-all | bytes 131072 | tf_op jit(solution)/shard_map/all_to_all | solution.py:860
  89.8 2.1 %carriers.3 = f32[4,16]{1,0:T(4,128)} custom-call(f32[16,8,128]{2,1,0:T(8,128)S(1)} %all_to_all.10.refs_0_, f32[48,128]{1,0:T(8,128)} %get-tuple-element.66.refs_1_), custom_call_target="tpu_custom_call" | custom-call | flops 2000000 | bytes 1000000 | tf_op jit(solution)/shard_map/carriers/pallas_call | solution.py:123
  91.8 1.4 %join.1 = (f32[1,32,32,128]{3,2,1,0:T(8,128)}, f32[1,32,32,128]{3,2,1,0:T(8,128)}, f32[1,32,32,128]{3,2,1,0:T(8,128)}, f32[1,32,32,128]{3,2,1,0:T(8,128)}, f32[1...) custom-call(f32[1,32,32,128]{3,2,1,0:T(8,128)} %get-tuple-element.52, ...), custom_call_target="tpu_custom_call", output_to_operand_aliasing={{0}: (0, {}), {1}: (1, {}), {2}: (2, {}), {3}: (3, {}), {4}... | custom-call | bytes 3000000 | tf_op jit(solution)/shard_map/join/pallas_call | solution.py:123
  (14 shorter events, 0.2 us)
Async XLA Ops:
  0.6 2.3 %collective-permute-start = (f32[1,32,32,128]{3,2,1,0:T(8,128)}, f32[1,32,32,128]{3,2,1,0:T(8,128)S(1)}, u32[]{:S(2)}, u32[]{:S(2)}) collective-permute-start(f32[1,32,32,128]{3,2,1,0:T(8,128)} %refs_5_.3), channel_id=1, source_target_pairs={{0,1},{1,0},{2,3},{3,2},{4,5},{5,4},{6,7},{7,6},{8,9},{9,8},{10,11... | collective-permute-start | bytes 1572872 | tf_op jit(solution)/shard_map/ppermute | solution.py:857
  1.1 2.8 %collective-permute-start.1 = (f32[1,32,32,128]{3,2,1,0:T(8,128)}, f32[1,32,32,128]{3,2,1,0:T(8,128)S(1)}, u32[]{:S(2)}, u32[]{:S(2)}) collective-permute-start(f32[1,32,32,128]{3,2,1,0:T(8,128)} %refs_6_.1), channel_id=1, source_target_pairs={{0,1},{1,0},{2,3},{3,2},{4,5},{5,4},{6,7},{7,6},{8,9},{9,8},{10,11... | collective-permute-start | bytes 1572872 | tf_op jit(solution)/shard_map/ppermute | solution.py:857
  1.2 3.2 %collective-permute-start.2 = (f32[1,32,32,128]{3,2,1,0:T(8,128)}, f32[1,32,32,128]{3,2,1,0:T(8,128)S(1)}, u32[]{:S(2)}, u32[]{:S(2)}) collective-permute-start(f32[1,32,32,128]{3,2,1,0:T(8,128)} %refs_7_.1), channel_id=1, source_target_pairs={{0,1},{1,0},{2,3},{3,2},{4,5},{5,4},{6,7},{7,6},{8,9},{9,8},{10,11... | collective-permute-start | bytes 1572872 | tf_op jit(solution)/shard_map/ppermute | solution.py:857
  1.7 3.5 %collective-permute-start.3 = (f32[1,32,32,128]{3,2,1,0:T(8,128)}, f32[1,32,32,128]{3,2,1,0:T(8,128)S(1)}, u32[]{:S(2)}, u32[]{:S(2)}) collective-permute-start(f32[1,32,32,128]{3,2,1,0:T(8,128)} %refs_8_.1), channel_id=1, source_target_pairs={{0,1},{1,0},{2,3},{3,2},{4,5},{5,4},{6,7},{7,6},{8,9},{9,8},{10,11... | collective-permute-start | bytes 1572872 | tf_op jit(solution)/shard_map/ppermute | solution.py:857
  1.7 4.2 %collective-permute-start.4 = (f32[1,32,32,128]{3,2,1,0:T(8,128)}, f32[1,32,32,128]{3,2,1,0:T(8,128)S(1)}, u32[]{:S(2)}, u32[]{:S(2)}) collective-permute-start(f32[1,32,32,128]{3,2,1,0:T(8,128)} %refs_9_.1), channel_id=1, source_target_pairs={{0,1},{1,0},{2,3},{3,2},{4,5},{5,4},{6,7},{7,6},{8,9},{9,8},{10,11... | collective-permute-start | bytes 1572872 | tf_op jit(solution)/shard_map/ppermute | solution.py:857
  2.9 3.7 %collective-permute-start.5 = (f32[1,32,32,128]{3,2,1,0:T(8,128)}, f32[1,32,32,128]{3,2,1,0:T(8,128)S(1)}, u32[]{:S(2)}, u32[]{:S(2)}) collective-permute-start(f32[1,32,32,128]{3,2,1,0:T(8,128)} %refs_10_.1), channel_id=1, source_target_pairs={{0,1},{1,0},{2,3},{3,2},{4,5},{5,4},{6,7},{7,6},{8,9},{9,8},{10,11... | collective-permute-start | bytes 1572872 | tf_op jit(solution)/shard_map/ppermute | solution.py:857
  6.6 0.7 copy-start
  10.1 15.6 %collective-permute-start.6 = (f32[109,8,128]{2,1,0:T(8,128)}, f32[109,8,128]{2,1,0:T(8,128)S(1)}, u32[]{:S(2)}, u32[]{:S(2)}) collective-permute-start(f32[109,8,128]{2,1,0:T(8,128)} %get-tuple-element.37), channel_id=1, source_target_pairs={{0,2},{1,3},{2,0},{3,1},{4,6},{5,7},{6,4},{7,5},{8,10},{9,11},{10,... | collective-permute-start | bytes 1339400 | tf_op jit(solution)/shard_map/ppermute | solution.py:857
  13.0 12.7 %collective-permute-start.9 = (f32[27,32,128]{2,1,0:T(8,128)}, f32[27,32,128]{2,1,0:T(8,128)S(1)}, u32[]{:S(2)}, u32[]{:S(2)}) collective-permute-start(f32[27,32,128]{2,1,0:T(8,128)} %get-tuple-element.40), channel_id=1, source_target_pairs={{1,4},{3,6},{4,1},{5,8},{6,3},{7,10},{8,5},{9,12},{10,7},{11,14},{... | collective-permute-start | bytes 1327112 | tf_op jit(solution)/shard_map/ppermute | solution.py:857
  13.7 12.0 %collective-permute-start.10 = (f32[26,32,128]{2,1,0:T(8,128)}, f32[26,32,128]{2,1,0:T(8,128)S(1)}, u32[]{:S(2)}, u32[]{:S(2)}) collective-permute-start(f32[26,32,128]{2,1,0:T(8,128)} %get-tuple-element.41), channel_id=1, source_target_pairs={{1,4},{3,6},{4,1},{5,8},{6,3},{7,10},{8,5},{9,12},{10,7},{11,14},{... | collective-permute-start | bytes 1277960 | tf_op jit(solution)/shard_map/ppermute | solution.py:857
  14.4 11.3 %collective-permute-start.7 = (f32[27,8,128]{2,1,0:T(8,128)}, f32[27,8,128]{2,1,0:T(8,128)S(1)}, u32[]{:S(2)}, u32[]{:S(2)}) collective-permute-start(f32[27,8,128]{2,1,0:T(8,128)} %get-tuple-element.38), channel_id=1, source_target_pairs={{0,3},{1,2},{2,1},{3,0},{4,7},{5,6},{6,5},{7,4},{8,11},{9,10},{10,... | collective-permute-start | bytes 331784 | tf_op jit(solution)/shard_map/ppermute | solution.py:857
  18.7 6.9 %collective-permute-start.8 = (f32[27,8,128]{2,1,0:T(8,128)}, f32[27,8,128]{2,1,0:T(8,128)S(1)}, u32[]{:S(2)}, u32[]{:S(2)}) collective-permute-start(f32[27,8,128]{2,1,0:T(8,128)} %get-tuple-element.39), channel_id=1, source_target_pairs={{1,6},{3,4},{4,3},{5,10},{6,1},{7,8},{8,7},{9,14},{10,5},{11,12},{... | collective-permute-start | bytes 331784 | tf_op jit(solution)/shard_map/ppermute | solution.py:857
  39.8 24.1 %collective-permute-start.14 = (f32[48,32,128]{2,1,0:T(8,128)}, f32[48,32,128]{2,1,0:T(8,128)S(1)}, u32[]{:S(2)}, u32[]{:S(2)}) collective-permute-start(f32[48,32,128]{2,1,0:T(8,128)} %get-tuple-element.46), channel_id=1, source_target_pairs={{1,4},{3,6},{4,1},{5,8},{6,3},{7,10},{8,5},{9,12},{10,7},{11,14},{... | collective-permute-start | bytes 2359304 | tf_op jit(solution)/shard_map/ppermute | solution.py:857
  40.5 23.4 %collective-permute-start.15 = (f32[12,4,32,128]{3,2,1,0:T(8,128)}, f32[12,4,32,128]{3,2,1,0:T(8,128)S(1)}, u32[]{:S(2)}, u32[]{:S(2)}) collective-permute-start(f32[12,4,32,128]{3,2,1,0:T(8,128)} %get-tuple-element.47), channel_id=1, source_target_pairs={{0,1},{1,0},{2,3},{3,2},{4,5},{5,4},{6,7},{7,6},{8,9},{9,8},{10,11... | collective-permute-start | bytes 2359304 | tf_op jit(solution)/shard_map/ppermute | solution.py:857
  48.1 15.7 %collective-permute-start.11 = (f32[96,8,128]{2,1,0:T(8,128)}, f32[96,8,128]{2,1,0:T(8,128)S(1)}, u32[]{:S(2)}, u32[]{:S(2)}) collective-permute-start(f32[96,8,128]{2,1,0:T(8,128)} %get-tuple-element.43), channel_id=1, source_target_pairs={{0,2},{1,3},{2,0},{3,1},{4,6},{5,7},{6,4},{7,5},{8,10},{9,11},{10,... | collective-permute-start | bytes 1179656 | tf_op jit(solution)/shard_map/ppermute | solution.py:857
  49.6 12.5 %all-to-all-start = ((f32[16,8,128]{2,1,0:T(8,128)}), f32[16,8,128]{2,1,0:T(8,128)S(1)}, u32[]{:S(2)}, u32[]{:S(2)}) async-start(f32[16,8,128]{2,1,0:T(8,128)} %get-tuple-element.50), calls=%async_computation | async-start | bytes 131072 | tf_op jit(solution)/shard_map/all_to_all | solution.py:860
  53.1 10.7 %collective-permute-start.12 = (f32[24,8,128]{2,1,0:T(8,128)}, f32[24,8,128]{2,1,0:T(8,128)S(1)}, u32[]{:S(2)}, u32[]{:S(2)}) collective-permute-start(f32[24,8,128]{2,1,0:T(8,128)} %get-tuple-element.44), channel_id=1, source_target_pairs={{0,3},{1,2},{2,1},{3,0},{4,7},{5,6},{6,5},{7,4},{8,11},{9,10},{10,... | collective-permute-start | bytes 294920 | tf_op jit(solution)/shard_map/ppermute | solution.py:857
  54.7 9.1 %collective-permute-start.13 = (f32[24,8,128]{2,1,0:T(8,128)}, f32[24,8,128]{2,1,0:T(8,128)S(1)}, u32[]{:S(2)}, u32[]{:S(2)}) collective-permute-start(f32[24,8,128]{2,1,0:T(8,128)} %get-tuple-element.45), channel_id=1, source_target_pairs={{1,6},{3,4},{4,3},{5,10},{6,1},{7,8},{8,7},{9,14},{10,5},{11,12},{... | collective-permute-start | bytes 294920 | tf_op jit(solution)/shard_map/ppermute | solution.py:857
  77.0 14.8 %collective-permute-start.16 = (f32[6,16,32,128]{3,2,1,0:T(8,128)}, f32[6,16,32,128]{3,2,1,0:T(8,128)S(1)}, u32[]{:S(2)}, u32[]{:S(2)}) collective-permute-start(f32[6,16,32,128]{3,2,1,0:T(8,128)} %get-tuple-element.58), channel_id=1, source_target_pairs={{0,1},{1,0},{2,3},{3,2},{4,5},{5,4},{6,7},{7,6},{8,9},{9,8},{10,11... | collective-permute-start | bytes 4718600 | tf_op jit(solution)/shard_map/ppermute | solution.py:857

commit v7 on v6

--- a/solution.py
+++ b/solution.py
@@ -128,11 +128,11 @@
 def pack_kernel(plan, *refs):
     raw, other, medium, nside = refs[:6], refs[6:12], refs[12], len(plan.sides)
     slab_in, table_in = refs[13:15]
-    outs = refs[15 : 18 + 3 * nside]
-    edge, edge_code, face, face_code, strips, corners, slab, table, coef, sems = refs[18 + 3 * nside :]
+    outs = refs[15 : 18 + 2 * nside]
+    edge, edge_code, face, face_code, strips, corners, slab, table, coef, sems = refs[18 + 2 * nside :]
     copies = Copies(sems)
     k = lax.axis_index("af")
-    mine = pl.ds(plan.own * k, plan.own)
+    mine = pl.ds((plan.own - DEEP) * k, plan.part)
     outer = pl.ds((plan.planes - DEEP) * k, DEEP)
     if plan.paired:
         tile_rows = [pl.multiple_of((plan.cols - 8) * (1 - lax.axis_index("gx")), 8)]
@@ -152,28 +152,30 @@
         late.append(copies.start(other[c].at[0, outer], face.at[pl.ds(DEEP * (6 + c), DEEP)]))
     late.append(copies.start(medium.at[outer], face_code))
     wait(early)
-    rows = plan.own // 2
+    rows = plan.part // 2
 
     def fill(slot, low):
         def one(q, _):
             for h in range(2):
-                half = slice(4 * h, 4 * h + 4)
+                four = slice(4 * h, 4 * h + 4)
                 for c in range(12):
-                    strips[slot, c * rows + q, half, :] = edge[slot, c, 2 * q + h, low : low + 4, :]
+                    strips[slot, c * rows + q, four, :] = edge[slot, c, 2 * q + h, low : low + 4, :]
                 code = edge_code[slot, 2 * q + h, low : low + 4, :]
-                strips[slot, 12 * rows + q, half, :] = code.astype(F32)
+                strips[slot, 12 * rows + q, four, :] = code.astype(F32)
             return 0
 
         lax.fori_loop(0, rows, one, 0)
 
     each_side(plan, lambda slot, side: fill(slot, 4 if plan.paired == (side == "high") else 0))
-    page = slab[...]
+    page, half = slab[...], DEEP // 2
     for n in range(nside):
-        for extra in range(13 * rows, strip_tiles(plan, 13)):
-            strips[n, extra] = page
-        corners[n, 0, 13 * DEEP // 2] = page
-        corners[n, 1, 13 * DEEP // 2] = page
-    send_strips(plan, copies, last, strips, corners, outs[2:-1], 13)
+        strips[n, 13 * rows] = page
+        last.append(copies.start(strips.at[n], outs[2 + 2 * n]))
+        corners[n, 13 * half] = page
+        for c in range(13):
+            for h in range(half):
+                corners[n, half * c + h] = strips[n, rows * c + (rows - half) * k + h]
+        last.append(copies.start(corners.at[n], outs[3 + 2 * n]))
     own, partner = jnp.where(k == 0, table[0:1], table[1:2]), jnp.where(k == 0, table[1:2], table[0:1])
     for s, row in enumerate((own, partner)):
         kerr, two, free = row[:, 0:1], row[:, 1:2], row[:, 2:3]
@@ -212,10 +214,9 @@
 
 
 def strip_tiles(plan, comps):
-    pages = DEEP * comps + (comps > 12)
     if comps == 12:
         return comps * plan.own // 2
-    return max(comps * plan.own // 2, (pages + 1) // 2 * (plan.cols // 8)) + 1
+    return comps * plan.part // 2 + 1
 
 
 def send_strips(plan, copies, started, strips, corners, outs, comps):
@@ -235,12 +236,9 @@
 
 
 def strip_shapes(plan, comps):
-    shapes = []
-    for _ in plan.sides:
-        tiles = corner_tiles(plan, comps)
-        for tiles in (strip_tiles(plan, comps), tiles, tiles):
-            shapes.append((tiles, 8, plan.lanes))
-    return shapes
+    tiles = corner_tiles(plan, comps)
+    one = [strip_tiles(plan, comps)] + [tiles] * (1 if comps > 12 else 2)
+    return [(count, 8, plan.lanes) for count in one * len(plan.sides)]
 
 
 def face_shapes(plan, pages):
@@ -252,12 +250,12 @@
     nside = len(plan.sides)
     pages = 13 * DEEP + 1
     scratch = [
-        pltpu.VMEM((nside, 12, plan.own, 8, plan.lanes), F32),
-        pltpu.VMEM((nside, plan.own, 8, plan.lanes), jnp.int32),
+        pltpu.VMEM((nside, 12, plan.part, 8, plan.lanes), F32),
+        pltpu.VMEM((nside, plan.part, 8, plan.lanes), jnp.int32),
         pltpu.VMEM((pages,) + wide, F32),
         pltpu.VMEM((DEEP,) + wide, jnp.int32),
         pltpu.VMEM((nside, strip_tiles(plan, 13), 8, plan.lanes), F32),
-        pltpu.VMEM((nside, 2, corner_tiles(plan, 13), 8, plan.lanes), F32),
+        pltpu.VMEM((nside, corner_tiles(plan, 13), 8, plan.lanes), F32),
         pltpu.VMEM((8, plan.lanes), F32),
         pltpu.VMEM(table.shape, F32),
         pltpu.VMEM((8, 8, plan.lanes), F32),
@@ -267,7 +265,7 @@
         pack_kernel,
         "pack",
         face_shapes(plan, pages) + strip_shapes(plan, 13) + [(8, 8, plan.lanes)],
-        [HBM] * 6 + [ANY] * 6 + [HBM, ANY, ANY],
+        [HBM] * 6 + [ANY] * 6 + [HBM, ANY, HBM],
         scratch,
         16 * nside + 18,
         moved=4_000_000,
@@ -496,11 +494,17 @@
     outward, inner = plan.part * k, plan.part * (1 - k)
 
     def place(slot, side):
-        whole, beside, corner = strips[3 * slot : 3 * slot + 3]
         at = strip_row(plan, side)
         same = list(enumerate(list(old) + code))
         flipped = list(enumerate(list(old[6:]) + list(old[:6]) + code))
         half, rows = DEEP // 2, plan.own // 2
+        if code:
+            whole, corner = strips[2 * slot : 2 * slot + 2]
+            near, rows = DEEP * (1 - k), plan.part // 2
+            spread_strip(same, whole, rows, 0, at, near, rows)
+            spread_strip(flipped, corner, half, 0, at, outward, half)
+            return
+        whole, beside, corner = strips[3 * slot : 3 * slot + 3]
         spread_strip(same, whole, rows, 0, at, DEEP, rows)
         spread_strip(flipped, beside, half, 0, at, inner, half)
         spread_strip(flipped, corner, half, 0, at, outward, half)
@@ -539,14 +543,14 @@
 
 def first_kernel(plan, *refs):
     nside = len(plan.sides)
-    strips_in, refs = refs[: 3 * nside], refs[3 * nside :]
+    strips_in, refs = refs[: 2 * nside], refs[2 * nside :]
     z_in, raw, other = refs[:2], refs[2:8], refs[8:14]
     medium, slab_in, under_in, coef_in = refs[14:18]
     own_out, core_out, gen_out, code_out = refs[18:22]
     z_out, strip_out = refs[22], refs[23 : 23 + 3 * nside]
     rest = refs[23 + 3 * nside :]
     old, new, (base, silicon, gen, charge, message, coef, code) = rest[:12], rest[12:24], rest[24:31]
-    codes, strips, (strip_mine, corners, slabs, sems) = rest[31], rest[32 : 32 + 3 * nside], rest[-4:]
+    codes, strips, (strip_mine, corners, slabs, sems) = rest[31], rest[32 : 32 + 2 * nside], rest[-4:]
     copies = Copies(sems)
     k = lax.axis_index("af")
     near = DEEP * (1 - k)
@@ -593,7 +597,7 @@
     set_media(plan, code, base, silicon)
     if plan.paired:
         charge_from_slabs(
-            plan, charge, slabs[0], slabs[1], strips[0][13 * plan.own // 2], strips[2][13 * DEEP // 2]
+            plan, charge, slabs[0], slabs[1], strips[0][13 * plan.part // 2], strips[1][13 * DEEP // 2]
         )
     wait(late)
     substeps(plan, old, new, base, silicon, charge, gen, coef)
@@ -653,7 +657,7 @@
         first_kernel,
         "first_round",
         shapes,
-        [ANY] * (2 + 3 * nside) + [HBM] * 6 + [ANY] * 6 + [HBM, ANY, ANY, HBM],
+        [ANY] * (2 + 2 * nside) + [HBM] * 6 + [ANY] * 6 + [HBM, ANY, ANY, HBM],
         scratch,
         42 + 3 * nside + plan.devices,
         round_flops(plan),
@@ -863,12 +867,14 @@
     beyond = lambda z, k: z - 1 if k == 0 else z + 1
 
     def exchange(face, strips):
-        got = []
+        got, each = [], len(strips) // len(plan.sides)
         for n, side in enumerate(plan.sides):
             to = functools.partial(across_step, side)
-            got.append(send(strips[3 * n], lambda z, x, k: (z, to(x), k)))
-            got.append(send(strips[3 * n + 1], lambda z, x, k: (z, to(x), 1 - k)))
-            got.append(send(strips[3 * n + 2], lambda z, x, k: (beyond(z, k), to(x), 1 - k)))
+            mine = strips[each * n : each * n + each]
+            got.append(send(mine[0], lambda z, x, k: (z, to(x), k)))
+            if each == 3:
+                got.append(send(mine[1], lambda z, x, k: (z, to(x), 1 - k)))
+            got.append(send(mine[-1], lambda z, x, k: (beyond(z, k), to(x), 1 - k)))
         return [send(part, lambda z, x, k: (beyond(z, k), x, 1 - k)) for part in face], got
 
     other = [send(r, core) for r in raw]

time: 93.7 us -> 92.6 us (0.988)
  starting transfers between devices: 27.2 us -> 22.9 us
  waiting for transfers between devices: 16.5 us -> 20.8 us
    ppermute x17 -> x16, waiting for transfers between devices: 9.69 us -> 14 us  [send(): return lax.ppermute(message, LINE, line_pairs(plan, target))]
    ppermute x17 -> x16, starting transfers between devices: 23.7 us -> 19.4 us  [send(): return lax.ppermute(message, LINE, line_pairs(plan, target))]
  transfers between devices with their start and end apart: 18 -> 17, of which waited for: 7 -> 7; matrix products, arithmetic and copies ran while one was open for 1% -> 1% of each run, Pallas kernels for 4% -> 4%
where the time goes in v7:
time: 92.6 us; the launch traced here: 92.1 us
  Pallas kernels  34.6 us (37%)
  starting transfers between devices  22.9 us (25%)
  waiting for transfers between devices  20.8 us (22%)
  blocking collectives  12.3 us (13%)
    pallas_call x6, Pallas kernels, run(): return kernel(*placed)  34.6 us
    ppermute x16, starting transfers between devices, send(): return lax.ppermute(message, LINE, line_pairs(plan, target))  19.4 us
    ppermute x16, waiting for transfers between devices, send(): return lax.ppermute(message, LINE, line_pairs(plan, target))  14 us
    all_to_all x1, blocking collectives, everywhere(): lax.all_to_all(message, axes, split_axis=0, concat_axis=0, tiled=True)  12.3 us
    all_to_all x1, waiting for transfers between devices, everywhere(): lax.all_to_all(message, axes, split_axis=0, concat_axis=0, tiled=True)  6.79 us
    all_to_all x1, starting transfers between devices, everywhere(): lax.all_to_all(message, axes, split_axis=0, concat_axis=0, tiled=True)  3.5 us
  transfers between devices with their start and end apart: 17, of which 7 were waited for; matrix products, arithmetic and copies ran while one was open for 1% of the time, Pallas kernels for 4%

profile of v7, /device:TPU:0, one launch (start us, length us, event | category | flops | bytes accessed | tf_op | source)
XLA Modules:
  0.0 92.1 jit_solution(11739799161556085689)
XLA Ops:
  0.6 0.5 collective-permute-start
  1.1 0.1 collective-permute-start.1
  1.2 0.4 collective-permute-start.2
  1.7 0.1 collective-permute-start.3
  1.7 0.4 collective-permute-start.4
  2.2 0.7 collective-permute-done.refs_6_.refs_10_
  2.9 0.4 collective-permute-start.5
  3.3 0.7 pad.4.refs_13_.refs_17_.refs_18_
  4.0 0.4 collective-permute-done.2.refs_8_.refs_12_
  4.4 0.7 collective-permute-done.3.refs_9_.refs_13_
  5.1 0.7 collective-permute-done.4.refs_10_.refs_14_
  5.9 0.7 collective-permute-done.5.refs_11_.refs_15_
  6.6 2.8 %pack.1 = (f32[27,32,128]{2,1,0:T(8,128)}, f32[26,32,128]{2,1,0:T(8,128)}, f32[131,8,128]{2,1,0:T(8,128)}, f32[27,8,128]{2,1,0:T(8,128)}, f32[8,8,128]{2,1,0:T(8,128)}) custom-call(f32[1,32,32,128]{3,2,1,0:T(8,128)} %refs_4_.3, f32[1,32,32,128]{3,2,1,0:T(8,128)} %refs_5_.3, f32[1,32,32,128]{3,2,1,0:T(8,128)} %refs_6_.1, f32[1,32,32,128]{3,2,1,0:T(8,128)} %refs_7_.1, ...), custom_call_target="tpu_custom_call" | custom-call | bytes 4000000 | tf_op jit(solution)/shard_map/pack/pallas_call | solution.py:123
  9.4 2.9 %collective-permute-start.6 = (f32[131,8,128]{2,1,0:T(8,128)}, f32[131,8,128]{2,1,0:T(8,128)S(1)}, u32[]{:S(2)}, u32[]{:S(2)}) collective-permute-start(f32[131,8,128]{2,1,0:T(8,128)} %get-tuple-element.36), channel_id=1, source_target_pairs={{0,2},{1,3},{2,0},{3,1},{4,6},{5,7},{6,4},{7,5},{8,10},{9,11},{10,... | collective-permute-start | bytes 1609736 | tf_op jit(solution)/shard_map/ppermute | solution.py:861
  12.3 0.7 collective-permute-start.8
  13.0 0.7 collective-permute-start.9
  13.7 0.7 collective-permute-start.7
  14.4 10.6 %collective-permute-done.6.refs_0_ = f32[131,8,128]{2,1,0:T(8,128)S(1)} collective-permute-done((f32[131,8,128]{2,1,0:T(8,128)}, f32[131,8,128]{2,1,0:T(8,128)S(1)}, u32[]{:S(2)}, u32[]{:S(2)}) %collective-permute-start.6) | collective-permute-done | bytes 536608 | tf_op jit(solution)/shard_map/ppermute | solution.py:861
  25.0 13.6 %first_round.1 = (f32[12,16,32,128]{3,2,1,0:T(8,128)}, f32[12,4,32,128]{3,2,1,0:T(8,128)}, f32[16,8,128]{2,1,0:T(8,128)}, f32[24,48,128]{2,1,0:T(8,128)}, f32[48...) custom-call(f32[131,8,128]{2,1,0:T(8,128)S(1)} %collective-permute-done.6.refs_0_, ...), custom_call_target="tpu_custom_call" | custom-call | flops 73728000 | bytes 10000000 | tf_op jit(solution)/shard_map/first_round/pallas_call | solution.py:123
  38.7 0.7 collective-permute-start.13
  39.4 7.7 %collective-permute-start.14 = (f32[12,4,32,128]{3,2,1,0:T(8,128)}, f32[12,4,32,128]{3,2,1,0:T(8,128)S(1)}, u32[]{:S(2)}, u32[]{:S(2)}) collective-permute-start(f32[12,4,32,128]{3,2,1,0:T(8,128)} %get-tuple-element.45), channel_id=1, source_target_pairs={{0,1},{1,0},{2,3},{3,2},{4,5},{5,4},{6,7},{7,6},{8,9},{9,8},{10,11... | collective-permute-start | bytes 2359304 | tf_op jit(solution)/shard_map/ppermute | solution.py:861
  47.0 1.5 %collective-permute-start.10 = (f32[96,8,128]{2,1,0:T(8,128)}, f32[96,8,128]{2,1,0:T(8,128)S(1)}, u32[]{:S(2)}, u32[]{:S(2)}) collective-permute-start(f32[96,8,128]{2,1,0:T(8,128)} %get-tuple-element.41), channel_id=1, source_target_pairs={{0,2},{1,3},{2,0},{3,1},{4,6},{5,7},{6,4},{7,5},{8,10},{9,11},{10,... | collective-permute-start | bytes 1179656 | tf_op jit(solution)/shard_map/ppermute | solution.py:861
  48.5 3.5 %all-to-all-start = ((f32[16,8,128]{2,1,0:T(8,128)}), f32[16,8,128]{2,1,0:T(8,128)S(1)}, u32[]{:S(2)}, u32[]{:S(2)}) async-start(f32[16,8,128]{2,1,0:T(8,128)} %get-tuple-element.48), calls=%async_computation | async-start | bytes 131072 | tf_op jit(solution)/shard_map/all_to_all | solution.py:864
  52.1 1.6 %collective-permute-start.11 = (f32[24,8,128]{2,1,0:T(8,128)}, f32[24,8,128]{2,1,0:T(8,128)S(1)}, u32[]{:S(2)}, u32[]{:S(2)}) collective-permute-start(f32[24,8,128]{2,1,0:T(8,128)} %get-tuple-element.42), channel_id=1, source_target_pairs={{0,3},{1,2},{2,1},{3,0},{4,7},{5,6},{6,5},{7,4},{8,11},{9,10},{10,... | collective-permute-start | bytes 294920 | tf_op jit(solution)/shard_map/ppermute | solution.py:861
  53.6 0.7 collective-permute-start.12
  54.3 6.8 %all-to-all-done.refs_0_ = f32[16,8,128]{2,1,0:T(8,128)S(1)} async-done(((f32[16,8,128]{2,1,0:T(8,128)}), f32[16,8,128]{2,1,0:T(8,128)S(1)}, u32[]{:S(2)}, u32[]{:S(2)}) %all-to-all-start) | async-done | bytes 65568 | tf_op jit(solution)/shard_map/all_to_all | solution.py:864
  61.1 1.6 %carriers.2 = (f32[48,128]{1,0:T(8,128)}, f32[6,40,128]{2,1,0:T(8,128)}) custom-call(f32[16,8,128]{2,1,0:T(8,128)S(1)} %all-to-all-done.refs_0_), custom_call_target="tpu_custom_call" | custom-call | flops 2000000 | bytes 1000000 | tf_op jit(solution)/shard_map/carriers/pallas_call | solution.py:123
  62.8 13.2 %second_round.1 = (f32[1,32,32,128]{3,2,1,0:T(8,128)}, f32[1,32,32,128]{3,2,1,0:T(8,128)}, f32[1,32,32,128]{3,2,1,0:T(8,128)}, f32[1,32,32,128]{3,2,1,0:T(8,128)...) custom-call(f32[96,8,128]{2,1,0:T(8,128)S(1)} %collective-permute-do, ...), custom_call_target="tpu_custom_call" | custom-call | flops 73728000 | bytes 10000000 | tf_op jit(solution)/shard_map/second_round/pallas_call | solution.py:123
  75.9 0.4 collective-permute-start.15
  76.3 12.3 %all_to_all.10.refs_0_ = f32[16,8,128]{2,1,0:T(8,128)S(1)} all-to-all(f32[16,8,128]{2,1,0:T(8,128)} %get-tuple-element.63), channel_id=1, replica_groups=mesh['group'=2,'gz'=4,'gx'=2,'af'=2] {'gz','gx','af'}, dimensions={0} | all-to-all | bytes 131072 | tf_op jit(solution)/shard_map/all_to_all | solution.py:864
  88.7 2.1 %carriers.3 = f32[4,16]{1,0:T(4,128)} custom-call(f32[16,8,128]{2,1,0:T(8,128)S(1)} %all_to_all.10.refs_0_, f32[48,128]{1,0:T(8,128)} %get-tuple-element.64.refs_1_), custom_call_target="tpu_custom_call" | custom-call | flops 2000000 | bytes 1000000 | tf_op jit(solution)/shard_map/carriers/pallas_call | solution.py:123
  90.7 1.4 %join.1 = (f32[1,32,32,128]{3,2,1,0:T(8,128)}, f32[1,32,32,128]{3,2,1,0:T(8,128)}, f32[1,32,32,128]{3,2,1,0:T(8,128)}, f32[1,32,32,128]{3,2,1,0:T(8,128)}, f32[1...) custom-call(f32[1,32,32,128]{3,2,1,0:T(8,128)} %get-tuple-element.50, ...), custom_call_target="tpu_custom_call", output_to_operand_aliasing={{0}: (0, {}), {1}: (1, {}), {2}: (2, {}), {3}: (3, {}), {4}... | custom-call | bytes 3000000 | tf_op jit(solution)/shard_map/join/pallas_call | solution.py:123
  (10 shorter events, 0.0 us)
Async XLA Ops:
  0.6 2.3 %collective-permute-start = (f32[1,32,32,128]{3,2,1,0:T(8,128)}, f32[1,32,32,128]{3,2,1,0:T(8,128)S(1)}, u32[]{:S(2)}, u32[]{:S(2)}) collective-permute-start(f32[1,32,32,128]{3,2,1,0:T(8,128)} %refs_4_.3), channel_id=1, source_target_pairs={{0,1},{1,0},{2,3},{3,2},{4,5},{5,4},{6,7},{7,6},{8,9},{9,8},{10,11... | collective-permute-start | bytes 1572872 | tf_op jit(solution)/shard_map/ppermute | solution.py:861
  1.1 2.8 %collective-permute-start.1 = (f32[1,32,32,128]{3,2,1,0:T(8,128)}, f32[1,32,32,128]{3,2,1,0:T(8,128)S(1)}, u32[]{:S(2)}, u32[]{:S(2)}) collective-permute-start(f32[1,32,32,128]{3,2,1,0:T(8,128)} %refs_5_.3), channel_id=1, source_target_pairs={{0,1},{1,0},{2,3},{3,2},{4,5},{5,4},{6,7},{7,6},{8,9},{9,8},{10,11... | collective-permute-start | bytes 1572872 | tf_op jit(solution)/shard_map/ppermute | solution.py:861
  1.2 3.2 %collective-permute-start.2 = (f32[1,32,32,128]{3,2,1,0:T(8,128)}, f32[1,32,32,128]{3,2,1,0:T(8,128)S(1)}, u32[]{:S(2)}, u32[]{:S(2)}) collective-permute-start(f32[1,32,32,128]{3,2,1,0:T(8,128)} %refs_6_.1), channel_id=1, source_target_pairs={{0,1},{1,0},{2,3},{3,2},{4,5},{5,4},{6,7},{7,6},{8,9},{9,8},{10,11... | collective-permute-start | bytes 1572872 | tf_op jit(solution)/shard_map/ppermute | solution.py:861
  1.7 3.5 %collective-permute-start.3 = (f32[1,32,32,128]{3,2,1,0:T(8,128)}, f32[1,32,32,128]{3,2,1,0:T(8,128)S(1)}, u32[]{:S(2)}, u32[]{:S(2)}) collective-permute-start(f32[1,32,32,128]{3,2,1,0:T(8,128)} %refs_7_.1), channel_id=1, source_target_pairs={{0,1},{1,0},{2,3},{3,2},{4,5},{5,4},{6,7},{7,6},{8,9},{9,8},{10,11... | collective-permute-start | bytes 1572872 | tf_op jit(solution)/shard_map/ppermute | solution.py:861
  1.7 4.2 %collective-permute-start.4 = (f32[1,32,32,128]{3,2,1,0:T(8,128)}, f32[1,32,32,128]{3,2,1,0:T(8,128)S(1)}, u32[]{:S(2)}, u32[]{:S(2)}) collective-permute-start(f32[1,32,32,128]{3,2,1,0:T(8,128)} %refs_8_.1), channel_id=1, source_target_pairs={{0,1},{1,0},{2,3},{3,2},{4,5},{5,4},{6,7},{7,6},{8,9},{9,8},{10,11... | collective-permute-start | bytes 1572872 | tf_op jit(solution)/shard_map/ppermute | solution.py:861
  2.9 3.7 %collective-permute-start.5 = (f32[1,32,32,128]{3,2,1,0:T(8,128)}, f32[1,32,32,128]{3,2,1,0:T(8,128)S(1)}, u32[]{:S(2)}, u32[]{:S(2)}) collective-permute-start(f32[1,32,32,128]{3,2,1,0:T(8,128)} %refs_9_.1), channel_id=1, source_target_pairs={{0,1},{1,0},{2,3},{3,2},{4,5},{5,4},{6,7},{7,6},{8,9},{9,8},{10,11... | collective-permute-start | bytes 1572872 | tf_op jit(solution)/shard_map/ppermute | solution.py:861
  9.4 15.6 %collective-permute-start.6 = (f32[131,8,128]{2,1,0:T(8,128)}, f32[131,8,128]{2,1,0:T(8,128)S(1)}, u32[]{:S(2)}, u32[]{:S(2)}) collective-permute-start(f32[131,8,128]{2,1,0:T(8,128)} %get-tuple-element.36), channel_id=1, source_target_pairs={{0,2},{1,3},{2,0},{3,1},{4,6},{5,7},{6,4},{7,5},{8,10},{9,11},{10,... | collective-permute-start | bytes 1609736 | tf_op jit(solution)/shard_map/ppermute | solution.py:861
  12.3 2.1 %collective-permute-start.8 = (f32[27,32,128]{2,1,0:T(8,128)}, f32[27,32,128]{2,1,0:T(8,128)S(1)}, u32[]{:S(2)}, u32[]{:S(2)}) collective-permute-start(f32[27,32,128]{2,1,0:T(8,128)} %get-tuple-element.38), channel_id=1, source_target_pairs={{1,4},{3,6},{4,1},{5,8},{6,3},{7,10},{8,5},{9,12},{10,7},{11,14},{... | collective-permute-start | bytes 1327112 | tf_op jit(solution)/shard_map/ppermute | solution.py:861
  13.0 1.4 %collective-permute-start.9 = (f32[26,32,128]{2,1,0:T(8,128)}, f32[26,32,128]{2,1,0:T(8,128)S(1)}, u32[]{:S(2)}, u32[]{:S(2)}) collective-permute-start(f32[26,32,128]{2,1,0:T(8,128)} %get-tuple-element.39), channel_id=1, source_target_pairs={{1,4},{3,6},{4,1},{5,8},{6,3},{7,10},{8,5},{9,12},{10,7},{11,14},{... | collective-permute-start | bytes 1277960 | tf_op jit(solution)/shard_map/ppermute | solution.py:861
  13.7 0.7 collective-permute-start.7
  38.7 24.1 %collective-permute-start.13 = (f32[48,32,128]{2,1,0:T(8,128)}, f32[48,32,128]{2,1,0:T(8,128)S(1)}, u32[]{:S(2)}, u32[]{:S(2)}) collective-permute-start(f32[48,32,128]{2,1,0:T(8,128)} %get-tuple-element.44), channel_id=1, source_target_pairs={{1,4},{3,6},{4,1},{5,8},{6,3},{7,10},{8,5},{9,12},{10,7},{11,14},{... | collective-permute-start | bytes 2359304 | tf_op jit(solution)/shard_map/ppermute | solution.py:861
  39.4 23.4 %collective-permute-start.14 = (f32[12,4,32,128]{3,2,1,0:T(8,128)}, f32[12,4,32,128]{3,2,1,0:T(8,128)S(1)}, u32[]{:S(2)}, u32[]{:S(2)}) collective-permute-start(f32[12,4,32,128]{3,2,1,0:T(8,128)} %get-tuple-element.45), channel_id=1, source_target_pairs={{0,1},{1,0},{2,3},{3,2},{4,5},{5,4},{6,7},{7,6},{8,9},{9,8},{10,11... | collective-permute-start | bytes 2359304 | tf_op jit(solution)/shard_map/ppermute | solution.py:861
  47.0 15.7 %collective-permute-start.10 = (f32[96,8,128]{2,1,0:T(8,128)}, f32[96,8,128]{2,1,0:T(8,128)S(1)}, u32[]{:S(2)}, u32[]{:S(2)}) collective-permute-start(f32[96,8,128]{2,1,0:T(8,128)} %get-tuple-element.41), channel_id=1, source_target_pairs={{0,2},{1,3},{2,0},{3,1},{4,6},{5,7},{6,4},{7,5},{8,10},{9,11},{10,... | collective-permute-start | bytes 1179656 | tf_op jit(solution)/shard_map/ppermute | solution.py:861
  48.5 12.5 %all-to-all-start = ((f32[16,8,128]{2,1,0:T(8,128)}), f32[16,8,128]{2,1,0:T(8,128)S(1)}, u32[]{:S(2)}, u32[]{:S(2)}) async-start(f32[16,8,128]{2,1,0:T(8,128)} %get-tuple-element.48), calls=%async_computation | async-start | bytes 131072 | tf_op jit(solution)/shard_map/all_to_all | solution.py:864
  52.1 10.7 %collective-permute-start.11 = (f32[24,8,128]{2,1,0:T(8,128)}, f32[24,8,128]{2,1,0:T(8,128)S(1)}, u32[]{:S(2)}, u32[]{:S(2)}) collective-permute-start(f32[24,8,128]{2,1,0:T(8,128)} %get-tuple-element.42), channel_id=1, source_target_pairs={{0,3},{1,2},{2,1},{3,0},{4,7},{5,6},{6,5},{7,4},{8,11},{9,10},{10,... | collective-permute-start | bytes 294920 | tf_op jit(solution)/shard_map/ppermute | solution.py:861
  53.6 9.1 %collective-permute-start.12 = (f32[24,8,128]{2,1,0:T(8,128)}, f32[24,8,128]{2,1,0:T(8,128)S(1)}, u32[]{:S(2)}, u32[]{:S(2)}) collective-permute-start(f32[24,8,128]{2,1,0:T(8,128)} %get-tuple-element.43), channel_id=1, source_target_pairs={{1,6},{3,4},{4,3},{5,10},{6,1},{7,8},{8,7},{9,14},{10,5},{11,12},{... | collective-permute-start | bytes 294920 | tf_op jit(solution)/shard_map/ppermute | solution.py:861
  75.9 14.8 %collective-permute-start.15 = (f32[6,16,32,128]{3,2,1,0:T(8,128)}, f32[6,16,32,128]{3,2,1,0:T(8,128)S(1)}, u32[]{:S(2)}, u32[]{:S(2)}) collective-permute-start(f32[6,16,32,128]{3,2,1,0:T(8,128)} %get-tuple-element.56), channel_id=1, source_target_pairs={{0,1},{1,0},{2,3},{3,2},{4,5},{5,4},{6,7},{7,6},{8,9},{9,8},{10,11... | collective-permute-start | bytes 4718600 | tf_op jit(solution)/shard_map/ppermute | solution.py:861

commit v8 on v7

--- a/solution.py
+++ b/solution.py
@@ -396,7 +396,7 @@
     def substep(old, new, n):
         begin = jnp.where(at_low, DEEP, n + 1)
         end = jnp.where(at_high, DEEP + plan.own, plan.ext - 1 - n)
-        odd = lax.rem(end - begin, 2)
+        rest = lax.rem(end - begin, 4)
 
         @pl.when(jnp.logical_not(at_low))
         def _():
@@ -413,17 +413,17 @@
                 for s in range(2):
                     magnetic(old, new, s, p + 1, t)
 
-        @pl.when(odd == 1)
-        def _():
-            advance(begin)
-
-        def step(m, _):
-            p = begin + odd + 2 * m
-            advance(p)
-            advance(p + 1)
+        def one(m, _):
+            advance(begin + m)
             return 0
 
-        lax.fori_loop(0, (end - begin) // 2, step, 0)
+        def four(m, _):
+            for h in range(4):
+                advance(begin + rest + 4 * m + h)
+            return 0
+
+        lax.fori_loop(0, rest, one, 0)
+        lax.fori_loop(0, (end - begin) // 4, four, 0)
 
     def pair(m, _):
         substep(first, second, 2 * m)

time: 92.6 us -> 91.6 us (0.989)
  no operation moved by 1% of the time
where the time goes in v8:
time: 91.6 us; the launch traced here: 91.1 us
  Pallas kernels  33.7 us (37%)
  starting transfers between devices  22.7 us (25%)
  waiting for transfers between devices  20.8 us (23%)
  blocking collectives  12.3 us (13%)
    pallas_call x6, Pallas kernels, run(): return kernel(*placed)  33.7 us
    ppermute x16, starting transfers between devices, send(): return lax.ppermute(message, LINE, line_pairs(plan, target))  19.2 us
    ppermute x16, waiting for transfers between devices, send(): return lax.ppermute(message, LINE, line_pairs(plan, target))  14 us
    all_to_all x1, blocking collectives, everywhere(): lax.all_to_all(message, axes, split_axis=0, concat_axis=0, tiled=True)  12.3 us
    all_to_all x1, waiting for transfers between devices, everywhere(): lax.all_to_all(message, axes, split_axis=0, concat_axis=0, tiled=True)  6.79 us
    all_to_all x1, starting transfers between devices, everywhere(): lax.all_to_all(message, axes, split_axis=0, concat_axis=0, tiled=True)  3.5 us
  transfers between devices with their start and end apart: 17, of which 7 were waited for; matrix products, arithmetic and copies ran while one was open for 1% of the time, Pallas kernels for 4%

profile of v8, /device:TPU:0, one launch (start us, length us, event | category | flops | bytes accessed | tf_op | source)
XLA Modules:
  0.0 91.1 jit_solution(18266835597202082691)
XLA Ops:
  0.6 0.5 collective-permute-start
  1.1 0.1 collective-permute-start.1
  1.2 0.4 collective-permute-start.2
  1.7 0.1 collective-permute-start.3
  1.7 0.4 collective-permute-start.4
  2.2 0.7 collective-permute-done.refs_6_.refs_10_
  2.9 0.4 collective-permute-start.5
  3.3 0.7 pad.4.refs_13_.refs_17_.refs_18_
  4.0 0.4 collective-permute-done.2.refs_8_.refs_12_
  4.4 0.7 collective-permute-done.3.refs_9_.refs_13_
  5.1 0.7 collective-permute-done.4.refs_10_.refs_14_
  5.9 0.7 collective-permute-done.5.refs_11_.refs_15_
  6.6 2.8 %pack.1 = (f32[27,32,128]{2,1,0:T(8,128)}, f32[26,32,128]{2,1,0:T(8,128)}, f32[131,8,128]{2,1,0:T(8,128)}, f32[27,8,128]{2,1,0:T(8,128)}, f32[8,8,128]{2,1,0:T(8,128)}) custom-call(f32[1,32,32,128]{3,2,1,0:T(8,128)} %refs_4_.3, f32[1,32,32,128]{3,2,1,0:T(8,128)} %refs_5_.3, f32[1,32,32,128]{3,2,1,0:T(8,128)} %refs_6_.1, f32[1,32,32,128]{3,2,1,0:T(8,128)} %refs_7_.1, ...), custom_call_target="tpu_custom_call" | custom-call | bytes 4000000 | tf_op jit(solution)/shard_map/pack/pallas_call | solution.py:123
  9.4 2.9 %collective-permute-start.6 = (f32[131,8,128]{2,1,0:T(8,128)}, f32[131,8,128]{2,1,0:T(8,128)S(1)}, u32[]{:S(2)}, u32[]{:S(2)}) collective-permute-start(f32[131,8,128]{2,1,0:T(8,128)} %get-tuple-element.36), channel_id=1, source_target_pairs={{0,2},{1,3},{2,0},{3,1},{4,6},{5,7},{6,4},{7,5},{8,10},{9,11},{10,... | collective-permute-start | bytes 1609736 | tf_op jit(solution)/shard_map/ppermute | solution.py:861
  12.3 0.7 collective-permute-start.8
  13.0 0.7 collective-permute-start.9
  13.7 0.7 collective-permute-start.7
  14.4 10.6 %collective-permute-done.6.refs_0_ = f32[131,8,128]{2,1,0:T(8,128)S(1)} collective-permute-done((f32[131,8,128]{2,1,0:T(8,128)}, f32[131,8,128]{2,1,0:T(8,128)S(1)}, u32[]{:S(2)}, u32[]{:S(2)}) %collective-permute-start.6) | collective-permute-done | bytes 536608 | tf_op jit(solution)/shard_map/ppermute | solution.py:861
  25.0 13.2 %first_round.1 = (f32[12,16,32,128]{3,2,1,0:T(8,128)}, f32[12,4,32,128]{3,2,1,0:T(8,128)}, f32[16,8,128]{2,1,0:T(8,128)}, f32[24,48,128]{2,1,0:T(8,128)}, f32[48...) custom-call(f32[131,8,128]{2,1,0:T(8,128)S(1)} %collective-permute-done.6.refs_0_, ...), custom_call_target="tpu_custom_call" | custom-call | flops 73728000 | bytes 10000000 | tf_op jit(solution)/shard_map/first_round/pallas_call | solution.py:123
  38.2 0.7 collective-permute-start.13
  38.9 7.6 %collective-permute-start.14 = (f32[12,4,32,128]{3,2,1,0:T(8,128)}, f32[12,4,32,128]{3,2,1,0:T(8,128)S(1)}, u32[]{:S(2)}, u32[]{:S(2)}) collective-permute-start(f32[12,4,32,128]{3,2,1,0:T(8,128)} %get-tuple-element.45), channel_id=1, source_target_pairs={{0,1},{1,0},{2,3},{3,2},{4,5},{5,4},{6,7},{7,6},{8,9},{9,8},{10,11... | collective-permute-start | bytes 2359304 | tf_op jit(solution)/shard_map/ppermute | solution.py:861
  46.5 1.5 %collective-permute-start.10 = (f32[96,8,128]{2,1,0:T(8,128)}, f32[96,8,128]{2,1,0:T(8,128)S(1)}, u32[]{:S(2)}, u32[]{:S(2)}) collective-permute-start(f32[96,8,128]{2,1,0:T(8,128)} %get-tuple-element.41), channel_id=1, source_target_pairs={{0,2},{1,3},{2,0},{3,1},{4,6},{5,7},{6,4},{7,5},{8,10},{9,11},{10,... | collective-permute-start | bytes 1179656 | tf_op jit(solution)/shard_map/ppermute | solution.py:861
  48.0 3.5 %all-to-all-start = ((f32[16,8,128]{2,1,0:T(8,128)}), f32[16,8,128]{2,1,0:T(8,128)S(1)}, u32[]{:S(2)}, u32[]{:S(2)}) async-start(f32[16,8,128]{2,1,0:T(8,128)} %get-tuple-element.48), calls=%async_computation | async-start | bytes 131072 | tf_op jit(solution)/shard_map/all_to_all | solution.py:864
  51.6 1.6 %collective-permute-start.11 = (f32[24,8,128]{2,1,0:T(8,128)}, f32[24,8,128]{2,1,0:T(8,128)S(1)}, u32[]{:S(2)}, u32[]{:S(2)}) collective-permute-start(f32[24,8,128]{2,1,0:T(8,128)} %get-tuple-element.42), channel_id=1, source_target_pairs={{0,3},{1,2},{2,1},{3,0},{4,7},{5,6},{6,5},{7,4},{8,11},{9,10},{10,... | collective-permute-start | bytes 294920 | tf_op jit(solution)/shard_map/ppermute | solution.py:861
  53.1 0.7 collective-permute-start.12
  53.8 6.8 %all-to-all-done.refs_0_ = f32[16,8,128]{2,1,0:T(8,128)S(1)} async-done(((f32[16,8,128]{2,1,0:T(8,128)}), f32[16,8,128]{2,1,0:T(8,128)S(1)}, u32[]{:S(2)}, u32[]{:S(2)}) %all-to-all-start) | async-done | bytes 65568 | tf_op jit(solution)/shard_map/all_to_all | solution.py:864
  60.6 1.6 %carriers.2 = (f32[48,128]{1,0:T(8,128)}, f32[6,40,128]{2,1,0:T(8,128)}) custom-call(f32[16,8,128]{2,1,0:T(8,128)S(1)} %all-to-all-done.refs_0_), custom_call_target="tpu_custom_call" | custom-call | flops 2000000 | bytes 1000000 | tf_op jit(solution)/shard_map/carriers/pallas_call | solution.py:123
  62.3 12.7 %second_round.1 = (f32[1,32,32,128]{3,2,1,0:T(8,128)}, f32[1,32,32,128]{3,2,1,0:T(8,128)}, f32[1,32,32,128]{3,2,1,0:T(8,128)}, f32[1,32,32,128]{3,2,1,0:T(8,128)...) custom-call(f32[96,8,128]{2,1,0:T(8,128)S(1)} %collective-permute-do, ...), custom_call_target="tpu_custom_call" | custom-call | flops 73728000 | bytes 10000000 | tf_op jit(solution)/shard_map/second_round/pallas_call | solution.py:123
  75.0 0.3 collective-permute-start.15
  75.3 12.3 %all_to_all.10.refs_0_ = f32[16,8,128]{2,1,0:T(8,128)S(1)} all-to-all(f32[16,8,128]{2,1,0:T(8,128)} %get-tuple-element.63), channel_id=1, replica_groups=mesh['group'=2,'gz'=4,'gx'=2,'af'=2] {'gz','gx','af'}, dimensions={0} | all-to-all | bytes 131072 | tf_op jit(solution)/shard_map/all_to_all | solution.py:864
  87.7 2.1 %carriers.3 = f32[4,16]{1,0:T(4,128)} custom-call(f32[16,8,128]{2,1,0:T(8,128)S(1)} %all_to_all.10.refs_0_, f32[48,128]{1,0:T(8,128)} %get-tuple-element.64.refs_1_), custom_call_target="tpu_custom_call" | custom-call | flops 2000000 | bytes 1000000 | tf_op jit(solution)/shard_map/carriers/pallas_call | solution.py:123
  89.7 1.4 %join.1 = (f32[1,32,32,128]{3,2,1,0:T(8,128)}, f32[1,32,32,128]{3,2,1,0:T(8,128)}, f32[1,32,32,128]{3,2,1,0:T(8,128)}, f32[1,32,32,128]{3,2,1,0:T(8,128)}, f32[1...) custom-call(f32[1,32,32,128]{3,2,1,0:T(8,128)} %get-tuple-element.50, ...), custom_call_target="tpu_custom_call", output_to_operand_aliasing={{0}: (0, {}), {1}: (1, {}), {2}: (2, {}), {3}: (3, {}), {4}... | custom-call | bytes 3000000 | tf_op jit(solution)/shard_map/join/pallas_call | solution.py:123
  (10 shorter events, 0.0 us)
Async XLA Ops:
  0.6 2.3 %collective-permute-start = (f32[1,32,32,128]{3,2,1,0:T(8,128)}, f32[1,32,32,128]{3,2,1,0:T(8,128)S(1)}, u32[]{:S(2)}, u32[]{:S(2)}) collective-permute-start(f32[1,32,32,128]{3,2,1,0:T(8,128)} %refs_4_.3), channel_id=1, source_target_pairs={{0,1},{1,0},{2,3},{3,2},{4,5},{5,4},{6,7},{7,6},{8,9},{9,8},{10,11... | collective-permute-start | bytes 1572872 | tf_op jit(solution)/shard_map/ppermute | solution.py:861
  1.1 2.8 %collective-permute-start.1 = (f32[1,32,32,128]{3,2,1,0:T(8,128)}, f32[1,32,32,128]{3,2,1,0:T(8,128)S(1)}, u32[]{:S(2)}, u32[]{:S(2)}) collective-permute-start(f32[1,32,32,128]{3,2,1,0:T(8,128)} %refs_5_.3), channel_id=1, source_target_pairs={{0,1},{1,0},{2,3},{3,2},{4,5},{5,4},{6,7},{7,6},{8,9},{9,8},{10,11... | collective-permute-start | bytes 1572872 | tf_op jit(solution)/shard_map/ppermute | solution.py:861
  1.2 3.2 %collective-permute-start.2 = (f32[1,32,32,128]{3,2,1,0:T(8,128)}, f32[1,32,32,128]{3,2,1,0:T(8,128)S(1)}, u32[]{:S(2)}, u32[]{:S(2)}) collective-permute-start(f32[1,32,32,128]{3,2,1,0:T(8,128)} %refs_6_.1), channel_id=1, source_target_pairs={{0,1},{1,0},{2,3},{3,2},{4,5},{5,4},{6,7},{7,6},{8,9},{9,8},{10,11... | collective-permute-start | bytes 1572872 | tf_op jit(solution)/shard_map/ppermute | solution.py:861
  1.7 3.5 %collective-permute-start.3 = (f32[1,32,32,128]{3,2,1,0:T(8,128)}, f32[1,32,32,128]{3,2,1,0:T(8,128)S(1)}, u32[]{:S(2)}, u32[]{:S(2)}) collective-permute-start(f32[1,32,32,128]{3,2,1,0:T(8,128)} %refs_7_.1), channel_id=1, source_target_pairs={{0,1},{1,0},{2,3},{3,2},{4,5},{5,4},{6,7},{7,6},{8,9},{9,8},{10,11... | collective-permute-start | bytes 1572872 | tf_op jit(solution)/shard_map/ppermute | solution.py:861
  1.7 4.2 %collective-permute-start.4 = (f32[1,32,32,128]{3,2,1,0:T(8,128)}, f32[1,32,32,128]{3,2,1,0:T(8,128)S(1)}, u32[]{:S(2)}, u32[]{:S(2)}) collective-permute-start(f32[1,32,32,128]{3,2,1,0:T(8,128)} %refs_8_.1), channel_id=1, source_target_pairs={{0,1},{1,0},{2,3},{3,2},{4,5},{5,4},{6,7},{7,6},{8,9},{9,8},{10,11... | collective-permute-start | bytes 1572872 | tf_op jit(solution)/shard_map/ppermute | solution.py:861
  2.9 3.7 %collective-permute-start.5 = (f32[1,32,32,128]{3,2,1,0:T(8,128)}, f32[1,32,32,128]{3,2,1,0:T(8,128)S(1)}, u32[]{:S(2)}, u32[]{:S(2)}) collective-permute-start(f32[1,32,32,128]{3,2,1,0:T(8,128)} %refs_9_.1), channel_id=1, source_target_pairs={{0,1},{1,0},{2,3},{3,2},{4,5},{5,4},{6,7},{7,6},{8,9},{9,8},{10,11... | collective-permute-start | bytes 1572872 | tf_op jit(solution)/shard_map/ppermute | solution.py:861
  9.4 15.6 %collective-permute-start.6 = (f32[131,8,128]{2,1,0:T(8,128)}, f32[131,8,128]{2,1,0:T(8,128)S(1)}, u32[]{:S(2)}, u32[]{:S(2)}) collective-permute-start(f32[131,8,128]{2,1,0:T(8,128)} %get-tuple-element.36), channel_id=1, source_target_pairs={{0,2},{1,3},{2,0},{3,1},{4,6},{5,7},{6,4},{7,5},{8,10},{9,11},{10,... | collective-permute-start | bytes 1609736 | tf_op jit(solution)/shard_map/ppermute | solution.py:861
  12.3 2.1 %collective-permute-start.8 = (f32[27,32,128]{2,1,0:T(8,128)}, f32[27,32,128]{2,1,0:T(8,128)S(1)}, u32[]{:S(2)}, u32[]{:S(2)}) collective-permute-start(f32[27,32,128]{2,1,0:T(8,128)} %get-tuple-element.38), channel_id=1, source_target_pairs={{1,4},{3,6},{4,1},{5,8},{6,3},{7,10},{8,5},{9,12},{10,7},{11,14},{... | collective-permute-start | bytes 1327112 | tf_op jit(solution)/shard_map/ppermute | solution.py:861
  13.0 1.4 %collective-permute-start.9 = (f32[26,32,128]{2,1,0:T(8,128)}, f32[26,32,128]{2,1,0:T(8,128)S(1)}, u32[]{:S(2)}, u32[]{:S(2)}) collective-permute-start(f32[26,32,128]{2,1,0:T(8,128)} %get-tuple-element.39), channel_id=1, source_target_pairs={{1,4},{3,6},{4,1},{5,8},{6,3},{7,10},{8,5},{9,12},{10,7},{11,14},{... | collective-permute-start | bytes 1277960 | tf_op jit(solution)/shard_map/ppermute | solution.py:861
  13.7 0.7 collective-permute-start.7
  38.2 24.0 %collective-permute-start.13 = (f32[48,32,128]{2,1,0:T(8,128)}, f32[48,32,128]{2,1,0:T(8,128)S(1)}, u32[]{:S(2)}, u32[]{:S(2)}) collective-permute-start(f32[48,32,128]{2,1,0:T(8,128)} %get-tuple-element.44), channel_id=1, source_target_pairs={{1,4},{3,6},{4,1},{5,8},{6,3},{7,10},{8,5},{9,12},{10,7},{11,14},{... | collective-permute-start | bytes 2359304 | tf_op jit(solution)/shard_map/ppermute | solution.py:861
  38.9 23.3 %collective-permute-start.14 = (f32[12,4,32,128]{3,2,1,0:T(8,128)}, f32[12,4,32,128]{3,2,1,0:T(8,128)S(1)}, u32[]{:S(2)}, u32[]{:S(2)}) collective-permute-start(f32[12,4,32,128]{3,2,1,0:T(8,128)} %get-tuple-element.45), channel_id=1, source_target_pairs={{0,1},{1,0},{2,3},{3,2},{4,5},{5,4},{6,7},{7,6},{8,9},{9,8},{10,11... | collective-permute-start | bytes 2359304 | tf_op jit(solution)/shard_map/ppermute | solution.py:861
  46.5 15.7 %collective-permute-start.10 = (f32[96,8,128]{2,1,0:T(8,128)}, f32[96,8,128]{2,1,0:T(8,128)S(1)}, u32[]{:S(2)}, u32[]{:S(2)}) collective-permute-start(f32[96,8,128]{2,1,0:T(8,128)} %get-tuple-element.41), channel_id=1, source_target_pairs={{0,2},{1,3},{2,0},{3,1},{4,6},{5,7},{6,4},{7,5},{8,10},{9,11},{10,... | collective-permute-start | bytes 1179656 | tf_op jit(solution)/shard_map/ppermute | solution.py:861
  48.0 12.5 %all-to-all-start = ((f32[16,8,128]{2,1,0:T(8,128)}), f32[16,8,128]{2,1,0:T(8,128)S(1)}, u32[]{:S(2)}, u32[]{:S(2)}) async-start(f32[16,8,128]{2,1,0:T(8,128)} %get-tuple-element.48), calls=%async_computation | async-start | bytes 131072 | tf_op jit(solution)/shard_map/all_to_all | solution.py:864
  51.6 10.7 %collective-permute-start.11 = (f32[24,8,128]{2,1,0:T(8,128)}, f32[24,8,128]{2,1,0:T(8,128)S(1)}, u32[]{:S(2)}, u32[]{:S(2)}) collective-permute-start(f32[24,8,128]{2,1,0:T(8,128)} %get-tuple-element.42), channel_id=1, source_target_pairs={{0,3},{1,2},{2,1},{3,0},{4,7},{5,6},{6,5},{7,4},{8,11},{9,10},{10,... | collective-permute-start | bytes 294920 | tf_op jit(solution)/shard_map/ppermute | solution.py:861
  53.1 9.1 %collective-permute-start.12 = (f32[24,8,128]{2,1,0:T(8,128)}, f32[24,8,128]{2,1,0:T(8,128)S(1)}, u32[]{:S(2)}, u32[]{:S(2)}) collective-permute-start(f32[24,8,128]{2,1,0:T(8,128)} %get-tuple-element.43), channel_id=1, source_target_pairs={{1,6},{3,4},{4,3},{5,10},{6,1},{7,8},{8,7},{9,14},{10,5},{11,12},{... | collective-permute-start | bytes 294920 | tf_op jit(solution)/shard_map/ppermute | solution.py:861
  75.0 14.7 %collective-permute-start.15 = (f32[6,16,32,128]{3,2,1,0:T(8,128)}, f32[6,16,32,128]{3,2,1,0:T(8,128)S(1)}, u32[]{:S(2)}, u32[]{:S(2)}) collective-permute-start(f32[6,16,32,128]{3,2,1,0:T(8,128)} %get-tuple-element.56), channel_id=1, source_target_pairs={{0,1},{1,0},{2,3},{3,2},{4,5},{5,4},{6,7},{7,6},{8,9},{9,8},{10,11... | collective-permute-start | bytes 4718600 | tf_op jit(solution)/shard_map/ppermute | solution.py:861

commit v9 on v8

--- a/solution.py
+++ b/solution.py
@@ -409,9 +409,9 @@
 
         def advance(p):
             for t in range(plan.tiles):
-                electric(old, new, p, t)
                 for s in range(2):
                     magnetic(old, new, s, p + 1, t)
+                electric(old, new, p, t)
 
         def one(m, _):
             advance(begin + m)

time: 91.6 us -> 91.6 us (level)
  no operation moved by 1% of the time
where the time goes in v9:
time: 91.6 us; the launch traced here: 91.1 us
  Pallas kernels  33.7 us (37%)
  starting transfers between devices  22.7 us (25%)
  waiting for transfers between devices  20.8 us (23%)
  blocking collectives  12.3 us (13%)
    pallas_call x6, Pallas kernels, run(): return kernel(*placed)  33.7 us
    ppermute x16, starting transfers between devices, send(): return lax.ppermute(message, LINE, line_pairs(plan, target))  19.2 us
    ppermute x16, waiting for transfers between devices, send(): return lax.ppermute(message, LINE, line_pairs(plan, target))  14 us
    all_to_all x1, blocking collectives, everywhere(): lax.all_to_all(message, axes, split_axis=0, concat_axis=0, tiled=True)  12.3 us
    all_to_all x1, waiting for transfers between devices, everywhere(): lax.all_to_all(message, axes, split_axis=0, concat_axis=0, tiled=True)  6.79 us
    all_to_all x1, starting transfers between devices, everywhere(): lax.all_to_all(message, axes, split_axis=0, concat_axis=0, tiled=True)  3.5 us
  transfers between devices with their start and end apart: 17, of which 7 were waited for; matrix products, arithmetic and copies ran while one was open for 1% of the time, Pallas kernels for 4%

profile of v9, /device:TPU:0, one launch (start us, length us, event | category | flops | bytes accessed | tf_op | source)
XLA Modules:
  0.0 91.1 jit_solution(11060751602209314022)
XLA Ops:
  0.6 0.5 collective-permute-start
  1.1 0.1 collective-permute-start.1
  1.2 0.4 collective-permute-start.2
  1.7 0.1 collective-permute-start.3
  1.7 0.4 collective-permute-start.4
  2.2 0.7 collective-permute-done.refs_6_.refs_10_
  2.9 0.4 collective-permute-start.5
  3.3 0.7 pad.4.refs_13_.refs_17_.refs_18_
  4.0 0.4 collective-permute-done.2.refs_8_.refs_12_
  4.4 0.7 collective-permute-done.3.refs_9_.refs_13_
  5.1 0.7 collective-permute-done.4.refs_10_.refs_14_
  5.9 0.7 collective-permute-done.5.refs_11_.refs_15_
  6.6 2.8 %pack.1 = (f32[27,32,128]{2,1,0:T(8,128)}, f32[26,32,128]{2,1,0:T(8,128)}, f32[131,8,128]{2,1,0:T(8,128)}, f32[27,8,128]{2,1,0:T(8,128)}, f32[8,8,128]{2,1,0:T(8,128)}) custom-call(f32[1,32,32,128]{3,2,1,0:T(8,128)} %refs_4_.3, f32[1,32,32,128]{3,2,1,0:T(8,128)} %refs_5_.3, f32[1,32,32,128]{3,2,1,0:T(8,128)} %refs_6_.1, f32[1,32,32,128]{3,2,1,0:T(8,128)} %refs_7_.1, ...), custom_call_target="tpu_custom_call" | custom-call | bytes 4000000 | tf_op jit(solution)/shard_map/pack/pallas_call | solution.py:123
  9.4 2.9 %collective-permute-start.6 = (f32[131,8,128]{2,1,0:T(8,128)}, f32[131,8,128]{2,1,0:T(8,128)S(1)}, u32[]{:S(2)}, u32[]{:S(2)}) collective-permute-start(f32[131,8,128]{2,1,0:T(8,128)} %get-tuple-element.36), channel_id=1, source_target_pairs={{0,2},{1,3},{2,0},{3,1},{4,6},{5,7},{6,4},{7,5},{8,10},{9,11},{10,... | collective-permute-start | bytes 1609736 | tf_op jit(solution)/shard_map/ppermute | solution.py:861
  12.3 0.7 collective-permute-start.8
  13.0 0.7 collective-permute-start.9
  13.7 0.7 collective-permute-start.7
  14.4 10.6 %collective-permute-done.6.refs_0_ = f32[131,8,128]{2,1,0:T(8,128)S(1)} collective-permute-done((f32[131,8,128]{2,1,0:T(8,128)}, f32[131,8,128]{2,1,0:T(8,128)S(1)}, u32[]{:S(2)}, u32[]{:S(2)}) %collective-permute-start.6) | collective-permute-done | bytes 536608 | tf_op jit(solution)/shard_map/ppermute | solution.py:861
  25.0 13.2 %first_round.1 = (f32[12,16,32,128]{3,2,1,0:T(8,128)}, f32[12,4,32,128]{3,2,1,0:T(8,128)}, f32[16,8,128]{2,1,0:T(8,128)}, f32[24,48,128]{2,1,0:T(8,128)}, f32[48...) custom-call(f32[131,8,128]{2,1,0:T(8,128)S(1)} %collective-permute-done.6.refs_0_, ...), custom_call_target="tpu_custom_call" | custom-call | flops 73728000 | bytes 10000000 | tf_op jit(solution)/shard_map/first_round/pallas_call | solution.py:123
  38.2 0.7 collective-permute-start.13
  38.9 7.6 %collective-permute-start.14 = (f32[12,4,32,128]{3,2,1,0:T(8,128)}, f32[12,4,32,128]{3,2,1,0:T(8,128)S(1)}, u32[]{:S(2)}, u32[]{:S(2)}) collective-permute-start(f32[12,4,32,128]{3,2,1,0:T(8,128)} %get-tuple-element.45), channel_id=1, source_target_pairs={{0,1},{1,0},{2,3},{3,2},{4,5},{5,4},{6,7},{7,6},{8,9},{9,8},{10,11... | collective-permute-start | bytes 2359304 | tf_op jit(solution)/shard_map/ppermute | solution.py:861
  46.5 1.5 %collective-permute-start.10 = (f32[96,8,128]{2,1,0:T(8,128)}, f32[96,8,128]{2,1,0:T(8,128)S(1)}, u32[]{:S(2)}, u32[]{:S(2)}) collective-permute-start(f32[96,8,128]{2,1,0:T(8,128)} %get-tuple-element.41), channel_id=1, source_target_pairs={{0,2},{1,3},{2,0},{3,1},{4,6},{5,7},{6,4},{7,5},{8,10},{9,11},{10,... | collective-permute-start | bytes 1179656 | tf_op jit(solution)/shard_map/ppermute | solution.py:861
  48.0 3.5 %all-to-all-start = ((f32[16,8,128]{2,1,0:T(8,128)}), f32[16,8,128]{2,1,0:T(8,128)S(1)}, u32[]{:S(2)}, u32[]{:S(2)}) async-start(f32[16,8,128]{2,1,0:T(8,128)} %get-tuple-element.48), calls=%async_computation | async-start | bytes 131072 | tf_op jit(solution)/shard_map/all_to_all | solution.py:864
  51.5 1.6 %collective-permute-start.11 = (f32[24,8,128]{2,1,0:T(8,128)}, f32[24,8,128]{2,1,0:T(8,128)S(1)}, u32[]{:S(2)}, u32[]{:S(2)}) collective-permute-start(f32[24,8,128]{2,1,0:T(8,128)} %get-tuple-element.42), channel_id=1, source_target_pairs={{0,3},{1,2},{2,1},{3,0},{4,7},{5,6},{6,5},{7,4},{8,11},{9,10},{10,... | collective-permute-start | bytes 294920 | tf_op jit(solution)/shard_map/ppermute | solution.py:861
  53.1 0.7 collective-permute-start.12
  53.8 6.8 %all-to-all-done.refs_0_ = f32[16,8,128]{2,1,0:T(8,128)S(1)} async-done(((f32[16,8,128]{2,1,0:T(8,128)}), f32[16,8,128]{2,1,0:T(8,128)S(1)}, u32[]{:S(2)}, u32[]{:S(2)}) %all-to-all-start) | async-done | bytes 65568 | tf_op jit(solution)/shard_map/all_to_all | solution.py:864
  60.6 1.6 %carriers.2 = (f32[48,128]{1,0:T(8,128)}, f32[6,40,128]{2,1,0:T(8,128)}) custom-call(f32[16,8,128]{2,1,0:T(8,128)S(1)} %all-to-all-done.refs_0_), custom_call_target="tpu_custom_call" | custom-call | flops 2000000 | bytes 1000000 | tf_op jit(solution)/shard_map/carriers/pallas_call | solution.py:123
  62.3 12.7 %second_round.1 = (f32[1,32,32,128]{3,2,1,0:T(8,128)}, f32[1,32,32,128]{3,2,1,0:T(8,128)}, f32[1,32,32,128]{3,2,1,0:T(8,128)}, f32[1,32,32,128]{3,2,1,0:T(8,128)...) custom-call(f32[96,8,128]{2,1,0:T(8,128)S(1)} %collective-permute-do, ...), custom_call_target="tpu_custom_call" | custom-call | flops 73728000 | bytes 10000000 | tf_op jit(solution)/shard_map/second_round/pallas_call | solution.py:123
  75.0 0.3 collective-permute-start.15
  75.3 12.3 %all_to_all.10.refs_0_ = f32[16,8,128]{2,1,0:T(8,128)S(1)} all-to-all(f32[16,8,128]{2,1,0:T(8,128)} %get-tuple-element.63), channel_id=1, replica_groups=mesh['group'=2,'gz'=4,'gx'=2,'af'=2] {'gz','gx','af'}, dimensions={0} | all-to-all | bytes 131072 | tf_op jit(solution)/shard_map/all_to_all | solution.py:864
  87.6 2.1 %carriers.3 = f32[4,16]{1,0:T(4,128)} custom-call(f32[16,8,128]{2,1,0:T(8,128)S(1)} %all_to_all.10.refs_0_, f32[48,128]{1,0:T(8,128)} %get-tuple-element.64.refs_1_), custom_call_target="tpu_custom_call" | custom-call | flops 2000000 | bytes 1000000 | tf_op jit(solution)/shard_map/carriers/pallas_call | solution.py:123
  89.7 1.4 %join.1 = (f32[1,32,32,128]{3,2,1,0:T(8,128)}, f32[1,32,32,128]{3,2,1,0:T(8,128)}, f32[1,32,32,128]{3,2,1,0:T(8,128)}, f32[1,32,32,128]{3,2,1,0:T(8,128)}, f32[1...) custom-call(f32[1,32,32,128]{3,2,1,0:T(8,128)} %get-tuple-element.50, ...), custom_call_target="tpu_custom_call", output_to_operand_aliasing={{0}: (0, {}), {1}: (1, {}), {2}: (2, {}), {3}: (3, {}), {4}... | custom-call | bytes 3000000 | tf_op jit(solution)/shard_map/join/pallas_call | solution.py:123
  (10 shorter events, 0.0 us)
Async XLA Ops:
  0.6 2.3 %collective-permute-start = (f32[1,32,32,128]{3,2,1,0:T(8,128)}, f32[1,32,32,128]{3,2,1,0:T(8,128)S(1)}, u32[]{:S(2)}, u32[]{:S(2)}) collective-permute-start(f32[1,32,32,128]{3,2,1,0:T(8,128)} %refs_4_.3), channel_id=1, source_target_pairs={{0,1},{1,0},{2,3},{3,2},{4,5},{5,4},{6,7},{7,6},{8,9},{9,8},{10,11... | collective-permute-start | bytes 1572872 | tf_op jit(solution)/shard_map/ppermute | solution.py:861
  1.1 2.8 %collective-permute-start.1 = (f32[1,32,32,128]{3,2,1,0:T(8,128)}, f32[1,32,32,128]{3,2,1,0:T(8,128)S(1)}, u32[]{:S(2)}, u32[]{:S(2)}) collective-permute-start(f32[1,32,32,128]{3,2,1,0:T(8,128)} %refs_5_.3), channel_id=1, source_target_pairs={{0,1},{1,0},{2,3},{3,2},{4,5},{5,4},{6,7},{7,6},{8,9},{9,8},{10,11... | collective-permute-start | bytes 1572872 | tf_op jit(solution)/shard_map/ppermute | solution.py:861
  1.2 3.2 %collective-permute-start.2 = (f32[1,32,32,128]{3,2,1,0:T(8,128)}, f32[1,32,32,128]{3,2,1,0:T(8,128)S(1)}, u32[]{:S(2)}, u32[]{:S(2)}) collective-permute-start(f32[1,32,32,128]{3,2,1,0:T(8,128)} %refs_6_.1), channel_id=1, source_target_pairs={{0,1},{1,0},{2,3},{3,2},{4,5},{5,4},{6,7},{7,6},{8,9},{9,8},{10,11... | collective-permute-start | bytes 1572872 | tf_op jit(solution)/shard_map/ppermute | solution.py:861
  1.7 3.5 %collective-permute-start.3 = (f32[1,32,32,128]{3,2,1,0:T(8,128)}, f32[1,32,32,128]{3,2,1,0:T(8,128)S(1)}, u32[]{:S(2)}, u32[]{:S(2)}) collective-permute-start(f32[1,32,32,128]{3,2,1,0:T(8,128)} %refs_7_.1), channel_id=1, source_target_pairs={{0,1},{1,0},{2,3},{3,2},{4,5},{5,4},{6,7},{7,6},{8,9},{9,8},{10,11... | collective-permute-start | bytes 1572872 | tf_op jit(solution)/shard_map/ppermute | solution.py:861
  1.7 4.2 %collective-permute-start.4 = (f32[1,32,32,128]{3,2,1,0:T(8,128)}, f32[1,32,32,128]{3,2,1,0:T(8,128)S(1)}, u32[]{:S(2)}, u32[]{:S(2)}) collective-permute-start(f32[1,32,32,128]{3,2,1,0:T(8,128)} %refs_8_.1), channel_id=1, source_target_pairs={{0,1},{1,0},{2,3},{3,2},{4,5},{5,4},{6,7},{7,6},{8,9},{9,8},{10,11... | collective-permute-start | bytes 1572872 | tf_op jit(solution)/shard_map/ppermute | solution.py:861
  2.9 3.7 %collective-permute-start.5 = (f32[1,32,32,128]{3,2,1,0:T(8,128)}, f32[1,32,32,128]{3,2,1,0:T(8,128)S(1)}, u32[]{:S(2)}, u32[]{:S(2)}) collective-permute-start(f32[1,32,32,128]{3,2,1,0:T(8,128)} %refs_9_.1), channel_id=1, source_target_pairs={{0,1},{1,0},{2,3},{3,2},{4,5},{5,4},{6,7},{7,6},{8,9},{9,8},{10,11... | collective-permute-start | bytes 1572872 | tf_op jit(solution)/shard_map/ppermute | solution.py:861
  9.4 15.6 %collective-permute-start.6 = (f32[131,8,128]{2,1,0:T(8,128)}, f32[131,8,128]{2,1,0:T(8,128)S(1)}, u32[]{:S(2)}, u32[]{:S(2)}) collective-permute-start(f32[131,8,128]{2,1,0:T(8,128)} %get-tuple-element.36), channel_id=1, source_target_pairs={{0,2},{1,3},{2,0},{3,1},{4,6},{5,7},{6,4},{7,5},{8,10},{9,11},{10,... | collective-permute-start | bytes 1609736 | tf_op jit(solution)/shard_map/ppermute | solution.py:861
  12.3 2.1 %collective-permute-start.8 = (f32[27,32,128]{2,1,0:T(8,128)}, f32[27,32,128]{2,1,0:T(8,128)S(1)}, u32[]{:S(2)}, u32[]{:S(2)}) collective-permute-start(f32[27,32,128]{2,1,0:T(8,128)} %get-tuple-element.38), channel_id=1, source_target_pairs={{1,4},{3,6},{4,1},{5,8},{6,3},{7,10},{8,5},{9,12},{10,7},{11,14},{... | collective-permute-start | bytes 1327112 | tf_op jit(solution)/shard_map/ppermute | solution.py:861
  13.0 1.4 %collective-permute-start.9 = (f32[26,32,128]{2,1,0:T(8,128)}, f32[26,32,128]{2,1,0:T(8,128)S(1)}, u32[]{:S(2)}, u32[]{:S(2)}) collective-permute-start(f32[26,32,128]{2,1,0:T(8,128)} %get-tuple-element.39), channel_id=1, source_target_pairs={{1,4},{3,6},{4,1},{5,8},{6,3},{7,10},{8,5},{9,12},{10,7},{11,14},{... | collective-permute-start | bytes 1277960 | tf_op jit(solution)/shard_map/ppermute | solution.py:861
  13.7 0.7 collective-permute-start.7
  38.2 24.0 %collective-permute-start.13 = (f32[48,32,128]{2,1,0:T(8,128)}, f32[48,32,128]{2,1,0:T(8,128)S(1)}, u32[]{:S(2)}, u32[]{:S(2)}) collective-permute-start(f32[48,32,128]{2,1,0:T(8,128)} %get-tuple-element.44), channel_id=1, source_target_pairs={{1,4},{3,6},{4,1},{5,8},{6,3},{7,10},{8,5},{9,12},{10,7},{11,14},{... | collective-permute-start | bytes 2359304 | tf_op jit(solution)/shard_map/ppermute | solution.py:861
  38.9 23.3 %collective-permute-start.14 = (f32[12,4,32,128]{3,2,1,0:T(8,128)}, f32[12,4,32,128]{3,2,1,0:T(8,128)S(1)}, u32[]{:S(2)}, u32[]{:S(2)}) collective-permute-start(f32[12,4,32,128]{3,2,1,0:T(8,128)} %get-tuple-element.45), channel_id=1, source_target_pairs={{0,1},{1,0},{2,3},{3,2},{4,5},{5,4},{6,7},{7,6},{8,9},{9,8},{10,11... | collective-permute-start | bytes 2359304 | tf_op jit(solution)/shard_map/ppermute | solution.py:861
  46.5 15.7 %collective-permute-start.10 = (f32[96,8,128]{2,1,0:T(8,128)}, f32[96,8,128]{2,1,0:T(8,128)S(1)}, u32[]{:S(2)}, u32[]{:S(2)}) collective-permute-start(f32[96,8,128]{2,1,0:T(8,128)} %get-tuple-element.41), channel_id=1, source_target_pairs={{0,2},{1,3},{2,0},{3,1},{4,6},{5,7},{6,4},{7,5},{8,10},{9,11},{10,... | collective-permute-start | bytes 1179656 | tf_op jit(solution)/shard_map/ppermute | solution.py:861
  48.0 12.5 %all-to-all-start = ((f32[16,8,128]{2,1,0:T(8,128)}), f32[16,8,128]{2,1,0:T(8,128)S(1)}, u32[]{:S(2)}, u32[]{:S(2)}) async-start(f32[16,8,128]{2,1,0:T(8,128)} %get-tuple-element.48), calls=%async_computation | async-start | bytes 131072 | tf_op jit(solution)/shard_map/all_to_all | solution.py:864
  51.5 10.7 %collective-permute-start.11 = (f32[24,8,128]{2,1,0:T(8,128)}, f32[24,8,128]{2,1,0:T(8,128)S(1)}, u32[]{:S(2)}, u32[]{:S(2)}) collective-permute-start(f32[24,8,128]{2,1,0:T(8,128)} %get-tuple-element.42), channel_id=1, source_target_pairs={{0,3},{1,2},{2,1},{3,0},{4,7},{5,6},{6,5},{7,4},{8,11},{9,10},{10,... | collective-permute-start | bytes 294920 | tf_op jit(solution)/shard_map/ppermute | solution.py:861
  53.1 9.1 %collective-permute-start.12 = (f32[24,8,128]{2,1,0:T(8,128)}, f32[24,8,128]{2,1,0:T(8,128)S(1)}, u32[]{:S(2)}, u32[]{:S(2)}) collective-permute-start(f32[24,8,128]{2,1,0:T(8,128)} %get-tuple-element.43), channel_id=1, source_target_pairs={{1,6},{3,4},{4,3},{5,10},{6,1},{7,8},{8,7},{9,14},{10,5},{11,12},{... | collective-permute-start | bytes 294920 | tf_op jit(solution)/shard_map/ppermute | solution.py:861
  75.0 14.7 %collective-permute-start.15 = (f32[6,16,32,128]{3,2,1,0:T(8,128)}, f32[6,16,32,128]{3,2,1,0:T(8,128)S(1)}, u32[]{:S(2)}, u32[]{:S(2)}) collective-permute-start(f32[6,16,32,128]{3,2,1,0:T(8,128)} %get-tuple-element.56), channel_id=1, source_target_pairs={{0,1},{1,0},{2,3},{3,2},{4,5},{5,4},{6,7},{7,6},{8,9},{9,8},{10,11... | collective-permute-start | bytes 4718600 | tf_op jit(solution)/shard_map/ppermute | solution.py:861
